TPU v7x, 32 devices: a whole 2x2x4 slice. The times are simulated.
32 devices in a mesh: pages: 16 (over z, y, x), slab: 2 (over core).
Axes of the slice: x: 2, y: 2, z: 4, core: 2. Of those that a mesh axis runs over, the one named last changes fastest.
Arguments:
- tokens: bfloat16 [32, 512, 768], P('pages', 'slab'), may hold values from -6 to 6
- boxes: int32 [32, 4, 512], P('pages'), may hold values from 0 to 1000, as said below
- lengths: int32 [32], P('pages'), may hold values from 40 to 512, as said below
- w_qkv: bfloat16 [768, 2304], replicated, may hold values from -0.21875 to 0.21875
- b_qkv: bfloat16 [2304], replicated, may hold values from -3 to 3
- w_posk: bfloat16 [256, 768], replicated, may hold values from -0.375 to 0.375
- w_posq: bfloat16 [256, 768], replicated, may hold values from -0.375 to 0.375
- w_out: bfloat16 [768, 768], replicated, may hold values from -0.75 to 0.75
- b_out: bfloat16 [768], replicated, may hold values from -2 to 2
- gain_one: bfloat16 [768], replicated, may hold values from 0.25 to 1.75
- shift_one: bfloat16 [768], replicated, may hold values from -2 to 2
- w_in: bfloat16 [768, 3072], replicated, may hold values from -0.21875 to 0.21875
- b_in: bfloat16 [3072], replicated, may hold values from -3 to 3
- w_down: bfloat16 [3072, 768], replicated, may hold values from -0.109375 to 0.109375
- b_down: bfloat16 [768], replicated, may hold values from -2 to 2
- gain_two: bfloat16 [768], replicated, may hold values from 0.25 to 1.75
- shift_two: bfloat16 [768], replicated, may hold values from -2 to 2
- cotangent: bfloat16 [32, 512, 768], P('pages', 'slab'), may hold values from -9 to 9
Outputs:
- output: bfloat16 [32, 512, 768], P('pages', 'slab')
- grad_tokens: bfloat16 [32, 512, 768], P('pages', 'slab')
- grad_w_qkv: float32 [768, 2304], P('pages')
- grad_b_qkv: float32 [2304], P('pages')
- grad_w_posk: float32 [256, 768], P('pages')
- grad_w_posq: float32 [256, 768], P('pages')
- grad_w_out: float32 [768, 768], P('pages')
- grad_b_out: float32 [768], P('pages')
- grad_gain_one: float32 [768], P('pages')
- grad_shift_one: float32 [768], P('pages')
- grad_w_in: float32 [768, 3072], P('pages')
- grad_b_in: float32 [3072], P('pages')
- grad_w_down: float32 [3072, 768], P('pages')
- grad_b_down: float32 [768], P('pages')
- grad_gain_two: float32 [768], P('pages')
- grad_shift_two: float32 [768], P('pages')
Inputs may be any that keep to these rules, and one draw needn't show every extreme that they name: `boxes`: every box has left <= right and top <= bottom. `lengths`: of the 2 pages of each index of pages, one has 512 real tokens.
All inputs are finite; a program needn't handle non-finite values.
Results may differ from a plain program's by a relative error of at most 0.02.
Values may be sent and summed in bfloat16 or wider, within the bound.
No kernel may reach another device: no remote copies, remote signals or barrier semaphores. Data moves between devices by JAX's collectives and lax.ppermute only.
A program may use at most 192 MiB of HBM per device.

v0:
```python
import math

import jax
import jax.numpy as jnp
from jax import lax
from jax.sharding import PartitionSpec as P

HEADS = 12


epsilon = 1e-06
masked_score = -1000000000.0
highest = lax.Precision.HIGHEST


def box_tables(boxes, quarter):
    rates = jnp.exp(jnp.arange(quarter, dtype=jnp.float32) * (-math.log(10000.0) / quarter))
    centre_x = (boxes[:, 0, :] + boxes[:, 2, :]).astype(jnp.float32) * 0.5
    centre_y = (boxes[:, 1, :] + boxes[:, 3, :]).astype(jnp.float32) * 0.5
    angle_x = centre_x[:, :, None] * rates
    angle_y = centre_y[:, :, None] * rates
    return (jnp.sin(angle_x), jnp.cos(angle_x), jnp.sin(angle_y), jnp.cos(angle_y))


def layer_norm(values, gain, shift):
    mean = jnp.mean(values, -1, keepdims=True)
    centred = values - mean
    variance = jnp.mean(centred * centred, -1, keepdims=True)
    return centred * lax.rsqrt(variance + epsilon) * gain + shift


def gelu_exact(values):
    return jax.nn.gelu(values, approximate=False)


def quarters(values):
    quarter = values.shape[-1] // 4
    return (
        values[..., :quarter],
        values[..., quarter : 2 * quarter],
        values[..., 2 * quarter : 3 * quarter],
        values[..., 3 * quarter :],
    )


def key_features(key_heads, pos_q, tables):
    sine_x, cosine_x, sine_y, cosine_y = tables
    sx = sine_x[:, :, None, :]
    cx = cosine_x[:, :, None, :]
    sy = sine_y[:, :, None, :]
    cy = cosine_y[:, :, None, :]
    b_mix = jnp.einsum("pjhe,khe->pjhk", key_heads, pos_q, preferred_element_type=jnp.float32)
    bxs, bxc, bys, byc = quarters(b_mix)
    return jnp.concatenate(
        [bxs * cx + bxc * sx, bxc * cx - bxs * sx, bys * cy + byc * sy, byc * cy - bys * sy], -1
    ).astype(jnp.bfloat16)


def rotate_back(d_z, tables):
    sine_x, cosine_x, sine_y, cosine_y = tables
    sx = sine_x[:, :, None, :]
    cx = cosine_x[:, :, None, :]
    sy = sine_y[:, :, None, :]
    cy = cosine_y[:, :, None, :]
    dz_one_x, dz_two_x, dz_one_y, dz_two_y = quarters(d_z)
    return jnp.concatenate(
        [
            dz_one_x * cx - dz_two_x * sx,
            dz_one_x * sx + dz_two_x * cx,
            dz_one_y * cy - dz_two_y * sy,
            dz_one_y * sy + dz_two_y * cy,
        ],
        -1,
    )


def body(
    tokens,
    boxes,
    lengths,
    w_qkv,
    b_qkv,
    w_posk,
    w_posq,
    w_out,
    b_out,
    gain_one,
    shift_one,
    w_in,
    b_in,
    w_down,
    b_down,
    gain_two,
    shift_two,
    cotangent,
):
    pages, rows, width = tokens.shape
    page_len = boxes.shape[2]
    heads = HEADS
    head_dim = width // heads
    pos_dim = w_posk.shape[0]
    scale = head_dim ** (-0.5)
    start = lax.axis_index("slab") * rows
    full_tables = box_tables(boxes, pos_dim // 4)
    own_tables = tuple((lax.dynamic_slice_in_dim(table, start, rows, 1) for table in full_tables))
    sine_x, cosine_x, sine_y, cosine_y = full_tables
    own_sx, own_cx, own_sy, own_cy = own_tables
    key_factor = jnp.concatenate([cosine_x, sine_x, cosine_y, sine_y], -1).astype(jnp.bfloat16)
    query_factor = jnp.concatenate([own_sx, own_cx, own_sy, own_cy], -1).astype(jnp.bfloat16)
    valid = jnp.arange(page_len, dtype=jnp.int32)[None, :] < lengths[:, None]
    pos_k = w_posk.reshape(pos_dim, heads, head_dim)
    pos_q = w_posq.reshape(pos_dim, heads, head_dim)
    pos_q_wide = pos_q.astype(jnp.float32)
    sxq = own_sx[:, :, None, :]
    cxq = own_cx[:, :, None, :]
    syq = own_sy[:, :, None, :]
    cyq = own_cy[:, :, None, :]
    proj = jnp.einsum(
        "prd,dc->prc", tokens, w_qkv, preferred_element_type=jnp.float32
    ) + b_qkv.astype(jnp.float32)
    proj_low = proj.astype(jnp.bfloat16)
    query = proj_low[..., :width].reshape(pages, rows, heads, head_dim)
    key_own = proj_low[..., width : 2 * width]
    value_own = proj_low[..., 2 * width :]
    key_all, value_all = (
        lax.all_gather(key_own, "slab", axis=1, tiled=True),
        lax.all_gather(value_own, "slab", axis=1, tiled=True),
    )
    key_heads = key_all.reshape(pages, page_len, heads, head_dim)
    z_all = key_features(key_heads, pos_q, full_tables)
    value_heads = value_all.reshape(pages, page_len, heads, head_dim)
    a_mix = jnp.einsum("prhe,khe->prhk", query, pos_k, preferred_element_type=jnp.float32)
    axs, axc, ays, ayc = quarters(a_mix)
    u_feat = jnp.concatenate(
        [
            axs * sxq + axc * cxq,
            axc * sxq - axs * cxq,
            ays * syq + ayc * cyq,
            ayc * syq - ays * cyq,
        ],
        -1,
    ).astype(jnp.bfloat16)

    def scores():
        text = jnp.einsum("pihe,pjhe->phij", query, key_heads, preferred_element_type=jnp.float32)
        text_pos = jnp.einsum(
            "pihk,pjk->phij", u_feat, key_factor, preferred_element_type=jnp.float32
        )
        pos_text = jnp.einsum(
            "pik,pjhk->phij", query_factor, z_all, preferred_element_type=jnp.float32
        )
        return jnp.where(
            valid[:, None, None, :], (text + text_pos + pos_text) * scale, masked_score
        )

    score = scores()
    top = jnp.max(score, -1, keepdims=True)
    log_norm = top + jnp.log(jnp.sum(jnp.exp(score - top), -1, keepdims=True))
    probs_low = jnp.exp(score - log_norm).astype(jnp.bfloat16)
    attended = jnp.einsum(
        "phij,pjhe->pihe", probs_low, value_heads, preferred_element_type=jnp.float32
    )
    attended = attended.reshape(pages, rows, width).astype(jnp.bfloat16)
    branch = jnp.einsum(
        "prd,dc->prc", attended, w_out, preferred_element_type=jnp.float32
    ) + b_out.astype(jnp.float32)
    tokens_wide = tokens.astype(jnp.float32)
    gain_one_wide = gain_one.astype(jnp.float32)
    shift_one_wide = shift_one.astype(jnp.float32)
    residual_one = tokens_wide + branch
    first = layer_norm(residual_one, gain_one_wide, shift_one_wide)
    first_low = first.astype(jnp.bfloat16)
    hidden = jnp.einsum(
        "prd,df->prf", first_low, w_in, preferred_element_type=jnp.float32
    ) + b_in.astype(jnp.float32)
    active = gelu_exact(hidden).astype(jnp.bfloat16)
    second = jnp.einsum(
        "prf,fd->prd", active, w_down, preferred_element_type=jnp.float32
    ) + b_down.astype(jnp.float32)
    residual_two = first + second
    output, norm_two_back = jax.vjp(
        layer_norm, residual_two, gain_two.astype(jnp.float32), shift_two.astype(jnp.float32)
    )
    d_res_two, g_gain_two, g_shift_two = norm_two_back(cotangent.astype(jnp.float32))
    d_second = d_res_two.astype(jnp.bfloat16)
    g_w_down = jnp.einsum("prf,prd->fd", active, d_second, preferred_element_type=jnp.float32)
    g_b_down = jnp.sum(d_second.astype(jnp.float32), (0, 1))
    d_active = jnp.einsum(
        "prd,fd->prf", d_second, w_down, preferred_element_type=jnp.float32
    ).astype(jnp.bfloat16)
    _, gelu_back = jax.vjp(gelu_exact, hidden)
    d_hidden = gelu_back(d_active.astype(jnp.float32))[0].astype(jnp.bfloat16)
    g_w_in = jnp.einsum("prd,prf->df", first_low, d_hidden, preferred_element_type=jnp.float32)
    g_b_in = jnp.sum(d_hidden.astype(jnp.float32), (0, 1))
    d_first_low = jnp.einsum(
        "prf,df->prd", d_hidden, w_in, preferred_element_type=jnp.float32
    ).astype(jnp.bfloat16)
    d_first = d_res_two + d_first_low.astype(jnp.float32)
    _, norm_one_back = jax.vjp(layer_norm, residual_one, gain_one_wide, shift_one_wide)
    d_res_one, g_gain_one, g_shift_one = norm_one_back(d_first)
    d_branch = d_res_one.astype(jnp.bfloat16)
    g_w_out = jnp.einsum("prd,prc->dc", attended, d_branch, preferred_element_type=jnp.float32)
    g_b_out = jnp.sum(d_branch.astype(jnp.float32), (0, 1))
    d_attended = jnp.einsum("prc,dc->prd", d_branch, w_out, preferred_element_type=jnp.float32)
    d_attended = d_attended.astype(jnp.bfloat16).reshape(pages, rows, heads, head_dim)
    score = scores()
    probs_wide = jnp.exp(score - log_norm)
    probs_again = probs_wide.astype(jnp.bfloat16)
    d_probs = jnp.einsum(
        "pihe,pjhe->phij", d_attended, value_heads, preferred_element_type=jnp.float32
    )
    d_score = (probs_wide * (d_probs - jnp.sum(d_probs * probs_wide, -1, keepdims=True))).astype(
        jnp.bfloat16
    )
    d_value_part = jnp.einsum(
        "phij,pihe->pjhe", probs_again, d_attended, preferred_element_type=jnp.float32
    )
    d_query_text = (
        jnp.einsum("phij,pjhe->pihe", d_score, key_heads, preferred_element_type=jnp.float32)
        * scale
    )
    d_u = (
        jnp.einsum("phij,pjk->pihk", d_score, key_factor, preferred_element_type=jnp.float32)
        * scale
    ).astype(jnp.bfloat16)
    d_key_part = (
        jnp.einsum("phij,pihe->pjhe", d_score, query, preferred_element_type=jnp.float32) * scale
    )
    d_z_part = (
        jnp.einsum("phij,pik->pjhk", d_score, query_factor, preferred_element_type=jnp.float32)
        * scale
    )
    d_key_sum, d_value_sum, d_z_sum = (
        lax.psum_scatter(
            d_key_part.reshape(pages, page_len, width).astype(jnp.bfloat16),
            "slab",
            scatter_dimension=1,
            tiled=True,
        ).astype(jnp.float32),
        lax.psum_scatter(
            d_value_part.reshape(pages, page_len, width).astype(jnp.bfloat16),
            "slab",
            scatter_dimension=1,
            tiled=True,
        ).astype(jnp.float32),
        lax.psum_scatter(
            d_z_part.reshape(pages, page_len, heads * pos_dim).astype(jnp.bfloat16),
            "slab",
            scatter_dimension=1,
            tiled=True,
        ).astype(jnp.float32),
    )
    d_b = rotate_back(d_z_sum.reshape(pages, rows, heads, pos_dim), own_tables)
    key_own_heads = key_own.reshape(pages, rows, heads, head_dim).astype(jnp.float32)
    d_key_pos = jnp.einsum("pjhk,khe->pjhe", d_b, pos_q_wide, precision=highest)
    g_w_posq = jnp.einsum("pjhk,pjhe->khe", d_b, key_own_heads, precision=highest).reshape(
        pos_dim, width
    )
    d_key = (d_key_sum + d_key_pos.reshape(pages, rows, width)).astype(jnp.bfloat16)
    d_value = d_value_sum.astype(jnp.bfloat16)
    du_one_x, du_two_x, du_one_y, du_two_y = quarters(d_u.astype(jnp.float32))
    d_a = jnp.concatenate(
        [
            du_one_x * sxq - du_two_x * cxq,
            du_one_x * cxq + du_two_x * sxq,
            du_one_y * syq - du_two_y * cyq,
            du_one_y * cyq + du_two_y * syq,
        ],
        -1,
    ).astype(jnp.bfloat16)
    d_query_pos = jnp.einsum("prhk,khe->prhe", d_a, pos_k, preferred_element_type=jnp.float32)
    g_w_posk = jnp.einsum("prhk,prhe->khe", d_a, query, preferred_element_type=jnp.float32).reshape(
        pos_dim, width
    )
    d_query = (d_query_text + d_query_pos).reshape(pages, rows, width).astype(jnp.bfloat16)
    d_proj = jnp.concatenate([d_query, d_key, d_value], -1)
    g_w_qkv = jnp.einsum("prd,prc->dc", tokens, d_proj, preferred_element_type=jnp.float32)
    g_b_qkv = jnp.sum(d_proj.astype(jnp.float32), (0, 1))
    d_tokens = d_res_one + jnp.einsum(
        "prc,dc->prd", d_proj, w_qkv, preferred_element_type=jnp.float32
    )
    parts = (
        lax.psum_scatter(g_w_qkv, "pages", scatter_dimension=0, tiled=True),
        lax.psum_scatter(g_b_qkv, "pages", scatter_dimension=0, tiled=True),
        lax.psum_scatter(g_w_posk, "pages", scatter_dimension=0, tiled=True),
        lax.psum_scatter(g_w_posq, "pages", scatter_dimension=0, tiled=True),
        lax.psum_scatter(g_w_out, "pages", scatter_dimension=0, tiled=True),
        lax.psum_scatter(g_b_out, "pages", scatter_dimension=0, tiled=True),
        lax.psum_scatter(g_gain_one, "pages", scatter_dimension=0, tiled=True),
        lax.psum_scatter(g_shift_one, "pages", scatter_dimension=0, tiled=True),
        lax.psum_scatter(g_w_in, "pages", scatter_dimension=0, tiled=True),
        lax.psum_scatter(g_b_in, "pages", scatter_dimension=0, tiled=True),
        lax.psum_scatter(g_w_down, "pages", scatter_dimension=0, tiled=True),
        lax.psum_scatter(g_b_down, "pages", scatter_dimension=0, tiled=True),
        lax.psum_scatter(g_gain_two, "pages", scatter_dimension=0, tiled=True),
        lax.psum_scatter(g_shift_two, "pages", scatter_dimension=0, tiled=True),
    )
    totals = (
        lax.psum(parts[0].astype(jnp.bfloat16), "slab").astype(jnp.float32),
        lax.psum(parts[1].astype(jnp.bfloat16), "slab").astype(jnp.float32),
        lax.psum(parts[2].astype(jnp.bfloat16), "slab").astype(jnp.float32),
        lax.psum(parts[3].astype(jnp.bfloat16), "slab").astype(jnp.float32),
        lax.psum(parts[4].astype(jnp.bfloat16), "slab").astype(jnp.float32),
        lax.psum(parts[5].astype(jnp.bfloat16), "slab").astype(jnp.float32),
        lax.psum(parts[6].astype(jnp.bfloat16), "slab").astype(jnp.float32),
        lax.psum(parts[7].astype(jnp.bfloat16), "slab").astype(jnp.float32),
        lax.psum(parts[8].astype(jnp.bfloat16), "slab").astype(jnp.float32),
        lax.psum(parts[9].astype(jnp.bfloat16), "slab").astype(jnp.float32),
        lax.psum(parts[10].astype(jnp.bfloat16), "slab").astype(jnp.float32),
        lax.psum(parts[11].astype(jnp.bfloat16), "slab").astype(jnp.float32),
        lax.psum(parts[12].astype(jnp.bfloat16), "slab").astype(jnp.float32),
        lax.psum(parts[13].astype(jnp.bfloat16), "slab").astype(jnp.float32),
    )
    return (
        output.astype(jnp.bfloat16),
        d_tokens.astype(jnp.bfloat16),
        totals[0],
        totals[1],
        totals[2],
        totals[3],
        totals[4],
        totals[5],
        totals[6],
        totals[7],
        totals[8],
        totals[9],
        totals[10],
        totals[11],
        totals[12],
        totals[13],
    )


def solution(mesh):
    return jax.shard_map(
        body,
        mesh=mesh,
        in_specs=(
            P("pages", "slab", None),
            P("pages", None, None),
            P("pages"),
            P(),
            P(),
            P(),
            P(),
            P(),
            P(),
            P(),
            P(),
            P(),
            P(),
            P(),
            P(),
            P(),
            P(),
            P("pages", "slab", None),
        ),
        out_specs=(
            P("pages", "slab", None),
            P("pages", "slab", None),
            P("pages", None),
            P("pages"),
            P("pages", None),
            P("pages", None),
            P("pages", None),
            P("pages"),
            P("pages"),
            P("pages"),
            P("pages", None),
            P("pages"),
            P("pages", None),
            P("pages"),
            P("pages"),
            P("pages"),
        ),
        check_vma=False,
    )
```

profile of v0, /device:TPU:1, one launch (start us, length us, event | category | flops | bytes accessed | tf_op | source)
XLA Modules:
  0.0 1156.4 jit_solution(6088040077680928997)
XLA Ops:
  9.2 3.1 fusion.35
  27.6 3.8 fusion.80
  34.9 2.4 copy.172
  40.9 5.6 fusion.39
  46.5 2.6 copy.173
  49.1 8.2 fusion.104
  59.2 4.3 add_convert_fusion.1
  63.5 18.0 %fusion.101 = (f32[2,12,256]{2,1,0:T(8,128)}, f32[2,12,256,512]{3,2,1,0:T(8,128)}) fusion(bf16[2,256,64]{1,2,0:T(8,128)(2,1)} %get-tuple-element.126, bf16[2,256,64]{1,2,0:T(8,128)(2,1)} %get-tuple-element.124, bf16[2,256,64]{1,2,0:T(8,128)(2,1)} %get-tuple-element.122, bf16[2,256,64]{1,2,0:T(8,128)(2,1)} %get-tuple-element.120, ...), kind=kOutput, calls=%fused_computation.189 | convolution fusion | flops 1652549632 | bytes 44327936 | tf_op jit(solution)/shard_map/pik,pjhk->phij/dot_general | solution.py:149
  81.5 7.2 exponential_reduce_fusion
  89.4 2.8 copy.171
  92.2 6.6 fusion.66
  100.2 7.1 fusion.59
  107.3 15.0 %multiply_convert_fusion.3 = (bf16[2,256,3072]{2,1,0:T(8,128)(2,1)S(1)}, f32[2,256,3072]{2,1,0:T(8,128)S(1)}) fusion(f32[2,256,3072]{2,1,0:T(8,128)S(1)} %get-tuple-element.182, f32[3072]{0:T(1024)S(1)} %convert_element_type.269, u8[256,3072]{1,0:T(8,128)(4,1)S(1)} %get-tuple-element.81, u8[256,3072]{1,0:T(8,128)(4,1)S(1)} %get-tuple-element.80), kind=kLoop, calls=%fused_computation.37 | loop fusion | flops 111673344 | bytes 17313792 | tf_op jit(solution)/shard_map/convert_element_type | solution.py:176
  122.4 6.3 fusion.103
  133.5 8.9 convert_reduce_fusion
  142.5 7.7 multiply_reduce_fusion.1
  155.5 2.4 copy.185
  157.8 11.9 %multiply_reduce_fusion = (f32[2,12,256]{2,1,0:T(8,128)S(1)}, f32[2,12,256,512]{3,2,1,0:T(8,128)}) fusion(f32[2,12,256,512]{3,2,1,0:T(8,128)} %get-tuple-element.179, f32[2,12,256]{2,1,0:T(8,128)} %log_add_fusion, bf16[2,256,12,64]{1,3,2,0:T(8,128)(2,1)} %bitcast.184, bf16[2,512,12,64]{1,3,2,0:T(8,128)(2,1)} %bitcast.182), kind=kOutput, calls=%fused_computation.6 | convolution fusion | flops 412084224 | bytes 27574272 | tf_op jit(solution)/shard_map/pihe,pjhe->phij/dot_general | solution.py:209
  171.2 6.4 multiply_convert_fusion.1
  177.6 4.5 multiply_convert_fusion
  182.2 5.4 multiply_convert_fusion.4
  187.5 2.7 copy.188
  190.3 10.4 convolution_convert_fusion
  200.6 2.6 copy.196
  203.3 3.6 convolution_bitcast_fusion.5
  207.1 9.4 convolution_bitcast_fusion.2
  216.8 8.4 convolution_bitcast_fusion.1
  225.3 6.5 fusion.105
  231.8 7.4 convert_bitcast_fusion
  239.2 2.9 fusion.99
  243.0 3.7 subtract_convert_fusion.3
  252.8 4.7 convolution_bitcast_fusion.6
  258.8 3.1 copy.195
  261.8 2.7 add_convert_fusion.3
  264.5 6.7 convolution_bitcast_fusion
  271.3 8.1 copy.235
  279.6 4.1 fusion.41
  288.4 7.3 fusion.11
  298.1 59.2 %reduce-scatter.22.cloned.1.call-done = f32[48,768]{1,0:T(8,128)} async-done(((f32[768,768]{1,0:T(8,128)}), f32[48,768]{1,0:T(8,128)}) %reduce-scatter.22.cloned.1.call-update) | async-done | bytes 147472 | tf_op jit(solution)/shard_map/reduce_scatter | solution.py:287
  358.9 174.7 %reduce-scatter.24.cloned.1.call-done = f32[48,3072]{1,0:T(8,128)} async-done(((f32[768,3072]{1,0:T(8,128)}), f32[48,3072]{1,0:T(8,128)}) %reduce-scatter.24.cloned.1.call-update) | async-done | bytes 589840 | tf_op jit(solution)/shard_map/reduce_scatter | solution.py:291
  535.4 174.9 %reduce-scatter.26.cloned.1.call-done = f32[192,768]{1,0:T(8,128)} async-done(((f32[3072,768]{1,0:T(8,128)}), f32[192,768]{1,0:T(8,128)}) %reduce-scatter.26.cloned.1.call-update) | async-done | bytes 589840 | tf_op jit(solution)/shard_map/reduce_scatter | solution.py:293
  712.1 153.5 %reduce-scatter.28.cloned.1.call-done = f32[48,2304]{1,0:T(8,128)} async-done(((f32[768,2304]{1,0:T(8,128)}), f32[48,2304]{1,0:T(8,128)}) %reduce-scatter.28.cloned.1.call-update) | async-done | bytes 442384
  872.2 61.9 %all-reduce.8 = (bf16[2304]{0:T(1024)(128)(2,1)}, bf16[768]{0:T(1024)(128)(2,1)}, bf16[768]{0:T(1024)(128)(2,1)}, bf16[768]{0:T(1024)(128)(2,1)}, bf16[3072]{0:T...) all-reduce(f32[2304]{0:T(1024)S(1)} %convert_reduce_fusion.1, ...), channel_id=6, replica_groups=mesh['pages'=16,'slab'=2] {'pages'}, use_global_device_ids=true, to_apply=%region_17.18.clone | all-reduce | flops 9984 | bytes 59904
  942.2 5.0 add_convert_fusion.2
  947.2 43.9 %reduce-scatter.18.cloned.1.call-done = f32[16,768]{1,0:T(8,128)} async-done(((f32[256,768]{1,0:T(8,128)}), f32[16,768]{1,0:T(8,128)}) %reduce-scatter.18.cloned.1.call-update) | async-done | bytes 49168 | tf_op jit(solution)/shard_map/reduce_scatter | solution.py:285
  992.5 124.8 %reduce-scatter.20.cloned.1.call-done = f32[16,768]{1,0:T(8,128)} async-done(((f32[256,768]{1,0:T(8,128)}), f32[16,768]{1,0:T(8,128)}) %reduce-scatter.20.cloned.1.call-update) | async-done | bytes 49168 | tf_op jit(solution)/shard_map/reduce_scatter | solution.py:286
  1118.6 6.9 all-reduce.9
  1137.5 4.5 all-reduce.13.cloned.1.call-done
  (248 shorter events, 95.6 us)
Async XLA Ops:
  7.2 39.3 %all-gather.5.cloned.1.call-start = ((), (), s32[]{:S(2)}) async-start(), calls=%async_computation.10 | async-start | bytes 2359296 | tf_op jit(solution)/shard_map/all_gather | solution.py:126
  12.3 4.2 copy-start.58
  12.4 4.8 copy-start.59
  12.4 4.8 copy-start.60
  12.4 5.3 copy-start.61
  13.9 75.5 %all-gather.3.cloned.1.call-start = ((), (), s32[]{:S(2)}) async-start(), calls=%async_computation.9 | async-start | bytes 2359296 | tf_op jit(solution)/shard_map/all_gather | solution.py:127
  14.6 224.6 %reduce-scatter.14.cloned.1.call-start = ((), (), s32[]{:S(2)}) async-start(), calls=%async_computation.12 | async-start | bytes 9437184 | tf_op jit(solution)/shard_map/reduce_scatter | solution.py:246
  49.1 8.2 copy-start.3
  49.1 8.2 copy-start.21
  81.5 7.2 copy-start.36
  92.2 6.6 copy-start.57
  92.2 6.6 copy-start.62
  92.2 6.6 copy-start.64
  99.8 22.6 %copy-start.6 = (f32[2,256,768]{2,1,0:T(8,128)}, f32[2,256,768]{2,1,0:T(8,128)S(1)}, u32[]{:S(2)}) copy-start(f32[2,256,768]{2,1,0:T(8,128)S(1)} %get-tuple-element.181) | copy-start | bytes 4718596
  99.8 50.4 %copy-start.45 = (f32[2,256]{1,0:T(2,128)}, f32[2,256]{1,0:T(2,128)S(1)}, u32[]{:S(2)}) copy-start(f32[2,256]{1,0:T(2,128)S(1)} %broadcast_multiply_fusion.1) | copy-start | bytes 6148
  100.2 50.1 %copy-start.51 = (f32[2,256]{1,0:T(2,128)}, f32[2,256]{1,0:T(2,128)S(1)}, u32[]{:S(2)}) copy-start(f32[2,256]{1,0:T(2,128)S(1)} %fusion.86) | copy-start | bytes 6148
  107.3 15.1 %copy-start.56 = (f32[768]{0:T(1024)S(1)}, f32[768]{0:T(1024)}, u32[]{:S(2)}) copy-start(f32[768]{0:T(1024)} %convert_element_type.271) | copy-start | bytes 9220
  122.4 6.3 copy-start.12
  122.4 6.3 copy-start.4
  133.5 9.0 copy-start.31
  142.5 7.8 copy-start.7
  157.8 11.9 %slice-start = ((s8[12582912]{0:T(1024)(128)(4,1)}), s8[4194304]{0:T(1024)(128)(4,1)S(1)}, s32[]{:S(2)}) async-start(s8[12582912]{0:T(1024)(128)(4,1)} %bitcast.171), calls=%async_computation.21 | async-start | bytes 8388608
  157.8 11.9 %slice-start.1 = ((s8[12582912]{0:T(1024)(128)(4,1)}), s8[4194304]{0:T(1024)(128)(4,1)S(1)}, s32[]{:S(2)}) async-start(s8[12582912]{0:T(1024)(128)(4,1)} %bitcast.171), calls=%async_computation.22 | async-start | bytes 8388608
  157.8 13.3 %slice-start.2 = ((s8[12582912]{0:T(1024)(128)(4,1)}), s8[4194304]{0:T(1024)(128)(4,1)S(1)}, s32[]{:S(2)}) async-start(s8[12582912]{0:T(1024)(128)(4,1)} %bitcast.171), calls=%async_computation.23 | async-start | bytes 8388608
  157.8 13.3 %copy-start.30 = (f32[2,12,256]{2,1,0:T(8,128)S(1)}, f32[2,12,256]{2,1,0:T(8,128)}, u32[]{:S(2)}) copy-start(f32[2,12,256]{2,1,0:T(8,128)} %log_add_fusion) | copy-start | bytes 73732
  171.1 6.4 copy-start.32
  171.1 6.4 copy-start.33
  171.1 6.4 copy-start.34
  171.2 6.4 copy-start.35
  177.6 4.5 copy-start.1
  182.1 79.7 %reduce-scatter.12.cloned.1.call-start = ((), (), s32[]{:S(2)}) async-start(), calls=%async_computation.11 | async-start | bytes 2359296 | tf_op jit(solution)/shard_map/reduce_scatter | solution.py:234
  190.2 74.3 %reduce-scatter.16.cloned.1.call-start = ((), (), s32[]{:S(2)}) async-start(), calls=%async_computation.13 | async-start | bytes 2359296 | tf_op jit(solution)/shard_map/reduce_scatter | solution.py:240
  203.3 154.1 %reduce-scatter.22.cloned.1.call-start = ((), (), s32[]{:S(2)}) async-start(), calls=%async_computation.16 | async-start | bytes 2506752 | tf_op jit(solution)/shard_map/reduce_scatter | solution.py:287
  207.0 326.6 %reduce-scatter.24.cloned.1.call-start = ((), (), s32[]{:S(2)}) async-start(), calls=%async_computation.17 | async-start | bytes 10027008 | tf_op jit(solution)/shard_map/reduce_scatter | solution.py:291
  216.5 493.8 %reduce-scatter.26.cloned.1.call-start = ((), (), s32[]{:S(2)}) async-start(), calls=%async_computation.18 | async-start | bytes 10027008 | tf_op jit(solution)/shard_map/reduce_scatter | solution.py:293
  225.2 640.3 %reduce-scatter.28.cloned.1.call-start = ((), (), s32[]{:S(2)}) async-start(), calls=%async_computation.19 | async-start | bytes 7520256
  225.3 6.6 copy-start.38
  225.3 6.5 copy-start.40
  225.3 6.5 copy-start.42
  225.3 6.5 copy-start.44
  239.2 3.8 slice-start.4
  239.2 3.8 copy-start.23
  239.2 3.8 copy-start.25
  279.3 711.7 %reduce-scatter.18.cloned.1.call-start = ((), (), s32[]{:S(2)}) async-start(), calls=%async_computation.14 | async-start | bytes 835584 | tf_op jit(solution)/shard_map/reduce_scatter | solution.py:285
  286.1 831.1 %reduce-scatter.20.cloned.1.call-start = ((), (), s32[]{:S(2)}) async-start(), calls=%async_computation.15 | async-start | bytes 835584 | tf_op jit(solution)/shard_map/reduce_scatter | solution.py:286
  295.7 571.9 %copy-start.65 = (u32[32]{0:T(128)S(1)}, u32[32]{0:T(128)}, u32[]{:S(2)}) copy-start(u32[32]{0:T(128)} %constant.106) | copy-start | bytes 388
  298.1 844.0 %all-reduce.13.cloned.1.call-start = ((), (), s32[]{:S(2)}) async-start(), calls=%async_computation.20 | async-start | bytes 2506752 | tf_op jit(solution)/shard_map/psum | solution.py:299
  358.9 513.3 %copy-start.47 = (f32[768]{0:T(1024)S(1)}, f32[768]{0:T(1024)}, u32[]{:S(2)}) copy-start(f32[768]{0:T(1024)} %get-tuple-element.89) | copy-start | bytes 9220
  (35 other events, 76.7 us)
Sparse Core Ops, SparseCore 0:
  14.0 12.2 all-gather.4
  27.8 10.9 all-gather.2
  182.2 16.9 reduce-scatter.13
  201.5 10.2 reduce-scatter.11
  213.8 10.2 reduce-scatter.15
  229.7 127.6 reduce-scatter.21
  363.0 170.4 reduce-scatter.23
  540.2 169.9 reduce-scatter.25
  715.6 149.9 reduce-scatter.27
  870.1 120.8 reduce-scatter.17
  995.8 121.4 reduce-scatter.19
  1120.8 21.1 all-reduce.12
where the time goes:
time: 1160 us
  waiting for transfers between devices  736 us (63%)
  matrix products  175 us (15%)
  other arithmetic  90.8 us (8%)
  blocking collectives  68.8 us (6%)
  local copies, waits for them, and re-layouts  67.1 us (6%)
  between operations  17.3 us (1%)
    reduce_scatter x1, waiting for transfers between devices, body(): lax.psum_scatter(g_w_down, 'pages', scatter_dimension=0, tiled=True)  175 us
    reduce_scatter x1, waiting for transfers between devices, body(): lax.psum_scatter(g_w_in, 'pages', scatter_dimension=0, tiled=True)  175 us
    unnamed x13, waiting for transfers between devices  154 us
    reduce_scatter x1, waiting for transfers between devices, body(): lax.psum_scatter(g_w_posq, 'pages', scatter_dimension=0, tiled=True)  125 us
    unnamed x1, blocking collectives  61.9 us
    reduce_scatter x1, waiting for transfers between devices, body(): lax.psum_scatter(g_w_out, 'pages', scatter_dimension=0, tiled=True)  59.2 us
    reduce_scatter x1, waiting for transfers between devices, body(): lax.psum_scatter(g_w_posk, 'pages', scatter_dimension=0, tiled=True)  43.9 us
    unnamed x157, local copies, waits for them, and re-layouts  33.8 us
  transfers between devices with their start and end apart: 12, of which 7 were waited for; matrix products, arithmetic and copies ran while one was open for 19% of the time, Pallas kernels for 0%

commit v1 on v0

v1 whole, which is shorter than its diff:
```python
import math

import jax
import jax.numpy as jnp
from jax import lax
from jax.sharding import PartitionSpec as P

HEADS = 12

epsilon = 1e-06
masked_score = -1000000000.0


def box_tables(boxes, quarter):
    rates = jnp.exp(jnp.arange(quarter, dtype=jnp.float32) * (-math.log(10000.0) / quarter))
    centre_x = (boxes[0] + boxes[2]).astype(jnp.float32) * 0.5
    centre_y = (boxes[1] + boxes[3]).astype(jnp.float32) * 0.5
    angle_x = centre_x[:, None] * rates
    angle_y = centre_y[:, None] * rates
    return (jnp.sin(angle_x), jnp.cos(angle_x), jnp.sin(angle_y), jnp.cos(angle_y))


def layer_norm(values, gain, shift):
    mean = jnp.mean(values, -1, keepdims=True)
    centred = values - mean
    variance = jnp.mean(centred * centred, -1, keepdims=True)
    return centred * lax.rsqrt(variance + epsilon) * gain + shift


def gelu_exact(values):
    return jax.nn.gelu(values, approximate=False)


def quarters(values):
    quarter = values.shape[-1] // 4
    return (
        values[..., :quarter],
        values[..., quarter : 2 * quarter],
        values[..., 2 * quarter : 3 * quarter],
        values[..., 3 * quarter :],
    )


def dot(spec, a, b):
    return jnp.einsum(spec, a, b, preferred_element_type=jnp.float32)


def swap(x):
    return lax.ppermute(x, "slab", [(0, 1), (1, 0)])


def own_page(x, core):
    mine = lax.dynamic_index_in_dim(x, core, 0, keepdims=False)
    other = swap(lax.dynamic_index_in_dim(x, 1 - core, 0, keepdims=False))
    return jnp.where(
        core == 0, jnp.concatenate([mine, other], 0), jnp.concatenate([other, mine], 0)
    )


def own_rows(x, core):
    x = x.reshape(2, x.shape[0] // 2, x.shape[1])
    mine = lax.dynamic_index_in_dim(x, core, 0, keepdims=False)
    other = swap(lax.dynamic_index_in_dim(x, 1 - core, 0, keepdims=False))
    return jnp.where(core == 0, jnp.stack([mine, other], 0), jnp.stack([other, mine], 0))


def scatter_sum(g, place, order):
    n, r, c = g.shape
    left = list(range(n.bit_length() - 2, -1, -1))
    acc = g.reshape((2,) * len(left) + (r, c))
    for bit in order:
        axis = left.index(bit)
        mine = (place >> bit) & 1
        send = lax.dynamic_index_in_dim(acc, 1 - mine, axis, keepdims=False)
        keep = lax.dynamic_index_in_dim(acc, mine, axis, keepdims=False)
        got = lax.ppermute(send, "pages", [(i, i ^ (1 << bit)) for i in range(n)])
        acc = (keep.astype(jnp.float32) + got.astype(jnp.float32)).astype(jnp.bfloat16)
        left.remove(bit)
    return acc


def orders(bits):
    low = list(range(bits - 1))
    return [low[i:] + low[:i] + [bits - 1] for i in range(3)]


def reduce_grad(g, place, core, n):
    rows, cols = g.shape
    halves = g.astype(jnp.bfloat16).reshape(n, rows // n, 2, cols // 2)
    keep = lax.dynamic_index_in_dim(halves, core, 2, keepdims=False)
    got = swap(lax.dynamic_index_in_dim(halves, 1 - core, 2, keepdims=False))
    acc = (keep.astype(jnp.float32) + got.astype(jnp.float32)).astype(jnp.bfloat16)
    width = cols // 6
    parts = [
        scatter_sum(acc[:, :, i * width : (i + 1) * width], place, order)
        for i, order in enumerate(orders(n.bit_length() - 1))
    ]
    mine = jnp.concatenate(parts, -1)
    other = swap(mine)
    return jnp.where(
        core == 0, jnp.concatenate([mine, other], -1), jnp.concatenate([other, mine], -1)
    ).astype(jnp.float32)


def body(
    n,
    tokens,
    boxes,
    lengths,
    w_qkv,
    b_qkv,
    w_posk,
    w_posq,
    w_out,
    b_out,
    gain_one,
    shift_one,
    w_in,
    b_in,
    w_down,
    b_down,
    gain_two,
    shift_two,
    cotangent,
):
    f32, bf16 = jnp.float32, jnp.bfloat16
    place, core = lax.axis_index("pages"), lax.axis_index("slab")
    tokens = own_page(tokens, core)
    cotangent = own_page(cotangent, core)
    boxes = lax.dynamic_index_in_dim(boxes, core, 0, keepdims=False)
    length = lax.dynamic_index_in_dim(lengths, core, 0, keepdims=False)
    rows, width = tokens.shape
    heads = HEADS
    head_dim = width // heads
    pos_dim = w_posk.shape[0]
    scale = head_dim ** (-0.5)
    sx, cx, sy, cy = box_tables(boxes, pos_dim // 4)
    key_factor = jnp.concatenate([cx, sx, cy, sy], -1).astype(bf16)
    query_factor = jnp.concatenate([sx, cx, sy, cy], -1).astype(bf16)
    sx, cx, sy, cy = (t[:, None, :] for t in (sx, cx, sy, cy))
    valid = jnp.arange(rows, dtype=jnp.int32) < length
    pos_k = w_posk.reshape(pos_dim, heads, head_dim)
    pos_q = w_posq.reshape(pos_dim, heads, head_dim)
    proj = (dot("rd,dc->rc", tokens, w_qkv) + b_qkv.astype(f32)).astype(bf16)
    query = proj[:, :width].reshape(rows, heads, head_dim)
    key = proj[:, width : 2 * width].reshape(rows, heads, head_dim)
    value = proj[:, 2 * width :].reshape(rows, heads, head_dim)
    bxs, bxc, bys, byc = quarters(dot("jhe,khe->jhk", key, pos_q))
    z = jnp.concatenate(
        [bxs * cx + bxc * sx, bxc * cx - bxs * sx, bys * cy + byc * sy, byc * cy - bys * sy], -1
    ).astype(bf16)
    axs, axc, ays, ayc = quarters(dot("ihe,khe->ihk", query, pos_k))
    u = jnp.concatenate(
        [axs * sx + axc * cx, axc * sx - axs * cx, ays * sy + ayc * cy, ayc * sy - ays * cy], -1
    ).astype(bf16)
    shape = (rows, heads, pos_dim)
    left = jnp.concatenate(
        [query, u, jnp.broadcast_to(query_factor[:, None, :], shape)], -1
    )
    right = jnp.concatenate([key, jnp.broadcast_to(key_factor[:, None, :], shape), z], -1)
    score = jnp.where(valid[None, None, :], dot("ihk,jhk->hij", left, right) * scale, masked_score)
    probs = jax.nn.softmax(score, -1).astype(bf16)
    attended = dot("hij,jhe->ihe", probs, value).reshape(rows, width).astype(bf16)
    branch = dot("rd,dc->rc", attended, w_out) + b_out.astype(f32)
    gain_one, shift_one = gain_one.astype(f32), shift_one.astype(f32)
    residual_one = tokens.astype(f32) + branch
    first = layer_norm(residual_one, gain_one, shift_one)
    first_low = first.astype(bf16)
    hidden = dot("rd,df->rf", first_low, w_in) + b_in.astype(f32)
    active = gelu_exact(hidden).astype(bf16)
    second = dot("rf,fd->rd", active, w_down) + b_down.astype(f32)
    output, norm_two_back = jax.vjp(
        layer_norm, first + second, gain_two.astype(f32), shift_two.astype(f32)
    )
    d_res_two, g_gain_two, g_shift_two = norm_two_back(cotangent.astype(f32))
    d_second = d_res_two.astype(bf16)
    g_w_down = dot("rf,rd->fd", active, d_second)
    g_b_down = jnp.sum(d_second.astype(f32), 0)
    d_active = dot("rd,fd->rf", d_second, w_down).astype(bf16)
    _, gelu_back = jax.vjp(gelu_exact, hidden)
    d_hidden = gelu_back(d_active.astype(f32))[0].astype(bf16)
    g_w_in = dot("rd,rf->df", first_low, d_hidden)
    g_b_in = jnp.sum(d_hidden.astype(f32), 0)
    d_first = d_res_two + dot("rf,df->rd", d_hidden, w_in).astype(bf16).astype(f32)
    _, norm_one_back = jax.vjp(layer_norm, residual_one, gain_one, shift_one)
    d_res_one, g_gain_one, g_shift_one = norm_one_back(d_first)
    d_branch = d_res_one.astype(bf16)
    g_w_out = dot("rd,rc->dc", attended, d_branch)
    g_b_out = jnp.sum(d_branch.astype(f32), 0)
    d_attended = dot("rc,dc->rd", d_branch, w_out).astype(bf16).reshape(rows, heads, head_dim)
    d_probs = dot("ihe,jhe->hij", d_attended, value)
    probs_wide = probs.astype(f32)
    d_score = (probs_wide * (d_probs - jnp.sum(d_probs * probs_wide, -1, keepdims=True))).astype(
        bf16
    )
    d_value = dot("hij,ihe->jhe", probs, d_attended).astype(bf16)
    d_query_text = dot("hij,jhe->ihe", d_score, key) * scale
    d_u = (dot("hij,jk->ihk", d_score, key_factor) * scale).astype(bf16)
    d_key_text = dot("hij,ihe->jhe", d_score, query) * scale
    d_z = dot("hij,ik->jhk", d_score, query_factor) * scale
    zx1, zx2, zy1, zy2 = quarters(d_z)
    d_b = jnp.concatenate(
        [zx1 * cx - zx2 * sx, zx1 * sx + zx2 * cx, zy1 * cy - zy2 * sy, zy1 * sy + zy2 * cy], -1
    ).astype(bf16)
    ux1, ux2, uy1, uy2 = quarters(d_u.astype(f32))
    d_a = jnp.concatenate(
        [ux1 * sx - ux2 * cx, ux1 * cx + ux2 * sx, uy1 * sy - uy2 * cy, uy1 * cy + uy2 * sy], -1
    ).astype(bf16)
    d_key = (d_key_text + dot("jhk,khe->jhe", d_b, pos_q)).astype(bf16)
    d_query = (d_query_text + dot("ihk,khe->ihe", d_a, pos_k)).astype(bf16)
    g_w_posq = dot("jhk,jhe->khe", d_b, key).reshape(pos_dim, width)
    g_w_posk = dot("ihk,ihe->khe", d_a, query).reshape(pos_dim, width)
    d_proj = jnp.concatenate(
        [x.reshape(rows, width) for x in (d_query, d_key, d_value)], -1
    )
    g_w_qkv = dot("rd,rc->dc", tokens, d_proj)
    g_b_qkv = jnp.sum(d_proj.astype(f32), 0)
    d_tokens = d_res_one + dot("rc,dc->rd", d_proj, w_qkv)
    big = [
        reduce_grad(g, place, core, n)
        for g in (g_w_down, g_w_in, g_w_out, g_w_posk, g_w_posq, g_w_qkv)
    ]
    small = (
        g_b_qkv, g_b_out, g_gain_one, g_shift_one, g_b_in, g_b_down, g_gain_two, g_shift_two
    )
    packed = jnp.concatenate([g.reshape(n, -1) for g in small], -1)
    packed = lax.psum(packed, ("pages", "slab"))
    packed = lax.dynamic_index_in_dim(packed, place, 0, keepdims=False)
    totals, at = [], 0
    for g in small:
        totals.append(packed[at : at + g.size // n])
        at += g.size // n
    return (
        own_rows(output.astype(bf16), core),
        own_rows(d_tokens.astype(bf16), core),
        big[5],
        totals[0],
        big[3],
        big[4],
        big[2],
        totals[1],
        totals[2],
        totals[3],
        big[1],
        totals[4],
        big[0],
        totals[5],
        totals[6],
        totals[7],
    )


def solution(mesh):
    import functools

    n = mesh.shape["pages"]
    rows = P("pages", "slab", None)
    mat, vec = P("pages", None), P("pages")
    return jax.shard_map(
        functools.partial(body, n),
        mesh=mesh,
        in_specs=(rows, P("pages", None, None), P("pages")) + (P(),) * 14 + (rows,),
        out_specs=(rows, rows, mat, vec, mat, mat, mat, vec, vec, vec, mat, vec, mat, vec, vec, vec),
        check_vma=False,
    )
```

time: 1160 us -> 588 us (0.51)
  waiting for transfers between devices: 736 us -> 68.8 us
  starting transfers between devices: 0.96 us -> 137 us
  local copies, waits for them, and re-layouts: 67.1 us -> 147 us
  matrix products: 175 us -> 114 us
  blocking collectives: 68.8 us -> 41.8 us
  other arithmetic: 90.8 us -> 65.6 us
  between operations: 17.3 us -> 3.07 us
    reduce_scatter x8 -> x0, waiting for transfers between devices: 577 us -> none  [the longest x1 175 us: body(): lax.psum_scatter(g_w_down, 'pages', scatter_dimension=0, tiled=True)]
    unnamed x13 -> x0, waiting for transfers between devices: 154 us -> none
    ppermute x0 -> x88, starting transfers between devices: none -> 137 us  [the longest x72 85.8 us: scatter_sum(): got = lax.ppermute(send, 'pages', [(i, i ^ 1 << bit) for i in range(n)])]
    dot_general x28 -> x25, matrix products: 175 us -> 99.8 us  [dot(): return jnp.einsum(spec, a, b, preferred_element_type=jnp.float32)]
    ppermute x0 -> x88, waiting for transfers between devices: none -> 68.8 us  [the longest x72 67.7 us: scatter_sum(): got = lax.ppermute(send, 'pages', [(i, i ^ 1 << bit) for i in range(n)])]
    unnamed x1 -> x0, blocking collectives: 61.9 us -> none
    dynamic_slice x0 -> x33, local copies, waits for them, and re-layouts: none -> 48.2 us  [the longest x4 45.1 us: reduce_grad(): keep = lax.dynamic_index_in_dim(halves, core, 2, keepdims=False)]
    psum x1, blocking collectives: 6.91 us -> 41.8 us  [body(): packed = lax.psum(packed, ('pages', 'slab'))]
  transfers between devices with their start and end apart: 12 -> 88, of which waited for: 7 -> 49; matrix products, arithmetic and copies ran while one was open for 19% -> 41% of each run, Pallas kernels for 0% -> 0%
where the time goes in v1:
time: 588 us; the launch traced here: 578 us
  local copies, waits for them, and re-layouts  147 us (25%)
  starting transfers between devices  137 us (23%)
  matrix products  114 us (19%)
  waiting for transfers between devices  68.8 us (12%)
  other arithmetic  65.6 us (11%)
  blocking collectives  41.8 us (7%)
    dot_general x25, matrix products, dot(): return jnp.einsum(spec, a, b, preferred_element_type=jnp.float32)  99.8 us
    ppermute x72, starting transfers between devices, scatter_sum(): got = lax.ppermute(send, 'pages', [(i, i ^ 1 << bit) for i in range(n)])  85.8 us
    ppermute x72, waiting for transfers between devices, scatter_sum(): got = lax.ppermute(send, 'pages', [(i, i ^ 1 << bit) for i in range(n)])  67.7 us
    ppermute x16, starting transfers between devices, swap(): return lax.ppermute(x, 'slab', [(0, 1), (1, 0)])  51.6 us
    dynamic_slice x4, local copies, waits for them, and re-layouts, reduce_grad(): keep = lax.dynamic_index_in_dim(halves, core, 2, keepdims=False)  45.1 us
    psum x1, blocking collectives, body(): packed = lax.psum(packed, ('pages', 'slab'))  41.8 us
    reshape x4, local copies, waits for them, and re-layouts, reduce_grad(): halves = g.astype(jnp.bfloat16).reshape(n, rows // n, 2, cols // 2)  33.3 us
    unnamed x157, local copies, waits for them, and re-layouts  22.3 us
  transfers between devices with their start and end apart: 88, of which 49 were waited for; matrix products, arithmetic and copies ran while one was open for 41% of the time, Pallas kernels for 0%

profile of v1, /device:TPU:1, one launch (start us, length us, event | category | flops | bytes accessed | tf_op | source)
XLA Modules:
  0.0 578.3 jit_solution(1420125887899697931)
XLA Ops:
  20.1 2.5 fusion.101
  23.6 3.4 fusion.22
  28.4 2.3 copy.115
  30.7 2.3 copy.113
  36.5 2.3 convolution_bitcast_fusion.1
  45.1 2.5 copy-done.47
  47.6 2.9 copy-done.46
  50.5 14.6 %fusion.211 = (f32[12,512]{1,0:T(8,128)}, f32[12,512,512]{1,2,0:T(8,128)}) fusion(pred[512]{0:T(512)(128)(4,1)S(1)} %copy-done.58, bf16[512,12,576]{0,2,1:T(8,128)(2,1)} %copy-done.46, bf16[512,12,576]{0,2,1:T(8,128)(2,1)} %copy-done.47), kind=kOutput, calls=%fused_computation.578 | convolution fusion | flops 3636462080 | bytes 26763776 | tf_op jit(solution)/shard_map/sub | solution.py:162
  65.1 9.1 %divide_convert_fusion = bf16[12,512,512]{1,2,0:T(8,128)(2,1)} fusion(f32[12,512,512]{1,2,0:T(8,128)} %get-tuple-element.143, f32[12,512]{1,0:T(8,128)} %get-tuple-element.142), kind=kLoop, calls=%fused_computation.5 | loop fusion | flops 6291456 | bytes 18898944 | tf_op jit(solution)/shard_map/convert_element_type | solution.py:162
  74.2 4.0 convolution_convert_fusion.8
  80.9 19.9 %multiply_convert_fusion.1 = (bf16[512,3072]{1,0:T(8,128)(2,1)S(1)}, f32[512,3072]{1,0:T(8,128)}, f32[512,3072]{1,0:T(8,128)}) fusion(f32[3072]{0:T(1024)S(1)} %copy-done.50, bf16[768,3072]{1,0:T(8,128)(2,1)} %param.29, f32[512,768]{1,0:T(8,128)S(1)} %get-tuple-element.145, f32[768]{0:T(1024)S(1)} %copy-done.51, f32[768]{0:T(1024)S(1)} %convert_element_type.1147, ...), kind=kOutput, calls=%fused_computation.24 | convolution fusion | flops 2521694208 | bytes 22042624 | tf_op jit(solution)/shard_map/rd,df->rf/dot_general | solution.py:45
  100.9 2.8 fusion.213
  106.0 3.0 fusion.202
  109.8 9.5 %convert_reduce_fusion = (f32[3072]{0:T(1024)}, bf16[512,3072]{1,0:T(8,128)(2,1)}) fusion(f32[512,3072]{1,0:T(8,128)} %get-tuple-element.31, bf16[512,768]{1,0:T(8,128)(2,1)S(1)} %get-tuple-element.23, bf16[3072,768]{1,0:T(8,128)(2,1)S(1)} %bitcast.717, f32[512,3072]{1,0:T(8,128)} %get-tuple-element.146, f32[3072]{0:T(1024)S(1)} %copy-done.50), kind=kOutput, calls=%fused_computation.21 | convolution fusion | flops 2445800448 | bytes 21258240 | tf_op jit(solution)/shard_map/rd,fd->rf/dot_general | solution.py:45
  119.3 5.8 %multiply_reduce_fusion = (f32[768]{0:T(1024)}, f32[512]{0:T(512)S(1)}, f32[768]{0:T(1024)}, f32[512,768]{1,0:T(8,128)S(1)}) fusion(f32[512,768]{1,0:T(8,128)S(1)} %get-tuple-element.145, f32[512]{0:T(512)S(1)} %fusion.190, f32[512]{0:T(512)S(1)} %broadcast_multiply_fusion.1, f32[768]{0:T(1024)S(1)} %copy-done.49, ...), kind=kOutput, calls=%fused_computation.79 | convolution fusion | flops 2420635648 | bytes 12600320 | tf_op jit(solution)/shard_map/rf,df->rd/dot_general | solution.py:45
  125.1 5.2 convolution_convert_fusion.1
  136.4 4.3 convolution_convert_fusion
  140.7 2.3 copy.118
  143.1 5.2 convolution_convert_fusion.6
  148.3 9.6 %fusion.1 = (f32[12,512]{1,0:T(8,128)S(1)}, f32[12,512,512]{1,2,0:T(8,128)}) fusion(bf16[12,512,512]{1,2,0:T(8,128)(2,1)} %divide_convert_fusion, bf16[512,12,64]{0,2,1:T(8,128)(2,1)S(1)} %bitcast.655, bf16[512,12,64]{0,2,1:T(8,128)(2,1)S(1)} %bitcast.653), kind=kOutput, calls=%fused_computation.3 | convolution fusion | flops 412084224 | bytes 20471808 | tf_op jit(solution)/shard_map/ihe,jhe->hij/dot_general | solution.py:45
  157.9 7.0 %fusion.2 = bf16[12,512,512]{1,2,0:T(8,128)(2,1)S(1)} fusion(f32[12,512,512]{1,2,0:T(8,128)} %get-tuple-element.151, f32[12,512]{1,0:T(8,128)S(1)} %get-tuple-element.150, f32[12,512,512]{1,2,0:T(8,128)S(1)} %bitcast.639, f32[12,512]{1,0:T(8,128)S(1)} %copy-done.45), kind=kLoop, calls=%fused_computation.4 | loop fusion | flops 18874368 | bytes 31506432 | tf_op jit(solution)/shard_map/convert_element_type | solution.py:193
  180.4 3.0 add_convert_fusion
  188.9 11.8 %reshape.684 = bf16[16,48,2,1536]{3,2,1,0:T(2,128)(2,1)} reshape(bf16[768,3072]{1,0:T(8,128)(2,1)} %convolution_convert_fusion.1) | data formatting | bytes 9437184 | tf_op jit(solution)/shard_map/reshape | solution.py:89
  204.7 3.6 reshape.680
  208.3 5.1 constant_dynamic-slice_fusion.33
  214.8 10.1 %reshape.688 = bf16[16,192,2,384]{3,2,1,0:T(2,128)(2,1)} reshape(bf16[3072,768]{1,0:T(8,128)(2,1)} %convolution_convert_fusion) | data formatting | bytes 9437184 | tf_op jit(solution)/shard_map/reshape | solution.py:89
  224.9 13.1 %constant_dynamic-slice_fusion.9 = (bf16[16,192,1,384]{3,2,1,0:T(2,128)(2,1)}, bf16[16,192,1,384]{3,2,1,0:T(2,128)(2,1)S(1)}) fusion(bf16[16,192,2,384]{3,2,1,0:T(2,128)(2,1)} %reshape.688, s32[]{:T(128)S(6)} %select_n.307, s32[]{:T(128)S(6)} %select_n.308), kind=kLoop, calls=%fused_computation.327 | loop fusion | bytes 9437192 | tf_op jit(solution)/shard_map/jit(dynamic_index_in_dim)/dynamic_slice | solution.py:90
  240.0 13.6 %constant_dynamic-slice_fusion.15 = (bf16[16,48,1,1536]{3,2,1,0:T(2,128)(2,1)}, bf16[16,48,1,1536]{3,2,1,0:T(2,128)(2,1)S(1)}) fusion(bf16[16,48,2,1536]{3,2,1,0:T(2,128)(2,1)} %reshape.684, s32[]{:T(128)S(6)} %select_n.307, s32[]{:T(128)S(6)} %select_n.308), kind=kLoop, calls=%fused_computation.333 | loop fusion | bytes 9437192 | tf_op jit(solution)/shard_map/jit(dynamic_index_in_dim)/dynamic_slice | solution.py:90
  259.5 41.8 %psum.7 = f32[16,624]{1,0:T(8,128)} all-reduce(f32[16,624]{1,0:T(8,128)} %concatenate.134), channel_id=1, replica_groups=mesh['pages'=16,'slab'=2] {'pages','slab'}, use_global_device_ids=true, to_apply=%region_19.20 | all-reduce | flops 9984 | bytes 79872 | tf_op jit(solution)/shard_map/psum | solution.py:227
  301.3 5.9 %convolution_convert_fusion.2 = bf16[768,2304]{1,0:T(8,128)(2,1)} fusion(bf16[512,768]{0,1:T(8,128)(2,1)} %bitcast.667, bf16[512,768]{0,1:T(8,128)(2,1)} %bitcast.689, bf16[512,768]{0,1:T(8,128)(2,1)} %bitcast.686, bf16[256,768]{1,0:T(8,128)(2,1)} %collective-permute-done, bf16[256,768]{1,0:T(8,128)(2,1)} %get-tuple-element.79, pred[]{:T(512)S(6)} %eq.2), kind=kOutput, calls=%fused_computation.43 | convolution fusion | flops 1824325632 | bytes 6684673 | tf_op jit(solution)/shard_map/rd,rc->dc/dot_general | solution.py:45
  307.3 7.8 %reshape.662 = bf16[16,48,2,1152]{3,2,1,0:T(2,128)(2,1)} reshape(bf16[768,2304]{1,0:T(8,128)(2,1)} %convolution_convert_fusion.2) | data formatting | bytes 7077888 | tf_op jit(solution)/shard_map/reshape | solution.py:89
  316.6 2.9 copy.139
  319.5 2.7 convert_element_type.1291
  322.2 2.9 copy.133
  325.1 2.9 convert_element_type.1235
  328.0 3.7 constant_dynamic-slice_fusion.58
  333.1 13.3 %constant_dynamic-slice_fusion.95 = (bf16[16,48,1,1152]{3,2,1,0:T(2,128)(2,1)}, bf16[16,48,1,1152]{3,2,1,0:T(2,128)(2,1)}) fusion(bf16[16,48,2,1152]{3,2,1,0:T(2,128)(2,1)} %reshape.662, s32[]{:T(128)S(6)} %select_n.307, s32[]{:T(128)S(6)} %select_n.308), kind=kLoop, calls=%fused_computation.413 | loop fusion | bytes 7077896 | tf_op jit(solution)/shard_map/jit(dynamic_index_in_dim)/dynamic_slice | solution.py:90
  346.4 2.3 copy.273
  423.4 27.3 %collective-permute-start.31 = (bf16[16,384]{1,0:T(8,128)(2,1)S(1)}, bf16[16,384]{1,0:T(8,128)(2,1)S(1)}, u32[]{:S(2)}, u32[]{:S(2)}) collective-permute-start(bf16[16,384]{1,0:T(8,128)(2,1)S(1)} %pad_maximum_fusion.13), channel_id=1, source_target_pairs={{0,1},{1,0},{2,3},{3,2},{4,5},{5,4},{6,7},{7,6},{8,9},{9,8},{10,11... | collective-permute-start | bytes 36872 | tf_op jit(solution)/shard_map/ppermute | solution.py:49
  482.0 6.9 %collective-permute-start.59 = (bf16[48,384]{1,0:T(8,128)(2,1)S(1)}, bf16[48,384]{1,0:T(8,128)(2,1)S(1)}, u32[]{:S(2)}, u32[]{:S(2)}) collective-permute-start(bf16[48,384]{1,0:T(8,128)(2,1)S(1)} %pad_maximum_fusion.12), channel_id=1, source_target_pairs={{0,1},{1,0},{2,3},{3,2},{4,5},{5,4},{6,7},{7,6},{8,9},{9,8},{10,11... | collective-permute-start | bytes 110600 | tf_op jit(solution)/shard_map/ppermute | solution.py:49
  493.2 4.9 collective-permute-done.5
  514.9 2.7 collective-permute-start.17
  517.6 2.5 fusion.20
  526.2 7.1 %collective-permute-done.79 = bf16[2,2,2,192,128]{4,3,0,2,1:T(8,128)(2,1)S(1)} collective-permute-done((bf16[2,2,2,192,128]{4,3,0,2,1:T(8,128)(2,1)S(1)}, bf16[2,2,2,192,128]{4,3,0,2,1:T(8,128)(2,1)S(1)}, u32[]{:S(2)}, u32[]{:S(2)}) %collective-permute-start.79) | collective-permute-done | bytes 393248 | tf_op jit(solution)/shard_map/ppermute | solution.py:76
  535.8 4.8 collective-permute-done.61
  544.6 2.4 collective-permute-done.76
  564.6 7.4 %collective-permute-start.87 = (bf16[192,384]{1,0:T(8,128)(2,1)S(1)}, bf16[192,384]{1,0:T(8,128)(2,1)S(1)}, u32[]{:S(2)}, u32[]{:S(2)}) collective-permute-start(bf16[192,384]{1,0:T(8,128)(2,1)S(1)} %pad_maximum_fusion.10), channel_id=1, source_target_pairs={{0,1},{1,0},{2,3},{3,2},{4,5},{5,4},{6,7},{7,6},{8,9},{9,8},{10,11... | collective-permute-start | bytes 442376 | tf_op jit(solution)/shard_map/ppermute | solution.py:49
  572.1 3.4 collective-permute-start.73
  (573 shorter events, 238.7 us)
Async XLA Ops:
  2.9 20.6 %collective-permute-start = (bf16[256,768]{1,0:T(8,128)(2,1)}, bf16[256,768]{1,0:T(8,128)(2,1)}, u32[]{:S(2)}, u32[]{:S(2)}) collective-permute-start(bf16[256,768]{1,0:T(8,128)(2,1)} %get-tuple-element.80), channel_id=1, source_target_pairs={{0,1},{1,0},{2,3},{3,2},{4,5},{5,4},{6,7},{7,6},{8,9},{9,8},{10,11... | collective-permute-start | bytes 1179656 | tf_op jit(solution)/shard_map/ppermute | solution.py:49
  5.0 99.0 %collective-permute-start.2 = (bf16[256,768]{1,0:T(8,128)(2,1)}, bf16[256,768]{1,0:T(8,128)(2,1)}, u32[]{:S(2)}, u32[]{:S(2)}) collective-permute-start(bf16[256,768]{1,0:T(8,128)(2,1)} %get-tuple-element.75), channel_id=1, source_target_pairs={{0,1},{1,0},{2,3},{3,2},{4,5},{5,4},{6,7},{7,6},{8,9},{9,8},{10,11... | collective-permute-start | bytes 1179656 | tf_op jit(solution)/shard_map/ppermute | solution.py:49
  186.7 267.0 %collective-permute-start.1 = (bf16[256,768]{1,0:T(8,128)(2,1)}, bf16[256,768]{1,0:T(8,128)(2,1)}, u32[]{:S(2)}, u32[]{:S(2)}) collective-permute-start(bf16[256,768]{1,0:T(8,128)(2,1)} %get-tuple-element.78), channel_id=1, source_target_pairs={{0,1},{1,0},{2,3},{3,2},{4,5},{5,4},{6,7},{7,6},{8,9},{9,8},{10,11... | collective-permute-start | bytes 1179656 | tf_op jit(solution)/shard_map/ppermute | solution.py:49
  214.3 243.8 %collective-permute-start.46 = (bf16[16,48,384]{2,1,0:T(8,128)(2,1)}, bf16[16,48,384]{2,1,0:T(8,128)(2,1)}, u32[]{:S(2)}, u32[]{:S(2)}) collective-permute-start(bf16[16,48,384]{2,1,0:T(8,128)(2,1)} %bitcast.622), channel_id=1, source_target_pairs={{0,1},{1,0},{2,3},{3,2},{4,5},{5,4},{6,7},{7,6},{8,9},{9,8},{10,11... | collective-permute-start | bytes 1769480 | tf_op jit(solution)/shard_map/ppermute | solution.py:49
  240.0 277.6 %collective-permute-start.74 = (bf16[16,192,384]{2,1,0:T(8,128)(2,1)}, bf16[16,192,384]{2,1,0:T(8,128)(2,1)}, u32[]{:S(2)}, u32[]{:S(2)}) collective-permute-start(bf16[16,192,384]{2,1,0:T(8,128)(2,1)} %bitcast.619), channel_id=1, source_target_pairs={{0,1},{1,0},{2,3},{3,2},{4,5},{5,4},{6,7},{7,6},{8,9},{9,8},{10,11... | collective-permute-start | bytes 7077896 | tf_op jit(solution)/shard_map/ppermute | solution.py:49
  315.1 140.9 %collective-permute-start.3 = (bf16[256,768]{1,0:T(8,128)(2,1)}, bf16[256,768]{1,0:T(8,128)(2,1)}, u32[]{:S(2)}, u32[]{:S(2)}) collective-permute-start(bf16[256,768]{1,0:T(8,128)(2,1)} %get-tuple-element.74), channel_id=1, source_target_pairs={{0,1},{1,0},{2,3},{3,2},{4,5},{5,4},{6,7},{7,6},{8,9},{9,8},{10,11... | collective-permute-start | bytes 1179656 | tf_op jit(solution)/shard_map/ppermute | solution.py:49
  333.1 19.9 %collective-permute-start.18 = (bf16[16,16,384]{2,1,0:T(8,128)(2,1)}, bf16[16,16,384]{2,1,0:T(8,128)(2,1)}, u32[]{:S(2)}, u32[]{:S(2)}) collective-permute-start(bf16[16,16,384]{2,1,0:T(8,128)(2,1)} %bitcast.630), channel_id=1, source_target_pairs={{0,1},{1,0},{2,3},{3,2},{4,5},{5,4},{6,7},{7,6},{8,9},{9,8},{10,11... | collective-permute-start | bytes 589832 | tf_op jit(solution)/shard_map/ppermute | solution.py:49
  423.4 28.2 %collective-permute-start.31 = (bf16[16,384]{1,0:T(8,128)(2,1)S(1)}, bf16[16,384]{1,0:T(8,128)(2,1)S(1)}, u32[]{:S(2)}, u32[]{:S(2)}) collective-permute-start(bf16[16,384]{1,0:T(8,128)(2,1)S(1)} %pad_maximum_fusion.13), channel_id=1, source_target_pairs={{0,1},{1,0},{2,3},{3,2},{4,5},{5,4},{6,7},{7,6},{8,9},{9,8},{10,11... | collective-permute-start | bytes 36872 | tf_op jit(solution)/shard_map/ppermute | solution.py:49
  452.7 71.4 %collective-permute-start.60 = (bf16[16,48,1536]{2,1,0:T(8,128)(2,1)S(1)}, bf16[16,48,1536]{2,1,0:T(8,128)(2,1)S(1)}, u32[]{:S(2)}, u32[]{:S(2)}) collective-permute-start(bf16[16,48,1536]{2,1,0:T(8,128)(2,1)S(1)} %bitcast.670), channel_id=1, source_target_pairs={{0,1},{1,0},{2,3},{3,2},{4,5},{5,4},{6,7},{7,6},{8,9},{9,8},{10,11... | collective-permute-start | bytes 7077896 | tf_op jit(solution)/shard_map/ppermute | solution.py:49
  453.7 35.2 %collective-permute-start.4 = (bf16[16,48,1152]{2,1,0:T(8,128)(2,1)S(1)}, bf16[16,48,1152]{2,1,0:T(8,128)(2,1)S(1)}, u32[]{:S(2)}, u32[]{:S(2)}) collective-permute-start(bf16[16,48,1152]{2,1,0:T(8,128)(2,1)S(1)} %bitcast.675), channel_id=1, source_target_pairs={{0,1},{1,0},{2,3},{3,2},{4,5},{5,4},{6,7},{7,6},{8,9},{9,8},{10,11... | collective-permute-start | bytes 5308424 | tf_op jit(solution)/shard_map/ppermute | solution.py:49
  459.7 4.1 collective-permute-start.47
  482.0 8.9 %collective-permute-start.59 = (bf16[48,384]{1,0:T(8,128)(2,1)S(1)}, bf16[48,384]{1,0:T(8,128)(2,1)S(1)}, u32[]{:S(2)}, u32[]{:S(2)}) collective-permute-start(bf16[48,384]{1,0:T(8,128)(2,1)S(1)} %pad_maximum_fusion.12), channel_id=1, source_target_pairs={{0,1},{1,0},{2,3},{3,2},{4,5},{5,4},{6,7},{7,6},{8,9},{9,8},{10,11... | collective-permute-start | bytes 110600 | tf_op jit(solution)/shard_map/ppermute | solution.py:49
  489.5 8.7 %collective-permute-start.5 = (bf16[2,2,2,48,384]{4,3,2,1,0:T(8,128)(2,1)S(1)}, bf16[2,2,2,48,384]{4,3,2,1,0:T(8,128)(2,1)S(1)}, u32[]{:S(2)}, u32[]{:S(2)}) collective-permute-start(bf16[2,2,2,48,384]{4,3,2,1,0:T(8,128)(2,1)S(1)} %dynamic-slice_bitcast_fusion.8), channel_id=1, source_target_pairs={{0,2},{2,0},{4,6},{6,4},{8,10},{10,8},{12,14},{14,12},{16,18},{18,... | collective-permute-start | bytes 884744 | tf_op jit(solution)/shard_map/ppermute | solution.py:76
  491.8 8.3 %collective-permute-start.9 = (bf16[2,2,2,48,384]{4,3,0,2,1:T(8,128)(2,1)S(1)}, bf16[2,2,2,48,384]{4,3,0,2,1:T(8,128)(2,1)S(1)}, u32[]{:S(2)}, u32[]{:S(2)}) collective-permute-start(bf16[2,2,2,48,384]{4,3,0,2,1:T(8,128)(2,1)S(1)} %bitcast.696), channel_id=1, source_target_pairs={{0,4},{2,6},{4,0},{6,2},{8,12},{10,14},{12,8},{14,10},{16,20},{18,... | collective-permute-start | bytes 884744 | tf_op jit(solution)/shard_map/ppermute | solution.py:76
  492.1 8.4 %collective-permute-start.13 = (bf16[2,2,2,48,384]{4,3,0,1,2:T(8,128)(2,1)S(1)}, bf16[2,2,2,48,384]{4,3,0,1,2:T(8,128)(2,1)S(1)}, u32[]{:S(2)}, u32[]{:S(2)}) collective-permute-start(bf16[2,2,2,48,384]{4,3,0,1,2:T(8,128)(2,1)S(1)} %bitcast.695), channel_id=1, source_target_pairs={{0,8},{2,10},{4,12},{6,14},{8,0},{10,2},{12,4},{14,6},{16,24},{18,... | collective-permute-start | bytes 884744 | tf_op jit(solution)/shard_map/ppermute | solution.py:76
  498.3 4.6 collective-permute-start.6
  500.6 4.4 collective-permute-start.14
  504.4 4.3 collective-permute-start.11
  505.0 4.6 collective-permute-start.15
  506.9 4.4 collective-permute-start.8
  508.8 4.2 collective-permute-start.12
  509.7 5.1 collective-permute-start.16
  514.9 60.6 %collective-permute-start.17 = (bf16[48,1152]{1,0:T(8,128)(2,1)S(1)}, bf16[48,1152]{1,0:T(8,128)(2,1)S(1)}, u32[]{:S(2)}, u32[]{:S(2)}) collective-permute-start(bf16[48,1152]{1,0:T(8,128)(2,1)S(1)} %pad_maximum_fusion.11), channel_id=1, source_target_pairs={{0,1},{1,0},{2,3},{3,2},{4,5},{5,4},{6,7},{7,6},{8,9},{9,8},{10,11... | collective-permute-start | bytes 331784 | tf_op jit(solution)/shard_map/ppermute | solution.py:49
  520.9 12.8 %collective-permute-start.75 = (bf16[2,2,2,192,128]{4,3,2,1,0:T(8,128)(2,1)S(1)}, bf16[2,2,2,192,128]{4,3,2,1,0:T(8,128)(2,1)S(1)}, u32[]{:S(2)}, u32[]{:S(2)}) collective-permute-start(bf16[2,2,2,192,128]{4,3,2,1,0:T(8,128)(2,1)S(1)} %dynamic-slice_bitcast_fusion), channel_id=1, source_target_pairs={{0,2},{2,0},{4,6},{6,4},{8,10},{10,8},{12,14},{14,12},{16,18},{18,... | collective-permute-start | bytes 1179656 | tf_op jit(solution)/shard_map/ppermute | solution.py:76
  522.8 10.5 %collective-permute-start.79 = (bf16[2,2,2,192,128]{4,3,0,2,1:T(8,128)(2,1)S(1)}, bf16[2,2,2,192,128]{4,3,0,2,1:T(8,128)(2,1)S(1)}, u32[]{:S(2)}, u32[]{:S(2)}) collective-permute-start(bf16[2,2,2,192,128]{4,3,0,2,1:T(8,128)(2,1)S(1)} %bitcast.694), channel_id=1, source_target_pairs={{0,4},{2,6},{4,0},{6,2},{8,12},{10,14},{12,8},{14,10},{16,20},{18,... | collective-permute-start | bytes 1179656 | tf_op jit(solution)/shard_map/ppermute | solution.py:76
  522.9 11.9 %collective-permute-start.83 = (bf16[2,2,2,192,128]{4,3,0,1,2:T(8,128)(2,1)S(1)}, bf16[2,2,2,192,128]{4,3,0,1,2:T(8,128)(2,1)S(1)}, u32[]{:S(2)}, u32[]{:S(2)}) collective-permute-start(bf16[2,2,2,192,128]{4,3,0,1,2:T(8,128)(2,1)S(1)} %bitcast.691), channel_id=1, source_target_pairs={{0,8},{2,10},{4,12},{6,14},{8,0},{10,2},{12,4},{14,6},{16,24},{18,... | collective-permute-start | bytes 1179656 | tf_op jit(solution)/shard_map/ppermute | solution.py:76
  525.5 15.1 %collective-permute-start.61 = (bf16[2,2,2,48,512]{4,3,2,1,0:T(8,128)(2,1)S(1)}, bf16[2,2,2,48,512]{4,3,2,1,0:T(8,128)(2,1)S(1)}, u32[]{:S(2)}, u32[]{:S(2)}) collective-permute-start(bf16[2,2,2,48,512]{4,3,2,1,0:T(8,128)(2,1)S(1)} %dynamic-slice_bitcast_fusion.1), channel_id=1, source_target_pairs={{0,2},{2,0},{4,6},{6,4},{8,10},{10,8},{12,14},{14,12},{16,18},{18,... | collective-permute-start | bytes 1179656 | tf_op jit(solution)/shard_map/ppermute | solution.py:76
  533.3 9.5 %collective-permute-start.65 = (bf16[2,2,2,48,512]{4,3,0,2,1:T(8,128)(2,1)S(1)}, bf16[2,2,2,48,512]{4,3,0,2,1:T(8,128)(2,1)S(1)}, u32[]{:S(2)}, u32[]{:S(2)}) collective-permute-start(bf16[2,2,2,48,512]{4,3,0,2,1:T(8,128)(2,1)S(1)} %bitcast.693), channel_id=1, source_target_pairs={{0,4},{2,6},{4,0},{6,2},{8,12},{10,14},{12,8},{14,10},{16,20},{18,... | collective-permute-start | bytes 1179656 | tf_op jit(solution)/shard_map/ppermute | solution.py:76
  533.7 9.8 %collective-permute-start.69 = (bf16[2,2,2,48,512]{4,3,0,1,2:T(8,128)(2,1)S(1)}, bf16[2,2,2,48,512]{4,3,0,1,2:T(8,128)(2,1)S(1)}, u32[]{:S(2)}, u32[]{:S(2)}) collective-permute-start(bf16[2,2,2,48,512]{4,3,0,1,2:T(8,128)(2,1)S(1)} %bitcast.692), channel_id=1, source_target_pairs={{0,8},{2,10},{4,12},{6,14},{8,0},{10,2},{12,4},{14,6},{16,24},{18,... | collective-permute-start | bytes 1179656 | tf_op jit(solution)/shard_map/ppermute | solution.py:76
  534.8 12.1 %collective-permute-start.76 = (bf16[2,2,192,128]{3,2,1,0:T(8,128)(2,1)S(1)}, bf16[2,2,192,128]{3,2,1,0:T(8,128)(2,1)S(1)}, u32[]{:S(2)}, u32[]{:S(2)}) collective-permute-start(bf16[2,2,192,128]{3,2,1,0:T(8,128)(2,1)S(1)} %dynamic-slice_bitcast_fusion.11), channel_id=1, source_target_pairs={{0,4},{2,6},{4,0},{6,2},{8,12},{10,14},{12,8},{14,10},{16,20},{18,... | collective-permute-start | bytes 589832 | tf_op jit(solution)/shard_map/ppermute | solution.py:76
  540.6 7.3 %collective-permute-start.80 = (bf16[2,2,192,128]{3,2,0,1:T(8,128)(2,1)S(1)}, bf16[2,2,192,128]{3,2,0,1:T(8,128)(2,1)S(1)}, u32[]{:S(2)}, u32[]{:S(2)}) collective-permute-start(bf16[2,2,192,128]{3,2,0,1:T(8,128)(2,1)S(1)} %dynamic-slice_bitcast_fusion.10), channel_id=1, source_target_pairs={{0,8},{2,10},{4,12},{6,14},{8,0},{10,2},{12,4},{14,6},{16,24},{18,... | collective-permute-start | bytes 589832 | tf_op jit(solution)/shard_map/ppermute | solution.py:76
  542.7 6.2 %collective-permute-start.84 = (bf16[2,2,192,128]{3,2,0,1:T(8,128)(2,1)S(1)}, bf16[2,2,192,128]{3,2,0,1:T(8,128)(2,1)S(1)}, u32[]{:S(2)}, u32[]{:S(2)}) collective-permute-start(bf16[2,2,192,128]{3,2,0,1:T(8,128)(2,1)S(1)} %dynamic-slice_bitcast_fusion.9), channel_id=1, source_target_pairs={{0,2},{2,0},{4,6},{6,4},{8,10},{10,8},{12,14},{14,12},{16,18},{18,... | collective-permute-start | bytes 589832 | tf_op jit(solution)/shard_map/ppermute | solution.py:76
  543.5 7.6 %collective-permute-start.62 = (bf16[2,2,48,512]{3,2,1,0:T(8,128)(2,1)S(1)}, bf16[2,2,48,512]{3,2,1,0:T(8,128)(2,1)S(1)}, u32[]{:S(2)}, u32[]{:S(2)}) collective-permute-start(bf16[2,2,48,512]{3,2,1,0:T(8,128)(2,1)S(1)} %dynamic-slice_bitcast_fusion.14), channel_id=1, source_target_pairs={{0,4},{2,6},{4,0},{6,2},{8,12},{10,14},{12,8},{14,10},{16,20},{18,... | collective-permute-start | bytes 589832 | tf_op jit(solution)/shard_map/ppermute | solution.py:76
  547.0 4.8 collective-permute-start.66
  547.9 6.0 %collective-permute-start.70 = (bf16[2,2,48,512]{3,2,0,1:T(8,128)(2,1)S(1)}, bf16[2,2,48,512]{3,2,0,1:T(8,128)(2,1)S(1)}, u32[]{:S(2)}, u32[]{:S(2)}) collective-permute-start(bf16[2,2,48,512]{3,2,0,1:T(8,128)(2,1)S(1)} %dynamic-slice_bitcast_fusion.12), channel_id=1, source_target_pairs={{0,2},{2,0},{4,6},{6,4},{8,10},{10,8},{12,14},{14,12},{16,18},{18,... | collective-permute-start | bytes 589832 | tf_op jit(solution)/shard_map/ppermute | solution.py:76
  548.9 5.0 collective-permute-start.77
  551.2 4.5 collective-permute-start.81
  553.8 4.6 collective-permute-start.63
  553.9 5.4 collective-permute-start.67
  555.7 5.3 collective-permute-start.71
  555.8 6.1 %collective-permute-start.78 = (bf16[192,128]{1,0:T(8,128)(2,1)S(1)}, bf16[192,128]{1,0:T(8,128)(2,1)S(1)}, u32[]{:S(2)}, u32[]{:S(2)}) collective-permute-start(bf16[192,128]{1,0:T(8,128)(2,1)S(1)} %dynamic-slice_bitcast_fusion.30), channel_id=1, source_target_pairs={{0,16},{2,18},{4,20},{6,22},{8,24},{10,26},{12,28},{14,30},{16,0},... | collective-permute-start | bytes 147464 | tf_op jit(solution)/shard_map/ppermute | solution.py:76
  558.5 5.1 collective-permute-start.82
  559.3 5.2 collective-permute-start.86
  561.0 10.9 %collective-permute-start.64 = (bf16[48,512]{1,0:T(8,128)(2,1)S(1)}, bf16[48,512]{1,0:T(8,128)(2,1)S(1)}, u32[]{:S(2)}, u32[]{:S(2)}) collective-permute-start(bf16[48,512]{1,0:T(8,128)(2,1)S(1)} %dynamic-slice_bitcast_fusion.33), channel_id=1, source_target_pairs={{0,16},{2,18},{4,20},{6,22},{8,24},{10,26},{12,28},{14,30},{16,0},... | collective-permute-start | bytes 147464 | tf_op jit(solution)/shard_map/ppermute | solution.py:76
  562.0 10.0 %collective-permute-start.68 = (bf16[48,512]{1,0:T(8,128)(2,1)S(1)}, bf16[48,512]{1,0:T(8,128)(2,1)S(1)}, u32[]{:S(2)}, u32[]{:S(2)}) collective-permute-start(bf16[48,512]{1,0:T(8,128)(2,1)S(1)} %dynamic-slice_bitcast_fusion.32), channel_id=1, source_target_pairs={{0,16},{2,18},{4,20},{6,22},{8,24},{10,26},{12,28},{14,30},{16,0},... | collective-permute-start | bytes 147464 | tf_op jit(solution)/shard_map/ppermute | solution.py:76
  563.6 8.4 %collective-permute-start.72 = (bf16[48,512]{1,0:T(8,128)(2,1)S(1)}, bf16[48,512]{1,0:T(8,128)(2,1)S(1)}, u32[]{:S(2)}, u32[]{:S(2)}) collective-permute-start(bf16[48,512]{1,0:T(8,128)(2,1)S(1)} %dynamic-slice_bitcast_fusion.31), channel_id=1, source_target_pairs={{0,16},{2,18},{4,20},{6,22},{8,24},{10,26},{12,28},{14,30},{16,0},... | collective-permute-start | bytes 147464 | tf_op jit(solution)/shard_map/ppermute | solution.py:76
  564.6 11.7 %collective-permute-start.87 = (bf16[192,384]{1,0:T(8,128)(2,1)S(1)}, bf16[192,384]{1,0:T(8,128)(2,1)S(1)}, u32[]{:S(2)}, u32[]{:S(2)}) collective-permute-start(bf16[192,384]{1,0:T(8,128)(2,1)S(1)} %pad_maximum_fusion.10), channel_id=1, source_target_pairs={{0,1},{1,0},{2,3},{3,2},{4,5},{5,4},{6,7},{7,6},{8,9},{9,8},{10,11... | collective-permute-start | bytes 442376 | tf_op jit(solution)/shard_map/ppermute | solution.py:49
  572.1 5.1 collective-permute-start.73
  (113 other events, 1087.5 us)

commit v2 on v1

v2 whole, which is shorter than its diff:
```python
import functools
import math

import jax
import jax.numpy as jnp
import numpy as np
from jax import lax
from jax.experimental import pallas as pl
from jax.experimental.pallas import tpu as pltpu
from jax.sharding import PartitionSpec as P

F32, BF16 = jnp.float32, jnp.bfloat16
HEADS = 12
PAIRS = HEADS // 2
BIG = 1e9
SDS = jax.ShapeDtypeStruct


def mm(a, b):
    return lax.dot_general(a, b, (((1,), (0,)), ((), ())), preferred_element_type=F32)


def mm_nt(a, b):
    return lax.dot_general(a, b, (((1,), (1,)), ((), ())), preferred_element_type=F32)


def whole(shape):
    return pl.BlockSpec(shape, lambda *_: (0,) * len(shape))


def call(kernel, name, grid, ids, args, in_specs, out_specs, out_shape, scratch=(), vmem=40, flops=0, moved=0):
    return pl.pallas_call(
        kernel,
        grid_spec=pltpu.PrefetchScalarGridSpec(
            num_scalar_prefetch=1, grid=grid, in_specs=in_specs, out_specs=out_specs, scratch_shapes=list(scratch)
        ),
        out_shape=out_shape,
        compiler_params=pltpu.CompilerParams(vmem_limit_bytes=vmem << 20),
        cost_estimate=pl.CostEstimate(flops=flops, bytes_accessed=moved, transcendentals=0),
        name=name,
    )(ids, *args)


def sin_cos(angle):
    turns = jnp.round(angle * (2.0 / math.pi))
    r = angle - turns * 1.5703125
    r = r - turns * 4.837512969970703125e-4
    r = r - turns * 7.54978995489188216e-8
    z = r * r
    s = ((-1.9515295891e-4 * z + 8.3321608736e-3) * z - 1.6666654611e-1) * z * r + r
    c = (
        (2.443315711809948e-5 * z - 1.388731625493765e-3) * z + 4.166664568298827e-2
    ) * z * z + (1.0 - 0.5 * z)
    q = turns.astype(jnp.int32)
    odd = (q & 1) == 1
    one, two = jnp.where(odd, c, s), jnp.where(odd, s, c)
    sine = jnp.where((q & 2) == 2, -one, one)
    cosine = jnp.where(((q + 1) & 2) == 2, -two, two)
    return sine, cosine


def project_kernel(ids, own_ref, other_ref, w_ref, b_ref, box_ref, rrow_ref, rcol_ref, wk_ref, wq_ref,
                   pt_ref, p_ref, xt_ref, kf_ref, tab_ref, tabt_ref, fkt_ref, fqt_ref, wkt_ref, wqt_ref, x):
    step = pl.program_id(0)

    @pl.when(step == 0)
    def _():
        half = own_ref.shape[1]
        x[:half, :] = own_ref[0]
        x[half:, :] = other_ref[0]
        xt_ref[...] = x[...].T
        wkt_ref[...] = wk_ref[...].T
        wqt_ref[...] = wq_ref[...].T
        box = box_ref[0].astype(F32)
        centre = (box[0:2, :] + box[2:4, :]) * 0.5
        turned = jnp.concatenate([centre[:, half:], centre[:, :half]], 1)
        centre = jnp.where(ids[1] == 0, centre, turned)
        column = jnp.concatenate([centre, jnp.zeros((6, 2 * half), F32)], 0).T
        front = lax.broadcasted_iota(jnp.int32, (2 * half, 128), 1) < 64
        for axis in range(2):
            s, c = sin_cos(column[:, axis : axis + 1] * rrow_ref[...])
            kf_ref[:, axis * 128 : axis * 128 + 128] = jnp.where(front, c, s).astype(BF16)
            tab_ref[axis] = c
            tab_ref[2 + axis] = jnp.where(front, s, -s)
            st, ct = sin_cos(rcol_ref[...] * centre[axis : axis + 1, :])
            tabt_ref[2 * axis] = st
            tabt_ref[2 * axis + 1] = ct
            sl, cl = st.astype(BF16), ct.astype(BF16)
            at = 128 * axis
            fkt_ref[at : at + 64, :] = cl
            fkt_ref[at + 64 : at + 128, :] = sl
            fqt_ref[at : at + 64, :] = sl * 0.125
            fqt_ref[at + 64 : at + 128, :] = cl * 0.125

    p = (mm(x[...], w_ref[...]) + b_ref[...]).astype(BF16)
    p_ref[...] = p
    pt_ref[...] = p.T


def page_specs(half, width):
    spec = pl.BlockSpec((1, half, width), lambda i, ids: (ids[1], 0, 0))
    return spec, spec


def project(ids, tokens, other, w, vectors, boxes, wk, wq):
    _, half, width = tokens.shape
    rows = 2 * half
    cols = w.shape[1]
    block = 768
    rates = np.exp(np.arange(64) * (-math.log(10000.0) / 64)).astype(np.float32)
    return call(
        project_kernel, "project", (cols // block,), ids,
        (tokens, other, w, vectors, boxes, np.tile(rates, 2)[None, :], rates[:, None], wk, wq),
        [
            *page_specs(half, width),
            pl.BlockSpec((width, block), lambda i, ids: (0, i)),
            pl.BlockSpec((1, block), lambda i, ids: (0, 4 + i)),
            pl.BlockSpec((1, 4, rows), lambda i, ids: (ids[1], 0, 0)),
            whole((1, 128)), whole((64, 1)), whole((256, width)), whole((256, width)),
        ],
        [
            pl.BlockSpec((block, rows), lambda i, ids: (i, 0)),
            pl.BlockSpec((rows, block), lambda i, ids: (0, i)),
            whole((width, rows)), whole((rows, 256)), whole((4, rows, 128)), whole((4, 64, rows)),
            whole((256, rows)), whole((256, rows)), whole((width, 256)), whole((width, 256)),
        ],
        [
            SDS((cols, rows), BF16), SDS((rows, cols), BF16), SDS((width, rows), BF16), SDS((rows, 256), BF16),
            SDS((4, rows, 128), F32), SDS((4, 64, rows), F32), SDS((256, rows), BF16), SDS((256, rows), BF16),
            SDS((width, 256), BF16), SDS((width, 256), BF16),
        ],
        [pltpu.VMEM((rows, width), BF16)],
        flops=2 * rows * width * cols, moved=2 * (width * cols + 2 * rows * cols),
    )


def attend_kernel(ids, qt_ref, vt_ref, k_ref, wk_ref, wq_ref, kf_ref, tab_ref, tabt_ref, fqt_ref,
                  e_ref, at_ref, r_ref, fk, fq):
    rows = k_ref.shape[0]

    @pl.when(pl.program_id(0) == 0)
    def _():
        lane = lax.broadcasted_iota(jnp.int32, (rows, 128), 1)
        at = lax.broadcasted_iota(jnp.int32, (rows, 128), 0)
        turned = jnp.where(at < rows // 2, at + rows // 2, at - rows // 2)
        at = jnp.where(ids[1] == 0, at, turned)
        fk[:, 0:256] = kf_ref[...]
        fk[:, 640:768] = jnp.where((lane == 0) & (at >= ids[2]), -BIG, 0.0).astype(BF16)
        fq[256:512, :] = fqt_ref[...]
        sub = lax.broadcasted_iota(jnp.int32, (128, rows), 0)
        fq[640:768, :] = jnp.where(sub == 0, 1.0, 0.0).astype(BF16)

    fk[:, 512:640] = k_ref[...]
    lane = lax.broadcasted_iota(jnp.int32, (256, 128), 1)
    for h in range(2):
        mine = (lane < 64) if h == 0 else (lane >= 64)
        qt = qt_ref[h * 64 : h * 64 + 64, :]
        zero = jnp.zeros_like(qt)
        pad = jnp.concatenate([qt, zero] if h == 0 else [zero, qt], 0)
        fq[512:640, :] = pad * 0.125
        a = mm(wk_ref[...], pad)
        sx, cx, sy, cy = (tabt_ref[i] * 0.125 for i in range(4))
        axs, axc, ays, ayc = (a[i * 64 : i * 64 + 64, :] for i in range(4))
        fq[0:64, :] = (axs * sx + axc * cx).astype(BF16)
        fq[64:128, :] = (axc * sx - axs * cx).astype(BF16)
        fq[128:192, :] = (ays * sy + ayc * cy).astype(BF16)
        fq[192:256, :] = (ayc * sy - ays * cy).astype(BF16)
        w = jnp.where(mine, wq_ref[...], 0).astype(BF16)
        b = mm_nt(k_ref[...], w)
        for axis in range(2):
            part = b[:, axis * 128 : axis * 128 + 128]
            turned = pltpu.roll(part, 64, 1)
            fk[:, 256 + axis * 128 : 384 + axis * 128] = (
                part * tab_ref[axis] + turned * tab_ref[2 + axis]
            ).astype(BF16)
        s = mm(fk[...], fq[...])
        e = jnp.exp(s - jnp.max(s, 0, keepdims=True))
        r = 1.0 / jnp.sum(e, 0, keepdims=True)
        low = e.astype(BF16)
        e_ref[h] = low
        at_ref[h * 64 : h * 64 + 64, :] = (mm(vt_ref[h * 64 : h * 64 + 64, :], low) * r).astype(BF16)
        r_ref[0, h : h + 1, :] = r


def attend(ids, pt, p, w_posk, w_posq, kf, tab, tabt, fqt):
    rows = p.shape[0]
    width = pt.shape[0] // 3
    return call(
        attend_kernel, "attend", (PAIRS,), ids, (pt, pt, p, w_posk, w_posq, kf, tab, tabt, fqt),
        [
            pl.BlockSpec((128, rows), lambda i, ids: (i, 0)),
            pl.BlockSpec((128, rows), lambda i, ids: (2 * PAIRS + i, 0)),
            pl.BlockSpec((rows, 128), lambda i, ids: (0, PAIRS + i)),
            pl.BlockSpec((256, 128), lambda i, ids: (0, i)),
            pl.BlockSpec((256, 128), lambda i, ids: (0, i)),
            whole((rows, 256)), whole((4, rows, 128)), whole((4, 64, rows)), whole((256, rows)),
        ],
        [
            pl.BlockSpec((2, rows, rows), lambda i, ids: (i, 0, 0)),
            pl.BlockSpec((128, rows), lambda i, ids: (i, 0)),
            pl.BlockSpec((1, 2, rows), lambda i, ids: (i, 0, 0)),
        ],
        [SDS((HEADS, rows, rows), BF16), SDS((width, rows), BF16), SDS((PAIRS, 2, rows), F32)],
        [pltpu.VMEM((rows, 768), BF16), pltpu.VMEM((768, rows), BF16)],
        flops=2 * HEADS * rows * rows * 640, moved=2 * HEADS * rows * rows,
    )


def feed_kernel(ids, at_ref, own_ref, other_ref, wo_ref, bo_ref, g1_ref, s1_ref, wi_ref, bi_ref, wd_ref, bd_ref,
                g2_ref, s2_ref, cown_ref, cother_ref,
                flt_ref, norm_ref, rstd_ref, slope_ref, actt_ref, keep_ref, give_ref, dres_ref, dsec_ref, send_ref,
                rows_ref, first, low, second, cot):
    step = pl.program_id(0)
    half = own_ref.shape[1]

    @pl.when(step == 0)
    def _():
        first[:half, :] = own_ref[0].astype(F32)
        first[half:, :] = other_ref[0].astype(F32)
        cot[:half, :] = cown_ref[0]
        cot[half:, :] = cother_ref[...]
        v = first[...] + (mm(at_ref[...].T, wo_ref[...]) + bo_ref[...])
        c = v - jnp.mean(v, -1, keepdims=True)
        rstd = lax.rsqrt(jnp.mean(c * c, -1, keepdims=True) + 1e-6)
        normed = c * rstd
        norm_ref[...] = normed
        rstd_ref[...] = rstd
        f = normed * g1_ref[...] + s1_ref[...]
        first[...] = f + bd_ref[...]
        l = f.astype(BF16)
        low[...] = l
        flt_ref[...] = l.T

    h = mm(low[...], wi_ref[...]) + bi_ref[...]
    cdf = 0.5 * lax.erf(h * (0.5 ** 0.5)) + 0.5
    active = (h * cdf).astype(BF16)
    slope_ref[...] = (cdf + h * (jnp.exp(-0.5 * h * h) * ((2.0 * math.pi) ** -0.5))).astype(BF16)
    actt_ref[...] = active.T
    part = mm(active, wd_ref[...])

    @pl.when(step == 0)
    def _():
        second[...] = part

    @pl.when(step > 0)
    def _():
        second[...] += part

    @pl.when(step == pl.num_programs(0) - 1)
    def _():
        v = first[...] + second[...]
        c = v - jnp.mean(v, -1, keepdims=True)
        rstd = lax.rsqrt(jnp.mean(c * c, -1, keepdims=True) + 1e-6)
        normed = c * rstd
        out = (normed * g2_ref[...] + s2_ref[...]).astype(BF16)
        keep_ref[...] = out[:half, :]
        give_ref[...] = out[half:, :]
        g = cot[...].astype(F32)
        gg = g * g2_ref[...]
        d = rstd * (
            gg - jnp.mean(gg, -1, keepdims=True) - normed * jnp.mean(gg * normed, -1, keepdims=True)
        )
        dres_ref[...] = d
        l = d.astype(BF16)
        dsec_ref[...] = l
        side = send_ref.shape[1]
        send_ref[...] = dsec_ref[:, pl.ds(pl.multiple_of((1 - ids[1]) * side, 128), side)]
        rows_ref[0:1, :] = jnp.sum(g * normed, 0, keepdims=True)
        rows_ref[1:2, :] = jnp.sum(g, 0, keepdims=True)
        rows_ref[2:3, :] = jnp.sum(l.astype(F32), 0, keepdims=True)
        rows_ref[3:8, :] = jnp.zeros((5, rows_ref.shape[1]), F32)


def vec(at):
    return pl.BlockSpec((1, 768), lambda i, ids: (0, at))


def feed(ids, att, tokens, other, w_out, w_in, w_down, vectors, cot, cot_other):
    _, half, width = tokens.shape
    rows = 2 * half
    ff = w_in.shape[1]
    block = 512
    mat = whole((rows, width))
    return call(
        feed_kernel, "feed", (ff // block,), ids,
        (att, tokens, other, w_out, vectors, vectors, vectors, w_in, vectors, w_down, vectors, vectors, vectors,
         cot, cot_other),
        [
            whole((width, rows)), *page_specs(half, width), whole((width, width)), vec(7), vec(8), vec(9),
            pl.BlockSpec((width, block), lambda i, ids: (0, i)),
            pl.BlockSpec((1, block), lambda i, ids: (0, i)),
            pl.BlockSpec((block, width), lambda i, ids: (i, 0)),
            vec(10), vec(11), vec(12), page_specs(half, width)[0], whole((half, width)),
        ],
        [
            whole((width, rows)), mat, whole((rows, 1)),
            pl.BlockSpec((rows, block), lambda i, ids: (0, i)),
            pl.BlockSpec((block, rows), lambda i, ids: (i, 0)),
            whole((half, width)), whole((half, width)), mat, mat, whole((rows, width // 2)), whole((8, width)),
        ],
        [
            SDS((width, rows), BF16), SDS((rows, width), F32), SDS((rows, 1), F32),
            SDS((rows, ff), BF16), SDS((ff, rows), BF16),
            SDS((half, width), BF16), SDS((half, width), BF16), SDS((rows, width), F32), SDS((rows, width), BF16),
            SDS((rows, width // 2), BF16), SDS((8, width), F32),
        ],
        [pltpu.VMEM((rows, width), F32), pltpu.VMEM((rows, width), BF16), pltpu.VMEM((rows, width), F32),
         pltpu.VMEM((rows, width), BF16)],
        flops=2 * rows * width * (width + 2 * ff), moved=2 * (2 * width * ff + 2 * rows * ff),
    )


def hidden_kernel(ids, ds_ref, wd_ref, slope_ref, send_ref, own_ref, rows_ref):
    step = pl.program_id(0)
    d = mm_nt(ds_ref[...], wd_ref[...]).astype(BF16).astype(F32)
    dh = (d * slope_ref[...].astype(F32)).astype(BF16)
    rows_ref[...] = jnp.sum(dh.astype(F32), 0, keepdims=True)
    sends = pl.num_programs(0) // 2

    @pl.when(step < sends)
    def _():
        send_ref[...] = dh

    @pl.when(step >= sends)
    def _():
        own_ref[...] = dh


def hidden_back(ids, dsec, w_down, slope):
    rows, width = dsec.shape
    ff = w_down.shape[0]
    block = 768
    steps = ff // block
    s = steps // 2
    at = lambda i, ids: jnp.where(ids[1] == 0, (i + s) % steps, i)
    return call(
        hidden_kernel, "hidden_back", (steps,), ids, (dsec, w_down, slope),
        [
            whole((rows, width)),
            pl.BlockSpec((block, width), lambda i, ids: (at(i, ids), 0)),
            pl.BlockSpec((rows, block), lambda i, ids: (0, at(i, ids))),
        ],
        [
            pl.BlockSpec((rows, block), lambda i, ids: (0, jnp.minimum(i, s - 1))),
            pl.BlockSpec((rows, block), lambda i, ids: (0, jnp.maximum(i - s, 0))),
            pl.BlockSpec((1, block), lambda i, ids: (0, at(i, ids))),
        ],
        [SDS((rows, ff // 2), BF16), SDS((rows, ff // 2), BF16), SDS((1, ff), F32)],
        flops=2 * rows * width * ff, moved=2 * (width * ff + 2 * rows * ff),
    )


def first_kernel(ids, dsend_ref, down_ref, wsend_ref, wown_ref, dres_ref, norm_ref, rstd_ref, g1_ref, wo_ref,
                 res_ref, branch_ref, send_ref, datt_ref, rows_ref, acc):
    step = pl.program_id(0)
    part = mm_nt(dsend_ref[...], wsend_ref[...]) + mm_nt(down_ref[...], wown_ref[...])

    @pl.when(step == 0)
    def _():
        acc[...] = part

    @pl.when(step > 0)
    def _():
        acc[...] += part

    @pl.when(step == pl.num_programs(0) - 1)
    def _():
        g = dres_ref[...] + acc[...].astype(BF16).astype(F32)
        normed = norm_ref[...]
        gg = g * g1_ref[...]
        d = rstd_ref[...] * (
            gg - jnp.mean(gg, -1, keepdims=True) - normed * jnp.mean(gg * normed, -1, keepdims=True)
        )
        res_ref[...] = d
        l = d.astype(BF16)
        branch_ref[...] = l
        side = send_ref.shape[1]
        send_ref[...] = branch_ref[:, pl.ds(pl.multiple_of((1 - ids[1]) * side, 128), side)]
        datt_ref[...] = mm_nt(wo_ref[...], l).astype(BF16)
        rows_ref[0:1, :] = jnp.sum(g * normed, 0, keepdims=True)
        rows_ref[1:2, :] = jnp.sum(g, 0, keepdims=True)
        rows_ref[2:3, :] = jnp.sum(l.astype(F32), 0, keepdims=True)
        rows_ref[3:8, :] = jnp.zeros((5, rows_ref.shape[1]), F32)


def first_back(ids, dsend, down, w_in, dres, norm, rstd, vectors, w_out):
    rows, width = dres.shape
    ff = w_in.shape[1]
    block = 512
    s = ff // block // 2
    mat = whole((rows, width))
    return call(
        first_kernel, "first_back", (s,), ids, (dsend, down, w_in, w_in, dres, norm, rstd, vectors, w_out),
        [
            pl.BlockSpec((rows, block), lambda i, ids: (0, i)),
            pl.BlockSpec((rows, block), lambda i, ids: (0, i)),
            pl.BlockSpec((width, block), lambda i, ids: (0, (1 - ids[1]) * s + i)),
            pl.BlockSpec((width, block), lambda i, ids: (0, ids[1] * s + i)),
            mat, mat, whole((rows, 1)), vec(8), whole((width, width)),
        ],
        [mat, mat, whole((rows, width // 2)), whole((width, rows)), whole((8, width))],
        [
            SDS((rows, width), F32), SDS((rows, width), BF16), SDS((rows, width // 2), BF16), SDS((width, rows), BF16),
            SDS((8, width), F32),
        ],
        [pltpu.VMEM((rows, width), F32)],
        flops=2 * rows * width * (width + ff), moved=2 * (width * ff + rows * ff + 5 * rows * width),
    )


def attend_back_kernel(ids, e_ref, r_ref, da_ref, at_ref, qt_ref, kt_ref, v_ref, wkt_ref, wqt_ref, fkt_ref, fqt_ref,
                       tabt_ref, dp_ref, gk_ref, gq_ref, left_k, left_q):
    @pl.when(pl.program_id(0) == 0)
    def _():
        left_k[64:320, :] = fkt_ref[...]
        left_q[64:320, :] = fqt_ref[...]

    sx, cx, sy, cy = (tabt_ref[i] for i in range(4))
    lane = lax.broadcasted_iota(jnp.int32, (256, 128), 1)
    gk, gq = [], []
    for h in range(2):
        own = slice(h * 64, h * 64 + 64)
        da = da_ref[own, :].astype(F32) * r_ref[0, h : h + 1, :]
        delta = jnp.sum(da * at_ref[own, :].astype(F32), 0, keepdims=True)
        da = da.astype(BF16)
        zero = jnp.zeros_like(da)
        pad = jnp.concatenate([da, zero] if h == 0 else [zero, da], 0)
        e = e_ref[h]
        ds = (e.astype(F32) * (mm(v_ref[...], pad) - delta)).astype(BF16)
        left_k[0:64, :] = kt_ref[own, :]
        left_q[0:64, :] = qt_ref[own, :] * 0.125
        one = mm(left_k[...], ds) * 0.125
        two = mm_nt(left_q[...], ds)
        dv = mm_nt(da, e)
        ux1, ux2, uy1, uy2 = (one[64 + i * 64 : 128 + i * 64, :].astype(BF16).astype(F32) for i in range(4))
        d_a = jnp.concatenate(
            [ux1 * sx - ux2 * cx, ux1 * cx + ux2 * sx, uy1 * sy - uy2 * cy, uy1 * cy + uy2 * sy], 0
        ).astype(BF16)
        zx1, zx2, zy1, zy2 = (two[64 + i * 64 : 128 + i * 64, :] for i in range(4))
        d_b = jnp.concatenate(
            [zx1 * cx - zx2 * sx, zx1 * sx + zx2 * cx, zy1 * cy - zy2 * sy, zy1 * sy + zy2 * cy], 0
        ).astype(BF16)
        dp_ref[0, own, :] = (one[0:64, :] + mm(wkt_ref[own, :], d_a)).astype(BF16)
        dp_ref[1, own, :] = (two[0:64, :] + mm(wqt_ref[own, :], d_b)).astype(BF16)
        dp_ref[2, own, :] = dv.astype(BF16)
        gk.append(mm_nt(d_a, qt_ref[...]))
        gq.append(mm_nt(d_b, kt_ref[...]))
    gk_ref[...] = jnp.where(lane < 64, gk[0], gk[1]).astype(BF16)
    gq_ref[...] = jnp.where(lane < 64, gq[0], gq[1]).astype(BF16)


def attend_back(ids, own, e, r, datt, att, pt, p, wkt, wqt, fkt, fqt, tabt):
    rows = p.shape[0]
    pairs = PAIRS // 2
    lo = lambda ids: (ids[1] if own else 1 - ids[1]) * pairs
    pair = lambda base: pl.BlockSpec((128, rows), lambda i, ids: (base + lo(ids) + i, 0))
    wt = pl.BlockSpec((128, 256), lambda i, ids: (lo(ids) + i, 0))
    return call(
        attend_back_kernel, "attend_back", (pairs,), ids, (e, r, datt, att, pt, pt, p, wkt, wqt, fkt, fqt, tabt),
        [
            pl.BlockSpec((2, rows, rows), lambda i, ids: (lo(ids) + i, 0, 0)),
            pl.BlockSpec((1, 2, rows), lambda i, ids: (lo(ids) + i, 0, 0)),
            pair(0), pair(0), pair(0), pair(PAIRS),
            pl.BlockSpec((rows, 128), lambda i, ids: (0, 2 * PAIRS + lo(ids) + i)),
            wt, wt, whole((256, rows)), whole((256, rows)), whole((4, 64, rows)),
        ],
        [
            pl.BlockSpec((3, 128, rows), lambda i, ids: (0, i, 0)),
            pl.BlockSpec((256, 128), lambda i, ids: (0, i)),
            pl.BlockSpec((256, 128), lambda i, ids: (0, i)),
        ],
        [SDS((3, 128 * pairs, rows), BF16), SDS((256, 128 * pairs), BF16), SDS((256, 128 * pairs), BF16)],
        [pltpu.VMEM((320, rows), BF16), pltpu.VMEM((320, rows), BF16)],
        flops=2 * 2 * pairs * rows * rows * 900, moved=2 * 2 * pairs * rows * rows,
    )


def tokens_kernel(ids, w_ref, ds_ref, do_ref, dres_ref, keep_ref, give_ref, rows_ref):
    width = w_ref.shape[1] // 3
    side = width // 2
    half = keep_ref.shape[0]
    acc = None
    for h, ref in ((1 - ids[1], ds_ref), (ids[1], do_ref)):
        for s in range(3):
            at = pl.multiple_of(s * width + h * side, 128)
            part = mm(w_ref[:, pl.ds(at, side)], ref[s])
            acc = part if acc is None else acc + part
    out = (dres_ref[...] + acc.T).astype(BF16)
    keep_ref[...] = out[:half, :]
    give_ref[...] = out[half:, :]

    @pl.when(pl.program_id(0) == 0)
    def _():
        ones = jnp.ones((8, ds_ref.shape[2]), BF16)
        for s in range(3):
            for h, ref in ((1 - ids[1], ds_ref), (ids[1], do_ref)):
                at = pl.multiple_of(h * side, 128)
                rows_ref[s : s + 1, pl.ds(at, side)] = mm_nt(ones, ref[s])[0:1, :]
        rows_ref[3:8, :] = jnp.zeros((5, width), F32)


def tokens_back(ids, w_qkv, dsend, down, dres):
    rows, width = dres.shape
    cols = w_qkv.shape[1]
    block = 256
    half = rows // 2
    blk = pl.BlockSpec((half, block), lambda i, ids: (0, i))
    return call(
        tokens_kernel, "tokens_back", (width // block,), ids, (w_qkv, dsend, down, dres),
        [
            pl.BlockSpec((block, cols), lambda i, ids: (i, 0)), whole(dsend.shape), whole(down.shape),
            pl.BlockSpec((rows, block), lambda i, ids: (0, i)),
        ],
        [blk, blk, whole((8, width))],
        [SDS((half, width), BF16), SDS((half, width), BF16), SDS((8, width), F32)],
        flops=2 * rows * width * cols, moved=2 * (width * cols + rows * cols + 3 * rows * width),
    )


def chosen(core, pair):
    return jnp.where(core == 0, pair[0], pair[1])


def drop_bit(p, bit):
    return ((p >> (bit + 1)) << bit) | (p & ((1 << bit) - 1))


def put(ids, bits, p, lanes, value, send_ref, keep_ref):
    bit = chosen(ids[1], bits)
    here = ((p >> bit) & 1) == ((ids[0] >> bit) & 1)
    at = drop_bit(p, bit)

    @pl.when(here)
    def _():
        keep_ref[at, 0 : value.shape[0], lanes] = value

    @pl.when(jnp.logical_not(here))
    def _():
        send_ref[at, 0 : value.shape[0], lanes] = value


def down_kernel(n, bits, ids, a0_ref, a1_ref, b0_ref, b1_ref, send_ref, keep_ref):
    places = n // pl.num_programs(0)
    r, w = keep_ref.shape[1:]
    acc = mm(a0_ref[...], b0_ref[...]) + mm(a1_ref[...], b1_ref[...])
    for k in range(places):
        p = pl.program_id(0) * places + k
        put(ids, bits, p, slice(0, w), acc[k * r : k * r + r, :].astype(BF16), send_ref, keep_ref)


def down_grad(ids, n, bits, actt, actt_other, dsec, dsec_other):
    ff, rows = actt.shape
    side = dsec_other.shape[1]
    block = ff // 4
    part = (n // 2, ff // n, side)
    a = pl.BlockSpec((block, rows), lambda i, ids: (i, 0))
    return call(
        functools.partial(down_kernel, n, bits), "down_grad", (4,), ids, (actt, actt_other, dsec, dsec_other),
        [a, a, pl.BlockSpec((rows, side), lambda i, ids: (0, ids[1])), whole((rows, side))],
        [whole(part)] * 2, [SDS(part, BF16)] * 2,
        flops=4 * ff * rows * side, moved=2 * (2 * ff * rows + ff * side),
    )


def mid_kernel(n, bits, ids, f0_ref, f1_ref, h0_ref, h1_ref, a0_ref, a1_ref, c0_ref, c1_ref, send_ref, keep_ref):
    step = pl.program_id(0)
    last = pl.num_programs(0) - 1
    r = keep_ref.shape[1]
    w = h0_ref.shape[1]

    @pl.when(step < last)
    def _():
        acc = mm(f0_ref[...], h0_ref[...]) + mm(f1_ref[...], h1_ref[...])
        lanes = pl.ds(pl.multiple_of(step * w, 128), w)
        for p in range(n):
            put(ids, bits, p, lanes, acc[p * r : p * r + r, :].astype(BF16), send_ref, keep_ref)

    @pl.when(step == last)
    def _():
        acc = mm(a0_ref[...], c0_ref[...]) + mm(a1_ref[...], c1_ref[...])
        lanes = slice(keep_ref.shape[2] - acc.shape[1], keep_ref.shape[2])
        for p in range(n):
            put(ids, bits, p, lanes, acc[p * r : p * r + r, :].astype(BF16), send_ref, keep_ref)


def mid_grad(ids, n, bits, flt, flt_other, dh, dh_other, att, att_other, branch, branch_other):
    width, rows = flt.shape
    ffs = dh.shape[1]
    side = branch_other.shape[1]
    block = 768
    steps = ffs // block
    part = (n // 2, width // n, ffs + side)
    b = pl.BlockSpec((rows, block), lambda i, ids: (0, jnp.minimum(i, steps - 1)))
    a = whole((width, rows))
    return call(
        functools.partial(mid_kernel, n, bits), "mid_grad", (steps + 1,), ids,
        (flt, flt_other, dh, dh_other, att, att_other, branch, branch_other),
        [a, a, b, b, a, a, pl.BlockSpec((rows, side), lambda i, ids: (0, ids[1])), whole((rows, side))],
        [whole(part)] * 2, [SDS(part, BF16)] * 2,
        flops=4 * width * rows * (ffs + side), moved=2 * (2 * ffs * rows + 2 * width * (ffs + side)),
    )


def chunks(n, size):
    return max(((p + 1) * size - 1) // 128 - p * size // 128 + 1 for p in range(n))


def small_plan(n, sizes):
    plan, at = [], 0
    for size in sizes:
        plan.append((size, chunks(n, size), at))
        at += chunks(n, size)
    return plan, at


def qkv_kernel(n, bits, sizes, ids, x0_ref, x1_ref, d0_ref, d1_ref, k0_ref, k1_ref, q0_ref, q1_ref,
               two_ref, one_ref, in_ref, qkv_ref, send_ref, keep_ref):
    step = pl.program_id(0)
    last = pl.num_programs(0) - 1
    r = keep_ref.shape[1]
    side = d0_ref.shape[1]

    @pl.when(step < last)
    def _():
        acc = mm_nt(x0_ref[...], d0_ref[0]) + mm_nt(x1_ref[...], d1_ref[0])
        lanes = pl.ds(pl.multiple_of(step * side, 128), side)
        for p in range(n):
            put(ids, bits, p, lanes, acc[p * r : p * r + r, :].astype(BF16), send_ref, keep_ref)

    @pl.when(step == last)
    def _():
        base = 3 * side
        for own_ref, other_ref in ((k0_ref, k1_ref), (q0_ref, q1_ref)):
            acc = (own_ref[...].astype(F32) + other_ref[...].astype(F32)).astype(BF16)
            s = acc.shape[0] // n
            for p in range(n):
                rows = acc[p * s : p * s + s, :]
                stacked = jnp.concatenate([rows[:, 128 * i : 128 * i + 128] for i in range(side // 128)], 0)
                put(ids, bits, p, slice(base, base + 128), stacked, send_ref, keep_ref)
            base += 128
        vectors = (qkv_ref, one_ref, one_ref, one_ref, in_ref, two_ref, two_ref, two_ref)
        index = (None, 2, 0, 1, 0, 2, 0, 1)
        plan, _ = small_plan(n, sizes)
        for p in range(n):
            found = []
            for (size, count, _), ref, row in zip(plan, vectors, index):
                for c in range(count):
                    at = min(p * size // 128 + c, n * size // 128 - 1)
                    if row is None:
                        i, at = at * 128 // ref.shape[1], at * 128 % ref.shape[1]
                        found.append(ref[i : i + 1, at : at + 128])
                    else:
                        found.append(ref[row : row + 1, at * 128 : at * 128 + 128])
            found = jnp.concatenate(found + [jnp.zeros((r - len(found), 128), F32)], 0).astype(BF16)
            put(ids, bits, p, slice(base, base + 128), found, send_ref, keep_ref)


def qkv_grad(ids, n, bits, sizes, xt, xt_other, dp, dp_other, gk, gk_other, gq, gq_other, two, one, into, qkv):
    width, rows = xt.shape
    side = dp.shape[1]
    part = (n // 2, width // n, 3 * side + 3 * 128)
    d = pl.BlockSpec((1, side, rows), lambda i, ids: (jnp.minimum(i, 2), 0, 0))
    return call(
        functools.partial(qkv_kernel, n, bits, sizes), "qkv_grad", (4,), ids,
        (xt, xt_other, dp, dp_other, gk, gk_other, gq, gq_other, two, one, into, qkv),
        [whole(xt.shape)] * 2 + [d, d] + [whole(a.shape) for a in (gk, gk, gq, gq, two, one, into, qkv)],
        [whole(part)] * 2, [SDS(part, BF16)] * 2,
        flops=4 * width * rows * 3 * side, moved=2 * (2 * 3 * side * rows + 2 * width * 3 * side),
    )


def add_split_kernel(bits, lows, ids, keep_ref, got_ref, send_ref, next_ref):
    low = chosen(ids[1], lows)
    mine = (ids[0] >> chosen(ids[1], bits)) & 1

    @pl.loop(0, next_ref.shape[0])
    def _(q):
        base = ((q >> low) << (low + 1)) | (q & ((1 << low) - 1))
        for which, ref in ((1 - mine, send_ref), (mine, next_ref)):
            p = base + (which << low)
            ref[q] = (keep_ref[p].astype(F32) + got_ref[p].astype(F32)).astype(BF16)


def add_split(ids, keep, got, bits, lows):
    m, r, w = keep.shape
    part = (m // 2, r, w)
    return call(
        functools.partial(add_split_kernel, bits, lows), "add_split", (1,), ids, (keep, got),
        [whole(keep.shape)] * 2, [whole(part)] * 2, [SDS(part, BF16)] * 2, vmem=24, moved=6 * m * r * w,
    )


def add_last_kernel(ids, keep_ref, got_ref, out_ref):
    out_ref[...] = (keep_ref[0].astype(F32) + got_ref[0].astype(F32)).astype(BF16)


def add_last(ids, keep, got):
    _, r, w = keep.shape
    return call(
        add_last_kernel, "add_last", (1,), ids, (keep, got), [whole(keep.shape)] * 2, whole((r, w)), SDS((r, w), BF16),
        vmem=16, moved=6 * r * w,
    )


def swap(x):
    return lax.ppermute(x, "slab", [(0, 1), (1, 0)])


def across(x, n, bits):
    pairs = [(2 * p + c, 2 * (p ^ (1 << bits[c])) + c) for p in range(n) for c in range(2)]
    return lax.ppermute(x, ("pages", "slab"), pairs)


def orders(n):
    low = list(range(n.bit_length() - 1))
    if len(low) < 3:
        return low, low[::-1]
    a = low
    b = [low[1], low[0]] + low[:1:-1]
    return a, b


class Exchange:
    def __init__(self, ids, n, send, keep, order):
        self.ids, self.n, self.order = ids, n, order
        self.left = [sorted(o) for o in order]
        self.at = 0
        self.keep = keep
        self.got = across(send, n, self.bits(0))

    def bits(self, step):
        return tuple(o[step] for o in self.order)

    def step(self):
        for l, b in zip(self.left, self.bits(self.at)):
            l.remove(b)
        self.at += 1
        if self.at == len(self.order[0]):
            self.mine = add_last(self.ids, self.keep, self.got)
            self.other = swap(self.mine)
            return
        bits = self.bits(self.at)
        lows = tuple(l.index(b) for l, b in zip(self.left, bits))
        send, self.keep = add_split(self.ids, self.keep, self.got, bits, lows)
        self.got = across(send, self.n, bits)


def join_kernel(ids, mine_ref, other_ref, *outs):
    core = ids[1]
    at = 0
    for out in outs:
        side = out.shape[1] // 2
        for who, ref in ((core, mine_ref), (1 - core, other_ref)):
            out[:, pl.ds(pl.multiple_of(who * side, 128), side)] = ref[:, at : at + side].astype(F32)
        at += side


def join(ids, mine, other, widths):
    r = mine.shape[0]
    return call(
        join_kernel, "join", (1,), ids, (mine, other), [whole(mine.shape)] * 2,
        [whole((r, w)) for w in widths], [SDS((r, w), F32) for w in widths], vmem=16, moved=12 * r * sum(widths),
    )


def join_qkv_kernel(ids, mine_ref, other_ref, qkv_ref, posk_ref, posq_ref, small_ref):
    core = ids[1]
    r = mine_ref.shape[0]
    s = posk_ref.shape[0]
    count = r // s
    side = 128 * count
    width = qkv_ref.shape[1] // 3
    for who, ref in ((core, mine_ref), (1 - core, other_ref)):
        for i in range(3):
            at = pl.multiple_of(i * width + who * side, 128)
            qkv_ref[:, pl.ds(at, side)] = ref[:, i * side : i * side + side].astype(F32)
        for j, out in enumerate((posk_ref, posq_ref)):
            lanes = slice(3 * side + 128 * j, 3 * side + 128 * j + 128)
            for i in range(count):
                at = pl.multiple_of(who * side + 128 * i, 128)
                out[:, pl.ds(at, 128)] = ref[i * s : i * s + s, lanes].astype(F32)
    small_ref[...] = mine_ref[:, 3 * side + 256 :].astype(F32) + other_ref[:, 3 * side + 256 :].astype(F32)


def join_qkv(ids, mine, other, width, pos):
    r = mine.shape[0]
    shapes = [(r, 3 * width), (pos, width), (pos, width), (r, 128)]
    return call(
        join_qkv_kernel, "join_qkv", (1,), ids, (mine, other), [whole(mine.shape)] * 2,
        [whole(s) for s in shapes], [SDS(s, F32) for s in shapes], vmem=16, moved=12 * r * 4 * width,
    )


def plain_sum(g, n, place):
    left = list(range(n.bit_length() - 2, -1, -1))
    acc = g.astype(BF16).reshape((2,) * len(left) + (g.shape[0] // n, g.shape[1]))
    for bit in sorted(left):
        axis = left.index(bit)
        mine = (place >> bit) & 1
        send = lax.dynamic_index_in_dim(acc, 1 - mine, axis, keepdims=False)
        keep = lax.dynamic_index_in_dim(acc, mine, axis, keepdims=False)
        acc = (keep.astype(F32) + across(send, n, (bit, bit)).astype(F32)).astype(BF16)
        left.remove(bit)
    return acc


def plain_join(core, g):
    got = swap(g)
    sides = jnp.where(core == 0, jnp.stack([g, got], 1), jnp.stack([got, g], 1))
    return sides.reshape(g.shape[0], -1).astype(F32)


def pages(core, keep, got):
    return jnp.where(core == 0, jnp.stack([keep, got], 0), jnp.stack([got, keep], 0))


def after(value, *others):
    return lax.optimization_barrier((value, *others))[0]


def body(n, tokens, boxes, lengths, w_qkv, b_qkv, w_posk, w_posq, w_out, b_out, gain_one, shift_one,
         w_in, b_in, w_down, b_down, gain_two, shift_two, cotangent):
    place = lax.axis_index("pages").astype(jnp.int32)
    core = lax.axis_index("slab").astype(jnp.int32)
    ids = jnp.stack([place, core, lax.dynamic_index_in_dim(lengths, core, 0, keepdims=False)])
    _, half, width = tokens.shape
    other = swap(tokens)
    vectors = jnp.concatenate(
        [b_in, b_qkv, b_out, gain_one, shift_one, b_down, gain_two, shift_two]
    ).astype(F32)[None, :]
    cot_other = swap(lax.dynamic_index_in_dim(cotangent, 1 - core, 0, keepdims=False))

    pt, p, xt, kf, tab, tabt, fkt, fqt, wkt, wqt = project(
        ids, tokens, other, w_qkv, vectors, boxes, w_posk, w_posq
    )
    e, att, r = attend(ids, pt, p, w_posk, w_posq, kf, tab, tabt, fqt)
    (flt, norm, rstd, slope, actt, out_keep, out_give, dres_two, dsec, dsec_send, rows_two) = feed(
        ids, att, tokens, other, w_out, w_in, w_down, vectors, cotangent, cot_other
    )
    xt_other, att_other, flt_other, actt_other = swap(xt), swap(att), swap(flt), swap(actt)
    dsec_other = swap(dsec_send)
    out_got = swap(out_give)
    dh_send, dh, row_in = hidden_back(ids, dsec, w_down, slope)
    dh_other = swap(dh_send)
    if width // n % 16:
        dres_one, branch, branch_send, datt, rows_one = first_back(
            ids, dh_send, dh, w_in, dres_two, norm, rstd, vectors, w_out
        )
        args = dict(e=e, r=r, datt=datt, att=att, pt=pt, p=p, wkt=wkt, wqt=wqt, fkt=fkt, fqt=fqt, tabt=tabt)
        dp_send, gk_send, gq_send = attend_back(ids, own=False, **args)
        dp, gk, gq = attend_back(ids, own=True, **args)
        tok_keep, tok_give, rows_qkv = tokens_back(ids, w_qkv, dp_send, dp, dres_one)
        dp_other = swap(dp_send)

        def side_of(a):
            size = a.shape[1] // 2
            return lax.dynamic_slice_in_dim(a, core * size, size, 1)

        def total(g):
            return plain_join(core, plain_sum(g, n, place))

        both = lambda op, a, b, c, d: op(a, b) + op(c, d)
        g_down = total(both(mm, actt, side_of(dsec), actt_other, dsec_other))
        g_in = total(both(mm, flt, dh, flt_other, dh_other))
        g_out = total(both(mm, att, side_of(branch), att_other, swap(branch_send)))
        g_posk = total(gk.astype(F32) + swap(gk_send).astype(F32))
        g_posq = total(gq.astype(F32) + swap(gq_send).astype(F32))
        g_qkv = jnp.concatenate([total(both(mm_nt, xt, dp[i], xt_other, dp_other[i])) for i in range(3)], 1)
        small = (rows_qkv[0:3], rows_one[2], rows_one[0], rows_one[1], row_in, rows_two[2], rows_two[0], rows_two[1])
        packed = lax.psum(jnp.concatenate([v.reshape(n, -1) for v in small], 1), ("pages", "slab"))
        packed = lax.dynamic_index_in_dim(packed, place, 0, keepdims=False)
        totals, at = [], 0
        for v in small:
            totals.append(packed[at : at + v.size // n])
            at += v.size // n
        return (pages(core, out_keep, out_got), pages(core, tok_keep, swap(tok_give)), g_qkv, totals[0], g_posk,
                g_posq, g_out, totals[1], totals[2], totals[3], g_in, totals[4], g_down, totals[5], totals[6],
                totals[7])

    order = orders(n)
    bits = tuple(o[0] for o in order)
    down = Exchange(ids, n, *down_grad(ids, n, bits, actt, actt_other, dsec, dsec_other), order)
    dres_two = after(dres_two, down.keep)
    dres_one, branch, branch_send, datt, rows_one = first_back(
        ids, dh_send, dh, w_in, dres_two, norm, rstd, vectors, w_out
    )
    branch_other = swap(branch_send)
    mid = Exchange(
        ids, n, *mid_grad(ids, n, bits, flt, flt_other, dh, dh_other, att, att_other, branch, branch_other), order
    )
    down.step()
    datt = after(datt, mid.keep, down.keep)
    back = functools.partial(
        attend_back, ids, e=e, r=r, datt=datt, att=att, pt=pt, p=p, wkt=wkt, wqt=wqt, fkt=fkt, fqt=fqt, tabt=tabt
    )
    dp_send, gk_send, gq_send = back(own=False)
    dp_other, gk_other, gq_other = swap(dp_send), swap(gk_send), swap(gq_send)
    down.step()
    mid.step()
    ids_two = after(ids, dp_send, down.keep, mid.keep)
    dp, gk, gq = attend_back(
        ids_two, own=True, e=e, r=r, datt=datt, att=att, pt=pt, p=p, wkt=wkt, wqt=wqt, fkt=fkt, fqt=fqt, tabt=tabt
    )
    tok_keep, tok_give, rows_qkv = tokens_back(ids, w_qkv, dp_send, dp, dres_one)
    tok_got = swap(tok_give)
    small = (3 * width, width, width, width, w_in.shape[1], width, width, width)
    sizes = tuple(s // n for s in small)
    last = Exchange(
        ids, n, *qkv_grad(ids, n, bits, sizes, xt, xt_other, dp, dp_other, gk, gk_other, gq, gq_other,
                          rows_two, rows_one, row_in, rows_qkv), order
    )
    while mid.at < len(order[0]) or down.at < len(order[0]):
        for x in (down, mid):
            if x.at < len(order[0]):
                x.step()
    while last.at < len(order[0]):
        last.step()
    (g_down,) = join(ids, down.mine, down.other, (width,))
    g_in, g_out = join(ids, mid.mine, mid.other, (w_in.shape[1], width))
    g_qkv, g_posk, g_posq, summed = join_qkv(ids, last.mine, last.other, width, w_posk.shape[0] // n)
    plan, _ = small_plan(n, sizes)
    totals = [
        lax.dynamic_slice_in_dim(summed[at : at + count].reshape(-1), place * size % 128, size, 0)
        for size, count, at in plan
    ]

    return (pages(core, out_keep, out_got), pages(core, tok_keep, tok_got), g_qkv, totals[0], g_posk, g_posq, g_out,
            totals[1], totals[2], totals[3], g_in, totals[4], g_down, totals[5], totals[6], totals[7])


def solution(mesh):
    n = mesh.shape["pages"]
    rows, mat, flat = P("pages", "slab", None), P("pages", None), P("pages")
    return jax.shard_map(
        functools.partial(body, n),
        mesh=mesh,
        in_specs=(rows, P("pages", None, None), flat) + (P(),) * 14 + (rows,),
        out_specs=(rows, rows, mat, flat, mat, mat, mat, flat, flat, flat, mat, flat, mat, flat, flat, flat),
        check_vma=False,
    )
```

time: 588 us -> 234 us (0.40); the launches traced: 578 us -> 233 us
  matrix products: 114 us -> 0 us
  local copies, waits for them, and re-layouts: 147 us -> 34.1 us
  starting transfers between devices: 137 us -> 26.6 us
  Pallas kernels: 0 us -> 108 us
  other arithmetic: 65.6 us -> 3.88 us
  blocking collectives: 41.8 us -> 0 us
  waiting for transfers between devices: 68.8 us -> 59.2 us
    pallas_call x0 -> x26, Pallas kernels: none -> 108 us  [call(): pl.pallas_call(kernel, grid_spec=pltpu.PrefetchScalarGridSpec(num_scalar_...]
    dot_general x25 -> x0, matrix products: 99.8 us -> none  [dot(): return jnp.einsum(spec, a, b, preferred_element_type=jnp.float32)]
    ppermute x72 -> x12, starting transfers between devices: 85.8 us -> 13.3 us  [across(): return lax.ppermute(x, ('pages', 'slab'), pairs)]
    reshape x12 -> x1, local copies, waits for them, and re-layouts: 42.2 us -> 0.01 us  [body(): summed[at:at + count].reshape(-1)]
    dynamic_slice x33 -> x9, local copies, waits for them, and re-layouts: 48.2 us -> 6.01 us  [the longest x8 4.76 us: body(): lax.dynamic_slice_in_dim(summed[at:at + count].reshape(-1), place * size...]
    psum x1 -> x0, blocking collectives: 41.8 us -> none  [body(): packed = lax.psum(packed, ('pages', 'slab'))]
    ppermute x16 -> x17, starting transfers between devices: 51.6 us -> 13.3 us  [swap(): return lax.ppermute(x, 'slab', [(0, 1), (1, 0)])]
    convert_element_type x94 -> x1, other arithmetic: 36.1 us -> 0.04 us  [body(): vectors = jnp.concatenate([b_in, b_qkv, b_out, gain_one, shift_one, b_dow...]
  transfers between devices with their start and end apart: 88 -> 29, of which waited for: 49 -> 9; matrix products, arithmetic and copies ran while one was open for 41% -> 5% of each run, Pallas kernels for 0% -> 37%
where the time goes in v2:
time: 234 us; the launch traced here: 233 us
  Pallas kernels  108 us (46%)
  waiting for transfers between devices  59.2 us (25%)
  local copies, waits for them, and re-layouts  34.1 us (15%)
  starting transfers between devices  26.6 us (11%)
  other arithmetic  3.88 us (2%)
    pallas_call x26, Pallas kernels, call(): pl.pallas_call(kernel, grid_spec=pltpu.PrefetchScalarGridSpec(num_scalar_...  108 us
    ppermute x12, waiting for transfers between devices, across(): return lax.ppermute(x, ('pages', 'slab'), pairs)  54.1 us
    unnamed x83, local copies, waits for them, and re-layouts  26.4 us
    ppermute x12, starting transfers between devices, across(): return lax.ppermute(x, ('pages', 'slab'), pairs)  13.3 us
    ppermute x17, starting transfers between devices, swap(): return lax.ppermute(x, 'slab', [(0, 1), (1, 0)])  13.3 us
    ppermute x17, waiting for transfers between devices, swap(): return lax.ppermute(x, 'slab', [(0, 1), (1, 0)])  5.09 us
    dynamic_slice x8, local copies, waits for them, and re-layouts, body(): lax.dynamic_slice_in_dim(summed[at:at + count].reshape(-1), place * size...  4.76 us
  transfers between devices with their start and end apart: 29, of which 9 were waited for; matrix products, arithmetic and copies ran while one was open for 5% of the time, Pallas kernels for 37%

profile of v2, /device:TPU:1, one launch (start us, length us, event | category | flops | bytes accessed | tf_op | source)
XLA Modules:
  0.0 232.6 jit_solution(714511736417496293)
XLA Ops:
  0.8 1.0 dynamic-slice_bitcast_fusion
  7.9 1.2 dynamic_slice.32
  9.9 1.1 copy-done.20
  11.0 1.0 copy-done.24
  12.0 1.0 copy-done.26
  15.1 6.6 %project.1 = (bf16[2304,512]{1,0:T(8,128)(2,1)S(1)}, bf16[512,2304]{1,0:T(8,128)(2,1)S(1)}, bf16[768,512]{1,0:T(8,128)(2,1)S(1)}, bf16[512,256]{1,0:T(8,128)(2,1...) custom-call(s32[3]{0:T(128)S(1)} %pad_add_fusion.ids, ...), custom_call_target="tpu_custom_call" | custom-call | flops 1811939328 | bytes 8257536 | tf_op jit(solution)/shard_map/project/pallas_call | solution.py:32
  22.7 16.3 %attend.1 = (bf16[12,512,512]{2,1,0:T(8,128)(2,1)}, bf16[768,512]{1,0:T(8,128)(2,1)S(1)}, f32[6,2,512]{2,1,0:T(2,128)S(1)}) custom-call(s32[3]{0:T(128)S(1)} %pad_add_fusion.ids, bf16[2304,512]{1,0:T(8,128)(2,1)S(1)} %get-tuple-element.90.qt_ref.vt_ref.kt_ref, bf16[2304,512]{1,0:T(8,128)(2,1)S(1)} %get-tuple-element.90.qt_ref.vt_ref.kt_ref, ...), custom_call_target="tpu_custom_call" | custom-call | flops 4026531840 | bytes 6291456 | tf_op jit(solution)/shard_map/attend/pallas_call | solution.py:32
  39.8 1.0 copy-done.30
  40.8 14.9 %feed.1 = (bf16[768,512]{1,0:T(8,128)(2,1)}, f32[512,768]{1,0:T(8,128)S(1)}, f32[512,1]{1,0:T(8,128)S(1)}, bf16[512,3072]{1,0:T(8,128)(2,1)S(1)}, bf16[3072,512]...) custom-call(s32[3]{0:T(128)S(1)} %pad_add_fusion.ids, ...), custom_call_target="tpu_custom_call" | custom-call | flops 5435817984 | bytes 15728640 | tf_op jit(solution)/shard_map/feed/pallas_call | solution.py:32
  56.4 1.6 copy-done.34
  58.1 2.9 %copy-done.18 = bf16[3072,768]{1,0:T(8,128)(2,1)S(1)} copy-done((bf16[3072,768]{1,0:T(8,128)(2,1)S(1)}, bf16[3072,768]{1,0:T(8,128)(2,1)}, u32[]{:S(2)}) %copy-start.18) | copy-done | bytes 4718616
  60.9 1.9 copy-done.35
  62.8 5.1 %hidden_back.1 = (bf16[512,1536]{1,0:T(8,128)(2,1)S(1)}, bf16[512,1536]{1,0:T(8,128)(2,1)S(1)}, f32[1,3072]{1,0:T(1,128)S(1)}) custom-call(s32[3]{0:T(128)S(1)} %pad_add_fusion.ids, bf16[512,768]{1,0:T(8,128)(2,1)S(1)} %get-tuple-element.101.ds_ref.b0_ref, bf16[3072,768]{1,0:T(8,128)(2,1)S(1)} %copy-done.18, bf16[512,3072]{1,0:T(8,128)(2,1)S(1)} %copy-done.35), custom_call_target="tpu_custom_call" | custom-call | flops 2415919104 | bytes 11010048 | tf_op jit(solution)/shard_map/hidden_back/pallas_call | solution.py:32
  69.0 3.7 %collective-permute-done.4.b1_ref = bf16[512,384]{1,0:T(8,128)(2,1)S(1)} collective-permute-done((bf16[512,384]{1,0:T(8,128)(2,1)S(1)}, bf16[512,384]{1,0:T(8,128)(2,1)S(1)}, u32[]{:S(2)}, u32[]{:S(2)}) %collective-permute-start.4) | collective-permute-done | bytes 393248 | tf_op jit(solution)/shard_map/ppermute | solution.py:706
  72.7 1.9 copy-done.19
  74.6 1.1 copy-done.37
  75.8 7.1 %down_grad.1 = (bf16[8,192,384]{2,1,0:T(8,128)(2,1)}, bf16[8,192,384]{2,1,0:T(8,128)(2,1)S(1)}) custom-call(s32[3]{0:T(128)S(1)} %pad_add_fusion.ids, bf16[3072,512]{1,0:T(8,128)(2,1)S(1)} %copy-done.19, bf16[3072,512]{1,0:T(8,128)(2,1)} %collective-permute-done.3.a1_ref, bf16[512,768]{1,0:T(8,128)(2,1)S(1)} %copy-done.37, ...), custom_call_target="tpu_custom_call" | custom-call | flops 2415919104 | bytes 8650752 | tf_op jit(solution)/shard_map/down_grad/pallas_call | solution.py:32
  82.9 1.0 copy-done.7
  83.9 2.6 %collective-permute-start.9 = (bf16[8,192,384]{2,1,0:T(8,128)(2,1)}, bf16[8,192,384]{2,1,0:T(8,128)(2,1)}, u32[]{:S(2)}, u32[]{:S(2)}) collective-permute-start(bf16[8,192,384]{2,1,0:T(8,128)(2,1)} %get-tuple-element.117), channel_id=1, source_target_pairs={{0,2},{1,5},{2,0},{3,7},{4,6},{5,1},{6,4},{7,3},{8,10},{9,13},{10,... | collective-permute-start | bytes 3538952 | tf_op jit(solution)/shard_map/ppermute | solution.py:711
  86.5 1.3 copy-done.6
  87.8 7.9 %first_back.1 = (f32[512,768]{1,0:T(8,128)S(1)}, bf16[512,768]{1,0:T(8,128)(2,1)S(1)}, bf16[512,384]{1,0:T(8,128)(2,1)S(1)}, bf16[768,512]{1,0:T(8,128)(2,1)S(1)}, f32[8,768]{1,0:T(8,128)S(1)}) custom-call(s32[3]{0:T(128)S(1)} %pad_add_fusion.ids, bf16[512,1536]{1,0:T(8,128)(2,1)S(1)} %get-tuple-element.103.dsend_ref, ...), custom_call_target="tpu_custom_call" | custom-call | flops 3019898880 | bytes 11796480 | tf_op jit(solution)/shard_map/first_back/pallas_call | solution.py:32
  95.7 1.2 copy-done.1
  97.3 1.3 collective-permute-done.8.c1_ref
  98.7 7.3 %mid_grad.1 = (bf16[8,48,1920]{2,1,0:T(8,128)(2,1)S(1)}, bf16[8,48,1920]{2,1,0:T(8,128)(2,1)S(1)}) custom-call(s32[3]{0:T(128)S(1)} %pad_add_fusion.ids, bf16[768,512]{1,0:T(8,128)(2,1)} %get-tuple-element.113.f0_ref, bf16[768,512]{1,0:T(8,128)(2,1)} %collective-permute-done.5.f1_ref, bf16[512,1536]{1,0:T(8,128)(2,1)S(1)} %get-tuple-element.104.down_ref.h0_ref, ...), custom_call_target="tpu_custom_call" | custom-call | flops 3019898880 | bytes 9043968 | tf_op jit(solution)/shard_map/mid_grad/pallas_call | solution.py:32
  106.0 1.3 collective-permute-start.11
  107.3 2.1 add_split.9
  109.5 8.6 %attend_back.2 = (bf16[3,384,512]{2,1,0:T(8,128)(2,1)S(1)}, bf16[256,384]{1,0:T(8,128)(2,1)S(1)}, bf16[256,384]{1,0:T(8,128)(2,1)S(1)}) custom-call(s32[3]{0:T(128)S(1)} %pad_add_fusion.ids, bf16[12,512,512]{2,1,0:T(8,128)(2,1)} %get-tuple-element.99.e_ref, f32[6,2,512]{2,1,0:T(2,128)S(1)} %get-tuple-element.100.r_ref, ...), custom_call_target="tpu_custom_call" | custom-call | flops 2831155200 | bytes 3145728 | tf_op jit(solution)/shard_map/attend_back/pallas_call | solution.py:32
  119.6 11.9 %collective-permute-done.10.got_ref = bf16[4,192,384]{2,1,0:T(8,128)(2,1)S(1)} collective-permute-done((bf16[4,192,384]{2,1,0:T(8,128)(2,1)S(1)}, bf16[4,192,384]{2,1,0:T(8,128)(2,1)S(1)}, u32[]{:S(2)}, u32[]{:S(2)}) %collective-permute-start.10) | collective-permute-done | bytes 589856 | tf_op jit(solution)/shard_map/ppermute | solution.py:711
  133.1 8.9 %attend_back.3 = (bf16[3,384,512]{2,1,0:T(8,128)(2,1)S(1)}, bf16[256,384]{1,0:T(8,128)(2,1)S(1)}, bf16[256,384]{1,0:T(8,128)(2,1)S(1)}) custom-call(s32[3]{0:T(128)S(1)} %pad_add_fusion.ids, bf16[12,512,512]{2,1,0:T(8,128)(2,1)} %get-tuple-element.99.e_ref, f32[6,2,512]{2,1,0:T(2,128)S(1)} %get-tuple-element.100.r_ref, ...), custom_call_target="tpu_custom_call" | custom-call | flops 2831155200 | bytes 3145728 | tf_op jit(solution)/shard_map/attend_back/pallas_call | solution.py:32
  142.1 5.4 %tokens_back.1 = (bf16[256,768]{1,0:T(8,128)(2,1)S(1)}, bf16[256,768]{1,0:T(8,128)(2,1)}, f32[8,768]{1,0:T(8,128)S(1)}) custom-call(s32[3]{0:T(128)S(1)} %pad_add_fusion.ids, bf16[768,2304]{1,0:T(8,128)(2,1)S(1)} %copy-done, bf16[3,384,512]{2,1,0:T(8,128)(2,1)S(1)} %get-tuple-element.123.ds_ref, bf16[3,384,512]{2,1,0:T(8,128)(2,1)S(1)} %get-tuple-element.129.do_ref.d0_ref, ...), custom_call_target="tpu_custom_call" | custom-call | flops 1811939328 | bytes 8257536 | tf_op jit(solution)/shard_map/tokens_back/pallas_call | solution.py:32
  147.5 5.7 %qkv_grad.1 = (bf16[8,48,1536]{2,1,0:T(8,128)(2,1)S(1)}, bf16[8,48,1536]{2,1,0:T(8,128)(2,1)S(1)}) custom-call(s32[3]{0:T(128)S(1)} %pad_add_fusion.ids, bf16[768,512]{1,0:T(8,128)(2,1)S(1)} %copy-done.23, bf16[768,512]{1,0:T(8,128)(2,1)S(1)} %collective-permute-done.13.x1_ref, bf16[3,384,512]{2,1,0:T(8,128)(2,1)S(1)} %get-tuple-element.129.do_ref.d0_ref, ...), custom_call_target="tpu_custom_call" | custom-call | flops 1811939328 | bytes 5898240 | tf_op jit(solution)/shard_map/qkv_grad/pallas_call | solution.py:32
  153.2 1.3 collective-permute-start.17
  154.8 21.8 %collective-permute-done.17.got_ref = bf16[8,48,1536]{2,1,0:T(8,128)(2,1)S(1)} collective-permute-done((bf16[8,48,1536]{2,1,0:T(8,128)(2,1)S(1)}, bf16[8,48,1536]{2,1,0:T(8,128)(2,1)S(1)}, u32[]{:S(2)}, u32[]{:S(2)}) %collective-permute-start.17) | collective-permute-done | bytes 1179680 | tf_op jit(solution)/shard_map/ppermute | solution.py:711
  177.4 1.1 collective-permute-start.18
  179.3 2.4 %collective-permute-start.23 = (bf16[2,48,1920]{2,1,0:T(8,128)(2,1)S(1)}, bf16[2,48,1920]{2,1,0:T(8,128)(2,1)S(1)}, u32[]{:S(2)}, u32[]{:S(2)}) collective-permute-start(bf16[2,48,1920]{2,1,0:T(8,128)(2,1)S(1)} %get-tuple-element.156), channel_id=1, source_target_pairs={{0,8},{1,17},{2,10},{3,19},{4,12},{5,21},{6,14},{7,23},{8,0},{9,25... | collective-permute-start | bytes 1105928 | tf_op jit(solution)/shard_map/ppermute | solution.py:711
  181.7 4.8 %collective-permute-done.18.got_ref = bf16[4,48,1536]{2,1,0:T(8,128)(2,1)S(1)} collective-permute-done((bf16[4,48,1536]{2,1,0:T(8,128)(2,1)S(1)}, bf16[4,48,1536]{2,1,0:T(8,128)(2,1)S(1)}, u32[]{:S(2)}, u32[]{:S(2)}) %collective-permute-start.18) | collective-permute-done | bytes 589856 | tf_op jit(solution)/shard_map/ppermute | solution.py:711
  187.2 2.4 %collective-permute-start.19 = (bf16[2,48,1536]{2,1,0:T(8,128)(2,1)S(1)}, bf16[2,48,1536]{2,1,0:T(8,128)(2,1)S(1)}, u32[]{:S(2)}, u32[]{:S(2)}) collective-permute-start(bf16[2,48,1536]{2,1,0:T(8,128)(2,1)S(1)} %get-tuple-element.147), channel_id=1, source_target_pairs={{0,8},{1,17},{2,10},{3,19},{4,12},{5,21},{6,14},{7,23},{8,0},{9,25... | collective-permute-start | bytes 884744 | tf_op jit(solution)/shard_map/ppermute | solution.py:711
  189.6 1.5 collective-permute-start.2
  192.3 6.8 %collective-permute-done.26.got_ref = bf16[2,192,384]{2,1,0:T(8,128)(2,1)S(1)} collective-permute-done((bf16[2,192,384]{2,1,0:T(8,128)(2,1)S(1)}, bf16[2,192,384]{2,1,0:T(8,128)(2,1)S(1)}, u32[]{:S(2)}, u32[]{:S(2)}) %collective-permute-start.26) | collective-permute-done | bytes 294944 | tf_op jit(solution)/shard_map/ppermute | solution.py:711
  199.7 6.7 %collective-permute-done.19.got_ref = bf16[2,48,1536]{2,1,0:T(8,128)(2,1)S(1)} collective-permute-done((bf16[2,48,1536]{2,1,0:T(8,128)(2,1)S(1)}, bf16[2,48,1536]{2,1,0:T(8,128)(2,1)S(1)}, u32[]{:S(2)}, u32[]{:S(2)}) %collective-permute-start.19) | collective-permute-done | bytes 294944 | tf_op jit(solution)/shard_map/ppermute | solution.py:711
  208.0 2.1 collective-permute-done.27.got_ref
  210.7 4.2 %collective-permute-start.28 = (bf16[192,384]{1,0:T(8,128)(2,1)S(1)}, bf16[192,384]{1,0:T(8,128)(2,1)S(1)}, u32[]{:S(2)}, u32[]{:S(2)}) collective-permute-start(bf16[192,384]{1,0:T(8,128)(2,1)S(1)} %add_last.5.mine_ref), channel_id=1, source_target_pairs={{0,1},{1,0},{2,3},{3,2},{4,5},{5,4},{6,7},{7,6},{8,9},{9,8},{10,11... | collective-permute-start | bytes 442376 | tf_op jit(solution)/shard_map/ppermute | solution.py:706
  216.1 4.3 %collective-permute-start.21 = (bf16[48,1536]{1,0:T(8,128)(2,1)S(1)}, bf16[48,1536]{1,0:T(8,128)(2,1)S(1)}, u32[]{:S(2)}, u32[]{:S(2)}) collective-permute-start(bf16[48,1536]{1,0:T(8,128)(2,1)S(1)} %add_last.3.mine_ref), channel_id=1, source_target_pairs={{0,1},{1,0},{2,3},{3,2},{4,5},{5,4},{6,7},{7,6},{8,9},{9,8},{10,11... | collective-permute-start | bytes 442376 | tf_op jit(solution)/shard_map/ppermute | solution.py:706
  220.5 2.1 maximum_select_fusion
  222.6 1.0 maximum_select_fusion.1
  223.6 1.4 join.3
  225.0 1.4 join.2
  226.4 1.4 join_qkv.1
  (135 shorter events, 28.7 us)
Async XLA Ops:
  0.6 9.2 %collective-permute-start = (bf16[2,256,768]{2,1,0:T(8,128)(2,1)}, bf16[2,256,768]{2,1,0:T(8,128)(2,1)S(1)}, u32[]{:S(2)}, u32[]{:S(2)}) collective-permute-start(bf16[2,256,768]{2,1,0:T(8,128)(2,1)} %own_ref.3), channel_id=1, source_target_pairs={{0,1},{1,0},{2,3},{3,2},{4,5},{5,4},{6,7},{7,6},{8,9},{9,8},{10,11... | collective-permute-start | bytes 2359304 | tf_op jit(solution)/shard_map/ppermute | solution.py:706
  1.8 37.2 %collective-permute-start.1 = (bf16[256,768]{1,0:T(8,128)(2,1)S(1)}, bf16[256,768]{1,0:T(8,128)(2,1)S(1)}, u32[]{:S(2)}, u32[]{:S(2)}) collective-permute-start(bf16[256,768]{1,0:T(8,128)(2,1)S(1)} %dynamic-slice_bitcast_fusion), channel_id=1, source_target_pairs={{0,1},{1,0},{2,3},{3,2},{4,5},{5,4},{6,7},{7,6},{8,9},{9,8},{10,11... | collective-permute-start | bytes 1179656 | tf_op jit(solution)/shard_map/ppermute | solution.py:706
  15.1 7.5 %copy-start.25 = (bf16[256,768]{1,0:T(8,128)(2,1)S(1)}, bf16[256,768]{1,0:T(8,128)(2,1)}, u32[]{:S(2)}) copy-start(bf16[256,768]{1,0:T(8,128)(2,1)} %wk_ref.3) | copy-start | bytes 1179652
  22.7 16.4 %copy-start.3 = (bf16[768,256]{1,0:T(8,128)(2,1)}, bf16[768,256]{1,0:T(8,128)(2,1)S(1)}, u32[]{:S(2)}) copy-start(bf16[768,256]{1,0:T(8,128)(2,1)S(1)} %get-tuple-element.121.wqt_ref) | copy-start | bytes 1179652
  22.7 16.4 %copy-start.9 = (bf16[256,512]{1,0:T(8,128)(2,1)}, bf16[256,512]{1,0:T(8,128)(2,1)S(1)}, u32[]{:S(2)}) copy-start(bf16[256,512]{1,0:T(8,128)(2,1)S(1)} %get-tuple-element.122.fkt_ref) | copy-start | bytes 786436
  22.7 16.4 %copy-start.11 = (bf16[256,512]{1,0:T(8,128)(2,1)}, bf16[256,512]{1,0:T(8,128)(2,1)S(1)}, u32[]{:S(2)}) copy-start(bf16[256,512]{1,0:T(8,128)(2,1)S(1)} %get-tuple-element.95.fqt_ref) | copy-start | bytes 786436
  22.7 17.1 %copy-start.5 = (bf16[768,768]{1,0:T(8,128)(2,1)S(1)}, bf16[768,768]{1,0:T(8,128)(2,1)}, u32[]{:S(2)}) copy-start(bf16[768,768]{1,0:T(8,128)(2,1)} %wo_ref.3) | copy-start | bytes 3538948
  22.7 17.1 %copy-start.17 = (bf16[2,256,768]{2,1,0:T(8,128)(2,1)S(1)}, bf16[2,256,768]{2,1,0:T(8,128)(2,1)}, u32[]{:S(2)}) copy-start(bf16[2,256,768]{2,1,0:T(8,128)(2,1)} %cown_ref.1) | copy-start | bytes 2359300
  22.7 17.1 %copy-start.21 = (bf16[2,256,768]{2,1,0:T(8,128)(2,1)S(1)}, bf16[2,256,768]{2,1,0:T(8,128)(2,1)}, u32[]{:S(2)}) copy-start(bf16[2,256,768]{2,1,0:T(8,128)(2,1)} %own_ref.3) | copy-start | bytes 2359300
  58.0 9.9 %copy-start.13 = (bf16[256,768]{1,0:T(8,128)(2,1)}, bf16[256,768]{1,0:T(8,128)(2,1)S(1)}, u32[]{:S(2)}) copy-start(bf16[256,768]{1,0:T(8,128)(2,1)S(1)} %get-tuple-element.97) | copy-start | bytes 1179652
  58.0 9.9 %copy-start.27 = (bf16[256,768]{1,0:T(8,128)(2,1)}, bf16[256,768]{1,0:T(8,128)(2,1)S(1)}, u32[]{:S(2)}) copy-start(bf16[256,768]{1,0:T(8,128)(2,1)S(1)} %get-tuple-element.98) | copy-start | bytes 1179652
  58.0 9.9 %copy-start.36 = (bf16[512,768]{1,0:T(8,128)(2,1)}, bf16[512,768]{1,0:T(8,128)(2,1)S(1)}, u32[]{:S(2)}) copy-start(bf16[512,768]{1,0:T(8,128)(2,1)S(1)} %get-tuple-element.101.ds_ref.b0_ref) | copy-start | bytes 2359300
  58.0 14.7 %collective-permute-start.3 = (bf16[3072,512]{1,0:T(8,128)(2,1)}, bf16[3072,512]{1,0:T(8,128)(2,1)}, u32[]{:S(2)}, u32[]{:S(2)}) collective-permute-start(bf16[3072,512]{1,0:T(8,128)(2,1)} %get-tuple-element.106.a0_ref), channel_id=1, source_target_pairs={{0,1},{1,0},{2,3},{3,2},{4,5},{5,4},{6,7},{7,6},{8,9},{9,8},{10,11... | collective-permute-start | bytes 9437192 | tf_op jit(solution)/shard_map/ppermute | solution.py:706
  67.9 29.4 %collective-permute-start.6 = (bf16[512,1536]{1,0:T(8,128)(2,1)S(1)}, bf16[512,1536]{1,0:T(8,128)(2,1)}, u32[]{:S(2)}, u32[]{:S(2)}) collective-permute-start(bf16[512,1536]{1,0:T(8,128)(2,1)S(1)} %get-tuple-element.103.dsend_ref), channel_id=1, source_target_pairs={{0,1},{1,0},{2,3},{3,2},{4,5},{5,4},{6,7},{7,6},{8,9},{9,8},{10,11... | collective-permute-start | bytes 4718600 | tf_op jit(solution)/shard_map/ppermute | solution.py:706
  68.0 4.7 %collective-permute-start.4 = (bf16[512,384]{1,0:T(8,128)(2,1)S(1)}, bf16[512,384]{1,0:T(8,128)(2,1)S(1)}, u32[]{:S(2)}, u32[]{:S(2)}) collective-permute-start(bf16[512,384]{1,0:T(8,128)(2,1)S(1)} %get-tuple-element.107), channel_id=1, source_target_pairs={{0,1},{1,0},{2,3},{3,2},{4,5},{5,4},{6,7},{7,6},{8,9},{9,8},{10,11... | collective-permute-start | bytes 1179656 | tf_op jit(solution)/shard_map/ppermute | solution.py:706
  68.5 28.8 %collective-permute-start.7 = (bf16[768,512]{1,0:T(8,128)(2,1)S(1)}, bf16[768,512]{1,0:T(8,128)(2,1)}, u32[]{:S(2)}, u32[]{:S(2)}) collective-permute-start(bf16[768,512]{1,0:T(8,128)(2,1)S(1)} %get-tuple-element.96.at_ref.a0_ref), channel_id=1, source_target_pairs={{0,1},{1,0},{2,3},{3,2},{4,5},{5,4},{6,7},{7,6},{8,9},{9,8},{10,11... | collective-permute-start | bytes 2359304 | tf_op jit(solution)/shard_map/ppermute | solution.py:706
  68.6 17.9 %copy-start.16 = (f32[512,1]{1,0:T(8,128)S(1)}, f32[512,1]{1,0:T(8,128)}, u32[]{:S(2)}) copy-start(f32[512,1]{1,0:T(8,128)} %copy-done.15) | copy-start | bytes 6148
  68.6 28.7 %collective-permute-start.5 = (bf16[768,512]{1,0:T(8,128)(2,1)}, bf16[768,512]{1,0:T(8,128)(2,1)}, u32[]{:S(2)}, u32[]{:S(2)}) collective-permute-start(bf16[768,512]{1,0:T(8,128)(2,1)} %get-tuple-element.113.f0_ref), channel_id=1, source_target_pairs={{0,1},{1,0},{2,3},{3,2},{4,5},{5,4},{6,7},{7,6},{8,9},{9,8},{10,11... | collective-permute-start | bytes 2359304 | tf_op jit(solution)/shard_map/ppermute | solution.py:706
  83.9 23.4 %collective-permute-start.9 = (bf16[8,192,384]{2,1,0:T(8,128)(2,1)}, bf16[8,192,384]{2,1,0:T(8,128)(2,1)}, u32[]{:S(2)}, u32[]{:S(2)}) collective-permute-start(bf16[8,192,384]{2,1,0:T(8,128)(2,1)} %get-tuple-element.117), channel_id=1, source_target_pairs={{0,2},{1,5},{2,0},{3,7},{4,6},{5,1},{6,4},{7,3},{8,10},{9,13},{10,... | collective-permute-start | bytes 3538952 | tf_op jit(solution)/shard_map/ppermute | solution.py:711
  96.9 1.7 collective-permute-start.8
  98.7 8.7 %copy-start.8 = (bf16[8,192,384]{2,1,0:T(8,128)(2,1)S(1)}, bf16[8,192,384]{2,1,0:T(8,128)(2,1)}, u32[]{:S(2)}) copy-start(bf16[8,192,384]{2,1,0:T(8,128)(2,1)} %copy-done.7) | copy-start | bytes 3538948
  106.0 3.5 %copy-start.4 = (bf16[768,256]{1,0:T(8,128)(2,1)S(1)}, bf16[768,256]{1,0:T(8,128)(2,1)}, u32[]{:S(2)}) copy-start(bf16[768,256]{1,0:T(8,128)(2,1)} %copy-done.3) | copy-start | bytes 1179652
  106.0 3.5 %copy-start.10 = (bf16[256,512]{1,0:T(8,128)(2,1)S(1)}, bf16[256,512]{1,0:T(8,128)(2,1)}, u32[]{:S(2)}) copy-start(bf16[256,512]{1,0:T(8,128)(2,1)} %copy-done.9) | copy-start | bytes 786436
  106.0 26.2 %collective-permute-start.11 = (bf16[8,48,1920]{2,1,0:T(8,128)(2,1)S(1)}, bf16[8,48,1920]{2,1,0:T(8,128)(2,1)S(1)}, u32[]{:S(2)}, u32[]{:S(2)}) collective-permute-start(bf16[8,48,1920]{2,1,0:T(8,128)(2,1)S(1)} %get-tuple-element.126), channel_id=1, source_target_pairs={{0,2},{1,5},{2,0},{3,7},{4,6},{5,1},{6,4},{7,3},{8,10},{9,13},{10,... | collective-permute-start | bytes 4423688 | tf_op jit(solution)/shard_map/ppermute | solution.py:711
  109.5 9.6 %copy-start.23 = (bf16[768,512]{1,0:T(8,128)(2,1)S(1)}, bf16[768,512]{1,0:T(8,128)(2,1)}, u32[]{:S(2)}) copy-start(bf16[768,512]{1,0:T(8,128)(2,1)} %copy-done.22) | copy-start | bytes 2359300
  118.1 29.4 %collective-permute-start.14 = (bf16[3,384,512]{2,1,0:T(8,128)(2,1)S(1)}, bf16[3,384,512]{2,1,0:T(8,128)(2,1)S(1)}, u32[]{:S(2)}, u32[]{:S(2)}) collective-permute-start(bf16[3,384,512]{2,1,0:T(8,128)(2,1)S(1)} %get-tuple-element.123.ds_ref), channel_id=1, source_target_pairs={{0,1},{1,0},{2,3},{3,2},{4,5},{5,4},{6,7},{7,6},{8,9},{9,8},{10,11... | collective-permute-start | bytes 3538952 | tf_op jit(solution)/shard_map/ppermute | solution.py:706
  118.6 12.9 %collective-permute-start.10 = (bf16[4,192,384]{2,1,0:T(8,128)(2,1)S(1)}, bf16[4,192,384]{2,1,0:T(8,128)(2,1)S(1)}, u32[]{:S(2)}, u32[]{:S(2)}) collective-permute-start(bf16[4,192,384]{2,1,0:T(8,128)(2,1)S(1)} %get-tuple-element.124), channel_id=1, source_target_pairs={{0,4},{1,3},{2,6},{3,1},{4,0},{5,7},{6,2},{7,5},{8,12},{9,11},{10,... | collective-permute-start | bytes 1769480 | tf_op jit(solution)/shard_map/ppermute | solution.py:711
  119.1 28.4 %collective-permute-start.13 = (bf16[768,512]{1,0:T(8,128)(2,1)S(1)}, bf16[768,512]{1,0:T(8,128)(2,1)S(1)}, u32[]{:S(2)}, u32[]{:S(2)}) collective-permute-start(bf16[768,512]{1,0:T(8,128)(2,1)S(1)} %copy-done.23), channel_id=1, source_target_pairs={{0,1},{1,0},{2,3},{3,2},{4,5},{5,4},{6,7},{7,6},{8,9},{9,8},{10,11... | collective-permute-start | bytes 2359304 | tf_op jit(solution)/shard_map/ppermute | solution.py:706
  119.5 28.0 %collective-permute-start.15 = (bf16[256,384]{1,0:T(8,128)(2,1)S(1)}, bf16[256,384]{1,0:T(8,128)(2,1)S(1)}, u32[]{:S(2)}, u32[]{:S(2)}) collective-permute-start(bf16[256,384]{1,0:T(8,128)(2,1)S(1)} %get-tuple-element.135), channel_id=1, source_target_pairs={{0,1},{1,0},{2,3},{3,2},{4,5},{5,4},{6,7},{7,6},{8,9},{9,8},{10,11... | collective-permute-start | bytes 589832 | tf_op jit(solution)/shard_map/ppermute | solution.py:706
  131.5 16.0 %collective-permute-start.16 = (bf16[256,384]{1,0:T(8,128)(2,1)S(1)}, bf16[256,384]{1,0:T(8,128)(2,1)S(1)}, u32[]{:S(2)}, u32[]{:S(2)}) collective-permute-start(bf16[256,384]{1,0:T(8,128)(2,1)S(1)} %get-tuple-element.137), channel_id=1, source_target_pairs={{0,1},{1,0},{2,3},{3,2},{4,5},{5,4},{6,7},{7,6},{8,9},{9,8},{10,11... | collective-permute-start | bytes 589832 | tf_op jit(solution)/shard_map/ppermute | solution.py:706
  133.1 8.9 %copy-start = (bf16[768,2304]{1,0:T(8,128)(2,1)S(1)}, bf16[768,2304]{1,0:T(8,128)(2,1)}, u32[]{:S(2)}) copy-start(bf16[768,2304]{1,0:T(8,128)(2,1)} %w_ref.3) | copy-start | bytes 10616836
  133.1 8.9 %copy-start.2 = (f32[512,768]{1,0:T(8,128)S(1)}, f32[512,768]{1,0:T(8,128)}, u32[]{:S(2)}) copy-start(f32[512,768]{1,0:T(8,128)} %copy-done.1) | copy-start | bytes 4718596
  153.2 23.3 %collective-permute-start.17 = (bf16[8,48,1536]{2,1,0:T(8,128)(2,1)S(1)}, bf16[8,48,1536]{2,1,0:T(8,128)(2,1)S(1)}, u32[]{:S(2)}, u32[]{:S(2)}) collective-permute-start(bf16[8,48,1536]{2,1,0:T(8,128)(2,1)S(1)} %get-tuple-element.143), channel_id=1, source_target_pairs={{0,2},{1,5},{2,0},{3,7},{4,6},{5,1},{6,4},{7,3},{8,10},{9,13},{10,... | collective-permute-start | bytes 3538952 | tf_op jit(solution)/shard_map/ppermute | solution.py:711
  154.5 24.0 %collective-permute-start.22 = (bf16[4,48,1920]{2,1,0:T(8,128)(2,1)S(1)}, bf16[4,48,1920]{2,1,0:T(8,128)(2,1)S(1)}, u32[]{:S(2)}, u32[]{:S(2)}) collective-permute-start(bf16[4,48,1920]{2,1,0:T(8,128)(2,1)S(1)} %get-tuple-element.154), channel_id=1, source_target_pairs={{0,4},{1,3},{2,6},{3,1},{4,0},{5,7},{6,2},{7,5},{8,12},{9,11},{10,... | collective-permute-start | bytes 2211848 | tf_op jit(solution)/shard_map/ppermute | solution.py:711
  177.4 12.2 %copy-start.28 = (bf16[256,768]{1,0:T(8,128)(2,1)S(1)}, bf16[256,768]{1,0:T(8,128)(2,1)}, u32[]{:S(2)}) copy-start(bf16[256,768]{1,0:T(8,128)(2,1)} %copy-done.27) | copy-start | bytes 1179652
  177.4 9.1 %collective-permute-start.18 = (bf16[4,48,1536]{2,1,0:T(8,128)(2,1)S(1)}, bf16[4,48,1536]{2,1,0:T(8,128)(2,1)S(1)}, u32[]{:S(2)}, u32[]{:S(2)}) collective-permute-start(bf16[4,48,1536]{2,1,0:T(8,128)(2,1)S(1)} %get-tuple-element.145), channel_id=1, source_target_pairs={{0,4},{1,3},{2,6},{3,1},{4,0},{5,7},{6,2},{7,5},{8,12},{9,11},{10,... | collective-permute-start | bytes 1769480 | tf_op jit(solution)/shard_map/ppermute | solution.py:711
  179.3 11.9 %collective-permute-start.23 = (bf16[2,48,1920]{2,1,0:T(8,128)(2,1)S(1)}, bf16[2,48,1920]{2,1,0:T(8,128)(2,1)S(1)}, u32[]{:S(2)}, u32[]{:S(2)}) collective-permute-start(bf16[2,48,1920]{2,1,0:T(8,128)(2,1)S(1)} %get-tuple-element.156), channel_id=1, source_target_pairs={{0,8},{1,17},{2,10},{3,19},{4,12},{5,21},{6,14},{7,23},{8,0},{9,25... | collective-permute-start | bytes 1105928 | tf_op jit(solution)/shard_map/ppermute | solution.py:711
  181.6 17.4 %collective-permute-start.26 = (bf16[2,192,384]{2,1,0:T(8,128)(2,1)S(1)}, bf16[2,192,384]{2,1,0:T(8,128)(2,1)S(1)}, u32[]{:S(2)}, u32[]{:S(2)}) collective-permute-start(bf16[2,192,384]{2,1,0:T(8,128)(2,1)S(1)} %get-tuple-element.161), channel_id=1, source_target_pairs={{0,8},{1,17},{2,10},{3,19},{4,12},{5,21},{6,14},{7,23},{8,0},{9,25... | collective-permute-start | bytes 884744 | tf_op jit(solution)/shard_map/ppermute | solution.py:711
  187.2 19.2 %collective-permute-start.19 = (bf16[2,48,1536]{2,1,0:T(8,128)(2,1)S(1)}, bf16[2,48,1536]{2,1,0:T(8,128)(2,1)S(1)}, u32[]{:S(2)}, u32[]{:S(2)}) collective-permute-start(bf16[2,48,1536]{2,1,0:T(8,128)(2,1)S(1)} %get-tuple-element.147), channel_id=1, source_target_pairs={{0,8},{1,17},{2,10},{3,19},{4,12},{5,21},{6,14},{7,23},{8,0},{9,25... | collective-permute-start | bytes 884744 | tf_op jit(solution)/shard_map/ppermute | solution.py:711
  189.6 30.9 %collective-permute-start.2 = (bf16[256,768]{1,0:T(8,128)(2,1)S(1)}, bf16[256,768]{1,0:T(8,128)(2,1)}, u32[]{:S(2)}, u32[]{:S(2)}) collective-permute-start(bf16[256,768]{1,0:T(8,128)(2,1)S(1)} %copy-done.28), channel_id=1, source_target_pairs={{0,1},{1,0},{2,3},{3,2},{4,5},{5,4},{6,7},{7,6},{8,9},{9,8},{10,11... | collective-permute-start | bytes 1179656 | tf_op jit(solution)/shard_map/ppermute | solution.py:706
  191.1 31.5 %collective-permute-start.12 = (bf16[256,768]{1,0:T(8,128)(2,1)}, bf16[256,768]{1,0:T(8,128)(2,1)S(1)}, u32[]{:S(2)}, u32[]{:S(2)}) collective-permute-start(bf16[256,768]{1,0:T(8,128)(2,1)} %get-tuple-element.132), channel_id=1, source_target_pairs={{0,1},{1,0},{2,3},{3,2},{4,5},{5,4},{6,7},{7,6},{8,9},{9,8},{10,11... | collective-permute-start | bytes 1179656 | tf_op jit(solution)/shard_map/ppermute | solution.py:706
  191.2 29.3 %copy-start.14 = (bf16[256,768]{1,0:T(8,128)(2,1)S(1)}, bf16[256,768]{1,0:T(8,128)(2,1)}, u32[]{:S(2)}) copy-start(bf16[256,768]{1,0:T(8,128)(2,1)} %copy-done.13) | copy-start | bytes 1179652
  191.8 23.1 %collective-permute-start.24 = (bf16[1,48,1920]{2,1,0:T(8,128)(2,1)S(1)}, bf16[1,48,1920]{2,1,0:T(8,128)(2,1)S(1)}, u32[]{:S(2)}, u32[]{:S(2)}) collective-permute-start(bf16[1,48,1920]{2,1,0:T(8,128)(2,1)S(1)} %get-tuple-element.158), channel_id=1, source_target_pairs={{0,16},{1,9},{2,18},{3,11},{4,20},{5,13},{6,22},{7,15},{8,24},{9,1... | collective-permute-start | bytes 552968 | tf_op jit(solution)/shard_map/ppermute | solution.py:711
  199.7 10.4 %collective-permute-start.27 = (bf16[1,192,384]{2,1,0:T(8,128)(2,1)S(1)}, bf16[1,192,384]{2,1,0:T(8,128)(2,1)S(1)}, u32[]{:S(2)}, u32[]{:S(2)}) collective-permute-start(bf16[1,192,384]{2,1,0:T(8,128)(2,1)S(1)} %get-tuple-element.163), channel_id=1, source_target_pairs={{0,16},{1,9},{2,18},{3,11},{4,20},{5,13},{6,22},{7,15},{8,24},{9,1... | collective-permute-start | bytes 442376 | tf_op jit(solution)/shard_map/ppermute | solution.py:711
  207.1 8.5 %collective-permute-start.20 = (bf16[1,48,1536]{2,1,0:T(8,128)(2,1)S(1)}, bf16[1,48,1536]{2,1,0:T(8,128)(2,1)S(1)}, u32[]{:S(2)}, u32[]{:S(2)}) collective-permute-start(bf16[1,48,1536]{2,1,0:T(8,128)(2,1)S(1)} %get-tuple-element.149), channel_id=1, source_target_pairs={{0,16},{1,9},{2,18},{3,11},{4,20},{5,13},{6,22},{7,15},{8,24},{9,1... | collective-permute-start | bytes 442376 | tf_op jit(solution)/shard_map/ppermute | solution.py:711
  210.7 12.9 %collective-permute-start.28 = (bf16[192,384]{1,0:T(8,128)(2,1)S(1)}, bf16[192,384]{1,0:T(8,128)(2,1)S(1)}, u32[]{:S(2)}, u32[]{:S(2)}) collective-permute-start(bf16[192,384]{1,0:T(8,128)(2,1)S(1)} %add_last.5.mine_ref), channel_id=1, source_target_pairs={{0,1},{1,0},{2,3},{3,2},{4,5},{5,4},{6,7},{7,6},{8,9},{9,8},{10,11... | collective-permute-start | bytes 442376 | tf_op jit(solution)/shard_map/ppermute | solution.py:706
  215.5 9.5 %collective-permute-start.25 = (bf16[48,1920]{1,0:T(8,128)(2,1)S(1)}, bf16[48,1920]{1,0:T(8,128)(2,1)S(1)}, u32[]{:S(2)}, u32[]{:S(2)}) collective-permute-start(bf16[48,1920]{1,0:T(8,128)(2,1)S(1)} %add_last.4.mine_ref), channel_id=1, source_target_pairs={{0,1},{1,0},{2,3},{3,2},{4,5},{5,4},{6,7},{7,6},{8,9},{9,8},{10,11... | collective-permute-start | bytes 552968 | tf_op jit(solution)/shard_map/ppermute | solution.py:706
  216.1 10.3 %collective-permute-start.21 = (bf16[48,1536]{1,0:T(8,128)(2,1)S(1)}, bf16[48,1536]{1,0:T(8,128)(2,1)S(1)}, u32[]{:S(2)}, u32[]{:S(2)}) collective-permute-start(bf16[48,1536]{1,0:T(8,128)(2,1)S(1)} %add_last.3.mine_ref), channel_id=1, source_target_pairs={{0,1},{1,0},{2,3},{3,2},{4,5},{5,4},{6,7},{7,6},{8,9},{9,8},{10,11... | collective-permute-start | bytes 442376 | tf_op jit(solution)/shard_map/ppermute | solution.py:706
  (19 other events, 24.9 us)

commit v3 on v2

--- a/solution.py
+++ b/solution.py
@@ -13,7 +13,9 @@
 HEADS = 12
 PAIRS = HEADS // 2
 BIG = 1e9
+COST = 0.6e9
 SDS = jax.ShapeDtypeStruct
+HBM = pltpu.HBM
 
 
 def mm(a, b):
@@ -24,11 +26,15 @@
     return lax.dot_general(a, b, (((1,), (1,)), ((), ())), preferred_element_type=F32)
 
 
+def wide(ref):
+    return ref[...].astype(F32).reshape(1, ref.shape[0])
+
+
 def whole(shape):
     return pl.BlockSpec(shape, lambda *_: (0,) * len(shape))
 
 
-def call(kernel, name, grid, ids, args, in_specs, out_specs, out_shape, scratch=(), vmem=40, flops=0, moved=0):
+def call(kernel, name, grid, ids, args, in_specs, out_specs, out_shape, scratch=(), vmem=17, us=1.0):
     return pl.pallas_call(
         kernel,
         grid_spec=pltpu.PrefetchScalarGridSpec(
@@ -36,7 +42,7 @@
         ),
         out_shape=out_shape,
         compiler_params=pltpu.CompilerParams(vmem_limit_bytes=vmem << 20),
-        cost_estimate=pl.CostEstimate(flops=flops, bytes_accessed=moved, transcendentals=0),
+        cost_estimate=pl.CostEstimate(flops=int(us * COST), bytes_accessed=0, transcendentals=0),
         name=name,
     )(ids, *args)
 
@@ -59,8 +65,50 @@
     return sine, cosine
 
 
-def project_kernel(ids, own_ref, other_ref, w_ref, b_ref, box_ref, rrow_ref, rcol_ref, wk_ref, wq_ref,
-                   pt_ref, p_ref, xt_ref, kf_ref, tab_ref, tabt_ref, fkt_ref, fqt_ref, wkt_ref, wqt_ref, x):
+def tables_kernel(ids, box_ref, rrow_ref, rcol_ref, wk_ref, wq_ref,
+                  kf_ref, tab_ref, tabt_ref, fkt_ref, fqt_ref, wkt_ref, wqt_ref):
+    half = kf_ref.shape[0] // 2
+    wkt_ref[...] = wk_ref[...].T
+    wqt_ref[...] = wq_ref[...].T
+    box = box_ref[0].astype(F32)
+    centre = (box[0:2, :] + box[2:4, :]) * 0.5
+    turned = jnp.concatenate([centre[:, half:], centre[:, :half]], 1)
+    centre = jnp.where(ids[1] == 0, centre, turned)
+    column = jnp.concatenate([centre, jnp.zeros((6, 2 * half), F32)], 0).T
+    front = lax.broadcasted_iota(jnp.int32, (2 * half, 128), 1) < 64
+    for axis in range(2):
+        s, c = sin_cos(column[:, axis : axis + 1] * rrow_ref[...])
+        kf_ref[:, axis * 128 : axis * 128 + 128] = jnp.where(front, c, s).astype(BF16)
+        tab_ref[axis] = c
+        tab_ref[2 + axis] = jnp.where(front, s, -s)
+        st, ct = sin_cos(rcol_ref[...] * centre[axis : axis + 1, :])
+        tabt_ref[2 * axis] = st
+        tabt_ref[2 * axis + 1] = ct
+        sl, cl = st.astype(BF16), ct.astype(BF16)
+        at = 128 * axis
+        fkt_ref[at : at + 64, :] = cl
+        fkt_ref[at + 64 : at + 128, :] = sl
+        fqt_ref[at : at + 64, :] = sl * 0.125
+        fqt_ref[at + 64 : at + 128, :] = cl * 0.125
+
+
+def tables(ids, boxes, wk, wq):
+    rows = boxes.shape[2]
+    width = wk.shape[1]
+    rates = np.exp(np.arange(64) * (-math.log(10000.0) / 64)).astype(np.float32)
+    shapes = [((rows, 256), BF16), ((4, rows, 128), F32), ((4, 64, rows), F32), ((256, rows), BF16), ((256, rows), BF16),
+              ((width, 256), BF16), ((width, 256), BF16)]
+    return call(
+        tables_kernel, "tables", (1,), ids, (boxes, np.tile(rates, 2)[None, :], rates[:, None], wk, wq),
+        [
+            pl.BlockSpec((1, 4, rows), lambda i, ids: (ids[1], 0, 0)),
+            whole((1, 128)), whole((64, 1)), whole((256, width)), whole((256, width)),
+        ],
+        [whole(s) for s, _ in shapes], [SDS(s, t) for s, t in shapes], us=3,
+    )
+
+
+def project_kernel(ids, own_ref, other_ref, w_ref, b_ref, pt_ref, p_ref, xt_ref, x, bias):
     step = pl.program_id(0)
 
     @pl.when(step == 0)
@@ -68,31 +116,12 @@
         half = own_ref.shape[1]
         x[:half, :] = own_ref[0]
         x[half:, :] = other_ref[0]
+        bias[...] = wide(b_ref)
         xt_ref[...] = x[...].T
-        wkt_ref[...] = wk_ref[...].T
-        wqt_ref[...] = wq_ref[...].T
-        box = box_ref[0].astype(F32)
-        centre = (box[0:2, :] + box[2:4, :]) * 0.5
-        turned = jnp.concatenate([centre[:, half:], centre[:, :half]], 1)
-        centre = jnp.where(ids[1] == 0, centre, turned)
-        column = jnp.concatenate([centre, jnp.zeros((6, 2 * half), F32)], 0).T
-        front = lax.broadcasted_iota(jnp.int32, (2 * half, 128), 1) < 64
-        for axis in range(2):
-            s, c = sin_cos(column[:, axis : axis + 1] * rrow_ref[...])
-            kf_ref[:, axis * 128 : axis * 128 + 128] = jnp.where(front, c, s).astype(BF16)
-            tab_ref[axis] = c
-            tab_ref[2 + axis] = jnp.where(front, s, -s)
-            st, ct = sin_cos(rcol_ref[...] * centre[axis : axis + 1, :])
-            tabt_ref[2 * axis] = st
-            tabt_ref[2 * axis + 1] = ct
-            sl, cl = st.astype(BF16), ct.astype(BF16)
-            at = 128 * axis
-            fkt_ref[at : at + 64, :] = cl
-            fkt_ref[at + 64 : at + 128, :] = sl
-            fqt_ref[at : at + 64, :] = sl * 0.125
-            fqt_ref[at + 64 : at + 128, :] = cl * 0.125
-
-    p = (mm(x[...], w_ref[...]) + b_ref[...]).astype(BF16)
+
+    block = w_ref.shape[1]
+    shift = bias[:, pl.ds(pl.multiple_of(step * block, 128), block)]
+    p = (mm(x[...], w_ref[...]) + shift).astype(BF16)
     p_ref[...] = p
     pt_ref[...] = p.T
 
@@ -102,39 +131,25 @@
     return spec, spec
 
 
-def project(ids, tokens, other, w, vectors, boxes, wk, wq):
+def project(ids, tokens, other, w, b):
     _, half, width = tokens.shape
     rows = 2 * half
     cols = w.shape[1]
     block = 768
-    rates = np.exp(np.arange(64) * (-math.log(10000.0) / 64)).astype(np.float32)
-    return call(
-        project_kernel, "project", (cols // block,), ids,
-        (tokens, other, w, vectors, boxes, np.tile(rates, 2)[None, :], rates[:, None], wk, wq),
-        [
-            *page_specs(half, width),
-            pl.BlockSpec((width, block), lambda i, ids: (0, i)),
-            pl.BlockSpec((1, block), lambda i, ids: (0, 4 + i)),
-            pl.BlockSpec((1, 4, rows), lambda i, ids: (ids[1], 0, 0)),
-            whole((1, 128)), whole((64, 1)), whole((256, width)), whole((256, width)),
-        ],
-        [
-            pl.BlockSpec((block, rows), lambda i, ids: (i, 0)),
-            pl.BlockSpec((rows, block), lambda i, ids: (0, i)),
-            whole((width, rows)), whole((rows, 256)), whole((4, rows, 128)), whole((4, 64, rows)),
-            whole((256, rows)), whole((256, rows)), whole((width, 256)), whole((width, 256)),
-        ],
-        [
-            SDS((cols, rows), BF16), SDS((rows, cols), BF16), SDS((width, rows), BF16), SDS((rows, 256), BF16),
-            SDS((4, rows, 128), F32), SDS((4, 64, rows), F32), SDS((256, rows), BF16), SDS((256, rows), BF16),
-            SDS((width, 256), BF16), SDS((width, 256), BF16),
-        ],
-        [pltpu.VMEM((rows, width), BF16)],
-        flops=2 * rows * width * cols, moved=2 * (width * cols + 2 * rows * cols),
-    )
-
-
-def attend_kernel(ids, qt_ref, vt_ref, k_ref, wk_ref, wq_ref, kf_ref, tab_ref, tabt_ref, fqt_ref,
+    return call(
+        project_kernel, "project", (cols // block,), ids, (tokens, other, w, b),
+        [*page_specs(half, width), pl.BlockSpec((width, block), lambda i, ids: (0, i)), whole((cols,))],
+        [
+            pl.BlockSpec((block, rows), lambda i, ids: (i, 0)), pl.BlockSpec((rows, block), lambda i, ids: (0, i)),
+            whole((width, rows)),
+        ],
+        [SDS((cols, rows), BF16), SDS((rows, cols), BF16), SDS((width, rows), BF16)],
+        [pltpu.VMEM((rows, width), BF16), pltpu.VMEM((1, cols), F32)],
+        us=5,
+    )
+
+
+def attend_kernel(ids, len_ref, qt_ref, vt_ref, k_ref, wk_ref, wq_ref, kf_ref, tab_ref, tabt_ref, fqt_ref,
                   e_ref, at_ref, r_ref, fk, fq):
     rows = k_ref.shape[0]
 
@@ -145,7 +160,7 @@
         turned = jnp.where(at < rows // 2, at + rows // 2, at - rows // 2)
         at = jnp.where(ids[1] == 0, at, turned)
         fk[:, 0:256] = kf_ref[...]
-        fk[:, 640:768] = jnp.where((lane == 0) & (at >= ids[2]), -BIG, 0.0).astype(BF16)
+        fk[:, 640:768] = jnp.where((lane == 0) & (at >= len_ref[ids[1]]), -BIG, 0.0).astype(BF16)
         fq[256:512, :] = fqt_ref[...]
         sub = lax.broadcasted_iota(jnp.int32, (128, rows), 0)
         fq[640:768, :] = jnp.where(sub == 0, 1.0, 0.0).astype(BF16)
@@ -182,12 +197,13 @@
         r_ref[0, h : h + 1, :] = r
 
 
-def attend(ids, pt, p, w_posk, w_posq, kf, tab, tabt, fqt):
+def attend(ids, lengths, pt, p, w_posk, w_posq, kf, tab, tabt, fqt):
     rows = p.shape[0]
     width = pt.shape[0] // 3
     return call(
-        attend_kernel, "attend", (PAIRS,), ids, (pt, pt, p, w_posk, w_posq, kf, tab, tabt, fqt),
-        [
+        attend_kernel, "attend", (PAIRS,), ids, (lengths, pt, pt, p, w_posk, w_posq, kf, tab, tabt, fqt),
+        [
+            pl.BlockSpec(memory_space=pltpu.SMEM),
             pl.BlockSpec((128, rows), lambda i, ids: (i, 0)),
             pl.BlockSpec((128, rows), lambda i, ids: (2 * PAIRS + i, 0)),
             pl.BlockSpec((rows, 128), lambda i, ids: (0, PAIRS + i)),
@@ -200,9 +216,9 @@
             pl.BlockSpec((128, rows), lambda i, ids: (i, 0)),
             pl.BlockSpec((1, 2, rows), lambda i, ids: (i, 0, 0)),
         ],
-        [SDS((HEADS, rows, rows), BF16), SDS((width, rows), BF16), SDS((PAIRS, 2, rows), F32)],
+        [HBM((HEADS, rows, rows), BF16), SDS((width, rows), BF16), SDS((PAIRS, 2, rows), F32)],
         [pltpu.VMEM((rows, 768), BF16), pltpu.VMEM((768, rows), BF16)],
-        flops=2 * HEADS * rows * rows * 640, moved=2 * HEADS * rows * rows,
+        us=17,
     )
 
 
@@ -218,20 +234,20 @@
         first[:half, :] = own_ref[0].astype(F32)
         first[half:, :] = other_ref[0].astype(F32)
         cot[:half, :] = cown_ref[0]
-        cot[half:, :] = cother_ref[...]
-        v = first[...] + (mm(at_ref[...].T, wo_ref[...]) + bo_ref[...])
+        cot[half:, :] = cother_ref[0]
+        v = first[...] + (mm(at_ref[...].T, wo_ref[...]) + wide(bo_ref))
         c = v - jnp.mean(v, -1, keepdims=True)
         rstd = lax.rsqrt(jnp.mean(c * c, -1, keepdims=True) + 1e-6)
         normed = c * rstd
         norm_ref[...] = normed
         rstd_ref[...] = rstd
-        f = normed * g1_ref[...] + s1_ref[...]
-        first[...] = f + bd_ref[...]
+        f = normed * wide(g1_ref) + wide(s1_ref)
+        first[...] = f + wide(bd_ref)
         l = f.astype(BF16)
         low[...] = l
         flt_ref[...] = l.T
 
-    h = mm(low[...], wi_ref[...]) + bi_ref[...]
+    h = mm(low[...], wi_ref[...]) + wide(bi_ref)
     cdf = 0.5 * lax.erf(h * (0.5 ** 0.5)) + 0.5
     active = (h * cdf).astype(BF16)
     slope_ref[...] = (cdf + h * (jnp.exp(-0.5 * h * h) * ((2.0 * math.pi) ** -0.5))).astype(BF16)
@@ -252,11 +268,11 @@
         c = v - jnp.mean(v, -1, keepdims=True)
         rstd = lax.rsqrt(jnp.mean(c * c, -1, keepdims=True) + 1e-6)
         normed = c * rstd
-        out = (normed * g2_ref[...] + s2_ref[...]).astype(BF16)
-        keep_ref[...] = out[:half, :]
+        out = (normed * wide(g2_ref) + wide(s2_ref)).astype(BF16)
+        keep_ref[0] = out[:half, :]
         give_ref[...] = out[half:, :]
         g = cot[...].astype(F32)
-        gg = g * g2_ref[...]
+        gg = g * wide(g2_ref)
         d = rstd * (
             gg - jnp.mean(gg, -1, keepdims=True) - normed * jnp.mean(gg * normed, -1, keepdims=True)
         )
@@ -271,11 +287,11 @@
         rows_ref[3:8, :] = jnp.zeros((5, rows_ref.shape[1]), F32)
 
 
-def vec(at):
-    return pl.BlockSpec((1, 768), lambda i, ids: (0, at))
-
-
-def feed(ids, att, tokens, other, w_out, w_in, w_down, vectors, cot, cot_other):
+def vec(size):
+    return pl.BlockSpec((size,), lambda i, ids: (0,))
+
+
+def feed(ids, att, tokens, other, w_out, w_in, w_down, b_out, g1, s1, b_in, b_down, g2, s2, cot, cot_other):
     _, half, width = tokens.shape
     rows = 2 * half
     ff = w_in.shape[1]
@@ -283,30 +299,29 @@
     mat = whole((rows, width))
     return call(
         feed_kernel, "feed", (ff // block,), ids,
-        (att, tokens, other, w_out, vectors, vectors, vectors, w_in, vectors, w_down, vectors, vectors, vectors,
-         cot, cot_other),
-        [
-            whole((width, rows)), *page_specs(half, width), whole((width, width)), vec(7), vec(8), vec(9),
+        (att, tokens, other, w_out, b_out, g1, s1, w_in, b_in, w_down, b_down, g2, s2, cot, cot_other),
+        [
+            whole((width, rows)), *page_specs(half, width), whole((width, width)), vec(width), vec(width), vec(width),
             pl.BlockSpec((width, block), lambda i, ids: (0, i)),
-            pl.BlockSpec((1, block), lambda i, ids: (0, i)),
+            pl.BlockSpec((block,), lambda i, ids: (i,)),
             pl.BlockSpec((block, width), lambda i, ids: (i, 0)),
-            vec(10), vec(11), vec(12), page_specs(half, width)[0], whole((half, width)),
+            vec(width), vec(width), vec(width), *page_specs(half, width),
         ],
         [
             whole((width, rows)), mat, whole((rows, 1)),
             pl.BlockSpec((rows, block), lambda i, ids: (0, i)),
             pl.BlockSpec((block, rows), lambda i, ids: (i, 0)),
-            whole((half, width)), whole((half, width)), mat, mat, whole((rows, width // 2)), whole((8, width)),
+            page_specs(half, width)[0], whole((half, width)), mat, mat, whole((rows, width // 2)), whole((8, width)),
         ],
         [
             SDS((width, rows), BF16), SDS((rows, width), F32), SDS((rows, 1), F32),
             SDS((rows, ff), BF16), SDS((ff, rows), BF16),
-            SDS((half, width), BF16), SDS((half, width), BF16), SDS((rows, width), F32), SDS((rows, width), BF16),
+            SDS((2, half, width), BF16), SDS((half, width), BF16), SDS((rows, width), F32), SDS((rows, width), BF16),
             SDS((rows, width // 2), BF16), SDS((8, width), F32),
         ],
         [pltpu.VMEM((rows, width), F32), pltpu.VMEM((rows, width), BF16), pltpu.VMEM((rows, width), F32),
          pltpu.VMEM((rows, width), BF16)],
-        flops=2 * rows * width * (width + 2 * ff), moved=2 * (2 * width * ff + 2 * rows * ff),
+        us=15,
     )
 
 
@@ -346,7 +361,7 @@
             pl.BlockSpec((1, block), lambda i, ids: (0, at(i, ids))),
         ],
         [SDS((rows, ff // 2), BF16), SDS((rows, ff // 2), BF16), SDS((1, ff), F32)],
-        flops=2 * rows * width * ff, moved=2 * (width * ff + 2 * rows * ff),
+        us=5,
     )
 
 
@@ -367,7 +382,7 @@
     def _():
         g = dres_ref[...] + acc[...].astype(BF16).astype(F32)
         normed = norm_ref[...]
-        gg = g * g1_ref[...]
+        gg = g * wide(g1_ref)
         d = rstd_ref[...] * (
             gg - jnp.mean(gg, -1, keepdims=True) - normed * jnp.mean(gg * normed, -1, keepdims=True)
         )
@@ -383,20 +398,20 @@
         rows_ref[3:8, :] = jnp.zeros((5, rows_ref.shape[1]), F32)
 
 
-def first_back(ids, dsend, down, w_in, dres, norm, rstd, vectors, w_out):
+def first_back(ids, dsend, down, w_in, dres, norm, rstd, g1, w_out):
     rows, width = dres.shape
     ff = w_in.shape[1]
     block = 512
     s = ff // block // 2
     mat = whole((rows, width))
     return call(
-        first_kernel, "first_back", (s,), ids, (dsend, down, w_in, w_in, dres, norm, rstd, vectors, w_out),
+        first_kernel, "first_back", (s,), ids, (dsend, down, w_in, w_in, dres, norm, rstd, g1, w_out),
         [
             pl.BlockSpec((rows, block), lambda i, ids: (0, i)),
             pl.BlockSpec((rows, block), lambda i, ids: (0, i)),
             pl.BlockSpec((width, block), lambda i, ids: (0, (1 - ids[1]) * s + i)),
             pl.BlockSpec((width, block), lambda i, ids: (0, ids[1] * s + i)),
-            mat, mat, whole((rows, 1)), vec(8), whole((width, width)),
+            mat, mat, whole((rows, 1)), vec(width), whole((width, width)),
         ],
         [mat, mat, whole((rows, width // 2)), whole((width, rows)), whole((8, width))],
         [
@@ -404,12 +419,12 @@
             SDS((8, width), F32),
         ],
         [pltpu.VMEM((rows, width), F32)],
-        flops=2 * rows * width * (width + ff), moved=2 * (width * ff + rows * ff + 5 * rows * width),
+        us=8,
     )
 
 
 def attend_back_kernel(ids, e_ref, r_ref, da_ref, at_ref, qt_ref, kt_ref, v_ref, wkt_ref, wqt_ref, fkt_ref, fqt_ref,
-                       tabt_ref, dp_ref, gk_ref, gq_ref, left_k, left_q):
+                       tabt_ref, dp_ref, gk_ref, gq_ref, rows_ref, left_k, left_q):
     @pl.when(pl.program_id(0) == 0)
     def _():
         left_k[64:320, :] = fkt_ref[...]
@@ -447,6 +462,9 @@
         gq.append(mm_nt(d_b, kt_ref[...]))
     gk_ref[...] = jnp.where(lane < 64, gk[0], gk[1]).astype(BF16)
     gq_ref[...] = jnp.where(lane < 64, gq[0], gq[1]).astype(BF16)
+    ones = jnp.ones((8, dp_ref.shape[2]), BF16)
+    for i in range(3):
+        rows_ref[8 * i : 8 * i + 8, :] = mm_nt(ones, dp_ref[i])
 
 
 def attend_back(ids, own, e, r, datt, att, pt, p, wkt, wqt, fkt, fqt, tabt):
@@ -468,17 +486,21 @@
             pl.BlockSpec((3, 128, rows), lambda i, ids: (0, i, 0)),
             pl.BlockSpec((256, 128), lambda i, ids: (0, i)),
             pl.BlockSpec((256, 128), lambda i, ids: (0, i)),
-        ],
-        [SDS((3, 128 * pairs, rows), BF16), SDS((256, 128 * pairs), BF16), SDS((256, 128 * pairs), BF16)],
+            pl.BlockSpec((24, 128), lambda i, ids: (0, i)),
+        ],
+        [
+            SDS((3, 128 * pairs, rows), BF16), SDS((256, 128 * pairs), BF16), SDS((256, 128 * pairs), BF16),
+            SDS((24, 128 * pairs), F32),
+        ],
         [pltpu.VMEM((320, rows), BF16), pltpu.VMEM((320, rows), BF16)],
-        flops=2 * 2 * pairs * rows * rows * 900, moved=2 * 2 * pairs * rows * rows,
-    )
-
-
-def tokens_kernel(ids, w_ref, ds_ref, do_ref, dres_ref, keep_ref, give_ref, rows_ref):
+        us=9,
+    )
+
+
+def tokens_kernel(ids, w_ref, ds_ref, do_ref, dres_ref, keep_ref, give_ref):
     width = w_ref.shape[1] // 3
     side = width // 2
-    half = keep_ref.shape[0]
+    half = keep_ref.shape[1]
     acc = None
     for h, ref in ((1 - ids[1], ds_ref), (ids[1], do_ref)):
         for s in range(3):
@@ -486,17 +508,8 @@
             part = mm(w_ref[:, pl.ds(at, side)], ref[s])
             acc = part if acc is None else acc + part
     out = (dres_ref[...] + acc.T).astype(BF16)
-    keep_ref[...] = out[:half, :]
+    keep_ref[0] = out[:half, :]
     give_ref[...] = out[half:, :]
-
-    @pl.when(pl.program_id(0) == 0)
-    def _():
-        ones = jnp.ones((8, ds_ref.shape[2]), BF16)
-        for s in range(3):
-            for h, ref in ((1 - ids[1], ds_ref), (ids[1], do_ref)):
-                at = pl.multiple_of(h * side, 128)
-                rows_ref[s : s + 1, pl.ds(at, side)] = mm_nt(ones, ref[s])[0:1, :]
-        rows_ref[3:8, :] = jnp.zeros((5, width), F32)
 
 
 def tokens_back(ids, w_qkv, dsend, down, dres):
@@ -511,9 +524,9 @@
             pl.BlockSpec((block, cols), lambda i, ids: (i, 0)), whole(dsend.shape), whole(down.shape),
             pl.BlockSpec((rows, block), lambda i, ids: (0, i)),
         ],
-        [blk, blk, whole((8, width))],
-        [SDS((half, width), BF16), SDS((half, width), BF16), SDS((8, width), F32)],
-        flops=2 * rows * width * cols, moved=2 * (width * cols + rows * cols + 3 * rows * width),
+        [pl.BlockSpec((1, half, block), lambda i, ids: (ids[1], 0, i)), blk],
+        [SDS((2, half, width), BF16), SDS((half, width), BF16)],
+        us=6,
     )
 
 
@@ -558,7 +571,7 @@
         functools.partial(down_kernel, n, bits), "down_grad", (4,), ids, (actt, actt_other, dsec, dsec_other),
         [a, a, pl.BlockSpec((rows, side), lambda i, ids: (0, ids[1])), whole((rows, side))],
         [whole(part)] * 2, [SDS(part, BF16)] * 2,
-        flops=4 * ff * rows * side, moved=2 * (2 * ff * rows + ff * side),
+        us=7,
     )
 
 
@@ -596,8 +609,7 @@
         functools.partial(mid_kernel, n, bits), "mid_grad", (steps + 1,), ids,
         (flt, flt_other, dh, dh_other, att, att_other, branch, branch_other),
         [a, a, b, b, a, a, pl.BlockSpec((rows, side), lambda i, ids: (0, ids[1])), whole((rows, side))],
-        [whole(part)] * 2, [SDS(part, BF16)] * 2,
-        flops=4 * width * rows * (ffs + side), moved=2 * (2 * ffs * rows + 2 * width * (ffs + side)),
+        [whole(part)] * 2, [SDS(part, BF16)] * 2, us=6,
     )
 
 
@@ -613,59 +625,76 @@
     return plan, at
 
 
-def qkv_kernel(n, bits, sizes, ids, x0_ref, x1_ref, d0_ref, d1_ref, k0_ref, k1_ref, q0_ref, q1_ref,
-               two_ref, one_ref, in_ref, qkv_ref, send_ref, keep_ref):
-    step = pl.program_id(0)
-    last = pl.num_programs(0) - 1
+def qk_kernel(n, bits, sizes, ids, x0_ref, x1_ref, d0_ref, d1_ref, two_ref, one_ref, in_ref, rs_ref, ro_ref,
+              send_ref, keep_ref, qkv_ref):
     r = keep_ref.shape[1]
     side = d0_ref.shape[1]
-
-    @pl.when(step < last)
-    def _():
-        acc = mm_nt(x0_ref[...], d0_ref[0]) + mm_nt(x1_ref[...], d1_ref[0])
-        lanes = pl.ds(pl.multiple_of(step * side, 128), side)
+    for who, ref in ((1 - ids[1], rs_ref), (ids[1], ro_ref)):
+        for i in range(3):
+            at = pl.multiple_of(who * side, 128)
+            qkv_ref[i : i + 1, pl.ds(at, side)] = ref[8 * i : 8 * i + 1, :]
+    for i in range(2):
+        acc = mm_nt(x0_ref[...], d0_ref[i]) + mm_nt(x1_ref[...], d1_ref[i])
         for p in range(n):
-            put(ids, bits, p, lanes, acc[p * r : p * r + r, :].astype(BF16), send_ref, keep_ref)
-
-    @pl.when(step == last)
-    def _():
-        base = 3 * side
-        for own_ref, other_ref in ((k0_ref, k1_ref), (q0_ref, q1_ref)):
-            acc = (own_ref[...].astype(F32) + other_ref[...].astype(F32)).astype(BF16)
-            s = acc.shape[0] // n
-            for p in range(n):
-                rows = acc[p * s : p * s + s, :]
-                stacked = jnp.concatenate([rows[:, 128 * i : 128 * i + 128] for i in range(side // 128)], 0)
-                put(ids, bits, p, slice(base, base + 128), stacked, send_ref, keep_ref)
-            base += 128
-        vectors = (qkv_ref, one_ref, one_ref, one_ref, in_ref, two_ref, two_ref, two_ref)
-        index = (None, 2, 0, 1, 0, 2, 0, 1)
-        plan, _ = small_plan(n, sizes)
-        for p in range(n):
-            found = []
-            for (size, count, _), ref, row in zip(plan, vectors, index):
-                for c in range(count):
-                    at = min(p * size // 128 + c, n * size // 128 - 1)
-                    if row is None:
-                        i, at = at * 128 // ref.shape[1], at * 128 % ref.shape[1]
-                        found.append(ref[i : i + 1, at : at + 128])
-                    else:
-                        found.append(ref[row : row + 1, at * 128 : at * 128 + 128])
-            found = jnp.concatenate(found + [jnp.zeros((r - len(found), 128), F32)], 0).astype(BF16)
-            put(ids, bits, p, slice(base, base + 128), found, send_ref, keep_ref)
-
-
-def qkv_grad(ids, n, bits, sizes, xt, xt_other, dp, dp_other, gk, gk_other, gq, gq_other, two, one, into, qkv):
+            put(ids, bits, p, slice(i * side, i * side + side), acc[p * r : p * r + r, :].astype(BF16), send_ref, keep_ref)
+    vectors = (qkv_ref, one_ref, one_ref, one_ref, in_ref, two_ref, two_ref, two_ref)
+    index = (None, 2, 0, 1, 0, 2, 0, 1)
+    plan, _ = small_plan(n, sizes)
+    for p in range(n):
+        found = []
+        for (size, count, _), ref, row in zip(plan, vectors, index):
+            for c in range(count):
+                at = min(p * size // 128 + c, n * size // 128 - 1)
+                if row is None:
+                    i, at = at * 128 // ref.shape[1], at * 128 % ref.shape[1]
+                    found.append(ref[i : i + 1, at : at + 128])
+                else:
+                    found.append(ref[row : row + 1, at * 128 : at * 128 + 128])
+        found = jnp.concatenate(found + [jnp.zeros((r - len(found), 128), F32)], 0).astype(BF16)
+        put(ids, bits, p, slice(2 * side, 2 * side + 128), found, send_ref, keep_ref)
+
+
+def qk_grad(ids, n, bits, sizes, xt, xt_other, dp, dp_other, two, one, into, rows_send, rows_own):
     width, rows = xt.shape
     side = dp.shape[1]
-    part = (n // 2, width // n, 3 * side + 3 * 128)
-    d = pl.BlockSpec((1, side, rows), lambda i, ids: (jnp.minimum(i, 2), 0, 0))
-    return call(
-        functools.partial(qkv_kernel, n, bits, sizes), "qkv_grad", (4,), ids,
-        (xt, xt_other, dp, dp_other, gk, gk_other, gq, gq_other, two, one, into, qkv),
-        [whole(xt.shape)] * 2 + [d, d] + [whole(a.shape) for a in (gk, gk, gq, gq, two, one, into, qkv)],
-        [whole(part)] * 2, [SDS(part, BF16)] * 2,
-        flops=4 * width * rows * 3 * side, moved=2 * (2 * 3 * side * rows + 2 * width * 3 * side),
+    part = (n // 2, width // n, 2 * side + 128)
+    d = pl.BlockSpec((2, side, rows), lambda i, ids: (0, 0, 0))
+    return call(
+        functools.partial(qk_kernel, n, bits, sizes), "qk_grad", (1,), ids,
+        (xt, xt_other, dp, dp_other, two, one, into, rows_send, rows_own),
+        [whole(xt.shape)] * 2 + [d, d] + [whole(a.shape) for a in (two, one, into, rows_send, rows_own)],
+        [whole(part)] * 2, [SDS(part, BF16)] * 2, [pltpu.VMEM((8, width), F32)],
+        us=4,
+    )
+
+
+def vp_kernel(n, bits, ids, x0_ref, x1_ref, d0_ref, d1_ref, k0_ref, k1_ref, q0_ref, q1_ref, send_ref, keep_ref):
+    r = keep_ref.shape[1]
+    side = d0_ref.shape[1]
+    acc = mm_nt(x0_ref[...], d0_ref[0]) + mm_nt(x1_ref[...], d1_ref[0])
+    for p in range(n):
+        put(ids, bits, p, slice(0, side), acc[p * r : p * r + r, :].astype(BF16), send_ref, keep_ref)
+    base = side
+    for own_ref, other_ref in ((k0_ref, k1_ref), (q0_ref, q1_ref)):
+        acc = (own_ref[...].astype(F32) + other_ref[...].astype(F32)).astype(BF16)
+        s = acc.shape[0] // n
+        for p in range(n):
+            rows = acc[p * s : p * s + s, :]
+            stacked = jnp.concatenate([rows[:, 128 * i : 128 * i + 128] for i in range(side // 128)], 0)
+            put(ids, bits, p, slice(base, base + 128), stacked, send_ref, keep_ref)
+        base += 128
+
+
+def vp_grad(ids, n, bits, xt, xt_other, dp, dp_other, gk, gk_other, gq, gq_other):
+    width, rows = xt.shape
+    side = dp.shape[1]
+    part = (n // 2, width // n, side + 256)
+    d = pl.BlockSpec((1, side, rows), lambda i, ids: (2, 0, 0))
+    return call(
+        functools.partial(vp_kernel, n, bits), "vp_grad", (1,), ids,
+        (xt, xt_other, dp, dp_other, gk, gk_other, gq, gq_other),
+        [whole(xt.shape)] * 2 + [d, d] + [whole(a.shape) for a in (gk, gk, gq, gq)],
+        [whole(part)] * 2, [SDS(part, BF16)] * 2, us=3,
     )
 
 
@@ -686,7 +715,7 @@
     part = (m // 2, r, w)
     return call(
         functools.partial(add_split_kernel, bits, lows), "add_split", (1,), ids, (keep, got),
-        [whole(keep.shape)] * 2, [whole(part)] * 2, [SDS(part, BF16)] * 2, vmem=24, moved=6 * m * r * w,
+        [whole(keep.shape)] * 2, [whole(part)] * 2, [SDS(part, BF16)] * 2, vmem=24, us=1,
     )
 
 
@@ -698,7 +727,7 @@
     _, r, w = keep.shape
     return call(
         add_last_kernel, "add_last", (1,), ids, (keep, got), [whole(keep.shape)] * 2, whole((r, w)), SDS((r, w), BF16),
-        vmem=16, moved=6 * r * w,
+        vmem=16, us=1,
     )
 
 
@@ -713,11 +742,13 @@
 
 def orders(n):
     low = list(range(n.bit_length() - 1))
-    if len(low) < 3:
-        return low, low[::-1]
-    a = low
-    b = [low[1], low[0]] + low[:1:-1]
-    return a, b
+    if len(low) != 4:
+        pair = (low, low[1::-1] + low[:1:-1])
+        return pair, pair, pair, pair
+    return ORDERS
+
+
+ORDERS = (((0, 1, 2, 3), (1, 0, 3, 2)),) * 4
 
 
 class Exchange:
@@ -725,8 +756,13 @@
         self.ids, self.n, self.order = ids, n, order
         self.left = [sorted(o) for o in order]
         self.at = 0
+        self.steps = len(order[0])
         self.keep = keep
         self.got = across(send, n, self.bits(0))
+
+    @staticmethod
+    def first(order):
+        return tuple(o[0] for o in order)
 
     def bits(self, step):
         return tuple(o[step] for o in self.order)
@@ -735,7 +771,7 @@
         for l, b in zip(self.left, self.bits(self.at)):
             l.remove(b)
         self.at += 1
-        if self.at == len(self.order[0]):
+        if self.at == self.steps:
             self.mine = add_last(self.ids, self.keep, self.got)
             self.other = swap(self.mine)
             return
@@ -759,35 +795,44 @@
     r = mine.shape[0]
     return call(
         join_kernel, "join", (1,), ids, (mine, other), [whole(mine.shape)] * 2,
-        [whole((r, w)) for w in widths], [SDS((r, w), F32) for w in widths], vmem=16, moved=12 * r * sum(widths),
-    )
-
-
-def join_qkv_kernel(ids, mine_ref, other_ref, qkv_ref, posk_ref, posq_ref, small_ref):
+        [whole((r, w)) for w in widths], [SDS((r, w), F32) for w in widths], vmem=16, us=2,
+    )
+
+
+def join_last_kernel(n, sizes, ids, qk_mine, qk_other, vo_mine, vo_other, qkv_ref, posk_ref, posq_ref, *vectors):
     core = ids[1]
-    r = mine_ref.shape[0]
+    r, width = qkv_ref.shape[0], qkv_ref.shape[1] // 3
+    side = width // 2
     s = posk_ref.shape[0]
-    count = r // s
-    side = 128 * count
-    width = qkv_ref.shape[1] // 3
-    for who, ref in ((core, mine_ref), (1 - core, other_ref)):
-        for i in range(3):
-            at = pl.multiple_of(i * width + who * side, 128)
-            qkv_ref[:, pl.ds(at, side)] = ref[:, i * side : i * side + side].astype(F32)
+
+    def lay(out, base, who, ref, at):
+        out[:, pl.ds(pl.multiple_of(base + who * side, 128), side)] = ref[:, at : at + side].astype(F32)
+
+    for who, qk, vo in ((core, qk_mine, vo_mine), (1 - core, qk_other, vo_other)):
+        lay(qkv_ref, 0, who, qk, 0)
+        lay(qkv_ref, width, who, qk, side)
+        lay(qkv_ref, 2 * width, who, vo, 0)
         for j, out in enumerate((posk_ref, posq_ref)):
-            lanes = slice(3 * side + 128 * j, 3 * side + 128 * j + 128)
-            for i in range(count):
+            lanes = slice(side + 128 * j, side + 128 * j + 128)
+            for i in range(r // s):
                 at = pl.multiple_of(who * side + 128 * i, 128)
-                out[:, pl.ds(at, 128)] = ref[i * s : i * s + s, lanes].astype(F32)
-    small_ref[...] = mine_ref[:, 3 * side + 256 :].astype(F32) + other_ref[:, 3 * side + 256 :].astype(F32)
-
-
-def join_qkv(ids, mine, other, width, pos):
-    r = mine.shape[0]
-    shapes = [(r, 3 * width), (pos, width), (pos, width), (r, 128)]
-    return call(
-        join_qkv_kernel, "join_qkv", (1,), ids, (mine, other), [whole(mine.shape)] * 2,
-        [whole(s) for s in shapes], [SDS(s, F32) for s in shapes], vmem=16, moved=12 * r * 4 * width,
+                out[:, pl.ds(at, 128)] = vo[i * s : i * s + s, lanes].astype(F32)
+    small = qk_mine[:, 2 * side :].astype(F32) + qk_other[:, 2 * side :].astype(F32)
+    plan, _ = small_plan(n, sizes)
+    for (size, count, at), out in zip(plan, vectors):
+        line = jnp.concatenate([small[at + c : at + c + 1, :] for c in range(count)], 1)
+        line = jnp.broadcast_to(line, (8, 128 * count))
+        start = lax.rem(ids[0] * size, 128)
+        out[...] = pltpu.roll(line, lax.rem(128 * count - start, 128 * count), 1)[0, :size]
+
+
+def join_last(ids, n, sizes, qk, vo, width, pos):
+    r = qk.mine.shape[0]
+    shapes = [(r, 3 * width), (pos, width), (pos, width)] + [(s,) for s in sizes]
+    return call(
+        functools.partial(join_last_kernel, n, sizes), "join_last", (1,), ids, (qk.mine, qk.other, vo.mine, vo.other),
+        [whole(qk.mine.shape)] * 2 + [whole(vo.mine.shape)] * 2,
+        [whole(s) for s in shapes], [SDS(s, F32) for s in shapes], vmem=16, us=2,
     )
 
 
@@ -811,7 +856,7 @@
 
 
 def pages(core, keep, got):
-    return jnp.where(core == 0, jnp.stack([keep, got], 0), jnp.stack([got, keep], 0))
+    return lax.dynamic_update_slice_in_dim(keep, got[None], 1 - core, 0)
 
 
 def after(value, *others):
@@ -822,20 +867,17 @@
          w_in, b_in, w_down, b_down, gain_two, shift_two, cotangent):
     place = lax.axis_index("pages").astype(jnp.int32)
     core = lax.axis_index("slab").astype(jnp.int32)
-    ids = jnp.stack([place, core, lax.dynamic_index_in_dim(lengths, core, 0, keepdims=False)])
-    _, half, width = tokens.shape
+    ids = jnp.stack([place, core])
+    width = tokens.shape[2]
     other = swap(tokens)
-    vectors = jnp.concatenate(
-        [b_in, b_qkv, b_out, gain_one, shift_one, b_down, gain_two, shift_two]
-    ).astype(F32)[None, :]
-    cot_other = swap(lax.dynamic_index_in_dim(cotangent, 1 - core, 0, keepdims=False))
-
-    pt, p, xt, kf, tab, tabt, fkt, fqt, wkt, wqt = project(
-        ids, tokens, other, w_qkv, vectors, boxes, w_posk, w_posq
-    )
-    e, att, r = attend(ids, pt, p, w_posk, w_posq, kf, tab, tabt, fqt)
+    cot_other = swap(cotangent)
+
+    kf, tab, tabt, fkt, fqt, wkt, wqt = tables(ids, boxes, w_posk, w_posq)
+    pt, p, xt = project(after(ids, kf), tokens, other, w_qkv, b_qkv)
+    e, att, r = attend(ids, lengths, pt, p, w_posk, w_posq, kf, tab, tabt, fqt)
     (flt, norm, rstd, slope, actt, out_keep, out_give, dres_two, dsec, dsec_send, rows_two) = feed(
-        ids, att, tokens, other, w_out, w_in, w_down, vectors, cotangent, cot_other
+        ids, att, tokens, other, w_out, w_in, w_down, b_out, gain_one, shift_one, b_in, b_down, gain_two, shift_two,
+        cotangent, cot_other
     )
     xt_other, att_other, flt_other, actt_other = swap(xt), swap(att), swap(flt), swap(actt)
     dsec_other = swap(dsec_send)
@@ -844,12 +886,14 @@
     dh_other = swap(dh_send)
     if width // n % 16:
         dres_one, branch, branch_send, datt, rows_one = first_back(
-            ids, dh_send, dh, w_in, dres_two, norm, rstd, vectors, w_out
+            ids, dh_send, dh, w_in, dres_two, norm, rstd, gain_one, w_out
         )
         args = dict(e=e, r=r, datt=datt, att=att, pt=pt, p=p, wkt=wkt, wqt=wqt, fkt=fkt, fqt=fqt, tabt=tabt)
-        dp_send, gk_send, gq_send = attend_back(ids, own=False, **args)
-        dp, gk, gq = attend_back(ids, own=True, **args)
-        tok_keep, tok_give, rows_qkv = tokens_back(ids, w_qkv, dp_send, dp, dres_one)
+        dp_send, gk_send, gq_send, bias_send = attend_back(ids, own=False, **args)
+        dp, gk, gq, bias_own = attend_back(ids, own=True, **args)
+        tok_keep, tok_give = tokens_back(ids, w_qkv, dp_send, dp, dres_one)
+        first, second = jnp.where(core == 0, bias_own, bias_send), jnp.where(core == 0, bias_send, bias_own)
+        rows_qkv = jnp.concatenate([first[::8], second[::8]], 1)
         dp_other = swap(dp_send)
 
         def side_of(a):
@@ -866,7 +910,7 @@
         g_posk = total(gk.astype(F32) + swap(gk_send).astype(F32))
         g_posq = total(gq.astype(F32) + swap(gq_send).astype(F32))
         g_qkv = jnp.concatenate([total(both(mm_nt, xt, dp[i], xt_other, dp_other[i])) for i in range(3)], 1)
-        small = (rows_qkv[0:3], rows_one[2], rows_one[0], rows_one[1], row_in, rows_two[2], rows_two[0], rows_two[1])
+        small = (rows_qkv, rows_one[2], rows_one[0], rows_one[1], row_in, rows_two[2], rows_two[0], rows_two[1])
         packed = lax.psum(jnp.concatenate([v.reshape(n, -1) for v in small], 1), ("pages", "slab"))
         packed = lax.dynamic_index_in_dim(packed, place, 0, keepdims=False)
         totals, at = [], 0
@@ -877,54 +921,48 @@
                 g_posq, g_out, totals[1], totals[2], totals[3], g_in, totals[4], g_down, totals[5], totals[6],
                 totals[7])
 
-    order = orders(n)
-    bits = tuple(o[0] for o in order)
-    down = Exchange(ids, n, *down_grad(ids, n, bits, actt, actt_other, dsec, dsec_other), order)
-    dres_two = after(dres_two, down.keep)
+    order_down, order_mid, order_qk, order_vp = orders(n)
+    first = Exchange.first
+    down = Exchange(
+        ids, n, *down_grad(ids, n, first(order_down), actt, actt_other, dsec, dsec_other), order_down
+    )
     dres_one, branch, branch_send, datt, rows_one = first_back(
-        ids, dh_send, dh, w_in, dres_two, norm, rstd, vectors, w_out
+        after(ids, down.keep), dh_send, dh, w_in, dres_two, norm, rstd, gain_one, w_out
     )
     branch_other = swap(branch_send)
     mid = Exchange(
-        ids, n, *mid_grad(ids, n, bits, flt, flt_other, dh, dh_other, att, att_other, branch, branch_other), order
+        ids, n, *mid_grad(ids, n, first(order_mid), flt, flt_other, dh, dh_other, att, att_other, branch, branch_other),
+        order_mid,
     )
     down.step()
-    datt = after(datt, mid.keep, down.keep)
     back = functools.partial(
-        attend_back, ids, e=e, r=r, datt=datt, att=att, pt=pt, p=p, wkt=wkt, wqt=wqt, fkt=fkt, fqt=fqt, tabt=tabt
-    )
-    dp_send, gk_send, gq_send = back(own=False)
+        attend_back, e=e, r=r, datt=datt, att=att, pt=pt, p=p, wkt=wkt, wqt=wqt, fkt=fkt, fqt=fqt, tabt=tabt
+    )
+    dp_send, gk_send, gq_send, bias_send = back(after(ids, mid.keep, down.keep), own=False)
     dp_other, gk_other, gq_other = swap(dp_send), swap(gk_send), swap(gq_send)
     down.step()
-    mid.step()
-    ids_two = after(ids, dp_send, down.keep, mid.keep)
-    dp, gk, gq = attend_back(
-        ids_two, own=True, e=e, r=r, datt=datt, att=att, pt=pt, p=p, wkt=wkt, wqt=wqt, fkt=fkt, fqt=fqt, tabt=tabt
-    )
-    tok_keep, tok_give, rows_qkv = tokens_back(ids, w_qkv, dp_send, dp, dres_one)
-    tok_got = swap(tok_give)
+    dp, gk, gq, bias_own = back(after(ids, dp_send, down.keep), own=True)
     small = (3 * width, width, width, width, w_in.shape[1], width, width, width)
     sizes = tuple(s // n for s in small)
-    last = Exchange(
-        ids, n, *qkv_grad(ids, n, bits, sizes, xt, xt_other, dp, dp_other, gk, gk_other, gq, gq_other,
-                          rows_two, rows_one, row_in, rows_qkv), order
-    )
-    while mid.at < len(order[0]) or down.at < len(order[0]):
-        for x in (down, mid):
-            if x.at < len(order[0]):
+    mid.step()
+    qk = Exchange(
+        ids, n, *qk_grad(after(ids, mid.keep), n, first(order_qk), sizes, xt, xt_other, dp, dp_other,
+                         rows_two, rows_one, row_in, bias_send, bias_own), order_qk
+    )
+    vp = Exchange(
+        ids, n, *vp_grad(after(ids, qk.keep), n, first(order_vp), xt, xt_other, dp, dp_other,
+                         gk, gk_other, gq, gq_other), order_vp
+    )
+    tok, tok_give = tokens_back(after(ids, vp.keep), w_qkv, dp_send, dp, dres_one)
+    tok_got = swap(tok_give)
+    while vp.at < vp.steps:
+        for x in (down, mid, qk, vp):
+            if x.at < x.steps:
                 x.step()
-    while last.at < len(order[0]):
-        last.step()
     (g_down,) = join(ids, down.mine, down.other, (width,))
     g_in, g_out = join(ids, mid.mine, mid.other, (w_in.shape[1], width))
-    g_qkv, g_posk, g_posq, summed = join_qkv(ids, last.mine, last.other, width, w_posk.shape[0] // n)
-    plan, _ = small_plan(n, sizes)
-    totals = [
-        lax.dynamic_slice_in_dim(summed[at : at + count].reshape(-1), place * size % 128, size, 0)
-        for size, count, at in plan
-    ]
-
-    return (pages(core, out_keep, out_got), pages(core, tok_keep, tok_got), g_qkv, totals[0], g_posk, g_posq, g_out,
+    g_qkv, g_posk, g_posq, *totals = join_last(ids, n, sizes, qk, vp, width, w_posk.shape[0] // n)
+    return (pages(core, out_keep, out_got), pages(core, tok, tok_got), g_qkv, totals[0], g_posk, g_posq, g_out,
             totals[1], totals[2], totals[3], g_in, totals[4], g_down, totals[5], totals[6], totals[7])
 
 

time: 234 us -> 165 us (0.71)
  waiting for transfers between devices: 59.2 us -> 13.5 us
  local copies, waits for them, and re-layouts: 34.1 us -> 7.22 us
  starting transfers between devices: 26.6 us -> 33.8 us
  other arithmetic: 3.88 us -> 0.08 us
    ppermute x12 -> x16, waiting for transfers between devices: 54.1 us -> 12.1 us  [across(): return lax.ppermute(x, ('pages', 'slab'), pairs)]
    unnamed x83 -> x96, local copies, waits for them, and re-layouts: 26.4 us -> 6.16 us
    dynamic_slice x9 -> x0, local copies, waits for them, and re-layouts: 6.01 us -> none  [the longest x8 4.76 us: body(): lax.dynamic_slice_in_dim(summed[at:at + count].reshape(-1), place * size...]
    ppermute x17 -> x18, starting transfers between devices: 13.3 us -> 17.1 us  [swap(): return lax.ppermute(x, 'slab', [(0, 1), (1, 0)])]
    ppermute x17 -> x18, waiting for transfers between devices: 5.09 us -> 1.4 us  [swap(): return lax.ppermute(x, 'slab', [(0, 1), (1, 0)])]
    ppermute x12 -> x16, starting transfers between devices: 13.3 us -> 16.6 us  [across(): return lax.ppermute(x, ('pages', 'slab'), pairs)]
    select_n x2 -> x0, other arithmetic: 3.12 us -> none  [pages(): jnp.where(core == 0, jnp.stack([keep, got], 0), jnp.stack([got, keep], 0))]
    pallas_call x26 -> x32, Pallas kernels: 108 us -> 108 us  [call(): pl.pallas_call(kernel, grid_spec=pltpu.PrefetchScalarGridSpec(num_scalar_...]
  transfers between devices with their start and end apart: 29 -> 34, of which waited for: 9 -> 7; matrix products, arithmetic and copies ran while one was open for 5% -> 1% of each run, Pallas kernels for 37% -> 56%
where the time goes in v3:
time: 165 us; the launch traced here: 164 us
  Pallas kernels  108 us (65%)
  starting transfers between devices  33.8 us (20%)
  waiting for transfers between devices  13.5 us (8%)
  local copies, waits for them, and re-layouts  7.22 us (4%)
    pallas_call x32, Pallas kernels, call(): pl.pallas_call(kernel, grid_spec=pltpu.PrefetchScalarGridSpec(num_scalar_...  108 us
    ppermute x18, starting transfers between devices, swap(): return lax.ppermute(x, 'slab', [(0, 1), (1, 0)])  17.1 us
    ppermute x16, starting transfers between devices, across(): return lax.ppermute(x, ('pages', 'slab'), pairs)  16.6 us
    ppermute x16, waiting for transfers between devices, across(): return lax.ppermute(x, ('pages', 'slab'), pairs)  12.1 us
    unnamed x96, local copies, waits for them, and re-layouts  6.16 us
  transfers between devices with their start and end apart: 34, of which 7 were waited for; matrix products, arithmetic and copies ran while one was open for 1% of the time, Pallas kernels for 56%

profile of v3, /device:TPU:1, one launch (start us, length us, event | category | flops | bytes accessed | tf_op | source)
XLA Modules:
  0.0 164.3 jit_solution(14741805841860168879)
XLA Ops:
  1.3 1.0 copy-done.8
  2.3 1.0 copy-done.10
  5.4 2.0 %tables.1 = (bf16[512,256]{1,0:T(8,128)(2,1)S(1)}, f32[4,512,128]{2,1,0:T(8,128)S(1)}, f32[4,64,512]{2,1,0:T(8,128)S(1)}, bf16[256,512]{1,0:T(8,128)(2,1)S(1)}, ...) custom-call(s32[2]{0:T(128)S(1)} %pad_add_fusion.ids, ...), custom_call_target="tpu_custom_call" | custom-call | flops 1800000000 | tf_op jit(solution)/shard_map/tables/pallas_call | solution.py:38
  7.6 5.1 %project.1 = (bf16[2304,512]{1,0:T(8,128)(2,1)S(1)}, bf16[512,2304]{1,0:T(8,128)(2,1)S(1)}, bf16[768,512]{1,0:T(8,128)(2,1)S(1)}) custom-call(s32[2]{0:T(128)S(1)} %pad_add_fusion.ids, bf16[2,256,768]{2,1,0:T(8,128)(2,1)S(1)} %copy-done.4, bf16[2,256,768]{2,1,0:T(8,128)(2,1)} %collective-permute-done.other_ref, bf16[768,2304]{1,0:T(8,128)(2,1)S(1)} %copy-done, ...), custom_call_target="tpu_custom_call" | custom-call | flops 3000000000 | tf_op jit(solution)/shard_map/project/pallas_call | solution.py:38
  12.9 16.4 %attend.1 = (bf16[12,512,512]{2,1,0:T(8,128)(2,1)}, bf16[768,512]{1,0:T(8,128)(2,1)S(1)}, f32[6,2,512]{2,1,0:T(2,128)S(1)}) custom-call(s32[2]{0:T(128)S(1)} %pad_add_fusion.ids, s32[2]{0:T(128)S(1)} %copy-done.21, bf16[2304,512]{1,0:T(8,128)(2,1)S(1)} %get-tuple-element.112.qt_ref.vt_ref.kt_ref, ...), custom_call_target="tpu_custom_call" | custom-call | flops 10200000512 | tf_op jit(solution)/shard_map/attend/pallas_call | solution.py:38
  29.5 14.7 %feed.1 = (bf16[768,512]{1,0:T(8,128)(2,1)S(1)}, f32[512,768]{1,0:T(8,128)S(1)}, f32[512,1]{1,0:T(8,128)S(1)}, bf16[512,3072]{1,0:T(8,128)(2,1)S(1)}, bf16[3072,...) custom-call(s32[2]{0:T(128)S(1)} %pad_add_fusion.ids, ...), custom_call_target="tpu_custom_call" | custom-call | flops 8999999488 | tf_op jit(solution)/shard_map/feed/pallas_call | solution.py:38
  44.7 5.1 %hidden_back.1 = (bf16[512,1536]{1,0:T(8,128)(2,1)S(1)}, bf16[512,1536]{1,0:T(8,128)(2,1)S(1)}, f32[1,3072]{1,0:T(1,128)S(1)}) custom-call(s32[2]{0:T(128)S(1)} %pad_add_fusion.ids, bf16[512,768]{1,0:T(8,128)(2,1)S(1)} %get-tuple-element.121.ds_ref.b0_ref, bf16[3072,768]{1,0:T(8,128)(2,1)S(1)} %bitcast.7, bf16[512,3072]{1,0:T(8,128)(2,1)S(1)} %get-tuple-element.122.slope_ref), custom_call_target="tpu_custom_call" | custom-call | flops 3000000000 | tf_op jit(solution)/shard_map/hidden_back/pallas_call | solution.py:38
  50.5 5.0 %down_grad.1 = (bf16[8,192,384]{2,1,0:T(8,128)(2,1)S(1)}, bf16[8,192,384]{2,1,0:T(8,128)(2,1)S(1)}) custom-call(s32[2]{0:T(128)S(1)} %pad_add_fusion.ids, bf16[3072,512]{1,0:T(8,128)(2,1)S(1)} %get-tuple-element.125.a0_ref, bf16[3072,512]{1,0:T(8,128)(2,1)S(1)} %collective-permute-done.6.a1_ref, bf16[512,768]{1,0:T(8,128)(2,1)S(1)} %get-tuple-element.121.ds_ref.b0_ref, ...), custom_call_target="tpu_custom_call" | custom-call | flops 4200000000 | tf_op jit(solution)/shard_map/down_grad/pallas_call | solution.py:38
  55.5 2.7 %collective-permute-start.11 = (bf16[8,192,384]{2,1,0:T(8,128)(2,1)S(1)}, bf16[8,192,384]{2,1,0:T(8,128)(2,1)S(1)}, u32[]{:S(2)}, u32[]{:S(2)}) collective-permute-start(bf16[8,192,384]{2,1,0:T(8,128)(2,1)S(1)} %get-tuple-element.139), channel_id=1, source_target_pairs={{0,2},{1,5},{2,0},{3,7},{4,6},{5,1},{6,4},{7,3},{8,10},{9,13},{10,... | collective-permute-start | bytes 3538952 | tf_op jit(solution)/shard_map/ppermute | solution.py:740
  58.3 6.7 %first_back.1 = (f32[512,768]{1,0:T(8,128)S(1)}, bf16[512,768]{1,0:T(8,128)(2,1)S(1)}, bf16[512,384]{1,0:T(8,128)(2,1)S(1)}, bf16[768,512]{1,0:T(8,128)(2,1)S(1)}, f32[8,768]{1,0:T(8,128)S(1)}) custom-call(s32[2]{0:T(128)S(1)} %pad_add_fusion.ids, bf16[512,1536]{1,0:T(8,128)(2,1)S(1)} %get-tuple-element.124.dsend_ref, ...), custom_call_target="tpu_custom_call" | custom-call | flops 4800000000 | tf_op jit(solution)/shard_map/first_back/pallas_call | solution.py:38
  65.4 1.4 collective-permute-done.8.c1_ref
  66.7 5.7 %mid_grad.1 = (bf16[8,48,1920]{2,1,0:T(8,128)(2,1)S(1)}, bf16[8,48,1920]{2,1,0:T(8,128)(2,1)S(1)}) custom-call(s32[2]{0:T(128)S(1)} %pad_add_fusion.ids, bf16[768,512]{1,0:T(8,128)(2,1)S(1)} %get-tuple-element.120.f0_ref, bf16[768,512]{1,0:T(8,128)(2,1)S(1)} %collective-permute-done.3.f1_ref, bf16[512,1536]{1,0:T(8,128)(2,1)S(1)} %get-tuple-element.123.down_ref.h0_ref, ...), custom_call_target="tpu_custom_call" | custom-call | flops 3600000000 | tf_op jit(solution)/shard_map/mid_grad/pallas_call | solution.py:38
  72.4 1.3 collective-permute-start.9
  73.7 0.8 add_split.13
  74.9 7.4 %attend_back.2 = (bf16[3,384,512]{2,1,0:T(8,128)(2,1)S(1)}, bf16[256,384]{1,0:T(8,128)(2,1)S(1)}, bf16[256,384]{1,0:T(8,128)(2,1)S(1)}, f32[24,384]{1,0:T(8,128)S(1)}) custom-call(s32[2]{0:T(128)S(1)} %pad_add_fusion.ids, bf16[12,512,512]{2,1,0:T(8,128)(2,1)S(1)} %bitcast.11, f32[6,2,512]{2,1,0:T(2,128)S(1)} %get-tuple-element.143.r_ref, ...), custom_call_target="tpu_custom_call" | custom-call | flops 5400000000 | tf_op jit(solution)/shard_map/attend_back/pallas_call | solution.py:38
  82.3 1.0 collective-permute-start.13
  83.8 6.2 %collective-permute-done.12.got_ref = bf16[4,192,384]{2,1,0:T(8,128)(2,1)S(1)} collective-permute-done((bf16[4,192,384]{2,1,0:T(8,128)(2,1)S(1)}, bf16[4,192,384]{2,1,0:T(8,128)(2,1)S(1)}, u32[]{:S(2)}, u32[]{:S(2)}) %collective-permute-start.12) | collective-permute-done | bytes 589856 | tf_op jit(solution)/shard_map/ppermute | solution.py:740
  90.0 1.3 collective-permute-start.14
  91.3 1.4 add_split.14
  92.7 7.4 %attend_back.3 = (bf16[3,384,512]{2,1,0:T(8,128)(2,1)S(1)}, bf16[256,384]{1,0:T(8,128)(2,1)S(1)}, bf16[256,384]{1,0:T(8,128)(2,1)S(1)}, f32[24,384]{1,0:T(8,128)S(1)}) custom-call(s32[2]{0:T(128)S(1)} %pad_add_fusion.ids, bf16[12,512,512]{2,1,0:T(8,128)(2,1)S(1)} %bitcast.11, f32[6,2,512]{2,1,0:T(2,128)S(1)} %get-tuple-element.143.r_ref, ...), custom_call_target="tpu_custom_call" | custom-call | flops 5400000000 | tf_op jit(solution)/shard_map/attend_back/pallas_call | solution.py:38
  100.2 1.8 %add_split.12 = (bf16[4,48,1920]{2,1,0:T(8,128)(2,1)}, bf16[4,48,1920]{2,1,0:T(8,128)(2,1)S(1)}) custom-call(s32[2]{0:T(128)S(1)} %pad_add_fusion.ids, bf16[8,48,1920]{2,1,0:T(8,128)(2,1)S(1)} %get-tuple-element.134.keep_ref, bf16[8,48,1920]{2,1,0:T(8,128)(2,1)S(1)} %collective-permute-done.9.got_ref), custom_call_target="tpu_custom_call" | custom-call | flops 600000000 | tf_op jit(solution)/shard_map/add_split/pallas_call | solution.py:38
  101.9 2.3 %collective-permute-start.31 = (bf16[2,192,384]{2,1,0:T(8,128)(2,1)}, bf16[2,192,384]{2,1,0:T(8,128)(2,1)}, u32[]{:S(2)}, u32[]{:S(2)}) collective-permute-start(bf16[2,192,384]{2,1,0:T(8,128)(2,1)} %get-tuple-element.198), channel_id=1, source_target_pairs={{0,8},{1,17},{2,10},{3,19},{4,12},{5,21},{6,14},{7,23},{8,0},{9,25... | collective-permute-start | bytes 884744 | tf_op jit(solution)/shard_map/ppermute | solution.py:740
  104.8 4.5 %qk_grad.1 = (bf16[8,48,896]{2,1,0:T(8,128)(2,1)}, bf16[8,48,896]{2,1,0:T(8,128)(2,1)S(1)}) custom-call(s32[2]{0:T(128)S(1)} %pad_add_fusion.ids, bf16[768,512]{1,0:T(8,128)(2,1)S(1)} %get-tuple-element.138.x0_ref, bf16[768,512]{1,0:T(8,128)(2,1)S(1)} %collective-permute-done.10.x1_ref, bf16[3,384,512]{2,1,0:T(8,128)(2,1)S(1)} %get-tuple-element.152.d0_ref.do_ref, ...), custom_call_target="tpu_custom_call" | custom-call | flops 2400000000 | tf_op jit(solution)/shard_map/qk_grad/pallas_call | solution.py:38
  109.2 1.3 collective-permute-start.17
  110.5 3.2 %vp_grad.1 = (bf16[8,48,640]{2,1,0:T(8,128)(2,1)}, bf16[8,48,640]{2,1,0:T(8,128)(2,1)S(1)}) custom-call(s32[2]{0:T(128)S(1)} %pad_add_fusion.ids, bf16[768,512]{1,0:T(8,128)(2,1)S(1)} %get-tuple-element.138.x0_ref, bf16[768,512]{1,0:T(8,128)(2,1)S(1)} %collective-permute-done.10.x1_ref, bf16[3,384,512]{2,1,0:T(8,128)(2,1)S(1)} %get-tuple-element.152.d0_ref.do_ref, ...), custom_call_target="tpu_custom_call" | custom-call | flops 1800000000 | tf_op jit(solution)/shard_map/vp_grad/pallas_call | solution.py:38
  114.8 1.0 copy-done.33
  115.8 1.6 add_split.23
  117.4 1.4 collective-permute-start.32
  118.7 1.0 bitcast_dynamic-update-slice_fusion.1
  119.8 2.1 %collective-permute-done.32.got_ref = bf16[1,192,384]{2,1,0:T(8,128)(2,1)S(1)} collective-permute-done((bf16[1,192,384]{2,1,0:T(8,128)(2,1)S(1)}, bf16[1,192,384]{2,1,0:T(8,128)(2,1)S(1)}, u32[]{:S(2)}, u32[]{:S(2)}) %collective-permute-start.32) | collective-permute-done | bytes 147488 | tf_op jit(solution)/shard_map/ppermute | solution.py:740
  122.4 3.8 %collective-permute-start.33 = (bf16[192,384]{1,0:T(8,128)(2,1)S(1)}, bf16[192,384]{1,0:T(8,128)(2,1)S(1)}, u32[]{:S(2)}, u32[]{:S(2)}) collective-permute-start(bf16[192,384]{1,0:T(8,128)(2,1)S(1)} %add_last.7.mine_ref), channel_id=1, source_target_pairs={{0,1},{1,0},{2,3},{3,2},{4,5},{5,4},{6,7},{7,6},{8,9},{9,8},{10,11... | collective-permute-start | bytes 442376 | tf_op jit(solution)/shard_map/ppermute | solution.py:735
  126.2 1.8 %add_split.21 = (bf16[2,48,1920]{2,1,0:T(8,128)(2,1)S(1)}, bf16[2,48,1920]{2,1,0:T(8,128)(2,1)S(1)}) custom-call(s32[2]{0:T(128)S(1)} %pad_add_fusion.ids, bf16[4,48,1920]{2,1,0:T(8,128)(2,1)S(1)} %copy-done.7, bf16[4,48,1920]{2,1,0:T(8,128)(2,1)} %collective-permute-done.27.got_ref), custom_call_target="tpu_custom_call" | custom-call | flops 600000000 | tf_op jit(solution)/shard_map/add_split/pallas_call | solution.py:38
  128.1 1.0 collective-permute-start.28
  129.1 1.7 %add_split.18 = (bf16[4,48,640]{2,1,0:T(8,128)(2,1)S(1)}, bf16[4,48,640]{2,1,0:T(8,128)(2,1)S(1)}) custom-call(s32[2]{0:T(128)S(1)} %pad_add_fusion.ids, bf16[8,48,640]{2,1,0:T(8,128)(2,1)S(1)} %copy-done.29, bf16[8,48,640]{2,1,0:T(8,128)(2,1)} %collective-permute-done.22.got_ref), custom_call_target="tpu_custom_call" | custom-call | flops 600000000 | tf_op jit(solution)/shard_map/add_split/pallas_call | solution.py:38
  130.8 1.3 collective-permute-start.23
  132.1 1.8 %add_split.15 = (bf16[4,48,896]{2,1,0:T(8,128)(2,1)S(1)}, bf16[4,48,896]{2,1,0:T(8,128)(2,1)S(1)}) custom-call(s32[2]{0:T(128)S(1)} %pad_add_fusion.ids, bf16[8,48,896]{2,1,0:T(8,128)(2,1)S(1)} %copy-done.27, bf16[8,48,896]{2,1,0:T(8,128)(2,1)} %collective-permute-done.17.got_ref), custom_call_target="tpu_custom_call" | custom-call | flops 600000000 | tf_op jit(solution)/shard_map/add_split/pallas_call | solution.py:38
  134.3 4.7 %tokens_back.1 = (bf16[2,256,768]{2,1,0:T(8,128)(2,1)}, bf16[256,768]{1,0:T(8,128)(2,1)S(1)}) custom-call(s32[2]{0:T(128)S(1)} %pad_add_fusion.ids, bf16[768,2304]{1,0:T(8,128)(2,1)S(1)} %copy-done, bf16[3,384,512]{2,1,0:T(8,128)(2,1)S(1)} %copy-done.3, bf16[3,384,512]{2,1,0:T(8,128)(2,1)S(1)} %copy-done.31, f32[512,768]{1,0:T(8,128)S(1)} %copy-done.25), custom_call_target="tpu_custom_call" | custom-call | flops 3600000000 | tf_op jit(solution)/shard_map/tokens_back/pallas_call | solution.py:38
  140.0 1.4 collective-permute-start.29
  141.9 1.2 collective-permute-start.24
  143.8 1.3 collective-permute-start.19
  145.1 1.4 join.3
  147.1 4.0 %collective-permute-start.30 = (bf16[48,1920]{1,0:T(8,128)(2,1)S(1)}, bf16[48,1920]{1,0:T(8,128)(2,1)S(1)}, u32[]{:S(2)}, u32[]{:S(2)}) collective-permute-start(bf16[48,1920]{1,0:T(8,128)(2,1)S(1)} %add_last.6.mine_ref), channel_id=1, source_target_pairs={{0,1},{1,0},{2,3},{3,2},{4,5},{5,4},{6,7},{7,6},{8,9},{9,8},{10,11... | collective-permute-start | bytes 552968 | tf_op jit(solution)/shard_map/ppermute | solution.py:735
  151.9 2.4 %collective-permute-done.19.got_ref = bf16[2,48,896]{2,1,0:T(8,128)(2,1)S(1)} collective-permute-done((bf16[2,48,896]{2,1,0:T(8,128)(2,1)S(1)}, bf16[2,48,896]{2,1,0:T(8,128)(2,1)S(1)}, u32[]{:S(2)}, u32[]{:S(2)}) %collective-permute-start.19) | collective-permute-done | bytes 172064 | tf_op jit(solution)/shard_map/ppermute | solution.py:740
  155.6 2.0 %collective-permute-start.26 = (bf16[48,640]{1,0:T(8,128)(2,1)S(1)}, bf16[48,640]{1,0:T(8,128)(2,1)S(1)}, u32[]{:S(2)}, u32[]{:S(2)}) collective-permute-start(bf16[48,640]{1,0:T(8,128)(2,1)S(1)} %add_last.5.vo_mine), channel_id=1, source_target_pairs={{0,1},{1,0},{2,3},{3,2},{4,5},{5,4},{6,7},{7,6},{8,9},{9,8},{10,11... | collective-permute-start | bytes 184328 | tf_op jit(solution)/shard_map/ppermute | solution.py:735
  157.6 1.0 collective-permute-done.20.got_ref
  159.1 2.3 %collective-permute-start.21 = (bf16[48,896]{1,0:T(8,128)(2,1)S(1)}, bf16[48,896]{1,0:T(8,128)(2,1)S(1)}, u32[]{:S(2)}, u32[]{:S(2)}) collective-permute-start(bf16[48,896]{1,0:T(8,128)(2,1)S(1)} %add_last.4.qk_mine), channel_id=1, source_target_pairs={{0,1},{1,0},{2,3},{3,2},{4,5},{5,4},{6,7},{7,6},{8,9},{9,8},{10,11... | collective-permute-start | bytes 258056 | tf_op jit(solution)/shard_map/ppermute | solution.py:735
  161.4 1.4 join.2
  162.9 1.4 join_last.1
  (154 shorter events, 13.4 us)
Async XLA Ops:
  0.6 6.9 %collective-permute-start = (bf16[2,256,768]{2,1,0:T(8,128)(2,1)}, bf16[2,256,768]{2,1,0:T(8,128)(2,1)}, u32[]{:S(2)}, u32[]{:S(2)}) collective-permute-start(bf16[2,256,768]{2,1,0:T(8,128)(2,1)} %own_ref.3), channel_id=1, source_target_pairs={{0,1},{1,0},{2,3},{3,2},{4,5},{5,4},{6,7},{7,6},{8,9},{9,8},{10,11... | collective-permute-start | bytes 2359304 | tf_op jit(solution)/shard_map/ppermute | solution.py:735
  0.8 28.6 %collective-permute-start.1 = (bf16[2,256,768]{2,1,0:T(8,128)(2,1)}, bf16[2,256,768]{2,1,0:T(8,128)(2,1)}, u32[]{:S(2)}, u32[]{:S(2)}) collective-permute-start(bf16[2,256,768]{2,1,0:T(8,128)(2,1)} %cown_ref.1), channel_id=1, source_target_pairs={{0,1},{1,0},{2,3},{3,2},{4,5},{5,4},{6,7},{7,6},{8,9},{9,8},{10,11... | collective-permute-start | bytes 2359304 | tf_op jit(solution)/shard_map/ppermute | solution.py:735
  7.6 21.7 %slice-start = ((s8[4718592]{0:T(1024)(128)(4,1)}), s8[4194304]{0:T(1024)(128)(4,1)S(1)}, s32[]{:S(2)}) async-start(s8[4718592]{0:T(1024)(128)(4,1)} %bitcast.6), calls=%async_computation | async-start | bytes 8388608
  7.6 21.7 %slice-start.2 = ((s8[4718592]{0:T(1024)(128)(4,1)}), s8[4194304]{0:T(1024)(128)(4,1)S(1)}, s32[]{:S(2)}) async-start(s8[4718592]{0:T(1024)(128)(4,1)} %bitcast.8), calls=%async_computation.2 | async-start | bytes 8388608
  12.8 16.6 %copy-start.34 = (bf16[2304,512]{1,0:T(8,128)(2,1)}, bf16[2304,512]{1,0:T(8,128)(2,1)S(1)}, u32[]{:S(2)}) copy-start(bf16[2304,512]{1,0:T(8,128)(2,1)S(1)} %get-tuple-element.112.qt_ref.vt_ref.kt_ref) | copy-start | bytes 7077892
  12.8 16.6 %copy-start.36 = (bf16[512,2304]{1,0:T(8,128)(2,1)}, bf16[512,2304]{1,0:T(8,128)(2,1)S(1)}, u32[]{:S(2)}) copy-start(bf16[512,2304]{1,0:T(8,128)(2,1)S(1)} %get-tuple-element.113.k_ref.v_ref) | copy-start | bytes 7077892
  12.8 16.6 %slice-start.1 = ((s8[4718592]{0:T(1024)(128)(4,1)}), s8[524288]{0:T(1024)(128)(4,1)S(1)}, s32[]{:S(2)}) async-start(s8[4718592]{0:T(1024)(128)(4,1)} %bitcast.6), calls=%async_computation.1 | async-start | bytes 1048576
  12.8 16.6 %slice-start.3 = ((s8[4718592]{0:T(1024)(128)(4,1)}), s8[524288]{0:T(1024)(128)(4,1)S(1)}, s32[]{:S(2)}) async-start(s8[4718592]{0:T(1024)(128)(4,1)} %bitcast.8), calls=%async_computation.3 | async-start | bytes 1048576
  12.8 16.6 %copy-start.1 = (bf16[768,768]{1,0:T(8,128)(2,1)S(1)}, bf16[768,768]{1,0:T(8,128)(2,1)}, u32[]{:S(2)}) copy-start(bf16[768,768]{1,0:T(8,128)(2,1)} %wo_ref.3) | copy-start | bytes 3538948
  12.8 16.6 %copy-start.5 = (bf16[2,256,768]{2,1,0:T(8,128)(2,1)S(1)}, bf16[2,256,768]{2,1,0:T(8,128)(2,1)}, u32[]{:S(2)}) copy-start(bf16[2,256,768]{2,1,0:T(8,128)(2,1)} %cown_ref.1) | copy-start | bytes 2359300
  12.9 16.6 %copy-start.14 = (bf16[3072]{0:T(1024)(128)(2,1)S(1)}, bf16[3072]{0:T(1024)(128)(2,1)}, u32[]{:S(2)}) copy-start(bf16[3072]{0:T(1024)(128)(2,1)} %bi_ref.1) | copy-start | bytes 18436
  12.9 16.5 %copy-start.15 = (bf16[768]{0:T(1024)(128)(2,1)S(1)}, bf16[768]{0:T(1024)(128)(2,1)}, u32[]{:S(2)}) copy-start(bf16[768]{0:T(1024)(128)(2,1)} %bo_ref.1) | copy-start | bytes 4612
  12.9 16.5 %copy-start.16 = (bf16[768]{0:T(1024)(128)(2,1)S(1)}, bf16[768]{0:T(1024)(128)(2,1)}, u32[]{:S(2)}) copy-start(bf16[768]{0:T(1024)(128)(2,1)} %s1_ref.1) | copy-start | bytes 4612
  12.9 16.5 %copy-start.17 = (bf16[768]{0:T(1024)(128)(2,1)S(1)}, bf16[768]{0:T(1024)(128)(2,1)}, u32[]{:S(2)}) copy-start(bf16[768]{0:T(1024)(128)(2,1)} %bd_ref.1) | copy-start | bytes 4612
  12.9 16.5 %copy-start.18 = (bf16[768]{0:T(1024)(128)(2,1)S(1)}, bf16[768]{0:T(1024)(128)(2,1)}, u32[]{:S(2)}) copy-start(bf16[768]{0:T(1024)(128)(2,1)} %g2_ref.1) | copy-start | bytes 4612
  44.2 6.3 %collective-permute-start.6 = (bf16[3072,512]{1,0:T(8,128)(2,1)S(1)}, bf16[3072,512]{1,0:T(8,128)(2,1)S(1)}, u32[]{:S(2)}, u32[]{:S(2)}) collective-permute-start(bf16[3072,512]{1,0:T(8,128)(2,1)S(1)} %get-tuple-element.125.a0_ref), channel_id=1, source_target_pairs={{0,1},{1,0},{2,3},{3,2},{4,5},{5,4},{6,7},{7,6},{8,9},{9,8},{10,11... | collective-permute-start | bytes 9437192 | tf_op jit(solution)/shard_map/ppermute | solution.py:735
  44.3 6.2 %collective-permute-start.7 = (bf16[512,384]{1,0:T(8,128)(2,1)S(1)}, bf16[512,384]{1,0:T(8,128)(2,1)S(1)}, u32[]{:S(2)}, u32[]{:S(2)}) collective-permute-start(bf16[512,384]{1,0:T(8,128)(2,1)S(1)} %get-tuple-element.126), channel_id=1, source_target_pairs={{0,1},{1,0},{2,3},{3,2},{4,5},{5,4},{6,7},{7,6},{8,9},{9,8},{10,11... | collective-permute-start | bytes 1179656 | tf_op jit(solution)/shard_map/ppermute | solution.py:735
  49.8 15.5 %collective-permute-start.4 = (bf16[512,1536]{1,0:T(8,128)(2,1)S(1)}, bf16[512,1536]{1,0:T(8,128)(2,1)S(1)}, u32[]{:S(2)}, u32[]{:S(2)}) collective-permute-start(bf16[512,1536]{1,0:T(8,128)(2,1)S(1)} %get-tuple-element.124.dsend_ref), channel_id=1, source_target_pairs={{0,1},{1,0},{2,3},{3,2},{4,5},{5,4},{6,7},{7,6},{8,9},{9,8},{10,11... | collective-permute-start | bytes 4718600 | tf_op jit(solution)/shard_map/ppermute | solution.py:735
  50.0 15.4 %collective-permute-start.5 = (bf16[768,512]{1,0:T(8,128)(2,1)S(1)}, bf16[768,512]{1,0:T(8,128)(2,1)S(1)}, u32[]{:S(2)}, u32[]{:S(2)}) collective-permute-start(bf16[768,512]{1,0:T(8,128)(2,1)S(1)} %get-tuple-element.117.at_ref.a0_ref), channel_id=1, source_target_pairs={{0,1},{1,0},{2,3},{3,2},{4,5},{5,4},{6,7},{7,6},{8,9},{9,8},{10,11... | collective-permute-start | bytes 2359304 | tf_op jit(solution)/shard_map/ppermute | solution.py:735
  50.4 14.9 %collective-permute-start.3 = (bf16[768,512]{1,0:T(8,128)(2,1)S(1)}, bf16[768,512]{1,0:T(8,128)(2,1)S(1)}, u32[]{:S(2)}, u32[]{:S(2)}) collective-permute-start(bf16[768,512]{1,0:T(8,128)(2,1)S(1)} %get-tuple-element.120.f0_ref), channel_id=1, source_target_pairs={{0,1},{1,0},{2,3},{3,2},{4,5},{5,4},{6,7},{7,6},{8,9},{9,8},{10,11... | collective-permute-start | bytes 2359304 | tf_op jit(solution)/shard_map/ppermute | solution.py:735
  55.5 18.2 %collective-permute-start.11 = (bf16[8,192,384]{2,1,0:T(8,128)(2,1)S(1)}, bf16[8,192,384]{2,1,0:T(8,128)(2,1)S(1)}, u32[]{:S(2)}, u32[]{:S(2)}) collective-permute-start(bf16[8,192,384]{2,1,0:T(8,128)(2,1)S(1)} %get-tuple-element.139), channel_id=1, source_target_pairs={{0,2},{1,5},{2,0},{3,7},{4,6},{5,1},{6,4},{7,3},{8,10},{9,13},{10,... | collective-permute-start | bytes 3538952 | tf_op jit(solution)/shard_map/ppermute | solution.py:740
  64.9 1.8 %collective-permute-start.8 = (bf16[512,384]{1,0:T(8,128)(2,1)S(1)}, bf16[512,384]{1,0:T(8,128)(2,1)S(1)}, u32[]{:S(2)}, u32[]{:S(2)}) collective-permute-start(bf16[512,384]{1,0:T(8,128)(2,1)S(1)} %get-tuple-element.133), channel_id=1, source_target_pairs={{0,1},{1,0},{2,3},{3,2},{4,5},{5,4},{6,7},{7,6},{8,9},{9,8},{10,11... | collective-permute-start | bytes 1179656 | tf_op jit(solution)/shard_map/ppermute | solution.py:735
  72.4 27.7 %collective-permute-start.9 = (bf16[8,48,1920]{2,1,0:T(8,128)(2,1)S(1)}, bf16[8,48,1920]{2,1,0:T(8,128)(2,1)S(1)}, u32[]{:S(2)}, u32[]{:S(2)}) collective-permute-start(bf16[8,48,1920]{2,1,0:T(8,128)(2,1)S(1)} %get-tuple-element.135), channel_id=1, source_target_pairs={{0,2},{1,5},{2,0},{3,7},{4,6},{5,1},{6,4},{7,3},{8,10},{9,13},{10,... | collective-permute-start | bytes 4423688 | tf_op jit(solution)/shard_map/ppermute | solution.py:740
  74.6 15.5 %collective-permute-start.12 = (bf16[4,192,384]{2,1,0:T(8,128)(2,1)S(1)}, bf16[4,192,384]{2,1,0:T(8,128)(2,1)S(1)}, u32[]{:S(2)}, u32[]{:S(2)}) collective-permute-start(bf16[4,192,384]{2,1,0:T(8,128)(2,1)S(1)} %get-tuple-element.149), channel_id=1, source_target_pairs={{0,4},{1,3},{2,6},{3,1},{4,0},{5,7},{6,2},{7,5},{8,12},{9,11},{10,... | collective-permute-start | bytes 1769480 | tf_op jit(solution)/shard_map/ppermute | solution.py:740
  82.3 17.8 %copy-start.2 = (bf16[3,384,512]{2,1,0:T(8,128)(2,1)}, bf16[3,384,512]{2,1,0:T(8,128)(2,1)S(1)}, u32[]{:S(2)}) copy-start(bf16[3,384,512]{2,1,0:T(8,128)(2,1)S(1)} %get-tuple-element.148.ds_ref) | copy-start | bytes 3538948
  82.3 21.9 %collective-permute-start.13 = (bf16[3,384,512]{2,1,0:T(8,128)(2,1)S(1)}, bf16[3,384,512]{2,1,0:T(8,128)(2,1)S(1)}, u32[]{:S(2)}, u32[]{:S(2)}) collective-permute-start(bf16[3,384,512]{2,1,0:T(8,128)(2,1)S(1)} %get-tuple-element.148.ds_ref), channel_id=1, source_target_pairs={{0,1},{1,0},{2,3},{3,2},{4,5},{5,4},{6,7},{7,6},{8,9},{9,8},{10,11... | collective-permute-start | bytes 3538952 | tf_op jit(solution)/shard_map/ppermute | solution.py:735
  83.3 18.6 %collective-permute-start.10 = (bf16[768,512]{1,0:T(8,128)(2,1)S(1)}, bf16[768,512]{1,0:T(8,128)(2,1)S(1)}, u32[]{:S(2)}, u32[]{:S(2)}) collective-permute-start(bf16[768,512]{1,0:T(8,128)(2,1)S(1)} %get-tuple-element.138.x0_ref), channel_id=1, source_target_pairs={{0,1},{1,0},{2,3},{3,2},{4,5},{5,4},{6,7},{7,6},{8,9},{9,8},{10,11... | collective-permute-start | bytes 2359304 | tf_op jit(solution)/shard_map/ppermute | solution.py:735
  83.4 35.3 %collective-permute-start.2 = (bf16[256,768]{1,0:T(8,128)(2,1)}, bf16[256,768]{1,0:T(8,128)(2,1)}, u32[]{:S(2)}, u32[]{:S(2)}) collective-permute-start(bf16[256,768]{1,0:T(8,128)(2,1)} %get-tuple-element.119), channel_id=1, source_target_pairs={{0,1},{1,0},{2,3},{3,2},{4,5},{5,4},{6,7},{7,6},{8,9},{9,8},{10,11... | collective-permute-start | bytes 1179656 | tf_op jit(solution)/shard_map/ppermute | solution.py:735
  90.0 19.2 %collective-permute-start.14 = (bf16[256,384]{1,0:T(8,128)(2,1)S(1)}, bf16[256,384]{1,0:T(8,128)(2,1)S(1)}, u32[]{:S(2)}, u32[]{:S(2)}) collective-permute-start(bf16[256,384]{1,0:T(8,128)(2,1)S(1)} %get-tuple-element.161), channel_id=1, source_target_pairs={{0,1},{1,0},{2,3},{3,2},{4,5},{5,4},{6,7},{7,6},{8,9},{9,8},{10,11... | collective-permute-start | bytes 589832 | tf_op jit(solution)/shard_map/ppermute | solution.py:735
  100.1 10.4 %collective-permute-start.15 = (bf16[256,384]{1,0:T(8,128)(2,1)S(1)}, bf16[256,384]{1,0:T(8,128)(2,1)S(1)}, u32[]{:S(2)}, u32[]{:S(2)}) collective-permute-start(bf16[256,384]{1,0:T(8,128)(2,1)S(1)} %get-tuple-element.163), channel_id=1, source_target_pairs={{0,1},{1,0},{2,3},{3,2},{4,5},{5,4},{6,7},{7,6},{8,9},{9,8},{10,11... | collective-permute-start | bytes 589832 | tf_op jit(solution)/shard_map/ppermute | solution.py:735
  101.9 12.9 %collective-permute-start.31 = (bf16[2,192,384]{2,1,0:T(8,128)(2,1)}, bf16[2,192,384]{2,1,0:T(8,128)(2,1)}, u32[]{:S(2)}, u32[]{:S(2)}) collective-permute-start(bf16[2,192,384]{2,1,0:T(8,128)(2,1)} %get-tuple-element.198), channel_id=1, source_target_pairs={{0,8},{1,17},{2,10},{3,19},{4,12},{5,21},{6,14},{7,23},{8,0},{9,25... | collective-permute-start | bytes 884744 | tf_op jit(solution)/shard_map/ppermute | solution.py:740
  104.3 22.0 %collective-permute-start.27 = (bf16[4,48,1920]{2,1,0:T(8,128)(2,1)}, bf16[4,48,1920]{2,1,0:T(8,128)(2,1)}, u32[]{:S(2)}, u32[]{:S(2)}) collective-permute-start(bf16[4,48,1920]{2,1,0:T(8,128)(2,1)} %get-tuple-element.187), channel_id=1, source_target_pairs={{0,4},{1,3},{2,6},{3,1},{4,0},{5,7},{6,2},{7,5},{8,12},{9,11},{10,... | collective-permute-start | bytes 2211848 | tf_op jit(solution)/shard_map/ppermute | solution.py:740
  109.2 22.9 %collective-permute-start.17 = (bf16[8,48,896]{2,1,0:T(8,128)(2,1)}, bf16[8,48,896]{2,1,0:T(8,128)(2,1)}, u32[]{:S(2)}, u32[]{:S(2)}) collective-permute-start(bf16[8,48,896]{2,1,0:T(8,128)(2,1)} %get-tuple-element.169), channel_id=1, source_target_pairs={{0,2},{1,5},{2,0},{3,7},{4,6},{5,1},{6,4},{7,3},{8,10},{9,13},{10,... | collective-permute-start | bytes 2064392 | tf_op jit(solution)/shard_map/ppermute | solution.py:740
  114.6 14.5 %collective-permute-start.22 = (bf16[8,48,640]{2,1,0:T(8,128)(2,1)}, bf16[8,48,640]{2,1,0:T(8,128)(2,1)}, u32[]{:S(2)}, u32[]{:S(2)}) collective-permute-start(bf16[8,48,640]{2,1,0:T(8,128)(2,1)} %get-tuple-element.176), channel_id=1, source_target_pairs={{0,2},{1,5},{2,0},{3,7},{4,6},{5,1},{6,4},{7,3},{8,10},{9,13},{10,... | collective-permute-start | bytes 1474568 | tf_op jit(solution)/shard_map/ppermute | solution.py:740
  117.4 4.5 %collective-permute-start.32 = (bf16[1,192,384]{2,1,0:T(8,128)(2,1)S(1)}, bf16[1,192,384]{2,1,0:T(8,128)(2,1)S(1)}, u32[]{:S(2)}, u32[]{:S(2)}) collective-permute-start(bf16[1,192,384]{2,1,0:T(8,128)(2,1)S(1)} %get-tuple-element.200), channel_id=1, source_target_pairs={{0,16},{1,9},{2,18},{3,11},{4,20},{5,13},{6,22},{7,15},{8,24},{9,1... | collective-permute-start | bytes 442376 | tf_op jit(solution)/shard_map/ppermute | solution.py:740
  122.4 22.7 %collective-permute-start.33 = (bf16[192,384]{1,0:T(8,128)(2,1)S(1)}, bf16[192,384]{1,0:T(8,128)(2,1)S(1)}, u32[]{:S(2)}, u32[]{:S(2)}) collective-permute-start(bf16[192,384]{1,0:T(8,128)(2,1)S(1)} %add_last.7.mine_ref), channel_id=1, source_target_pairs={{0,1},{1,0},{2,3},{3,2},{4,5},{5,4},{6,7},{7,6},{8,9},{9,8},{10,11... | collective-permute-start | bytes 442376 | tf_op jit(solution)/shard_map/ppermute | solution.py:735
  128.1 11.2 %collective-permute-start.28 = (bf16[2,48,1920]{2,1,0:T(8,128)(2,1)S(1)}, bf16[2,48,1920]{2,1,0:T(8,128)(2,1)S(1)}, u32[]{:S(2)}, u32[]{:S(2)}) collective-permute-start(bf16[2,48,1920]{2,1,0:T(8,128)(2,1)S(1)} %get-tuple-element.189), channel_id=1, source_target_pairs={{0,8},{1,17},{2,10},{3,19},{4,12},{5,21},{6,14},{7,23},{8,0},{9,25... | collective-permute-start | bytes 1105928 | tf_op jit(solution)/shard_map/ppermute | solution.py:740
  130.8 10.5 %collective-permute-start.23 = (bf16[4,48,640]{2,1,0:T(8,128)(2,1)S(1)}, bf16[4,48,640]{2,1,0:T(8,128)(2,1)S(1)}, u32[]{:S(2)}, u32[]{:S(2)}) collective-permute-start(bf16[4,48,640]{2,1,0:T(8,128)(2,1)S(1)} %get-tuple-element.178), channel_id=1, source_target_pairs={{0,4},{1,3},{2,6},{3,1},{4,0},{5,7},{6,2},{7,5},{8,12},{9,11},{10,... | collective-permute-start | bytes 737288 | tf_op jit(solution)/shard_map/ppermute | solution.py:740
  133.9 9.2 %collective-permute-start.18 = (bf16[4,48,896]{2,1,0:T(8,128)(2,1)S(1)}, bf16[4,48,896]{2,1,0:T(8,128)(2,1)S(1)}, u32[]{:S(2)}, u32[]{:S(2)}) collective-permute-start(bf16[4,48,896]{2,1,0:T(8,128)(2,1)S(1)} %get-tuple-element.171), channel_id=1, source_target_pairs={{0,4},{1,3},{2,6},{3,1},{4,0},{5,7},{6,2},{7,5},{8,12},{9,11},{10,... | collective-permute-start | bytes 1032200 | tf_op jit(solution)/shard_map/ppermute | solution.py:740
  139.0 16.0 %collective-permute-start.16 = (bf16[256,768]{1,0:T(8,128)(2,1)S(1)}, bf16[256,768]{1,0:T(8,128)(2,1)S(1)}, u32[]{:S(2)}, u32[]{:S(2)}) collective-permute-start(bf16[256,768]{1,0:T(8,128)(2,1)S(1)} %get-tuple-element.168), channel_id=1, source_target_pairs={{0,1},{1,0},{2,3},{3,2},{4,5},{5,4},{6,7},{7,6},{8,9},{9,8},{10,11... | collective-permute-start | bytes 1179656 | tf_op jit(solution)/shard_map/ppermute | solution.py:735
  140.0 6.5 %collective-permute-start.29 = (bf16[1,48,1920]{2,1,0:T(8,128)(2,1)S(1)}, bf16[1,48,1920]{2,1,0:T(8,128)(2,1)S(1)}, u32[]{:S(2)}, u32[]{:S(2)}) collective-permute-start(bf16[1,48,1920]{2,1,0:T(8,128)(2,1)S(1)} %get-tuple-element.191), channel_id=1, source_target_pairs={{0,16},{1,9},{2,18},{3,11},{4,20},{5,13},{6,22},{7,15},{8,24},{9,1... | collective-permute-start | bytes 552968 | tf_op jit(solution)/shard_map/ppermute | solution.py:740
  141.9 9.3 %collective-permute-start.24 = (bf16[2,48,640]{2,1,0:T(8,128)(2,1)S(1)}, bf16[2,48,640]{2,1,0:T(8,128)(2,1)S(1)}, u32[]{:S(2)}, u32[]{:S(2)}) collective-permute-start(bf16[2,48,640]{2,1,0:T(8,128)(2,1)S(1)} %get-tuple-element.180), channel_id=1, source_target_pairs={{0,8},{1,17},{2,10},{3,19},{4,12},{5,21},{6,14},{7,23},{8,0},{9,25... | collective-permute-start | bytes 368648 | tf_op jit(solution)/shard_map/ppermute | solution.py:740
  143.8 10.5 %collective-permute-start.19 = (bf16[2,48,896]{2,1,0:T(8,128)(2,1)S(1)}, bf16[2,48,896]{2,1,0:T(8,128)(2,1)S(1)}, u32[]{:S(2)}, u32[]{:S(2)}) collective-permute-start(bf16[2,48,896]{2,1,0:T(8,128)(2,1)S(1)} %get-tuple-element.173), channel_id=1, source_target_pairs={{0,8},{1,17},{2,10},{3,19},{4,12},{5,21},{6,14},{7,23},{8,0},{9,25... | collective-permute-start | bytes 516104 | tf_op jit(solution)/shard_map/ppermute | solution.py:740
  147.1 14.3 %collective-permute-start.30 = (bf16[48,1920]{1,0:T(8,128)(2,1)S(1)}, bf16[48,1920]{1,0:T(8,128)(2,1)S(1)}, u32[]{:S(2)}, u32[]{:S(2)}) collective-permute-start(bf16[48,1920]{1,0:T(8,128)(2,1)S(1)} %add_last.6.mine_ref), channel_id=1, source_target_pairs={{0,1},{1,0},{2,3},{3,2},{4,5},{5,4},{6,7},{7,6},{8,9},{9,8},{10,11... | collective-permute-start | bytes 552968 | tf_op jit(solution)/shard_map/ppermute | solution.py:735
  151.8 3.2 %collective-permute-start.25 = (bf16[1,48,640]{2,1,0:T(8,128)(2,1)S(1)}, bf16[1,48,640]{2,1,0:T(8,128)(2,1)S(1)}, u32[]{:S(2)}, u32[]{:S(2)}) collective-permute-start(bf16[1,48,640]{2,1,0:T(8,128)(2,1)S(1)} %get-tuple-element.182), channel_id=1, source_target_pairs={{0,16},{1,9},{2,18},{3,11},{4,20},{5,13},{6,22},{7,15},{8,24},{9,1... | collective-permute-start | bytes 184328 | tf_op jit(solution)/shard_map/ppermute | solution.py:740
  154.9 3.7 %collective-permute-start.20 = (bf16[1,48,896]{2,1,0:T(8,128)(2,1)S(1)}, bf16[1,48,896]{2,1,0:T(8,128)(2,1)S(1)}, u32[]{:S(2)}, u32[]{:S(2)}) collective-permute-start(bf16[1,48,896]{2,1,0:T(8,128)(2,1)S(1)} %get-tuple-element.175), channel_id=1, source_target_pairs={{0,16},{1,9},{2,18},{3,11},{4,20},{5,13},{6,22},{7,15},{8,24},{9,1... | collective-permute-start | bytes 258056 | tf_op jit(solution)/shard_map/ppermute | solution.py:740
  155.6 7.3 %collective-permute-start.26 = (bf16[48,640]{1,0:T(8,128)(2,1)S(1)}, bf16[48,640]{1,0:T(8,128)(2,1)S(1)}, u32[]{:S(2)}, u32[]{:S(2)}) collective-permute-start(bf16[48,640]{1,0:T(8,128)(2,1)S(1)} %add_last.5.vo_mine), channel_id=1, source_target_pairs={{0,1},{1,0},{2,3},{3,2},{4,5},{5,4},{6,7},{7,6},{8,9},{9,8},{10,11... | collective-permute-start | bytes 184328 | tf_op jit(solution)/shard_map/ppermute | solution.py:735
  159.1 3.7 %collective-permute-start.21 = (bf16[48,896]{1,0:T(8,128)(2,1)S(1)}, bf16[48,896]{1,0:T(8,128)(2,1)S(1)}, u32[]{:S(2)}, u32[]{:S(2)}) collective-permute-start(bf16[48,896]{1,0:T(8,128)(2,1)S(1)} %add_last.4.qk_mine), channel_id=1, source_target_pairs={{0,1},{1,0},{2,3},{3,2},{4,5},{5,4},{6,7},{7,6},{8,9},{9,8},{10,11... | collective-permute-start | bytes 258056 | tf_op jit(solution)/shard_map/ppermute | solution.py:735
  (34 other events, 180.3 us)

commit v4 on v3

--- a/solution.py
+++ b/solution.py
@@ -3,7 +3,6 @@
 
 import jax
 import jax.numpy as jnp
-import numpy as np
 from jax import lax
 from jax.experimental import pallas as pl
 from jax.experimental.pallas import tpu as pltpu
@@ -13,7 +12,7 @@
 HEADS = 12
 PAIRS = HEADS // 2
 BIG = 1e9
-COST = 0.6e9
+COST = 0.65e9
 SDS = jax.ShapeDtypeStruct
 HBM = pltpu.HBM
 
@@ -65,11 +64,14 @@
     return sine, cosine
 
 
-def tables_kernel(ids, box_ref, rrow_ref, rcol_ref, wk_ref, wq_ref,
-                  kf_ref, tab_ref, tabt_ref, fkt_ref, fqt_ref, wkt_ref, wqt_ref):
+def rates(shape, dim):
+    at = lax.broadcasted_iota(jnp.int32, shape, dim) & 63
+    return jnp.exp(at.astype(F32) * (-math.log(10000.0) / 64))
+
+
+def tables_kernel(ids, box_ref, kf_ref, tab_ref, tabt_ref, fkt_ref, fqt_ref):
     half = kf_ref.shape[0] // 2
-    wkt_ref[...] = wk_ref[...].T
-    wqt_ref[...] = wq_ref[...].T
+    rate_row, rate_column = rates((8, 128), 1)[0:1, :], rates((64, 128), 0)[:, 0:1]
     box = box_ref[0].astype(F32)
     centre = (box[0:2, :] + box[2:4, :]) * 0.5
     turned = jnp.concatenate([centre[:, half:], centre[:, :half]], 1)
@@ -77,11 +79,11 @@
     column = jnp.concatenate([centre, jnp.zeros((6, 2 * half), F32)], 0).T
     front = lax.broadcasted_iota(jnp.int32, (2 * half, 128), 1) < 64
     for axis in range(2):
-        s, c = sin_cos(column[:, axis : axis + 1] * rrow_ref[...])
+        s, c = sin_cos(column[:, axis : axis + 1] * rate_row)
         kf_ref[:, axis * 128 : axis * 128 + 128] = jnp.where(front, c, s).astype(BF16)
         tab_ref[axis] = c
         tab_ref[2 + axis] = jnp.where(front, s, -s)
-        st, ct = sin_cos(rcol_ref[...] * centre[axis : axis + 1, :])
+        st, ct = sin_cos(rate_column * centre[axis : axis + 1, :])
         tabt_ref[2 * axis] = st
         tabt_ref[2 * axis + 1] = ct
         sl, cl = st.astype(BF16), ct.astype(BF16)
@@ -92,18 +94,11 @@
         fqt_ref[at + 64 : at + 128, :] = cl * 0.125
 
 
-def tables(ids, boxes, wk, wq):
+def tables(ids, boxes):
     rows = boxes.shape[2]
-    width = wk.shape[1]
-    rates = np.exp(np.arange(64) * (-math.log(10000.0) / 64)).astype(np.float32)
-    shapes = [((rows, 256), BF16), ((4, rows, 128), F32), ((4, 64, rows), F32), ((256, rows), BF16), ((256, rows), BF16),
-              ((width, 256), BF16), ((width, 256), BF16)]
-    return call(
-        tables_kernel, "tables", (1,), ids, (boxes, np.tile(rates, 2)[None, :], rates[:, None], wk, wq),
-        [
-            pl.BlockSpec((1, 4, rows), lambda i, ids: (ids[1], 0, 0)),
-            whole((1, 128)), whole((64, 1)), whole((256, width)), whole((256, width)),
-        ],
+    shapes = [((rows, 256), BF16), ((4, rows, 128), F32), ((4, 64, rows), F32), ((256, rows), BF16), ((256, rows), BF16)]
+    return call(
+        tables_kernel, "tables", (1,), ids, (boxes,), [pl.BlockSpec((1, 4, rows), lambda i, ids: (ids[1], 0, 0))],
         [whole(s) for s, _ in shapes], [SDS(s, t) for s, t in shapes], us=3,
     )
 
@@ -150,8 +145,11 @@
 
 
 def attend_kernel(ids, len_ref, qt_ref, vt_ref, k_ref, wk_ref, wq_ref, kf_ref, tab_ref, tabt_ref, fqt_ref,
-                  e_ref, at_ref, r_ref, fk, fq):
+                  e_ref, at_ref, r_ref, wkt_ref, wqt_ref, fk, fq):
     rows = k_ref.shape[0]
+    wkt_ref[...] = wk_ref[...].T
+    wqt_ref[...] = wq_ref[...].T
+    heads = k_ref.shape[1] // 64
 
     @pl.when(pl.program_id(0) == 0)
     def _():
@@ -159,66 +157,77 @@
         at = lax.broadcasted_iota(jnp.int32, (rows, 128), 0)
         turned = jnp.where(at < rows // 2, at + rows // 2, at - rows // 2)
         at = jnp.where(ids[1] == 0, at, turned)
-        fk[:, 0:256] = kf_ref[...]
-        fk[:, 640:768] = jnp.where((lane == 0) & (at >= len_ref[ids[1]]), -BIG, 0.0).astype(BF16)
-        fq[256:512, :] = fqt_ref[...]
+        mask = jnp.where((lane == 0) & (at >= len_ref[ids[1]]), -BIG, 0.0).astype(BF16)
         sub = lax.broadcasted_iota(jnp.int32, (128, rows), 0)
-        fq[640:768, :] = jnp.where(sub == 0, 1.0, 0.0).astype(BF16)
-
-    fk[:, 512:640] = k_ref[...]
+        for h in range(heads):
+            fk[h, :, 0:256] = kf_ref[...]
+            fk[h, :, 640:768] = mask
+            fq[h, 256:512, :] = fqt_ref[...]
+            fq[h, 640:768, :] = jnp.where(sub == 0, 1.0, 0.0).astype(BF16)
+
     lane = lax.broadcasted_iota(jnp.int32, (256, 128), 1)
-    for h in range(2):
-        mine = (lane < 64) if h == 0 else (lane >= 64)
+    for h in range(heads):
+        two = slice(h // 2 * 128, h // 2 * 128 + 128)
+        fk[h, :, 512:640] = k_ref[:, two]
+        mine = (lane < 64) if h % 2 == 0 else (lane >= 64)
         qt = qt_ref[h * 64 : h * 64 + 64, :]
         zero = jnp.zeros_like(qt)
-        pad = jnp.concatenate([qt, zero] if h == 0 else [zero, qt], 0)
-        fq[512:640, :] = pad * 0.125
-        a = mm(wk_ref[...], pad)
+        pad = jnp.concatenate([qt, zero] if h % 2 == 0 else [zero, qt], 0)
+        fq[h, 512:640, :] = pad * 0.125
+        a = mm(wk_ref[:, two], pad)
         sx, cx, sy, cy = (tabt_ref[i] * 0.125 for i in range(4))
         axs, axc, ays, ayc = (a[i * 64 : i * 64 + 64, :] for i in range(4))
-        fq[0:64, :] = (axs * sx + axc * cx).astype(BF16)
-        fq[64:128, :] = (axc * sx - axs * cx).astype(BF16)
-        fq[128:192, :] = (ays * sy + ayc * cy).astype(BF16)
-        fq[192:256, :] = (ayc * sy - ays * cy).astype(BF16)
-        w = jnp.where(mine, wq_ref[...], 0).astype(BF16)
-        b = mm_nt(k_ref[...], w)
+        fq[h, 0:64, :] = (axs * sx + axc * cx).astype(BF16)
+        fq[h, 64:128, :] = (axc * sx - axs * cx).astype(BF16)
+        fq[h, 128:192, :] = (ays * sy + ayc * cy).astype(BF16)
+        fq[h, 192:256, :] = (ayc * sy - ays * cy).astype(BF16)
+        w = jnp.where(mine, wq_ref[:, two], 0).astype(BF16)
+        b = mm_nt(k_ref[:, two], w)
         for axis in range(2):
             part = b[:, axis * 128 : axis * 128 + 128]
             turned = pltpu.roll(part, 64, 1)
-            fk[:, 256 + axis * 128 : 384 + axis * 128] = (
+            fk[h, :, 256 + axis * 128 : 384 + axis * 128] = (
                 part * tab_ref[axis] + turned * tab_ref[2 + axis]
             ).astype(BF16)
-        s = mm(fk[...], fq[...])
+    for h in range(heads):
+        if h % 4 == 0:
+            scores = [mm(fk[g], fq[g]) for g in range(h, h + 4)]
+        s = scores[h % 4]
         e = jnp.exp(s - jnp.max(s, 0, keepdims=True))
         r = 1.0 / jnp.sum(e, 0, keepdims=True)
         low = e.astype(BF16)
         e_ref[h] = low
         at_ref[h * 64 : h * 64 + 64, :] = (mm(vt_ref[h * 64 : h * 64 + 64, :], low) * r).astype(BF16)
-        r_ref[0, h : h + 1, :] = r
+        r_ref[h // 2, h % 2 : h % 2 + 1, :] = r
 
 
 def attend(ids, lengths, pt, p, w_posk, w_posq, kf, tab, tabt, fqt):
     rows = p.shape[0]
     width = pt.shape[0] // 3
     return call(
-        attend_kernel, "attend", (PAIRS,), ids, (lengths, pt, pt, p, w_posk, w_posq, kf, tab, tabt, fqt),
+        attend_kernel, "attend", (PAIRS // 2,), ids, (lengths, pt, pt, p, w_posk, w_posq, kf, tab, tabt, fqt),
         [
             pl.BlockSpec(memory_space=pltpu.SMEM),
-            pl.BlockSpec((128, rows), lambda i, ids: (i, 0)),
-            pl.BlockSpec((128, rows), lambda i, ids: (2 * PAIRS + i, 0)),
-            pl.BlockSpec((rows, 128), lambda i, ids: (0, PAIRS + i)),
-            pl.BlockSpec((256, 128), lambda i, ids: (0, i)),
-            pl.BlockSpec((256, 128), lambda i, ids: (0, i)),
+            pl.BlockSpec((256, rows), lambda i, ids: (i, 0)),
+            pl.BlockSpec((256, rows), lambda i, ids: (2 * PAIRS // 2 + i, 0)),
+            pl.BlockSpec((rows, 256), lambda i, ids: (0, PAIRS // 2 + i)),
+            pl.BlockSpec((256, 256), lambda i, ids: (0, i)),
+            pl.BlockSpec((256, 256), lambda i, ids: (0, i)),
             whole((rows, 256)), whole((4, rows, 128)), whole((4, 64, rows)), whole((256, rows)),
         ],
         [
-            pl.BlockSpec((2, rows, rows), lambda i, ids: (i, 0, 0)),
-            pl.BlockSpec((128, rows), lambda i, ids: (i, 0)),
-            pl.BlockSpec((1, 2, rows), lambda i, ids: (i, 0, 0)),
-        ],
-        [HBM((HEADS, rows, rows), BF16), SDS((width, rows), BF16), SDS((PAIRS, 2, rows), F32)],
-        [pltpu.VMEM((rows, 768), BF16), pltpu.VMEM((768, rows), BF16)],
-        us=17,
+            pl.BlockSpec((4, rows, rows), lambda i, ids: (i, 0, 0)),
+            pl.BlockSpec((256, rows), lambda i, ids: (i, 0)),
+            pl.BlockSpec((2, 2, rows), lambda i, ids: (i, 0, 0)),
+            pl.BlockSpec((256, 256), lambda i, ids: (i, 0)),
+            pl.BlockSpec((256, 256), lambda i, ids: (i, 0)),
+        ],
+        [
+            HBM((HEADS, rows, rows), BF16), SDS((width, rows), BF16), SDS((PAIRS, 2, rows), F32),
+            SDS((width, 256), BF16), SDS((width, 256), BF16),
+        ],
+        [pltpu.VMEM((4, rows, 768), BF16), pltpu.VMEM((4, 768, rows), BF16)],
+        vmem=22, us=17,
     )
 
 
@@ -295,7 +304,7 @@
     _, half, width = tokens.shape
     rows = 2 * half
     ff = w_in.shape[1]
-    block = 512
+    block = 1024
     mat = whole((rows, width))
     return call(
         feed_kernel, "feed", (ff // block,), ids,
@@ -321,7 +330,7 @@
         ],
         [pltpu.VMEM((rows, width), F32), pltpu.VMEM((rows, width), BF16), pltpu.VMEM((rows, width), F32),
          pltpu.VMEM((rows, width), BF16)],
-        us=15,
+        vmem=24, us=15,
     )
 
 
@@ -425,28 +434,36 @@
 
 def attend_back_kernel(ids, e_ref, r_ref, da_ref, at_ref, qt_ref, kt_ref, v_ref, wkt_ref, wqt_ref, fkt_ref, fqt_ref,
                        tabt_ref, dp_ref, gk_ref, gq_ref, rows_ref, left_k, left_q):
+    heads = 2
+
     @pl.when(pl.program_id(0) == 0)
     def _():
-        left_k[64:320, :] = fkt_ref[...]
-        left_q[64:320, :] = fqt_ref[...]
+        for h in range(heads):
+            left_k[h, 64:320, :] = fkt_ref[...]
+            left_q[h, 64:320, :] = fqt_ref[...]
 
     sx, cx, sy, cy = (tabt_ref[i] for i in range(4))
     lane = lax.broadcasted_iota(jnp.int32, (256, 128), 1)
-    gk, gq = [], []
-    for h in range(2):
-        own = slice(h * 64, h * 64 + 64)
-        da = da_ref[own, :].astype(F32) * r_ref[0, h : h + 1, :]
-        delta = jnp.sum(da * at_ref[own, :].astype(F32), 0, keepdims=True)
+    own = [slice(h * 64, h * 64 + 64) for h in range(heads)]
+    das, deltas, dps = [], [], []
+    for h in range(heads):
+        left_k[h, 0:64, :] = kt_ref[own[h], :]
+        left_q[h, 0:64, :] = qt_ref[own[h], :] * 0.125
+        da = da_ref[own[h], :].astype(F32) * r_ref[0, h : h + 1, :]
+        deltas.append(jnp.sum(da * at_ref[own[h], :].astype(F32), 0, keepdims=True))
         da = da.astype(BF16)
+        das.append(da)
         zero = jnp.zeros_like(da)
         pad = jnp.concatenate([da, zero] if h == 0 else [zero, da], 0)
-        e = e_ref[h]
-        ds = (e.astype(F32) * (mm(v_ref[...], pad) - delta)).astype(BF16)
-        left_k[0:64, :] = kt_ref[own, :]
-        left_q[0:64, :] = qt_ref[own, :] * 0.125
-        one = mm(left_k[...], ds) * 0.125
-        two = mm_nt(left_q[...], ds)
-        dv = mm_nt(da, e)
+        dps.append(mm(v_ref[...], pad))
+    dss = [(e_ref[h].astype(F32) * (dps[h] - deltas[h])).astype(BF16) for h in range(heads)]
+    ones = [mm(left_k[h], dss[h]) * 0.125 for h in range(heads)]
+    twos = [mm_nt(left_q[h], dss[h]) for h in range(heads)]
+    gk, gq = [], []
+    for h in range(heads):
+        dp_ref[2, own[h], :] = mm_nt(das[h], e_ref[h]).astype(BF16)
+    for h in range(heads):
+        one, two = ones[h], twos[h]
         ux1, ux2, uy1, uy2 = (one[64 + i * 64 : 128 + i * 64, :].astype(BF16).astype(F32) for i in range(4))
         d_a = jnp.concatenate(
             [ux1 * sx - ux2 * cx, ux1 * cx + ux2 * sx, uy1 * sy - uy2 * cy, uy1 * cy + uy2 * sy], 0
@@ -455,16 +472,15 @@
         d_b = jnp.concatenate(
             [zx1 * cx - zx2 * sx, zx1 * sx + zx2 * cx, zy1 * cy - zy2 * sy, zy1 * sy + zy2 * cy], 0
         ).astype(BF16)
-        dp_ref[0, own, :] = (one[0:64, :] + mm(wkt_ref[own, :], d_a)).astype(BF16)
-        dp_ref[1, own, :] = (two[0:64, :] + mm(wqt_ref[own, :], d_b)).astype(BF16)
-        dp_ref[2, own, :] = dv.astype(BF16)
+        dp_ref[0, own[h], :] = (one[0:64, :] + mm(wkt_ref[own[h], :], d_a)).astype(BF16)
+        dp_ref[1, own[h], :] = (two[0:64, :] + mm(wqt_ref[own[h], :], d_b)).astype(BF16)
         gk.append(mm_nt(d_a, qt_ref[...]))
         gq.append(mm_nt(d_b, kt_ref[...]))
     gk_ref[...] = jnp.where(lane < 64, gk[0], gk[1]).astype(BF16)
     gq_ref[...] = jnp.where(lane < 64, gq[0], gq[1]).astype(BF16)
-    ones = jnp.ones((8, dp_ref.shape[2]), BF16)
+    unit = jnp.ones((8, dp_ref.shape[2]), BF16)
     for i in range(3):
-        rows_ref[8 * i : 8 * i + 8, :] = mm_nt(ones, dp_ref[i])
+        rows_ref[8 * i : 8 * i + 8, :] = mm_nt(unit, dp_ref[i])
 
 
 def attend_back(ids, own, e, r, datt, att, pt, p, wkt, wqt, fkt, fqt, tabt):
@@ -492,7 +508,7 @@
             SDS((3, 128 * pairs, rows), BF16), SDS((256, 128 * pairs), BF16), SDS((256, 128 * pairs), BF16),
             SDS((24, 128 * pairs), F32),
         ],
-        [pltpu.VMEM((320, rows), BF16), pltpu.VMEM((320, rows), BF16)],
+        [pltpu.VMEM((2, 320, rows), BF16), pltpu.VMEM((2, 320, rows), BF16)],
         us=9,
     )
 
@@ -748,17 +764,31 @@
     return ORDERS
 
 
-ORDERS = (((0, 1, 2, 3), (1, 0, 3, 2)),) * 4
+ORDERS = (
+    ((0, 2, 1, 3), (1, 2, 0, 3)),
+    ((0, 1, 2, 3), (1, 0, 3, 2)),
+    ((0, 1, 2, 3), (1, 0, 3, 2)),
+    ((0, 1, 2, 3), (1, 0, 3, 2)),
+)
+
+
+class Chain:
+    def __init__(self, ids):
+        self.ids = ids
+
+    def run(self, kernel, *args, **kwargs):
+        out = kernel(self.ids, *args, **kwargs)
+        self.ids = after(self.ids, out[0] if isinstance(out, (list, tuple)) else out)
+        return out
 
 
 class Exchange:
-    def __init__(self, ids, n, send, keep, order):
-        self.ids, self.n, self.order = ids, n, order
+    def __init__(self, chain, n, send, keep, order):
+        self.chain, self.n, self.order = chain, n, order
         self.left = [sorted(o) for o in order]
         self.at = 0
         self.steps = len(order[0])
-        self.keep = keep
-        self.got = across(send, n, self.bits(0))
+        self.send, self.keep = send, keep
 
     @staticmethod
     def first(order):
@@ -766,19 +796,22 @@
 
     def bits(self, step):
         return tuple(o[step] for o in self.order)
+
+    def start(self):
+        self.got = across(self.send, self.n, self.bits(self.at))
 
     def step(self):
         for l, b in zip(self.left, self.bits(self.at)):
             l.remove(b)
         self.at += 1
         if self.at == self.steps:
-            self.mine = add_last(self.ids, self.keep, self.got)
+            self.mine = self.chain.run(add_last, self.keep, self.got)
             self.other = swap(self.mine)
             return
         bits = self.bits(self.at)
         lows = tuple(l.index(b) for l, b in zip(self.left, bits))
-        send, self.keep = add_split(self.ids, self.keep, self.got, bits, lows)
-        self.got = across(send, self.n, bits)
+        self.send, self.keep = self.chain.run(add_split, self.keep, self.got, bits, lows)
+        self.start()
 
 
 def join_kernel(ids, mine_ref, other_ref, *outs):
@@ -872,9 +905,9 @@
     other = swap(tokens)
     cot_other = swap(cotangent)
 
-    kf, tab, tabt, fkt, fqt, wkt, wqt = tables(ids, boxes, w_posk, w_posq)
+    kf, tab, tabt, fkt, fqt = tables(ids, boxes)
     pt, p, xt = project(after(ids, kf), tokens, other, w_qkv, b_qkv)
-    e, att, r = attend(ids, lengths, pt, p, w_posk, w_posq, kf, tab, tabt, fqt)
+    e, att, r, wkt, wqt = attend(ids, lengths, pt, p, w_posk, w_posq, kf, tab, tabt, fqt)
     (flt, norm, rstd, slope, actt, out_keep, out_give, dres_two, dsec, dsec_send, rows_two) = feed(
         ids, att, tokens, other, w_out, w_in, w_down, b_out, gain_one, shift_one, b_in, b_down, gain_two, shift_two,
         cotangent, cot_other
@@ -923,44 +956,60 @@
 
     order_down, order_mid, order_qk, order_vp = orders(n)
     first = Exchange.first
+    chain = Chain(after(ids, dh))
     down = Exchange(
-        ids, n, *down_grad(ids, n, first(order_down), actt, actt_other, dsec, dsec_other), order_down
-    )
-    dres_one, branch, branch_send, datt, rows_one = first_back(
-        after(ids, down.keep), dh_send, dh, w_in, dres_two, norm, rstd, gain_one, w_out
+        chain, n, *chain.run(down_grad, n, first(order_down), actt, actt_other, dsec, dsec_other), order_down
+    )
+    down.start()
+    dres_one, branch, branch_send, datt, rows_one = chain.run(
+        first_back, dh_send, dh, w_in, dres_two, norm, rstd, gain_one, w_out
     )
     branch_other = swap(branch_send)
     mid = Exchange(
-        ids, n, *mid_grad(ids, n, first(order_mid), flt, flt_other, dh, dh_other, att, att_other, branch, branch_other),
+        chain, n,
+        *chain.run(mid_grad, n, first(order_mid), flt, flt_other, dh, dh_other, att, att_other, branch, branch_other),
         order_mid,
     )
     down.step()
+    mid.send = after(mid.send, down.send)
+    mid.start()
     back = functools.partial(
-        attend_back, e=e, r=r, datt=datt, att=att, pt=pt, p=p, wkt=wkt, wqt=wqt, fkt=fkt, fqt=fqt, tabt=tabt
-    )
-    dp_send, gk_send, gq_send, bias_send = back(after(ids, mid.keep, down.keep), own=False)
+        chain.run, attend_back, e=e, r=r, datt=datt, att=att, pt=pt, p=p, wkt=wkt, wqt=wqt, fkt=fkt, fqt=fqt, tabt=tabt
+    )
+    dp_send, gk_send, gq_send, bias_send = back(own=False)
     dp_other, gk_other, gq_other = swap(dp_send), swap(gk_send), swap(gq_send)
     down.step()
-    dp, gk, gq, bias_own = back(after(ids, dp_send, down.keep), own=True)
+    dp, gk, gq, bias_own = back(own=True)
     small = (3 * width, width, width, width, w_in.shape[1], width, width, width)
     sizes = tuple(s // n for s in small)
+    down.step()
     mid.step()
     qk = Exchange(
-        ids, n, *qk_grad(after(ids, mid.keep), n, first(order_qk), sizes, xt, xt_other, dp, dp_other,
-                         rows_two, rows_one, row_in, bias_send, bias_own), order_qk
-    )
+        chain, n, *chain.run(qk_grad, n, first(order_qk), sizes, xt, xt_other, dp, dp_other,
+                             rows_two, rows_one, row_in, bias_send, bias_own), order_qk
+    )
+    qk.start()
     vp = Exchange(
-        ids, n, *vp_grad(after(ids, qk.keep), n, first(order_vp), xt, xt_other, dp, dp_other,
-                         gk, gk_other, gq, gq_other), order_vp
-    )
-    tok, tok_give = tokens_back(after(ids, vp.keep), w_qkv, dp_send, dp, dres_one)
+        chain, n, *chain.run(vp_grad, n, first(order_vp), xt, xt_other, dp, dp_other,
+                             gk, gk_other, gq, gq_other), order_vp
+    )
+    vp.start()
+    down.step()
+    mid.step()
+    tok, tok_give = chain.run(tokens_back, w_qkv, dp_send, dp, dres_one)
     tok_got = swap(tok_give)
-    while vp.at < vp.steps:
-        for x in (down, mid, qk, vp):
-            if x.at < x.steps:
-                x.step()
-    (g_down,) = join(ids, down.mine, down.other, (width,))
-    g_in, g_out = join(ids, mid.mine, mid.other, (w_in.shape[1], width))
+    qk.step()
+    vp.step()
+    mid.step()
+    (g_down,) = chain.run(join, down.mine, down.other, (width,))
+    qk.step()
+    vp.step()
+    mid.step()
+    qk.step()
+    vp.step()
+    g_in, g_out = chain.run(join, mid.mine, mid.other, (w_in.shape[1], width))
+    qk.step()
+    vp.step()
     g_qkv, g_posk, g_posq, *totals = join_last(ids, n, sizes, qk, vp, width, w_posk.shape[0] // n)
     return (pages(core, out_keep, out_got), pages(core, tok, tok_got), g_qkv, totals[0], g_posk, g_posq, g_out,
             totals[1], totals[2], totals[3], g_in, totals[4], g_down, totals[5], totals[6], totals[7])

time: 165 us -> 146 us (0.88)
  Pallas kernels: 108 us -> 93.9 us
  local copies, waits for them, and re-layouts: 7.22 us -> 3.75 us
    pallas_call x32, Pallas kernels: 108 us -> 93.9 us  [call(): pl.pallas_call(kernel, grid_spec=pltpu.PrefetchScalarGridSpec(num_scalar_...]
    ppermute x18, starting transfers between devices: 17.1 us -> 11.6 us  [swap(): return lax.ppermute(x, 'slab', [(0, 1), (1, 0)])]
    ppermute x16, starting transfers between devices: 16.6 us -> 20.7 us  [across(): return lax.ppermute(x, ('pages', 'slab'), pairs)]
    unnamed x96 -> x76, local copies, waits for them, and re-layouts: 6.16 us -> 2.7 us
  transfers between devices with their start and end apart: 34 -> 34, of which waited for: 7 -> 7; matrix products, arithmetic and copies ran while one was open for 1% -> 1% of each run, Pallas kernels for 56% -> 55%
where the time goes in v4:
time: 146 us; the launch traced here: 145 us
  Pallas kernels  93.9 us (64%)
  starting transfers between devices  32.3 us (22%)
  waiting for transfers between devices  13.6 us (9%)
  local copies, waits for them, and re-layouts  3.75 us (3%)
  between operations  1.51 us (1%)
    pallas_call x32, Pallas kernels, call(): pl.pallas_call(kernel, grid_spec=pltpu.PrefetchScalarGridSpec(num_scalar_...  93.9 us
    ppermute x16, starting transfers between devices, across(): return lax.ppermute(x, ('pages', 'slab'), pairs)  20.7 us
    ppermute x18, starting transfers between devices, swap(): return lax.ppermute(x, 'slab', [(0, 1), (1, 0)])  11.6 us
    ppermute x16, waiting for transfers between devices, across(): return lax.ppermute(x, ('pages', 'slab'), pairs)  11.4 us
  transfers between devices with their start and end apart: 34, of which 7 were waited for; matrix products, arithmetic and copies ran while one was open for 1% of the time, Pallas kernels for 55%

profile of v4, /device:TPU:1, one launch (start us, length us, event | category | flops | bytes accessed | tf_op | source)
XLA Modules:
  0.0 145.1 jit_solution(10622890538179128062)
XLA Ops:
  1.3 0.7 copy-done.6
  2.0 1.7 %tables.1 = (bf16[512,256]{1,0:T(8,128)(2,1)S(1)}, f32[4,512,128]{2,1,0:T(8,128)S(1)}, f32[4,64,512]{2,1,0:T(8,128)S(1)}, bf16[256,512]{1,0:T(8,128)(2,1)S(1)}, bf16[256,512]{1,0:T(8,128)(2,1)S(1)}) custom-call(s32[2]{0:T(128)S(1)} %pad_add_fusion.ids, s32[2,4,512]{2,1,0:T(4,128)S(1)} %copy-done.6), custom_call_target="tpu_custom_call" | custom-call | flops 1950000000 | tf_op jit(solution)/shard_map/tables/pallas_call | solution.py:37
  4.2 3.8 %project.1 = (bf16[2304,512]{1,0:T(8,128)(2,1)S(1)}, bf16[512,2304]{1,0:T(8,128)(2,1)S(1)}, bf16[768,512]{1,0:T(8,128)(2,1)S(1)}) custom-call(s32[2]{0:T(128)S(1)} %pad_add_fusion.ids, bf16[2,256,768]{2,1,0:T(8,128)(2,1)S(1)} %copy-done.2, bf16[2,256,768]{2,1,0:T(8,128)(2,1)S(1)} %collective-permute-done.other_ref, bf16[768,2304]{1,0:T(8,128)(2,1)S(1)} %copy-done, ...), custom_call_target="tpu_custom_call" | custom-call | flops 3249999872 | tf_op jit(solution)/shard_map/project/pallas_call | solution.py:37
  8.2 13.8 %attend.1 = (bf16[12,512,512]{2,1,0:T(8,128)(2,1)}, bf16[768,512]{1,0:T(8,128)(2,1)S(1)}, f32[6,2,512]{2,1,0:T(2,128)S(1)}, bf16[768,256]{1,0:T(8,128)(2,1)S(1)}, bf16[768,256]{1,0:T(8,128)(2,1)S(1)}) custom-call(s32[2]{0:T(128)S(1)} %pad_add_fusion.ids, s32[2]{0:T(128)S(1)} %copy-done.15, bf16[2304,512]{1,0:T(8,128)(2,1)S(1)} %get-tuple-element.133.qt_ref.vt_ref.kt_ref, ...), custom_call_target="tpu_custom_call" | custom-call | flops 11050000384 | tf_op jit(solution)/shard_map/attend/pallas_call | solution.py:37
  22.2 12.5 %feed.1 = (bf16[768,512]{1,0:T(8,128)(2,1)S(1)}, f32[512,768]{1,0:T(8,128)S(1)}, f32[512,1]{1,0:T(8,128)S(1)}, bf16[512,3072]{1,0:T(8,128)(2,1)S(1)}, bf16[3072,...) custom-call(s32[2]{0:T(128)S(1)} %pad_add_fusion.ids, ...), custom_call_target="tpu_custom_call" | custom-call | flops 9749999616 | tf_op jit(solution)/shard_map/feed/pallas_call | solution.py:37
  35.3 5.1 %hidden_back.1 = (bf16[512,1536]{1,0:T(8,128)(2,1)S(1)}, bf16[512,1536]{1,0:T(8,128)(2,1)S(1)}, f32[1,3072]{1,0:T(1,128)S(1)}) custom-call(s32[2]{0:T(128)S(1)} %pad_add_fusion.ids, bf16[512,768]{1,0:T(8,128)(2,1)S(1)} %get-tuple-element.141.ds_ref.b0_ref, bf16[3072,768]{1,0:T(8,128)(2,1)S(1)} %bitcast.7, bf16[512,3072]{1,0:T(8,128)(2,1)S(1)} %get-tuple-element.142.slope_ref), custom_call_target="tpu_custom_call" | custom-call | flops 3249999872 | tf_op jit(solution)/shard_map/hidden_back/pallas_call | solution.py:37
  41.1 5.2 %down_grad.1 = (bf16[8,192,384]{2,1,0:T(8,128)(2,1)S(1)}, bf16[8,192,384]{2,1,0:T(8,128)(2,1)S(1)}) custom-call(s32[2]{0:T(128)S(1)} %pad_add_fusion.ids, bf16[3072,512]{1,0:T(8,128)(2,1)S(1)} %get-tuple-element.145.a0_ref, bf16[3072,512]{1,0:T(8,128)(2,1)S(1)} %collective-permute-done.3.a1_ref, bf16[512,768]{1,0:T(8,128)(2,1)S(1)} %get-tuple-element.141.ds_ref.b0_ref, ...), custom_call_target="tpu_custom_call" | custom-call | flops 4550000128 | tf_op jit(solution)/shard_map/down_grad/pallas_call | solution.py:37
  46.3 2.7 %collective-permute-start.9 = (bf16[8,192,384]{2,1,0:T(8,128)(2,1)S(1)}, bf16[8,192,384]{2,1,0:T(8,128)(2,1)S(1)}, u32[]{:S(2)}, u32[]{:S(2)}) collective-permute-start(bf16[8,192,384]{2,1,0:T(8,128)(2,1)S(1)} %get-tuple-element.147), channel_id=1, source_target_pairs={{0,2},{1,5},{2,0},{3,7},{4,6},{5,1},{6,4},{7,3},{8,10},{9,13},{10,... | collective-permute-start | bytes 3538952 | tf_op jit(solution)/shard_map/ppermute | solution.py:756
  49.0 6.6 %first_back.1 = (f32[512,768]{1,0:T(8,128)S(1)}, bf16[512,768]{1,0:T(8,128)(2,1)S(1)}, bf16[512,384]{1,0:T(8,128)(2,1)S(1)}, bf16[768,512]{1,0:T(8,128)(2,1)S(1)}, f32[8,768]{1,0:T(8,128)S(1)}) custom-call(s32[2]{0:T(128)S(1)} %pad_add_fusion.ids, bf16[512,1536]{1,0:T(8,128)(2,1)S(1)} %get-tuple-element.149.dsend_ref, ...), custom_call_target="tpu_custom_call" | custom-call | flops 5200000000 | tf_op jit(solution)/shard_map/first_back/pallas_call | solution.py:37
  56.0 1.4 collective-permute-done.8.c1_ref
  57.4 5.7 %mid_grad.1 = (bf16[8,48,1920]{2,1,0:T(8,128)(2,1)S(1)}, bf16[8,48,1920]{2,1,0:T(8,128)(2,1)S(1)}) custom-call(s32[2]{0:T(128)S(1)} %pad_add_fusion.ids, bf16[768,512]{1,0:T(8,128)(2,1)S(1)} %get-tuple-element.155.f0_ref, bf16[768,512]{1,0:T(8,128)(2,1)S(1)} %collective-permute-done.5.f1_ref, bf16[512,1536]{1,0:T(8,128)(2,1)S(1)} %get-tuple-element.143.down_ref.h0_ref, ...), custom_call_target="tpu_custom_call" | custom-call | flops 3900000000 | tf_op jit(solution)/shard_map/mid_grad/pallas_call | solution.py:37
  63.1 0.9 add_split.12
  64.0 1.3 collective-permute-start.12
  65.3 1.3 collective-permute-start.10
  66.6 6.8 %attend_back.2 = (bf16[3,384,512]{2,1,0:T(8,128)(2,1)S(1)}, bf16[256,384]{1,0:T(8,128)(2,1)S(1)}, bf16[256,384]{1,0:T(8,128)(2,1)S(1)}, f32[24,384]{1,0:T(8,128)S(1)}) custom-call(s32[2]{0:T(128)S(1)} %pad_add_fusion.ids, bf16[12,512,512]{2,1,0:T(8,128)(2,1)S(1)} %bitcast.11, f32[6,2,512]{2,1,0:T(2,128)S(1)} %get-tuple-element.164.r_ref, ...), custom_call_target="tpu_custom_call" | custom-call | flops 5849999872 | tf_op jit(solution)/shard_map/attend_back/pallas_call | solution.py:37
  73.5 1.5 %collective-permute-start.14 = (bf16[3,384,512]{2,1,0:T(8,128)(2,1)S(1)}, bf16[3,384,512]{2,1,0:T(8,128)(2,1)S(1)}, u32[]{:S(2)}, u32[]{:S(2)}) collective-permute-start(bf16[3,384,512]{2,1,0:T(8,128)(2,1)S(1)} %get-tuple-element.169.ds_ref), channel_id=1, source_target_pairs={{0,1},{1,0},{2,3},{3,2},{4,5},{5,4},{6,7},{7,6},{8,9},{9,8},{10,11... | collective-permute-start | bytes 3538952 | tf_op jit(solution)/shard_map/ppermute | solution.py:751
  75.1 3.9 %collective-permute-done.10.got_ref = bf16[4,192,384]{2,1,0:T(8,128)(2,1)S(1)} collective-permute-done((bf16[4,192,384]{2,1,0:T(8,128)(2,1)S(1)}, bf16[4,192,384]{2,1,0:T(8,128)(2,1)S(1)}, u32[]{:S(2)}, u32[]{:S(2)}) %collective-permute-start.10) | collective-permute-done | bytes 589856 | tf_op jit(solution)/shard_map/ppermute | solution.py:756
  78.9 0.7 add_split.13
  79.6 2.7 %collective-permute-start.11 = (bf16[2,192,384]{2,1,0:T(8,128)(2,1)S(1)}, bf16[2,192,384]{2,1,0:T(8,128)(2,1)S(1)}, u32[]{:S(2)}, u32[]{:S(2)}) collective-permute-start(bf16[2,192,384]{2,1,0:T(8,128)(2,1)S(1)} %get-tuple-element.172), channel_id=1, source_target_pairs={{0,4},{1,3},{2,6},{3,1},{4,0},{5,7},{6,2},{7,5},{8,12},{9,11},{10,... | collective-permute-start | bytes 884744 | tf_op jit(solution)/shard_map/ppermute | solution.py:756
  82.4 6.8 %attend_back.3 = (bf16[3,384,512]{2,1,0:T(8,128)(2,1)S(1)}, bf16[256,384]{1,0:T(8,128)(2,1)S(1)}, bf16[256,384]{1,0:T(8,128)(2,1)S(1)}, f32[24,384]{1,0:T(8,128)S(1)}) custom-call(s32[2]{0:T(128)S(1)} %pad_add_fusion.ids, bf16[12,512,512]{2,1,0:T(8,128)(2,1)S(1)} %bitcast.11, f32[6,2,512]{2,1,0:T(2,128)S(1)} %get-tuple-element.164.r_ref, ...), custom_call_target="tpu_custom_call" | custom-call | flops 5849999872 | tf_op jit(solution)/shard_map/attend_back/pallas_call | solution.py:37
  89.8 0.9 add_split.15
  90.9 1.4 collective-permute-start.15
  92.3 3.7 %qk_grad.1 = (bf16[8,48,896]{2,1,0:T(8,128)(2,1)S(1)}, bf16[8,48,896]{2,1,0:T(8,128)(2,1)S(1)}) custom-call(s32[2]{0:T(128)S(1)} %pad_add_fusion.ids, bf16[768,512]{1,0:T(8,128)(2,1)S(1)} %get-tuple-element.183.x0_ref, bf16[768,512]{1,0:T(8,128)(2,1)S(1)} %collective-permute-done.13.x1_ref, bf16[3,384,512]{2,1,0:T(8,128)(2,1)S(1)} %get-tuple-element.174.d0_ref.do_ref, ...), custom_call_target="tpu_custom_call" | custom-call | flops 2600000000 | tf_op jit(solution)/shard_map/qk_grad/pallas_call | solution.py:37
  96.3 2.3 %collective-permute-start.17 = (bf16[1,192,384]{2,1,0:T(8,128)(2,1)S(1)}, bf16[1,192,384]{2,1,0:T(8,128)(2,1)S(1)}, u32[]{:S(2)}, u32[]{:S(2)}) collective-permute-start(bf16[1,192,384]{2,1,0:T(8,128)(2,1)S(1)} %get-tuple-element.177), channel_id=1, source_target_pairs={{0,16},{1,17},{2,18},{3,19},{4,20},{5,21},{6,22},{7,23},{8,24},{9,... | collective-permute-start | bytes 442376 | tf_op jit(solution)/shard_map/ppermute | solution.py:756
  98.6 2.5 %vp_grad.1 = (bf16[8,48,640]{2,1,0:T(8,128)(2,1)S(1)}, bf16[8,48,640]{2,1,0:T(8,128)(2,1)S(1)}) custom-call(s32[2]{0:T(128)S(1)} %pad_add_fusion.ids, bf16[768,512]{1,0:T(8,128)(2,1)S(1)} %get-tuple-element.183.x0_ref, bf16[768,512]{1,0:T(8,128)(2,1)S(1)} %collective-permute-done.13.x1_ref, bf16[3,384,512]{2,1,0:T(8,128)(2,1)S(1)} %get-tuple-element.174.d0_ref.do_ref, ...), custom_call_target="tpu_custom_call" | custom-call | flops 1950000000 | tf_op jit(solution)/shard_map/vp_grad/pallas_call | solution.py:37
  101.1 1.3 collective-permute-start.21
  102.4 2.7 %collective-permute-done.17.got_ref = bf16[1,192,384]{2,1,0:T(8,128)(2,1)S(1)} collective-permute-done((bf16[1,192,384]{2,1,0:T(8,128)(2,1)S(1)}, bf16[1,192,384]{2,1,0:T(8,128)(2,1)S(1)}, u32[]{:S(2)}, u32[]{:S(2)}) %collective-permute-start.17) | collective-permute-done | bytes 147488 | tf_op jit(solution)/shard_map/ppermute | solution.py:756
  105.6 0.7 add_split.16
  106.4 4.7 %tokens_back.1 = (bf16[2,256,768]{2,1,0:T(8,128)(2,1)}, bf16[256,768]{1,0:T(8,128)(2,1)S(1)}) custom-call(s32[2]{0:T(128)S(1)} %pad_add_fusion.ids, bf16[768,2304]{1,0:T(8,128)(2,1)S(1)} %copy-done, bf16[3,384,512]{2,1,0:T(8,128)(2,1)S(1)} %get-tuple-element.169.ds_ref, bf16[3,384,512]{2,1,0:T(8,128)(2,1)S(1)} %get-tuple-element.174.d0_ref.do_ref, ...), custom_call_target="tpu_custom_call" | custom-call | flops 3900000000 | tf_op jit(solution)/shard_map/tokens_back/pallas_call | solution.py:37
  111.2 0.7 add_split.17
  111.9 0.7 copy-done.20
  112.6 1.2 collective-permute-start.24
  113.9 2.5 %collective-permute-start.23 = (bf16[192,384]{1,0:T(8,128)(2,1)S(1)}, bf16[192,384]{1,0:T(8,128)(2,1)S(1)}, u32[]{:S(2)}, u32[]{:S(2)}) collective-permute-start(bf16[192,384]{1,0:T(8,128)(2,1)S(1)} %add_last.4.mine_ref), channel_id=1, source_target_pairs={{0,1},{1,0},{2,3},{3,2},{4,5},{5,4},{6,7},{7,6},{8,9},{9,8},{10,11... | collective-permute-start | bytes 442376 | tf_op jit(solution)/shard_map/ppermute | solution.py:751
  116.4 0.7 add_split.18
  117.1 0.7 copy-done.22
  117.7 1.2 collective-permute-start.25
  119.6 3.0 %collective-permute-start.26 = (bf16[1,48,1920]{2,1,0:T(8,128)(2,1)S(1)}, bf16[1,48,1920]{2,1,0:T(8,128)(2,1)S(1)}, u32[]{:S(2)}, u32[]{:S(2)}) collective-permute-start(bf16[1,48,1920]{2,1,0:T(8,128)(2,1)S(1)} %get-tuple-element.212), channel_id=1, source_target_pairs={{0,16},{1,9},{2,18},{3,11},{4,20},{5,13},{6,22},{7,15},{8,24},{9,1... | collective-permute-start | bytes 552968 | tf_op jit(solution)/shard_map/ppermute | solution.py:756
  122.6 1.4 join.2
  124.7 0.7 collective-permute-start.27
  126.1 1.8 %collective-permute-start.28 = (bf16[2,48,640]{2,1,0:T(8,128)(2,1)S(1)}, bf16[2,48,640]{2,1,0:T(8,128)(2,1)S(1)}, u32[]{:S(2)}, u32[]{:S(2)}) collective-permute-start(bf16[2,48,640]{2,1,0:T(8,128)(2,1)S(1)} %get-tuple-element.219), channel_id=1, source_target_pairs={{0,8},{1,17},{2,10},{3,19},{4,12},{5,21},{6,14},{7,23},{8,0},{9,25... | collective-permute-start | bytes 368648 | tf_op jit(solution)/shard_map/ppermute | solution.py:756
  128.4 0.9 collective-permute-start.29
  129.3 1.0 bitcast_dynamic-update-slice_fusion.1
  130.4 3.2 %collective-permute-done.27.got_ref = bf16[2,48,896]{2,1,0:T(8,128)(2,1)S(1)} collective-permute-done((bf16[2,48,896]{2,1,0:T(8,128)(2,1)S(1)}, bf16[2,48,896]{2,1,0:T(8,128)(2,1)S(1)}, u32[]{:S(2)}, u32[]{:S(2)}) %collective-permute-start.27) | collective-permute-done | bytes 172064 | tf_op jit(solution)/shard_map/ppermute | solution.py:756
  134.2 1.0 collective-permute-done.28.got_ref
  136.3 1.4 join.3
  139.8 2.8 %collective-permute-start.33 = (bf16[48,640]{1,0:T(8,128)(2,1)S(1)}, bf16[48,640]{1,0:T(8,128)(2,1)S(1)}, u32[]{:S(2)}, u32[]{:S(2)}) collective-permute-start(bf16[48,640]{1,0:T(8,128)(2,1)S(1)} %add_last.7.vo_mine), channel_id=1, source_target_pairs={{0,1},{1,0},{2,3},{3,2},{4,5},{5,4},{6,7},{7,6},{8,9},{9,8},{10,11... | collective-permute-start | bytes 184328 | tf_op jit(solution)/shard_map/ppermute | solution.py:751
  142.7 0.8 collective-permute-done.33.vo_other
  143.5 1.4 join_last.1
  (134 shorter events, 10.9 us)
Async XLA Ops:
  0.6 3.2 %collective-permute-start = (bf16[2,256,768]{2,1,0:T(8,128)(2,1)}, bf16[2,256,768]{2,1,0:T(8,128)(2,1)S(1)}, u32[]{:S(2)}, u32[]{:S(2)}) collective-permute-start(bf16[2,256,768]{2,1,0:T(8,128)(2,1)} %own_ref.3), channel_id=1, source_target_pairs={{0,1},{1,0},{2,3},{3,2},{4,5},{5,4},{6,7},{7,6},{8,9},{9,8},{10,11... | collective-permute-start | bytes 2359304 | tf_op jit(solution)/shard_map/ppermute | solution.py:751
  0.8 21.3 %collective-permute-start.1 = (bf16[2,256,768]{2,1,0:T(8,128)(2,1)}, bf16[2,256,768]{2,1,0:T(8,128)(2,1)S(1)}, u32[]{:S(2)}, u32[]{:S(2)}) collective-permute-start(bf16[2,256,768]{2,1,0:T(8,128)(2,1)} %cown_ref.1), channel_id=1, source_target_pairs={{0,1},{1,0},{2,3},{3,2},{4,5},{5,4},{6,7},{7,6},{8,9},{9,8},{10,11... | collective-permute-start | bytes 2359304 | tf_op jit(solution)/shard_map/ppermute | solution.py:751
  4.2 17.9 %slice-start = ((s8[4718592]{0:T(1024)(128)(4,1)}), s8[4194304]{0:T(1024)(128)(4,1)S(1)}, s32[]{:S(2)}) async-start(s8[4718592]{0:T(1024)(128)(4,1)} %bitcast.6), calls=%async_computation | async-start | bytes 8388608
  4.2 17.9 %slice-start.2 = ((s8[4718592]{0:T(1024)(128)(4,1)}), s8[4194304]{0:T(1024)(128)(4,1)S(1)}, s32[]{:S(2)}) async-start(s8[4718592]{0:T(1024)(128)(4,1)} %bitcast.8), calls=%async_computation.2 | async-start | bytes 8388608
  8.0 14.0 %copy-start.24 = (bf16[512,2304]{1,0:T(8,128)(2,1)}, bf16[512,2304]{1,0:T(8,128)(2,1)S(1)}, u32[]{:S(2)}) copy-start(bf16[512,2304]{1,0:T(8,128)(2,1)S(1)} %get-tuple-element.134.k_ref.v_ref) | copy-start | bytes 7077892
  8.1 14.0 %slice-start.1 = ((s8[4718592]{0:T(1024)(128)(4,1)}), s8[524288]{0:T(1024)(128)(4,1)S(1)}, s32[]{:S(2)}) async-start(s8[4718592]{0:T(1024)(128)(4,1)} %bitcast.6), calls=%async_computation.1 | async-start | bytes 1048576
  8.1 14.0 %slice-start.3 = ((s8[4718592]{0:T(1024)(128)(4,1)}), s8[524288]{0:T(1024)(128)(4,1)S(1)}, s32[]{:S(2)}) async-start(s8[4718592]{0:T(1024)(128)(4,1)} %bitcast.8), calls=%async_computation.3 | async-start | bytes 1048576
  8.1 14.0 %copy-start.1 = (bf16[768,768]{1,0:T(8,128)(2,1)S(1)}, bf16[768,768]{1,0:T(8,128)(2,1)}, u32[]{:S(2)}) copy-start(bf16[768,768]{1,0:T(8,128)(2,1)} %wo_ref.3) | copy-start | bytes 3538948
  8.1 14.0 %copy-start.3 = (bf16[2,256,768]{2,1,0:T(8,128)(2,1)S(1)}, bf16[2,256,768]{2,1,0:T(8,128)(2,1)}, u32[]{:S(2)}) copy-start(bf16[2,256,768]{2,1,0:T(8,128)(2,1)} %cown_ref.1) | copy-start | bytes 2359300
  8.1 14.0 %copy-start.8 = (bf16[3072]{0:T(1024)(128)(2,1)S(1)}, bf16[3072]{0:T(1024)(128)(2,1)}, u32[]{:S(2)}) copy-start(bf16[3072]{0:T(1024)(128)(2,1)} %bi_ref.1) | copy-start | bytes 18436
  8.1 14.0 %copy-start.9 = (bf16[768]{0:T(1024)(128)(2,1)S(1)}, bf16[768]{0:T(1024)(128)(2,1)}, u32[]{:S(2)}) copy-start(bf16[768]{0:T(1024)(128)(2,1)} %bo_ref.1) | copy-start | bytes 4612
  8.2 14.0 %copy-start.10 = (bf16[768]{0:T(1024)(128)(2,1)S(1)}, bf16[768]{0:T(1024)(128)(2,1)}, u32[]{:S(2)}) copy-start(bf16[768]{0:T(1024)(128)(2,1)} %s1_ref.1) | copy-start | bytes 4612
  8.2 14.0 %copy-start.11 = (bf16[768]{0:T(1024)(128)(2,1)S(1)}, bf16[768]{0:T(1024)(128)(2,1)}, u32[]{:S(2)}) copy-start(bf16[768]{0:T(1024)(128)(2,1)} %bd_ref.1) | copy-start | bytes 4612
  8.2 14.0 %copy-start.12 = (bf16[768]{0:T(1024)(128)(2,1)S(1)}, bf16[768]{0:T(1024)(128)(2,1)}, u32[]{:S(2)}) copy-start(bf16[768]{0:T(1024)(128)(2,1)} %g2_ref.1) | copy-start | bytes 4612
  8.2 14.0 %copy-start.13 = (bf16[768]{0:T(1024)(128)(2,1)S(1)}, bf16[768]{0:T(1024)(128)(2,1)}, u32[]{:S(2)}) copy-start(bf16[768]{0:T(1024)(128)(2,1)} %s2_ref.1) | copy-start | bytes 4612
  8.2 14.0 %copy-start.14 = (bf16[768]{0:T(1024)(128)(2,1)S(1)}, bf16[768]{0:T(1024)(128)(2,1)}, u32[]{:S(2)}) copy-start(bf16[768]{0:T(1024)(128)(2,1)} %g1_ref.3) | copy-start | bytes 4612
  34.8 6.3 %collective-permute-start.3 = (bf16[3072,512]{1,0:T(8,128)(2,1)S(1)}, bf16[3072,512]{1,0:T(8,128)(2,1)S(1)}, u32[]{:S(2)}, u32[]{:S(2)}) collective-permute-start(bf16[3072,512]{1,0:T(8,128)(2,1)S(1)} %get-tuple-element.145.a0_ref), channel_id=1, source_target_pairs={{0,1},{1,0},{2,3},{3,2},{4,5},{5,4},{6,7},{7,6},{8,9},{9,8},{10,11... | collective-permute-start | bytes 9437192 | tf_op jit(solution)/shard_map/ppermute | solution.py:751
  34.8 6.3 %collective-permute-start.4 = (bf16[512,384]{1,0:T(8,128)(2,1)S(1)}, bf16[512,384]{1,0:T(8,128)(2,1)S(1)}, u32[]{:S(2)}, u32[]{:S(2)}) collective-permute-start(bf16[512,384]{1,0:T(8,128)(2,1)S(1)} %get-tuple-element.146), channel_id=1, source_target_pairs={{0,1},{1,0},{2,3},{3,2},{4,5},{5,4},{6,7},{7,6},{8,9},{9,8},{10,11... | collective-permute-start | bytes 1179656 | tf_op jit(solution)/shard_map/ppermute | solution.py:751
  40.4 15.6 %collective-permute-start.6 = (bf16[512,1536]{1,0:T(8,128)(2,1)S(1)}, bf16[512,1536]{1,0:T(8,128)(2,1)S(1)}, u32[]{:S(2)}, u32[]{:S(2)}) collective-permute-start(bf16[512,1536]{1,0:T(8,128)(2,1)S(1)} %get-tuple-element.149.dsend_ref), channel_id=1, source_target_pairs={{0,1},{1,0},{2,3},{3,2},{4,5},{5,4},{6,7},{7,6},{8,9},{9,8},{10,11... | collective-permute-start | bytes 4718600 | tf_op jit(solution)/shard_map/ppermute | solution.py:751
  40.6 15.5 %collective-permute-start.7 = (bf16[768,512]{1,0:T(8,128)(2,1)S(1)}, bf16[768,512]{1,0:T(8,128)(2,1)S(1)}, u32[]{:S(2)}, u32[]{:S(2)}) collective-permute-start(bf16[768,512]{1,0:T(8,128)(2,1)S(1)} %get-tuple-element.138.at_ref.a0_ref), channel_id=1, source_target_pairs={{0,1},{1,0},{2,3},{3,2},{4,5},{5,4},{6,7},{7,6},{8,9},{9,8},{10,11... | collective-permute-start | bytes 2359304 | tf_op jit(solution)/shard_map/ppermute | solution.py:751
  41.0 15.0 %collective-permute-start.5 = (bf16[768,512]{1,0:T(8,128)(2,1)S(1)}, bf16[768,512]{1,0:T(8,128)(2,1)S(1)}, u32[]{:S(2)}, u32[]{:S(2)}) collective-permute-start(bf16[768,512]{1,0:T(8,128)(2,1)S(1)} %get-tuple-element.155.f0_ref), channel_id=1, source_target_pairs={{0,1},{1,0},{2,3},{3,2},{4,5},{5,4},{6,7},{7,6},{8,9},{9,8},{10,11... | collective-permute-start | bytes 2359304 | tf_op jit(solution)/shard_map/ppermute | solution.py:751
  46.3 16.8 %collective-permute-start.9 = (bf16[8,192,384]{2,1,0:T(8,128)(2,1)S(1)}, bf16[8,192,384]{2,1,0:T(8,128)(2,1)S(1)}, u32[]{:S(2)}, u32[]{:S(2)}) collective-permute-start(bf16[8,192,384]{2,1,0:T(8,128)(2,1)S(1)} %get-tuple-element.147), channel_id=1, source_target_pairs={{0,2},{1,5},{2,0},{3,7},{4,6},{5,1},{6,4},{7,3},{8,10},{9,13},{10,... | collective-permute-start | bytes 3538952 | tf_op jit(solution)/shard_map/ppermute | solution.py:756
  55.6 1.8 %collective-permute-start.8 = (bf16[512,384]{1,0:T(8,128)(2,1)S(1)}, bf16[512,384]{1,0:T(8,128)(2,1)S(1)}, u32[]{:S(2)}, u32[]{:S(2)}) collective-permute-start(bf16[512,384]{1,0:T(8,128)(2,1)S(1)} %get-tuple-element.157), channel_id=1, source_target_pairs={{0,1},{1,0},{2,3},{3,2},{4,5},{5,4},{6,7},{7,6},{8,9},{9,8},{10,11... | collective-permute-start | bytes 1179656 | tf_op jit(solution)/shard_map/ppermute | solution.py:751
  64.0 25.8 %collective-permute-start.12 = (bf16[8,48,1920]{2,1,0:T(8,128)(2,1)S(1)}, bf16[8,48,1920]{2,1,0:T(8,128)(2,1)S(1)}, u32[]{:S(2)}, u32[]{:S(2)}) collective-permute-start(bf16[8,48,1920]{2,1,0:T(8,128)(2,1)S(1)} %get-tuple-element.180), channel_id=1, source_target_pairs={{0,2},{1,5},{2,0},{3,7},{4,6},{5,1},{6,4},{7,3},{8,10},{9,13},{10,... | collective-permute-start | bytes 4423688 | tf_op jit(solution)/shard_map/ppermute | solution.py:756
  65.3 13.6 %collective-permute-start.10 = (bf16[4,192,384]{2,1,0:T(8,128)(2,1)S(1)}, bf16[4,192,384]{2,1,0:T(8,128)(2,1)S(1)}, u32[]{:S(2)}, u32[]{:S(2)}) collective-permute-start(bf16[4,192,384]{2,1,0:T(8,128)(2,1)S(1)} %get-tuple-element.161), channel_id=1, source_target_pairs={{0,8},{1,9},{2,10},{3,11},{4,12},{5,13},{6,14},{7,15},{8,0},{9,1},... | collective-permute-start | bytes 1769480 | tf_op jit(solution)/shard_map/ppermute | solution.py:756
  73.5 18.8 %collective-permute-start.14 = (bf16[3,384,512]{2,1,0:T(8,128)(2,1)S(1)}, bf16[3,384,512]{2,1,0:T(8,128)(2,1)S(1)}, u32[]{:S(2)}, u32[]{:S(2)}) collective-permute-start(bf16[3,384,512]{2,1,0:T(8,128)(2,1)S(1)} %get-tuple-element.169.ds_ref), channel_id=1, source_target_pairs={{0,1},{1,0},{2,3},{3,2},{4,5},{5,4},{6,7},{7,6},{8,9},{9,8},{10,11... | collective-permute-start | bytes 3538952 | tf_op jit(solution)/shard_map/ppermute | solution.py:751
  75.0 17.3 %collective-permute-start.13 = (bf16[768,512]{1,0:T(8,128)(2,1)S(1)}, bf16[768,512]{1,0:T(8,128)(2,1)S(1)}, u32[]{:S(2)}, u32[]{:S(2)}) collective-permute-start(bf16[768,512]{1,0:T(8,128)(2,1)S(1)} %get-tuple-element.183.x0_ref), channel_id=1, source_target_pairs={{0,1},{1,0},{2,3},{3,2},{4,5},{5,4},{6,7},{7,6},{8,9},{9,8},{10,11... | collective-permute-start | bytes 2359304 | tf_op jit(solution)/shard_map/ppermute | solution.py:751
  79.6 9.6 %collective-permute-start.11 = (bf16[2,192,384]{2,1,0:T(8,128)(2,1)S(1)}, bf16[2,192,384]{2,1,0:T(8,128)(2,1)S(1)}, u32[]{:S(2)}, u32[]{:S(2)}) collective-permute-start(bf16[2,192,384]{2,1,0:T(8,128)(2,1)S(1)} %get-tuple-element.172), channel_id=1, source_target_pairs={{0,4},{1,3},{2,6},{3,1},{4,0},{5,7},{6,2},{7,5},{8,12},{9,11},{10,... | collective-permute-start | bytes 884744 | tf_op jit(solution)/shard_map/ppermute | solution.py:756
  90.8 14.8 %collective-permute-start.18 = (bf16[4,48,1920]{2,1,0:T(8,128)(2,1)S(1)}, bf16[4,48,1920]{2,1,0:T(8,128)(2,1)S(1)}, u32[]{:S(2)}, u32[]{:S(2)}) collective-permute-start(bf16[4,48,1920]{2,1,0:T(8,128)(2,1)S(1)} %get-tuple-element.181), channel_id=1, source_target_pairs={{0,4},{1,3},{2,6},{3,1},{4,0},{5,7},{6,2},{7,5},{8,12},{9,11},{10,... | collective-permute-start | bytes 2211848 | tf_op jit(solution)/shard_map/ppermute | solution.py:756
  90.9 7.7 %collective-permute-start.15 = (bf16[256,384]{1,0:T(8,128)(2,1)S(1)}, bf16[256,384]{1,0:T(8,128)(2,1)S(1)}, u32[]{:S(2)}, u32[]{:S(2)}) collective-permute-start(bf16[256,384]{1,0:T(8,128)(2,1)S(1)} %get-tuple-element.192), channel_id=1, source_target_pairs={{0,1},{1,0},{2,3},{3,2},{4,5},{5,4},{6,7},{7,6},{8,9},{9,8},{10,11... | collective-permute-start | bytes 589832 | tf_op jit(solution)/shard_map/ppermute | solution.py:751
  92.3 6.3 %collective-permute-start.16 = (bf16[256,384]{1,0:T(8,128)(2,1)S(1)}, bf16[256,384]{1,0:T(8,128)(2,1)S(1)}, u32[]{:S(2)}, u32[]{:S(2)}) collective-permute-start(bf16[256,384]{1,0:T(8,128)(2,1)S(1)} %get-tuple-element.194), channel_id=1, source_target_pairs={{0,1},{1,0},{2,3},{3,2},{4,5},{5,4},{6,7},{7,6},{8,9},{9,8},{10,11... | collective-permute-start | bytes 589832 | tf_op jit(solution)/shard_map/ppermute | solution.py:751
  96.0 15.2 %collective-permute-start.20 = (bf16[8,48,896]{2,1,0:T(8,128)(2,1)S(1)}, bf16[8,48,896]{2,1,0:T(8,128)(2,1)S(1)}, u32[]{:S(2)}, u32[]{:S(2)}) collective-permute-start(bf16[8,48,896]{2,1,0:T(8,128)(2,1)S(1)} %get-tuple-element.189), channel_id=1, source_target_pairs={{0,2},{1,5},{2,0},{3,7},{4,6},{5,1},{6,4},{7,3},{8,10},{9,13},{10,... | collective-permute-start | bytes 2064392 | tf_op jit(solution)/shard_map/ppermute | solution.py:756
  96.3 8.7 %collective-permute-start.17 = (bf16[1,192,384]{2,1,0:T(8,128)(2,1)S(1)}, bf16[1,192,384]{2,1,0:T(8,128)(2,1)S(1)}, u32[]{:S(2)}, u32[]{:S(2)}) collective-permute-start(bf16[1,192,384]{2,1,0:T(8,128)(2,1)S(1)} %get-tuple-element.177), channel_id=1, source_target_pairs={{0,16},{1,17},{2,18},{3,19},{4,20},{5,21},{6,22},{7,23},{8,24},{9,... | collective-permute-start | bytes 442376 | tf_op jit(solution)/shard_map/ppermute | solution.py:756
  101.1 15.3 %collective-permute-start.21 = (bf16[8,48,640]{2,1,0:T(8,128)(2,1)S(1)}, bf16[8,48,640]{2,1,0:T(8,128)(2,1)S(1)}, u32[]{:S(2)}, u32[]{:S(2)}) collective-permute-start(bf16[8,48,640]{2,1,0:T(8,128)(2,1)S(1)} %get-tuple-element.195), channel_id=1, source_target_pairs={{0,2},{1,5},{2,0},{3,7},{4,6},{5,1},{6,4},{7,3},{8,10},{9,13},{10,... | collective-permute-start | bytes 1474568 | tf_op jit(solution)/shard_map/ppermute | solution.py:756
  106.4 12.6 %collective-permute-start.22 = (bf16[2,48,1920]{2,1,0:T(8,128)(2,1)S(1)}, bf16[2,48,1920]{2,1,0:T(8,128)(2,1)S(1)}, u32[]{:S(2)}, u32[]{:S(2)}) collective-permute-start(bf16[2,48,1920]{2,1,0:T(8,128)(2,1)S(1)} %get-tuple-element.200), channel_id=1, source_target_pairs={{0,8},{1,17},{2,10},{3,19},{4,12},{5,21},{6,14},{7,23},{8,0},{9,25... | collective-permute-start | bytes 1105928 | tf_op jit(solution)/shard_map/ppermute | solution.py:756
  112.6 11.4 %collective-permute-start.24 = (bf16[4,48,896]{2,1,0:T(8,128)(2,1)S(1)}, bf16[4,48,896]{2,1,0:T(8,128)(2,1)S(1)}, u32[]{:S(2)}, u32[]{:S(2)}) collective-permute-start(bf16[4,48,896]{2,1,0:T(8,128)(2,1)S(1)} %get-tuple-element.206), channel_id=1, source_target_pairs={{0,4},{1,3},{2,6},{3,1},{4,0},{5,7},{6,2},{7,5},{8,12},{9,11},{10,... | collective-permute-start | bytes 1032200 | tf_op jit(solution)/shard_map/ppermute | solution.py:756
  113.9 5.8 %collective-permute-start.23 = (bf16[192,384]{1,0:T(8,128)(2,1)S(1)}, bf16[192,384]{1,0:T(8,128)(2,1)S(1)}, u32[]{:S(2)}, u32[]{:S(2)}) collective-permute-start(bf16[192,384]{1,0:T(8,128)(2,1)S(1)} %add_last.4.mine_ref), channel_id=1, source_target_pairs={{0,1},{1,0},{2,3},{3,2},{4,5},{5,4},{6,7},{7,6},{8,9},{9,8},{10,11... | collective-permute-start | bytes 442376 | tf_op jit(solution)/shard_map/ppermute | solution.py:751
  116.3 13.0 %collective-permute-start.2 = (bf16[256,768]{1,0:T(8,128)(2,1)S(1)}, bf16[256,768]{1,0:T(8,128)(2,1)}, u32[]{:S(2)}, u32[]{:S(2)}) collective-permute-start(bf16[256,768]{1,0:T(8,128)(2,1)S(1)} %get-tuple-element.140), channel_id=1, source_target_pairs={{0,1},{1,0},{2,3},{3,2},{4,5},{5,4},{6,7},{7,6},{8,9},{9,8},{10,11... | collective-permute-start | bytes 1179656 | tf_op jit(solution)/shard_map/ppermute | solution.py:751
  117.7 7.7 %collective-permute-start.25 = (bf16[4,48,640]{2,1,0:T(8,128)(2,1)S(1)}, bf16[4,48,640]{2,1,0:T(8,128)(2,1)S(1)}, u32[]{:S(2)}, u32[]{:S(2)}) collective-permute-start(bf16[4,48,640]{2,1,0:T(8,128)(2,1)S(1)} %get-tuple-element.209), channel_id=1, source_target_pairs={{0,4},{1,3},{2,6},{3,1},{4,0},{5,7},{6,2},{7,5},{8,12},{9,11},{10,... | collective-permute-start | bytes 737288 | tf_op jit(solution)/shard_map/ppermute | solution.py:756
  119.0 23.7 %collective-permute-start.19 = (bf16[256,768]{1,0:T(8,128)(2,1)S(1)}, bf16[256,768]{1,0:T(8,128)(2,1)S(1)}, u32[]{:S(2)}, u32[]{:S(2)}) collective-permute-start(bf16[256,768]{1,0:T(8,128)(2,1)S(1)} %get-tuple-element.203), channel_id=1, source_target_pairs={{0,1},{1,0},{2,3},{3,2},{4,5},{5,4},{6,7},{7,6},{8,9},{9,8},{10,11... | collective-permute-start | bytes 1179656 | tf_op jit(solution)/shard_map/ppermute | solution.py:751
  119.6 8.2 %collective-permute-start.26 = (bf16[1,48,1920]{2,1,0:T(8,128)(2,1)S(1)}, bf16[1,48,1920]{2,1,0:T(8,128)(2,1)S(1)}, u32[]{:S(2)}, u32[]{:S(2)}) collective-permute-start(bf16[1,48,1920]{2,1,0:T(8,128)(2,1)S(1)} %get-tuple-element.212), channel_id=1, source_target_pairs={{0,16},{1,9},{2,18},{3,11},{4,20},{5,13},{6,22},{7,15},{8,24},{9,1... | collective-permute-start | bytes 552968 | tf_op jit(solution)/shard_map/ppermute | solution.py:756
  124.7 8.8 %collective-permute-start.27 = (bf16[2,48,896]{2,1,0:T(8,128)(2,1)S(1)}, bf16[2,48,896]{2,1,0:T(8,128)(2,1)S(1)}, u32[]{:S(2)}, u32[]{:S(2)}) collective-permute-start(bf16[2,48,896]{2,1,0:T(8,128)(2,1)S(1)} %get-tuple-element.216), channel_id=1, source_target_pairs={{0,8},{1,17},{2,10},{3,19},{4,12},{5,21},{6,14},{7,23},{8,0},{9,25... | collective-permute-start | bytes 516104 | tf_op jit(solution)/shard_map/ppermute | solution.py:756
  126.1 9.1 %collective-permute-start.28 = (bf16[2,48,640]{2,1,0:T(8,128)(2,1)S(1)}, bf16[2,48,640]{2,1,0:T(8,128)(2,1)S(1)}, u32[]{:S(2)}, u32[]{:S(2)}) collective-permute-start(bf16[2,48,640]{2,1,0:T(8,128)(2,1)S(1)} %get-tuple-element.219), channel_id=1, source_target_pairs={{0,8},{1,17},{2,10},{3,19},{4,12},{5,21},{6,14},{7,23},{8,0},{9,25... | collective-permute-start | bytes 368648 | tf_op jit(solution)/shard_map/ppermute | solution.py:756
  128.4 7.9 %collective-permute-start.29 = (bf16[48,1920]{1,0:T(8,128)(2,1)S(1)}, bf16[48,1920]{1,0:T(8,128)(2,1)S(1)}, u32[]{:S(2)}, u32[]{:S(2)}) collective-permute-start(bf16[48,1920]{1,0:T(8,128)(2,1)S(1)} %add_last.5.mine_ref), channel_id=1, source_target_pairs={{0,1},{1,0},{2,3},{3,2},{4,5},{5,4},{6,7},{7,6},{8,9},{9,8},{10,11... | collective-permute-start | bytes 552968 | tf_op jit(solution)/shard_map/ppermute | solution.py:751
  134.1 4.3 %collective-permute-start.30 = (bf16[1,48,896]{2,1,0:T(8,128)(2,1)S(1)}, bf16[1,48,896]{2,1,0:T(8,128)(2,1)S(1)}, u32[]{:S(2)}, u32[]{:S(2)}) collective-permute-start(bf16[1,48,896]{2,1,0:T(8,128)(2,1)S(1)} %get-tuple-element.224), channel_id=1, source_target_pairs={{0,16},{1,9},{2,18},{3,11},{4,20},{5,13},{6,22},{7,15},{8,24},{9,1... | collective-permute-start | bytes 258056 | tf_op jit(solution)/shard_map/ppermute | solution.py:756
  135.8 3.5 %collective-permute-start.32 = (bf16[1,48,640]{2,1,0:T(8,128)(2,1)S(1)}, bf16[1,48,640]{2,1,0:T(8,128)(2,1)S(1)}, u32[]{:S(2)}, u32[]{:S(2)}) collective-permute-start(bf16[1,48,640]{2,1,0:T(8,128)(2,1)S(1)} %get-tuple-element.227), channel_id=1, source_target_pairs={{0,16},{1,9},{2,18},{3,11},{4,20},{5,13},{6,22},{7,15},{8,24},{9,1... | collective-permute-start | bytes 184328 | tf_op jit(solution)/shard_map/ppermute | solution.py:756
  139.0 4.5 %collective-permute-start.31 = (bf16[48,896]{1,0:T(8,128)(2,1)S(1)}, bf16[48,896]{1,0:T(8,128)(2,1)S(1)}, u32[]{:S(2)}, u32[]{:S(2)}) collective-permute-start(bf16[48,896]{1,0:T(8,128)(2,1)S(1)} %add_last.6.qk_mine), channel_id=1, source_target_pairs={{0,1},{1,0},{2,3},{3,2},{4,5},{5,4},{6,7},{7,6},{8,9},{9,8},{10,11... | collective-permute-start | bytes 258056 | tf_op jit(solution)/shard_map/ppermute | solution.py:751
  139.8 3.7 %collective-permute-start.33 = (bf16[48,640]{1,0:T(8,128)(2,1)S(1)}, bf16[48,640]{1,0:T(8,128)(2,1)S(1)}, u32[]{:S(2)}, u32[]{:S(2)}) collective-permute-start(bf16[48,640]{1,0:T(8,128)(2,1)S(1)} %add_last.7.vo_mine), channel_id=1, source_target_pairs={{0,1},{1,0},{2,3},{3,2},{4,5},{5,4},{6,7},{7,6},{8,9},{9,8},{10,11... | collective-permute-start | bytes 184328 | tf_op jit(solution)/shard_map/ppermute | solution.py:751
  (24 other events, 101.9 us)

commit v5 on v4

--- a/solution.py
+++ b/solution.py
@@ -27,6 +27,14 @@
 
 def wide(ref):
     return ref[...].astype(F32).reshape(1, ref.shape[0])
+
+
+def beside(*values):
+    return jnp.concatenate(values, 1)
+
+
+def below(*values):
+    return jnp.concatenate(values, 0)
 
 
 def whole(shape):
@@ -353,7 +361,7 @@
 def hidden_back(ids, dsec, w_down, slope):
     rows, width = dsec.shape
     ff = w_down.shape[0]
-    block = 768
+    block = 1536
     steps = ff // block
     s = steps // 2
     at = lambda i, ids: jnp.where(ids[1] == 0, (i + s) % steps, i)
@@ -377,7 +385,7 @@
 def first_kernel(ids, dsend_ref, down_ref, wsend_ref, wown_ref, dres_ref, norm_ref, rstd_ref, g1_ref, wo_ref,
                  res_ref, branch_ref, send_ref, datt_ref, rows_ref, acc):
     step = pl.program_id(0)
-    part = mm_nt(dsend_ref[...], wsend_ref[...]) + mm_nt(down_ref[...], wown_ref[...])
+    part = mm_nt(beside(dsend_ref[...], down_ref[...]), beside(wsend_ref[...], wown_ref[...]))
 
     @pl.when(step == 0)
     def _():
@@ -410,7 +418,7 @@
 def first_back(ids, dsend, down, w_in, dres, norm, rstd, g1, w_out):
     rows, width = dres.shape
     ff = w_in.shape[1]
-    block = 512
+    block = 768
     s = ff // block // 2
     mat = whole((rows, width))
     return call(
@@ -517,12 +525,12 @@
     width = w_ref.shape[1] // 3
     side = width // 2
     half = keep_ref.shape[1]
-    acc = None
+    left, right = [], []
     for h, ref in ((1 - ids[1], ds_ref), (ids[1], do_ref)):
         for s in range(3):
-            at = pl.multiple_of(s * width + h * side, 128)
-            part = mm(w_ref[:, pl.ds(at, side)], ref[s])
-            acc = part if acc is None else acc + part
+            left.append(w_ref[:, pl.ds(pl.multiple_of(s * width + h * side, 128), side)])
+            right.append(ref[s])
+    acc = mm(beside(*left), below(*right))
     out = (dres_ref[...] + acc.T).astype(BF16)
     keep_ref[0] = out[:half, :]
     give_ref[...] = out[half:, :]
@@ -571,7 +579,7 @@
 def down_kernel(n, bits, ids, a0_ref, a1_ref, b0_ref, b1_ref, send_ref, keep_ref):
     places = n // pl.num_programs(0)
     r, w = keep_ref.shape[1:]
-    acc = mm(a0_ref[...], b0_ref[...]) + mm(a1_ref[...], b1_ref[...])
+    acc = mm(beside(a0_ref[...], a1_ref[...]), below(b0_ref[...], b1_ref[...]))
     for k in range(places):
         p = pl.program_id(0) * places + k
         put(ids, bits, p, slice(0, w), acc[k * r : k * r + r, :].astype(BF16), send_ref, keep_ref)
@@ -599,14 +607,14 @@
 
     @pl.when(step < last)
     def _():
-        acc = mm(f0_ref[...], h0_ref[...]) + mm(f1_ref[...], h1_ref[...])
+        acc = mm(beside(f0_ref[...], f1_ref[...]), below(h0_ref[...], h1_ref[...]))
         lanes = pl.ds(pl.multiple_of(step * w, 128), w)
         for p in range(n):
             put(ids, bits, p, lanes, acc[p * r : p * r + r, :].astype(BF16), send_ref, keep_ref)
 
     @pl.when(step == last)
     def _():
-        acc = mm(a0_ref[...], c0_ref[...]) + mm(a1_ref[...], c1_ref[...])
+        acc = mm(beside(a0_ref[...], a1_ref[...]), below(c0_ref[...], c1_ref[...]))
         lanes = slice(keep_ref.shape[2] - acc.shape[1], keep_ref.shape[2])
         for p in range(n):
             put(ids, bits, p, lanes, acc[p * r : p * r + r, :].astype(BF16), send_ref, keep_ref)
@@ -649,10 +657,9 @@
         for i in range(3):
             at = pl.multiple_of(who * side, 128)
             qkv_ref[i : i + 1, pl.ds(at, side)] = ref[8 * i : 8 * i + 1, :]
-    for i in range(2):
-        acc = mm_nt(x0_ref[...], d0_ref[i]) + mm_nt(x1_ref[...], d1_ref[i])
-        for p in range(n):
-            put(ids, bits, p, slice(i * side, i * side + side), acc[p * r : p * r + r, :].astype(BF16), send_ref, keep_ref)
+    acc = mm_nt(beside(x0_ref[...], x1_ref[...]), below(beside(d0_ref[0], d1_ref[0]), beside(d0_ref[1], d1_ref[1])))
+    for p in range(n):
+        put(ids, bits, p, slice(0, 2 * side), acc[p * r : p * r + r, :].astype(BF16), send_ref, keep_ref)
     vectors = (qkv_ref, one_ref, one_ref, one_ref, in_ref, two_ref, two_ref, two_ref)
     index = (None, 2, 0, 1, 0, 2, 0, 1)
     plan, _ = small_plan(n, sizes)
@@ -687,7 +694,7 @@
 def vp_kernel(n, bits, ids, x0_ref, x1_ref, d0_ref, d1_ref, k0_ref, k1_ref, q0_ref, q1_ref, send_ref, keep_ref):
     r = keep_ref.shape[1]
     side = d0_ref.shape[1]
-    acc = mm_nt(x0_ref[...], d0_ref[0]) + mm_nt(x1_ref[...], d1_ref[0])
+    acc = mm_nt(beside(x0_ref[...], x1_ref[...]), beside(d0_ref[0], d1_ref[0]))
     for p in range(n):
         put(ids, bits, p, slice(0, side), acc[p * r : p * r + r, :].astype(BF16), send_ref, keep_ref)
     base = side
@@ -982,8 +989,8 @@
     dp, gk, gq, bias_own = back(own=True)
     small = (3 * width, width, width, width, w_in.shape[1], width, width, width)
     sizes = tuple(s // n for s in small)
+    mid.step()
     down.step()
-    mid.step()
     qk = Exchange(
         chain, n, *chain.run(qk_grad, n, first(order_qk), sizes, xt, xt_other, dp, dp_other,
                              rows_two, rows_one, row_in, bias_send, bias_own), order_qk

time: 146 us -> 145 us (level); the launches traced: 145 us -> 142 us
  Pallas kernels: 93.9 us -> 91.2 us
    pallas_call x32, Pallas kernels: 93.9 us -> 91.2 us  [call(): pl.pallas_call(kernel, grid_spec=pltpu.PrefetchScalarGridSpec(num_scalar_...]
  transfers between devices with their start and end apart: 34 -> 34, of which waited for: 7 -> 8; matrix products, arithmetic and copies ran while one was open for 1% -> 1% of each run, Pallas kernels for 55% -> 54%
where the time goes in v5:
time: 145 us; the launch traced here: 142 us
  Pallas kernels  91.2 us (63%)
  starting transfers between devices  32.5 us (22%)
  waiting for transfers between devices  13.5 us (9%)
  local copies, waits for them, and re-layouts  3.74 us (3%)
  between operations  1.5 us (1%)
    pallas_call x32, Pallas kernels, call(): pl.pallas_call(kernel, grid_spec=pltpu.PrefetchScalarGridSpec(num_scalar_...  91.2 us
    ppermute x16, starting transfers between devices, across(): return lax.ppermute(x, ('pages', 'slab'), pairs)  20.3 us
    ppermute x18, starting transfers between devices, swap(): return lax.ppermute(x, 'slab', [(0, 1), (1, 0)])  12.1 us
    ppermute x16, waiting for transfers between devices, across(): return lax.ppermute(x, ('pages', 'slab'), pairs)  10.7 us
  transfers between devices with their start and end apart: 34, of which 8 were waited for; matrix products, arithmetic and copies ran while one was open for 1% of the time, Pallas kernels for 54%

profile of v5, /device:TPU:1, one launch (start us, length us, event | category | flops | bytes accessed | tf_op | source)
XLA Modules:
  0.0 142.4 jit_solution(16403050349530005296)
XLA Ops:
  1.3 0.7 copy-done.6
  2.0 1.7 %tables.1 = (bf16[512,256]{1,0:T(8,128)(2,1)S(1)}, f32[4,512,128]{2,1,0:T(8,128)S(1)}, f32[4,64,512]{2,1,0:T(8,128)S(1)}, bf16[256,512]{1,0:T(8,128)(2,1)S(1)}, bf16[256,512]{1,0:T(8,128)(2,1)S(1)}) custom-call(s32[2]{0:T(128)S(1)} %pad_add_fusion.ids, s32[2,4,512]{2,1,0:T(4,128)S(1)} %copy-done.6), custom_call_target="tpu_custom_call" | custom-call | flops 1950000000 | tf_op jit(solution)/shard_map/tables/pallas_call | solution.py:45
  4.2 3.8 %project.1 = (bf16[2304,512]{1,0:T(8,128)(2,1)S(1)}, bf16[512,2304]{1,0:T(8,128)(2,1)S(1)}, bf16[768,512]{1,0:T(8,128)(2,1)S(1)}) custom-call(s32[2]{0:T(128)S(1)} %pad_add_fusion.ids, bf16[2,256,768]{2,1,0:T(8,128)(2,1)S(1)} %copy-done.2, bf16[2,256,768]{2,1,0:T(8,128)(2,1)S(1)} %collective-permute-done.other_ref, bf16[768,2304]{1,0:T(8,128)(2,1)S(1)} %copy-done, ...), custom_call_target="tpu_custom_call" | custom-call | flops 3249999872 | tf_op jit(solution)/shard_map/project/pallas_call | solution.py:45
  8.2 13.9 %attend.1 = (bf16[12,512,512]{2,1,0:T(8,128)(2,1)}, bf16[768,512]{1,0:T(8,128)(2,1)S(1)}, f32[6,2,512]{2,1,0:T(2,128)S(1)}, bf16[768,256]{1,0:T(8,128)(2,1)S(1)}, bf16[768,256]{1,0:T(8,128)(2,1)S(1)}) custom-call(s32[2]{0:T(128)S(1)} %pad_add_fusion.ids, s32[2]{0:T(128)S(1)} %copy-done.15, bf16[2304,512]{1,0:T(8,128)(2,1)S(1)} %get-tuple-element.133.qt_ref.vt_ref.kt_ref, ...), custom_call_target="tpu_custom_call" | custom-call | flops 11050000384 | tf_op jit(solution)/shard_map/attend/pallas_call | solution.py:45
  22.2 12.5 %feed.1 = (bf16[768,512]{1,0:T(8,128)(2,1)S(1)}, f32[512,768]{1,0:T(8,128)S(1)}, f32[512,1]{1,0:T(8,128)S(1)}, bf16[512,3072]{1,0:T(8,128)(2,1)S(1)}, bf16[3072,...) custom-call(s32[2]{0:T(128)S(1)} %pad_add_fusion.ids, ...), custom_call_target="tpu_custom_call" | custom-call | flops 9749999616 | tf_op jit(solution)/shard_map/feed/pallas_call | solution.py:45
  35.3 4.4 %hidden_back.1 = (bf16[512,1536]{1,0:T(8,128)(2,1)S(1)}, bf16[512,1536]{1,0:T(8,128)(2,1)S(1)}, f32[1,3072]{1,0:T(1,128)S(1)}) custom-call(s32[2]{0:T(128)S(1)} %pad_add_fusion.ids, bf16[512,768]{1,0:T(8,128)(2,1)S(1)} %get-tuple-element.141.ds_ref.b0_ref, bf16[3072,768]{1,0:T(8,128)(2,1)S(1)} %bitcast.7, bf16[512,3072]{1,0:T(8,128)(2,1)S(1)} %get-tuple-element.142.slope_ref), custom_call_target="tpu_custom_call" | custom-call | flops 3249999872 | tf_op jit(solution)/shard_map/hidden_back/pallas_call | solution.py:45
  41.0 5.0 %down_grad.1 = (bf16[8,192,384]{2,1,0:T(8,128)(2,1)S(1)}, bf16[8,192,384]{2,1,0:T(8,128)(2,1)S(1)}) custom-call(s32[2]{0:T(128)S(1)} %pad_add_fusion.ids, bf16[3072,512]{1,0:T(8,128)(2,1)S(1)} %get-tuple-element.145.a0_ref, bf16[3072,512]{1,0:T(8,128)(2,1)S(1)} %collective-permute-done.3.a1_ref, bf16[512,768]{1,0:T(8,128)(2,1)S(1)} %get-tuple-element.141.ds_ref.b0_ref, ...), custom_call_target="tpu_custom_call" | custom-call | flops 4550000128 | tf_op jit(solution)/shard_map/down_grad/pallas_call | solution.py:45
  46.0 2.4 %collective-permute-start.9 = (bf16[8,192,384]{2,1,0:T(8,128)(2,1)S(1)}, bf16[8,192,384]{2,1,0:T(8,128)(2,1)S(1)}, u32[]{:S(2)}, u32[]{:S(2)}) collective-permute-start(bf16[8,192,384]{2,1,0:T(8,128)(2,1)S(1)} %get-tuple-element.147), channel_id=1, source_target_pairs={{0,2},{1,5},{2,0},{3,7},{4,6},{5,1},{6,4},{7,3},{8,10},{9,13},{10,... | collective-permute-start | bytes 3538952 | tf_op jit(solution)/shard_map/ppermute | solution.py:763
  48.4 6.2 %first_back.1 = (f32[512,768]{1,0:T(8,128)S(1)}, bf16[512,768]{1,0:T(8,128)(2,1)S(1)}, bf16[512,384]{1,0:T(8,128)(2,1)S(1)}, bf16[768,512]{1,0:T(8,128)(2,1)S(1)}, f32[8,768]{1,0:T(8,128)S(1)}) custom-call(s32[2]{0:T(128)S(1)} %pad_add_fusion.ids, bf16[512,1536]{1,0:T(8,128)(2,1)S(1)} %get-tuple-element.149.dsend_ref, ...), custom_call_target="tpu_custom_call" | custom-call | flops 5200000000 | tf_op jit(solution)/shard_map/first_back/pallas_call | solution.py:45
  54.7 0.7 collective-permute-start.8
  55.4 1.3 collective-permute-done.8.c1_ref
  56.7 5.7 %mid_grad.1 = (bf16[8,48,1920]{2,1,0:T(8,128)(2,1)S(1)}, bf16[8,48,1920]{2,1,0:T(8,128)(2,1)S(1)}) custom-call(s32[2]{0:T(128)S(1)} %pad_add_fusion.ids, bf16[768,512]{1,0:T(8,128)(2,1)S(1)} %get-tuple-element.155.f0_ref, bf16[768,512]{1,0:T(8,128)(2,1)S(1)} %collective-permute-done.5.f1_ref, bf16[512,1536]{1,0:T(8,128)(2,1)S(1)} %get-tuple-element.143.down_ref.h0_ref, ...), custom_call_target="tpu_custom_call" | custom-call | flops 3900000000 | tf_op jit(solution)/shard_map/mid_grad/pallas_call | solution.py:45
  62.4 0.9 add_split.12
  63.3 1.5 %collective-permute-start.11 = (bf16[8,48,1920]{2,1,0:T(8,128)(2,1)S(1)}, bf16[8,48,1920]{2,1,0:T(8,128)(2,1)S(1)}, u32[]{:S(2)}, u32[]{:S(2)}) collective-permute-start(bf16[8,48,1920]{2,1,0:T(8,128)(2,1)S(1)} %get-tuple-element.177), channel_id=1, source_target_pairs={{0,2},{1,5},{2,0},{3,7},{4,6},{5,1},{6,4},{7,3},{8,10},{9,13},{10,... | collective-permute-start | bytes 4423688 | tf_op jit(solution)/shard_map/ppermute | solution.py:763
  64.7 1.3 collective-permute-start.10
  66.0 6.9 %attend_back.2 = (bf16[3,384,512]{2,1,0:T(8,128)(2,1)S(1)}, bf16[256,384]{1,0:T(8,128)(2,1)S(1)}, bf16[256,384]{1,0:T(8,128)(2,1)S(1)}, f32[24,384]{1,0:T(8,128)S(1)}) custom-call(s32[2]{0:T(128)S(1)} %pad_add_fusion.ids, bf16[12,512,512]{2,1,0:T(8,128)(2,1)S(1)} %bitcast.11, f32[6,2,512]{2,1,0:T(2,128)S(1)} %get-tuple-element.164.r_ref, ...), custom_call_target="tpu_custom_call" | custom-call | flops 5849999872 | tf_op jit(solution)/shard_map/attend_back/pallas_call | solution.py:45
  72.9 1.8 %collective-permute-start.14 = (bf16[3,384,512]{2,1,0:T(8,128)(2,1)S(1)}, bf16[3,384,512]{2,1,0:T(8,128)(2,1)S(1)}, u32[]{:S(2)}, u32[]{:S(2)}) collective-permute-start(bf16[3,384,512]{2,1,0:T(8,128)(2,1)S(1)} %get-tuple-element.169.ds_ref), channel_id=1, source_target_pairs={{0,1},{1,0},{2,3},{3,2},{4,5},{5,4},{6,7},{7,6},{8,9},{9,8},{10,11... | collective-permute-start | bytes 3538952 | tf_op jit(solution)/shard_map/ppermute | solution.py:758
  74.8 3.3 %collective-permute-done.10.got_ref = bf16[4,192,384]{2,1,0:T(8,128)(2,1)S(1)} collective-permute-done((bf16[4,192,384]{2,1,0:T(8,128)(2,1)S(1)}, bf16[4,192,384]{2,1,0:T(8,128)(2,1)S(1)}, u32[]{:S(2)}, u32[]{:S(2)}) %collective-permute-start.10) | collective-permute-done | bytes 589856 | tf_op jit(solution)/shard_map/ppermute | solution.py:763
  78.1 0.7 add_split.13
  78.8 2.8 %collective-permute-start.12 = (bf16[2,192,384]{2,1,0:T(8,128)(2,1)S(1)}, bf16[2,192,384]{2,1,0:T(8,128)(2,1)S(1)}, u32[]{:S(2)}, u32[]{:S(2)}) collective-permute-start(bf16[2,192,384]{2,1,0:T(8,128)(2,1)S(1)} %get-tuple-element.172), channel_id=1, source_target_pairs={{0,4},{1,3},{2,6},{3,1},{4,0},{5,7},{6,2},{7,5},{8,12},{9,11},{10,... | collective-permute-start | bytes 884744 | tf_op jit(solution)/shard_map/ppermute | solution.py:763
  81.6 6.8 %attend_back.3 = (bf16[3,384,512]{2,1,0:T(8,128)(2,1)S(1)}, bf16[256,384]{1,0:T(8,128)(2,1)S(1)}, bf16[256,384]{1,0:T(8,128)(2,1)S(1)}, f32[24,384]{1,0:T(8,128)S(1)}) custom-call(s32[2]{0:T(128)S(1)} %pad_add_fusion.ids, bf16[12,512,512]{2,1,0:T(8,128)(2,1)S(1)} %bitcast.11, f32[6,2,512]{2,1,0:T(2,128)S(1)} %get-tuple-element.164.r_ref, ...), custom_call_target="tpu_custom_call" | custom-call | flops 5849999872 | tf_op jit(solution)/shard_map/attend_back/pallas_call | solution.py:45
  88.4 0.9 add_split.14
  89.4 1.7 %collective-permute-start.15 = (bf16[256,384]{1,0:T(8,128)(2,1)S(1)}, bf16[256,384]{1,0:T(8,128)(2,1)S(1)}, u32[]{:S(2)}, u32[]{:S(2)}) collective-permute-start(bf16[256,384]{1,0:T(8,128)(2,1)S(1)} %get-tuple-element.192), channel_id=1, source_target_pairs={{0,1},{1,0},{2,3},{3,2},{4,5},{5,4},{6,7},{7,6},{8,9},{9,8},{10,11... | collective-permute-start | bytes 589832 | tf_op jit(solution)/shard_map/ppermute | solution.py:758
  91.7 2.8 %qk_grad.1 = (bf16[8,48,896]{2,1,0:T(8,128)(2,1)S(1)}, bf16[8,48,896]{2,1,0:T(8,128)(2,1)S(1)}) custom-call(s32[2]{0:T(128)S(1)} %pad_add_fusion.ids, bf16[768,512]{1,0:T(8,128)(2,1)S(1)} %get-tuple-element.183.x0_ref, bf16[768,512]{1,0:T(8,128)(2,1)S(1)} %collective-permute-done.13.x1_ref, bf16[3,384,512]{2,1,0:T(8,128)(2,1)S(1)} %get-tuple-element.174.d0_ref.do_ref, ...), custom_call_target="tpu_custom_call" | custom-call | flops 2600000000 | tf_op jit(solution)/shard_map/qk_grad/pallas_call | solution.py:45
  94.7 2.4 %collective-permute-start.17 = (bf16[1,192,384]{2,1,0:T(8,128)(2,1)S(1)}, bf16[1,192,384]{2,1,0:T(8,128)(2,1)S(1)}, u32[]{:S(2)}, u32[]{:S(2)}) collective-permute-start(bf16[1,192,384]{2,1,0:T(8,128)(2,1)S(1)} %get-tuple-element.181), channel_id=1, source_target_pairs={{0,16},{1,17},{2,18},{3,19},{4,20},{5,21},{6,22},{7,23},{8,24},{9,... | collective-permute-start | bytes 442376 | tf_op jit(solution)/shard_map/ppermute | solution.py:763
  97.2 2.5 %vp_grad.1 = (bf16[8,48,640]{2,1,0:T(8,128)(2,1)S(1)}, bf16[8,48,640]{2,1,0:T(8,128)(2,1)S(1)}) custom-call(s32[2]{0:T(128)S(1)} %pad_add_fusion.ids, bf16[768,512]{1,0:T(8,128)(2,1)S(1)} %get-tuple-element.183.x0_ref, bf16[768,512]{1,0:T(8,128)(2,1)S(1)} %collective-permute-done.13.x1_ref, bf16[3,384,512]{2,1,0:T(8,128)(2,1)S(1)} %get-tuple-element.174.d0_ref.do_ref, ...), custom_call_target="tpu_custom_call" | custom-call | flops 1950000000 | tf_op jit(solution)/shard_map/vp_grad/pallas_call | solution.py:45
  99.7 1.3 collective-permute-start.21
  101.0 2.5 %collective-permute-done.17.got_ref = bf16[1,192,384]{2,1,0:T(8,128)(2,1)S(1)} collective-permute-done((bf16[1,192,384]{2,1,0:T(8,128)(2,1)S(1)}, bf16[1,192,384]{2,1,0:T(8,128)(2,1)S(1)}, u32[]{:S(2)}, u32[]{:S(2)}) %collective-permute-start.17) | collective-permute-done | bytes 147488 | tf_op jit(solution)/shard_map/ppermute | solution.py:763
  104.1 0.7 add_split.16
  104.9 4.1 %tokens_back.1 = (bf16[2,256,768]{2,1,0:T(8,128)(2,1)}, bf16[256,768]{1,0:T(8,128)(2,1)S(1)}) custom-call(s32[2]{0:T(128)S(1)} %pad_add_fusion.ids, bf16[768,2304]{1,0:T(8,128)(2,1)S(1)} %copy-done, bf16[3,384,512]{2,1,0:T(8,128)(2,1)S(1)} %get-tuple-element.169.ds_ref, bf16[3,384,512]{2,1,0:T(8,128)(2,1)S(1)} %get-tuple-element.174.d0_ref.do_ref, ...), custom_call_target="tpu_custom_call" | custom-call | flops 3900000000 | tf_op jit(solution)/shard_map/tokens_back/pallas_call | solution.py:45
  109.0 0.7 add_split.17
  109.8 0.7 copy-done.18
  110.5 1.4 collective-permute-start.24
  111.9 2.9 %collective-permute-start.23 = (bf16[192,384]{1,0:T(8,128)(2,1)S(1)}, bf16[192,384]{1,0:T(8,128)(2,1)S(1)}, u32[]{:S(2)}, u32[]{:S(2)}) collective-permute-start(bf16[192,384]{1,0:T(8,128)(2,1)S(1)} %add_last.4.mine_ref), channel_id=1, source_target_pairs={{0,1},{1,0},{2,3},{3,2},{4,5},{5,4},{6,7},{7,6},{8,9},{9,8},{10,11... | collective-permute-start | bytes 442376 | tf_op jit(solution)/shard_map/ppermute | solution.py:758
  115.4 0.7 copy-done.20
  116.1 1.2 collective-permute-start.25
  118.0 2.6 %collective-permute-start.26 = (bf16[1,48,1920]{2,1,0:T(8,128)(2,1)S(1)}, bf16[1,48,1920]{2,1,0:T(8,128)(2,1)S(1)}, u32[]{:S(2)}, u32[]{:S(2)}) collective-permute-start(bf16[1,48,1920]{2,1,0:T(8,128)(2,1)S(1)} %get-tuple-element.212), channel_id=1, source_target_pairs={{0,16},{1,9},{2,18},{3,11},{4,20},{5,13},{6,22},{7,15},{8,24},{9,1... | collective-permute-start | bytes 552968 | tf_op jit(solution)/shard_map/ppermute | solution.py:763
  120.6 1.4 join.2
  122.7 1.4 collective-permute-start.27
  124.7 1.1 collective-permute-start.28
  126.4 0.7 collective-permute-start.29
  127.1 1.0 bitcast_dynamic-update-slice_fusion.1
  128.1 3.4 %collective-permute-done.27.got_ref = bf16[2,48,896]{2,1,0:T(8,128)(2,1)S(1)} collective-permute-done((bf16[2,48,896]{2,1,0:T(8,128)(2,1)S(1)}, bf16[2,48,896]{2,1,0:T(8,128)(2,1)S(1)}, u32[]{:S(2)}, u32[]{:S(2)}) %collective-permute-start.27) | collective-permute-done | bytes 172064 | tf_op jit(solution)/shard_map/ppermute | solution.py:763
  132.2 1.0 collective-permute-done.28.got_ref
  134.3 1.4 %join.3 = (f32[48,3072]{1,0:T(8,128)}, f32[48,768]{1,0:T(8,128)}) custom-call(s32[2]{0:T(128)S(1)} %pad_add_fusion.ids, bf16[48,1920]{1,0:T(8,128)(2,1)S(1)} %add_last.5.mine_ref, bf16[48,1920]{1,0:T(8,128)(2,1)S(1)} %collective-permute-done.29.other_ref), custom_call_target="tpu_custom_call" | custom-call | flops 1300000000 | tf_op jit(solution)/shard_map/join/pallas_call | solution.py:45
  137.8 2.1 %collective-permute-start.33 = (bf16[48,640]{1,0:T(8,128)(2,1)S(1)}, bf16[48,640]{1,0:T(8,128)(2,1)S(1)}, u32[]{:S(2)}, u32[]{:S(2)}) collective-permute-start(bf16[48,640]{1,0:T(8,128)(2,1)S(1)} %add_last.7.vo_mine), channel_id=1, source_target_pairs={{0,1},{1,0},{2,3},{3,2},{4,5},{5,4},{6,7},{7,6},{8,9},{9,8},{10,11... | collective-permute-start | bytes 184328 | tf_op jit(solution)/shard_map/ppermute | solution.py:758
  140.0 0.8 collective-permute-done.33.vo_other
  140.9 1.4 join_last.1
  (130 shorter events, 11.7 us)
Async XLA Ops:
  0.6 3.2 %collective-permute-start = (bf16[2,256,768]{2,1,0:T(8,128)(2,1)}, bf16[2,256,768]{2,1,0:T(8,128)(2,1)S(1)}, u32[]{:S(2)}, u32[]{:S(2)}) collective-permute-start(bf16[2,256,768]{2,1,0:T(8,128)(2,1)} %own_ref.3), channel_id=1, source_target_pairs={{0,1},{1,0},{2,3},{3,2},{4,5},{5,4},{6,7},{7,6},{8,9},{9,8},{10,11... | collective-permute-start | bytes 2359304 | tf_op jit(solution)/shard_map/ppermute | solution.py:758
  0.8 21.3 %collective-permute-start.1 = (bf16[2,256,768]{2,1,0:T(8,128)(2,1)}, bf16[2,256,768]{2,1,0:T(8,128)(2,1)S(1)}, u32[]{:S(2)}, u32[]{:S(2)}) collective-permute-start(bf16[2,256,768]{2,1,0:T(8,128)(2,1)} %cown_ref.1), channel_id=1, source_target_pairs={{0,1},{1,0},{2,3},{3,2},{4,5},{5,4},{6,7},{7,6},{8,9},{9,8},{10,11... | collective-permute-start | bytes 2359304 | tf_op jit(solution)/shard_map/ppermute | solution.py:758
  4.2 17.9 %slice-start = ((s8[4718592]{0:T(1024)(128)(4,1)}), s8[4194304]{0:T(1024)(128)(4,1)S(1)}, s32[]{:S(2)}) async-start(s8[4718592]{0:T(1024)(128)(4,1)} %bitcast.6), calls=%async_computation | async-start | bytes 8388608
  4.2 17.9 %slice-start.2 = ((s8[4718592]{0:T(1024)(128)(4,1)}), s8[4194304]{0:T(1024)(128)(4,1)S(1)}, s32[]{:S(2)}) async-start(s8[4718592]{0:T(1024)(128)(4,1)} %bitcast.8), calls=%async_computation.2 | async-start | bytes 8388608
  8.0 14.0 %copy-start.22 = (bf16[512,2304]{1,0:T(8,128)(2,1)}, bf16[512,2304]{1,0:T(8,128)(2,1)S(1)}, u32[]{:S(2)}) copy-start(bf16[512,2304]{1,0:T(8,128)(2,1)S(1)} %get-tuple-element.134.k_ref.v_ref) | copy-start | bytes 7077892
  8.1 14.0 %slice-start.1 = ((s8[4718592]{0:T(1024)(128)(4,1)}), s8[524288]{0:T(1024)(128)(4,1)S(1)}, s32[]{:S(2)}) async-start(s8[4718592]{0:T(1024)(128)(4,1)} %bitcast.6), calls=%async_computation.1 | async-start | bytes 1048576
  8.1 14.0 %slice-start.3 = ((s8[4718592]{0:T(1024)(128)(4,1)}), s8[524288]{0:T(1024)(128)(4,1)S(1)}, s32[]{:S(2)}) async-start(s8[4718592]{0:T(1024)(128)(4,1)} %bitcast.8), calls=%async_computation.3 | async-start | bytes 1048576
  8.1 14.0 %copy-start.1 = (bf16[768,768]{1,0:T(8,128)(2,1)S(1)}, bf16[768,768]{1,0:T(8,128)(2,1)}, u32[]{:S(2)}) copy-start(bf16[768,768]{1,0:T(8,128)(2,1)} %wo_ref.3) | copy-start | bytes 3538948
  8.1 14.0 %copy-start.3 = (bf16[2,256,768]{2,1,0:T(8,128)(2,1)S(1)}, bf16[2,256,768]{2,1,0:T(8,128)(2,1)}, u32[]{:S(2)}) copy-start(bf16[2,256,768]{2,1,0:T(8,128)(2,1)} %cown_ref.1) | copy-start | bytes 2359300
  8.1 14.0 %copy-start.8 = (bf16[3072]{0:T(1024)(128)(2,1)S(1)}, bf16[3072]{0:T(1024)(128)(2,1)}, u32[]{:S(2)}) copy-start(bf16[3072]{0:T(1024)(128)(2,1)} %bi_ref.1) | copy-start | bytes 18436
  8.1 14.0 %copy-start.9 = (bf16[768]{0:T(1024)(128)(2,1)S(1)}, bf16[768]{0:T(1024)(128)(2,1)}, u32[]{:S(2)}) copy-start(bf16[768]{0:T(1024)(128)(2,1)} %bo_ref.1) | copy-start | bytes 4612
  8.2 14.0 %copy-start.10 = (bf16[768]{0:T(1024)(128)(2,1)S(1)}, bf16[768]{0:T(1024)(128)(2,1)}, u32[]{:S(2)}) copy-start(bf16[768]{0:T(1024)(128)(2,1)} %s1_ref.1) | copy-start | bytes 4612
  8.2 14.0 %copy-start.11 = (bf16[768]{0:T(1024)(128)(2,1)S(1)}, bf16[768]{0:T(1024)(128)(2,1)}, u32[]{:S(2)}) copy-start(bf16[768]{0:T(1024)(128)(2,1)} %bd_ref.1) | copy-start | bytes 4612
  8.2 14.0 %copy-start.12 = (bf16[768]{0:T(1024)(128)(2,1)S(1)}, bf16[768]{0:T(1024)(128)(2,1)}, u32[]{:S(2)}) copy-start(bf16[768]{0:T(1024)(128)(2,1)} %g2_ref.1) | copy-start | bytes 4612
  8.2 14.0 %copy-start.13 = (bf16[768]{0:T(1024)(128)(2,1)S(1)}, bf16[768]{0:T(1024)(128)(2,1)}, u32[]{:S(2)}) copy-start(bf16[768]{0:T(1024)(128)(2,1)} %s2_ref.1) | copy-start | bytes 4612
  8.2 14.0 %copy-start.14 = (bf16[768]{0:T(1024)(128)(2,1)S(1)}, bf16[768]{0:T(1024)(128)(2,1)}, u32[]{:S(2)}) copy-start(bf16[768]{0:T(1024)(128)(2,1)} %g1_ref.3) | copy-start | bytes 4612
  34.8 6.2 %collective-permute-start.3 = (bf16[3072,512]{1,0:T(8,128)(2,1)S(1)}, bf16[3072,512]{1,0:T(8,128)(2,1)S(1)}, u32[]{:S(2)}, u32[]{:S(2)}) collective-permute-start(bf16[3072,512]{1,0:T(8,128)(2,1)S(1)} %get-tuple-element.145.a0_ref), channel_id=1, source_target_pairs={{0,1},{1,0},{2,3},{3,2},{4,5},{5,4},{6,7},{7,6},{8,9},{9,8},{10,11... | collective-permute-start | bytes 9437192 | tf_op jit(solution)/shard_map/ppermute | solution.py:758
  34.9 6.1 %collective-permute-start.4 = (bf16[512,384]{1,0:T(8,128)(2,1)S(1)}, bf16[512,384]{1,0:T(8,128)(2,1)S(1)}, u32[]{:S(2)}, u32[]{:S(2)}) collective-permute-start(bf16[512,384]{1,0:T(8,128)(2,1)S(1)} %get-tuple-element.146), channel_id=1, source_target_pairs={{0,1},{1,0},{2,3},{3,2},{4,5},{5,4},{6,7},{7,6},{8,9},{9,8},{10,11... | collective-permute-start | bytes 1179656 | tf_op jit(solution)/shard_map/ppermute | solution.py:758
  39.7 15.6 %collective-permute-start.6 = (bf16[512,1536]{1,0:T(8,128)(2,1)S(1)}, bf16[512,1536]{1,0:T(8,128)(2,1)S(1)}, u32[]{:S(2)}, u32[]{:S(2)}) collective-permute-start(bf16[512,1536]{1,0:T(8,128)(2,1)S(1)} %get-tuple-element.149.dsend_ref), channel_id=1, source_target_pairs={{0,1},{1,0},{2,3},{3,2},{4,5},{5,4},{6,7},{7,6},{8,9},{9,8},{10,11... | collective-permute-start | bytes 4718600 | tf_op jit(solution)/shard_map/ppermute | solution.py:758
  39.9 15.5 %collective-permute-start.7 = (bf16[768,512]{1,0:T(8,128)(2,1)S(1)}, bf16[768,512]{1,0:T(8,128)(2,1)S(1)}, u32[]{:S(2)}, u32[]{:S(2)}) collective-permute-start(bf16[768,512]{1,0:T(8,128)(2,1)S(1)} %get-tuple-element.138.at_ref.a0_ref), channel_id=1, source_target_pairs={{0,1},{1,0},{2,3},{3,2},{4,5},{5,4},{6,7},{7,6},{8,9},{9,8},{10,11... | collective-permute-start | bytes 2359304 | tf_op jit(solution)/shard_map/ppermute | solution.py:758
  40.3 15.0 %collective-permute-start.5 = (bf16[768,512]{1,0:T(8,128)(2,1)S(1)}, bf16[768,512]{1,0:T(8,128)(2,1)S(1)}, u32[]{:S(2)}, u32[]{:S(2)}) collective-permute-start(bf16[768,512]{1,0:T(8,128)(2,1)S(1)} %get-tuple-element.155.f0_ref), channel_id=1, source_target_pairs={{0,1},{1,0},{2,3},{3,2},{4,5},{5,4},{6,7},{7,6},{8,9},{9,8},{10,11... | collective-permute-start | bytes 2359304 | tf_op jit(solution)/shard_map/ppermute | solution.py:758
  46.0 16.4 %collective-permute-start.9 = (bf16[8,192,384]{2,1,0:T(8,128)(2,1)S(1)}, bf16[8,192,384]{2,1,0:T(8,128)(2,1)S(1)}, u32[]{:S(2)}, u32[]{:S(2)}) collective-permute-start(bf16[8,192,384]{2,1,0:T(8,128)(2,1)S(1)} %get-tuple-element.147), channel_id=1, source_target_pairs={{0,2},{1,5},{2,0},{3,7},{4,6},{5,1},{6,4},{7,3},{8,10},{9,13},{10,... | collective-permute-start | bytes 3538952 | tf_op jit(solution)/shard_map/ppermute | solution.py:763
  54.7 2.0 %collective-permute-start.8 = (bf16[512,384]{1,0:T(8,128)(2,1)S(1)}, bf16[512,384]{1,0:T(8,128)(2,1)S(1)}, u32[]{:S(2)}, u32[]{:S(2)}) collective-permute-start(bf16[512,384]{1,0:T(8,128)(2,1)S(1)} %get-tuple-element.157), channel_id=1, source_target_pairs={{0,1},{1,0},{2,3},{3,2},{4,5},{5,4},{6,7},{7,6},{8,9},{9,8},{10,11... | collective-permute-start | bytes 1179656 | tf_op jit(solution)/shard_map/ppermute | solution.py:758
  63.3 25.1 %collective-permute-start.11 = (bf16[8,48,1920]{2,1,0:T(8,128)(2,1)S(1)}, bf16[8,48,1920]{2,1,0:T(8,128)(2,1)S(1)}, u32[]{:S(2)}, u32[]{:S(2)}) collective-permute-start(bf16[8,48,1920]{2,1,0:T(8,128)(2,1)S(1)} %get-tuple-element.177), channel_id=1, source_target_pairs={{0,2},{1,5},{2,0},{3,7},{4,6},{5,1},{6,4},{7,3},{8,10},{9,13},{10,... | collective-permute-start | bytes 4423688 | tf_op jit(solution)/shard_map/ppermute | solution.py:763
  64.7 13.3 %collective-permute-start.10 = (bf16[4,192,384]{2,1,0:T(8,128)(2,1)S(1)}, bf16[4,192,384]{2,1,0:T(8,128)(2,1)S(1)}, u32[]{:S(2)}, u32[]{:S(2)}) collective-permute-start(bf16[4,192,384]{2,1,0:T(8,128)(2,1)S(1)} %get-tuple-element.161), channel_id=1, source_target_pairs={{0,8},{1,9},{2,10},{3,11},{4,12},{5,13},{6,14},{7,15},{8,0},{9,1},... | collective-permute-start | bytes 1769480 | tf_op jit(solution)/shard_map/ppermute | solution.py:763
  72.9 18.8 %collective-permute-start.14 = (bf16[3,384,512]{2,1,0:T(8,128)(2,1)S(1)}, bf16[3,384,512]{2,1,0:T(8,128)(2,1)S(1)}, u32[]{:S(2)}, u32[]{:S(2)}) collective-permute-start(bf16[3,384,512]{2,1,0:T(8,128)(2,1)S(1)} %get-tuple-element.169.ds_ref), channel_id=1, source_target_pairs={{0,1},{1,0},{2,3},{3,2},{4,5},{5,4},{6,7},{7,6},{8,9},{9,8},{10,11... | collective-permute-start | bytes 3538952 | tf_op jit(solution)/shard_map/ppermute | solution.py:758
  74.7 17.0 %collective-permute-start.13 = (bf16[768,512]{1,0:T(8,128)(2,1)S(1)}, bf16[768,512]{1,0:T(8,128)(2,1)S(1)}, u32[]{:S(2)}, u32[]{:S(2)}) collective-permute-start(bf16[768,512]{1,0:T(8,128)(2,1)S(1)} %get-tuple-element.183.x0_ref), channel_id=1, source_target_pairs={{0,1},{1,0},{2,3},{3,2},{4,5},{5,4},{6,7},{7,6},{8,9},{9,8},{10,11... | collective-permute-start | bytes 2359304 | tf_op jit(solution)/shard_map/ppermute | solution.py:758
  78.8 12.3 %collective-permute-start.12 = (bf16[2,192,384]{2,1,0:T(8,128)(2,1)S(1)}, bf16[2,192,384]{2,1,0:T(8,128)(2,1)S(1)}, u32[]{:S(2)}, u32[]{:S(2)}) collective-permute-start(bf16[2,192,384]{2,1,0:T(8,128)(2,1)S(1)} %get-tuple-element.172), channel_id=1, source_target_pairs={{0,4},{1,3},{2,6},{3,1},{4,0},{5,7},{6,2},{7,5},{8,12},{9,11},{10,... | collective-permute-start | bytes 884744 | tf_op jit(solution)/shard_map/ppermute | solution.py:763
  89.3 14.8 %collective-permute-start.18 = (bf16[4,48,1920]{2,1,0:T(8,128)(2,1)S(1)}, bf16[4,48,1920]{2,1,0:T(8,128)(2,1)S(1)}, u32[]{:S(2)}, u32[]{:S(2)}) collective-permute-start(bf16[4,48,1920]{2,1,0:T(8,128)(2,1)S(1)} %get-tuple-element.178), channel_id=1, source_target_pairs={{0,4},{1,3},{2,6},{3,1},{4,0},{5,7},{6,2},{7,5},{8,12},{9,11},{10,... | collective-permute-start | bytes 2211848 | tf_op jit(solution)/shard_map/ppermute | solution.py:763
  89.4 7.8 %collective-permute-start.15 = (bf16[256,384]{1,0:T(8,128)(2,1)S(1)}, bf16[256,384]{1,0:T(8,128)(2,1)S(1)}, u32[]{:S(2)}, u32[]{:S(2)}) collective-permute-start(bf16[256,384]{1,0:T(8,128)(2,1)S(1)} %get-tuple-element.192), channel_id=1, source_target_pairs={{0,1},{1,0},{2,3},{3,2},{4,5},{5,4},{6,7},{7,6},{8,9},{9,8},{10,11... | collective-permute-start | bytes 589832 | tf_op jit(solution)/shard_map/ppermute | solution.py:758
  91.1 6.1 %collective-permute-start.16 = (bf16[256,384]{1,0:T(8,128)(2,1)S(1)}, bf16[256,384]{1,0:T(8,128)(2,1)S(1)}, u32[]{:S(2)}, u32[]{:S(2)}) collective-permute-start(bf16[256,384]{1,0:T(8,128)(2,1)S(1)} %get-tuple-element.194), channel_id=1, source_target_pairs={{0,1},{1,0},{2,3},{3,2},{4,5},{5,4},{6,7},{7,6},{8,9},{9,8},{10,11... | collective-permute-start | bytes 589832 | tf_op jit(solution)/shard_map/ppermute | solution.py:758
  94.6 14.5 %collective-permute-start.20 = (bf16[8,48,896]{2,1,0:T(8,128)(2,1)S(1)}, bf16[8,48,896]{2,1,0:T(8,128)(2,1)S(1)}, u32[]{:S(2)}, u32[]{:S(2)}) collective-permute-start(bf16[8,48,896]{2,1,0:T(8,128)(2,1)S(1)} %get-tuple-element.189), channel_id=1, source_target_pairs={{0,2},{1,5},{2,0},{3,7},{4,6},{5,1},{6,4},{7,3},{8,10},{9,13},{10,... | collective-permute-start | bytes 2064392 | tf_op jit(solution)/shard_map/ppermute | solution.py:763
  94.7 8.8 %collective-permute-start.17 = (bf16[1,192,384]{2,1,0:T(8,128)(2,1)S(1)}, bf16[1,192,384]{2,1,0:T(8,128)(2,1)S(1)}, u32[]{:S(2)}, u32[]{:S(2)}) collective-permute-start(bf16[1,192,384]{2,1,0:T(8,128)(2,1)S(1)} %get-tuple-element.181), channel_id=1, source_target_pairs={{0,16},{1,17},{2,18},{3,19},{4,20},{5,21},{6,22},{7,23},{8,24},{9,... | collective-permute-start | bytes 442376 | tf_op jit(solution)/shard_map/ppermute | solution.py:763
  99.7 15.1 %collective-permute-start.21 = (bf16[8,48,640]{2,1,0:T(8,128)(2,1)S(1)}, bf16[8,48,640]{2,1,0:T(8,128)(2,1)S(1)}, u32[]{:S(2)}, u32[]{:S(2)}) collective-permute-start(bf16[8,48,640]{2,1,0:T(8,128)(2,1)S(1)} %get-tuple-element.195), channel_id=1, source_target_pairs={{0,2},{1,5},{2,0},{3,7},{4,6},{5,1},{6,4},{7,3},{8,10},{9,13},{10,... | collective-permute-start | bytes 1474568 | tf_op jit(solution)/shard_map/ppermute | solution.py:763
  104.8 12.5 %collective-permute-start.22 = (bf16[2,48,1920]{2,1,0:T(8,128)(2,1)S(1)}, bf16[2,48,1920]{2,1,0:T(8,128)(2,1)S(1)}, u32[]{:S(2)}, u32[]{:S(2)}) collective-permute-start(bf16[2,48,1920]{2,1,0:T(8,128)(2,1)S(1)} %get-tuple-element.200), channel_id=1, source_target_pairs={{0,8},{1,17},{2,10},{3,19},{4,12},{5,21},{6,14},{7,23},{8,0},{9,25... | collective-permute-start | bytes 1105928 | tf_op jit(solution)/shard_map/ppermute | solution.py:763
  110.5 11.5 %collective-permute-start.24 = (bf16[4,48,896]{2,1,0:T(8,128)(2,1)S(1)}, bf16[4,48,896]{2,1,0:T(8,128)(2,1)S(1)}, u32[]{:S(2)}, u32[]{:S(2)}) collective-permute-start(bf16[4,48,896]{2,1,0:T(8,128)(2,1)S(1)} %get-tuple-element.206), channel_id=1, source_target_pairs={{0,4},{1,3},{2,6},{3,1},{4,0},{5,7},{6,2},{7,5},{8,12},{9,11},{10,... | collective-permute-start | bytes 1032200 | tf_op jit(solution)/shard_map/ppermute | solution.py:763
  111.9 6.1 %collective-permute-start.23 = (bf16[192,384]{1,0:T(8,128)(2,1)S(1)}, bf16[192,384]{1,0:T(8,128)(2,1)S(1)}, u32[]{:S(2)}, u32[]{:S(2)}) collective-permute-start(bf16[192,384]{1,0:T(8,128)(2,1)S(1)} %add_last.4.mine_ref), channel_id=1, source_target_pairs={{0,1},{1,0},{2,3},{3,2},{4,5},{5,4},{6,7},{7,6},{8,9},{9,8},{10,11... | collective-permute-start | bytes 442376 | tf_op jit(solution)/shard_map/ppermute | solution.py:758
  114.7 12.4 %collective-permute-start.2 = (bf16[256,768]{1,0:T(8,128)(2,1)S(1)}, bf16[256,768]{1,0:T(8,128)(2,1)}, u32[]{:S(2)}, u32[]{:S(2)}) collective-permute-start(bf16[256,768]{1,0:T(8,128)(2,1)S(1)} %get-tuple-element.140), channel_id=1, source_target_pairs={{0,1},{1,0},{2,3},{3,2},{4,5},{5,4},{6,7},{7,6},{8,9},{9,8},{10,11... | collective-permute-start | bytes 1179656 | tf_op jit(solution)/shard_map/ppermute | solution.py:758
  116.1 7.9 %collective-permute-start.25 = (bf16[4,48,640]{2,1,0:T(8,128)(2,1)S(1)}, bf16[4,48,640]{2,1,0:T(8,128)(2,1)S(1)}, u32[]{:S(2)}, u32[]{:S(2)}) collective-permute-start(bf16[4,48,640]{2,1,0:T(8,128)(2,1)S(1)} %get-tuple-element.209), channel_id=1, source_target_pairs={{0,4},{1,3},{2,6},{3,1},{4,0},{5,7},{6,2},{7,5},{8,12},{9,11},{10,... | collective-permute-start | bytes 737288 | tf_op jit(solution)/shard_map/ppermute | solution.py:763
  117.3 22.7 %collective-permute-start.19 = (bf16[256,768]{1,0:T(8,128)(2,1)S(1)}, bf16[256,768]{1,0:T(8,128)(2,1)S(1)}, u32[]{:S(2)}, u32[]{:S(2)}) collective-permute-start(bf16[256,768]{1,0:T(8,128)(2,1)S(1)} %get-tuple-element.203), channel_id=1, source_target_pairs={{0,1},{1,0},{2,3},{3,2},{4,5},{5,4},{6,7},{7,6},{8,9},{9,8},{10,11... | collective-permute-start | bytes 1179656 | tf_op jit(solution)/shard_map/ppermute | solution.py:758
  118.0 7.8 %collective-permute-start.26 = (bf16[1,48,1920]{2,1,0:T(8,128)(2,1)S(1)}, bf16[1,48,1920]{2,1,0:T(8,128)(2,1)S(1)}, u32[]{:S(2)}, u32[]{:S(2)}) collective-permute-start(bf16[1,48,1920]{2,1,0:T(8,128)(2,1)S(1)} %get-tuple-element.212), channel_id=1, source_target_pairs={{0,16},{1,9},{2,18},{3,11},{4,20},{5,13},{6,22},{7,15},{8,24},{9,1... | collective-permute-start | bytes 552968 | tf_op jit(solution)/shard_map/ppermute | solution.py:763
  122.7 8.9 %collective-permute-start.27 = (bf16[2,48,896]{2,1,0:T(8,128)(2,1)S(1)}, bf16[2,48,896]{2,1,0:T(8,128)(2,1)S(1)}, u32[]{:S(2)}, u32[]{:S(2)}) collective-permute-start(bf16[2,48,896]{2,1,0:T(8,128)(2,1)S(1)} %get-tuple-element.216), channel_id=1, source_target_pairs={{0,8},{1,17},{2,10},{3,19},{4,12},{5,21},{6,14},{7,23},{8,0},{9,25... | collective-permute-start | bytes 516104 | tf_op jit(solution)/shard_map/ppermute | solution.py:763
  124.7 8.5 %collective-permute-start.28 = (bf16[2,48,640]{2,1,0:T(8,128)(2,1)S(1)}, bf16[2,48,640]{2,1,0:T(8,128)(2,1)S(1)}, u32[]{:S(2)}, u32[]{:S(2)}) collective-permute-start(bf16[2,48,640]{2,1,0:T(8,128)(2,1)S(1)} %get-tuple-element.219), channel_id=1, source_target_pairs={{0,8},{1,17},{2,10},{3,19},{4,12},{5,21},{6,14},{7,23},{8,0},{9,25... | collective-permute-start | bytes 368648 | tf_op jit(solution)/shard_map/ppermute | solution.py:763
  126.4 7.9 %collective-permute-start.29 = (bf16[48,1920]{1,0:T(8,128)(2,1)S(1)}, bf16[48,1920]{1,0:T(8,128)(2,1)S(1)}, u32[]{:S(2)}, u32[]{:S(2)}) collective-permute-start(bf16[48,1920]{1,0:T(8,128)(2,1)S(1)} %add_last.5.mine_ref), channel_id=1, source_target_pairs={{0,1},{1,0},{2,3},{3,2},{4,5},{5,4},{6,7},{7,6},{8,9},{9,8},{10,11... | collective-permute-start | bytes 552968 | tf_op jit(solution)/shard_map/ppermute | solution.py:758
  132.1 4.1 %collective-permute-start.30 = (bf16[1,48,896]{2,1,0:T(8,128)(2,1)S(1)}, bf16[1,48,896]{2,1,0:T(8,128)(2,1)S(1)}, u32[]{:S(2)}, u32[]{:S(2)}) collective-permute-start(bf16[1,48,896]{2,1,0:T(8,128)(2,1)S(1)} %get-tuple-element.224), channel_id=1, source_target_pairs={{0,16},{1,9},{2,18},{3,11},{4,20},{5,13},{6,22},{7,15},{8,24},{9,1... | collective-permute-start | bytes 258056 | tf_op jit(solution)/shard_map/ppermute | solution.py:763
  133.8 3.5 %collective-permute-start.32 = (bf16[1,48,640]{2,1,0:T(8,128)(2,1)S(1)}, bf16[1,48,640]{2,1,0:T(8,128)(2,1)S(1)}, u32[]{:S(2)}, u32[]{:S(2)}) collective-permute-start(bf16[1,48,640]{2,1,0:T(8,128)(2,1)S(1)} %get-tuple-element.227), channel_id=1, source_target_pairs={{0,16},{1,9},{2,18},{3,11},{4,20},{5,13},{6,22},{7,15},{8,24},{9,1... | collective-permute-start | bytes 184328 | tf_op jit(solution)/shard_map/ppermute | solution.py:763
  136.8 4.0 %collective-permute-start.31 = (bf16[48,896]{1,0:T(8,128)(2,1)S(1)}, bf16[48,896]{1,0:T(8,128)(2,1)S(1)}, u32[]{:S(2)}, u32[]{:S(2)}) collective-permute-start(bf16[48,896]{1,0:T(8,128)(2,1)S(1)} %add_last.6.qk_mine), channel_id=1, source_target_pairs={{0,1},{1,0},{2,3},{3,2},{4,5},{5,4},{6,7},{7,6},{8,9},{9,8},{10,11... | collective-permute-start | bytes 258056 | tf_op jit(solution)/shard_map/ppermute | solution.py:758
  137.8 3.0 %collective-permute-start.33 = (bf16[48,640]{1,0:T(8,128)(2,1)S(1)}, bf16[48,640]{1,0:T(8,128)(2,1)S(1)}, u32[]{:S(2)}, u32[]{:S(2)}) collective-permute-start(bf16[48,640]{1,0:T(8,128)(2,1)S(1)} %add_last.7.vo_mine), channel_id=1, source_target_pairs={{0,1},{1,0},{2,3},{3,2},{4,5},{5,4},{6,7},{7,6},{8,9},{9,8},{10,11... | collective-permute-start | bytes 184328 | tf_op jit(solution)/shard_map/ppermute | solution.py:758
  (22 other events, 89.9 us)

commit v6 on v5

--- a/solution.py
+++ b/solution.py
@@ -588,11 +588,11 @@
 def down_grad(ids, n, bits, actt, actt_other, dsec, dsec_other):
     ff, rows = actt.shape
     side = dsec_other.shape[1]
-    block = ff // 4
+    block = ff // 2
     part = (n // 2, ff // n, side)
     a = pl.BlockSpec((block, rows), lambda i, ids: (i, 0))
     return call(
-        functools.partial(down_kernel, n, bits), "down_grad", (4,), ids, (actt, actt_other, dsec, dsec_other),
+        functools.partial(down_kernel, n, bits), "down_grad", (2,), ids, (actt, actt_other, dsec, dsec_other),
         [a, a, pl.BlockSpec((rows, side), lambda i, ids: (0, ids[1])), whole((rows, side))],
         [whole(part)] * 2, [SDS(part, BF16)] * 2,
         us=7,

time: 145 us -> 145 us (level)
  no operation moved by 1% of the time
where the time goes in v6:
time: 145 us; the launch traced here: 142 us
  Pallas kernels  90.9 us (63%)
  starting transfers between devices  32.6 us (22%)
  waiting for transfers between devices  13.4 us (9%)
  local copies, waits for them, and re-layouts  3.74 us (3%)
  between operations  1.51 us (1%)
    pallas_call x32, Pallas kernels, call(): pl.pallas_call(kernel, grid_spec=pltpu.PrefetchScalarGridSpec(num_scalar_...  90.9 us
    ppermute x16, starting transfers between devices, across(): return lax.ppermute(x, ('pages', 'slab'), pairs)  19.9 us
    ppermute x18, starting transfers between devices, swap(): return lax.ppermute(x, 'slab', [(0, 1), (1, 0)])  12.7 us
    ppermute x16, waiting for transfers between devices, across(): return lax.ppermute(x, ('pages', 'slab'), pairs)  10.6 us
  transfers between devices with their start and end apart: 34, of which 8 were waited for; matrix products, arithmetic and copies ran while one was open for 1% of the time, Pallas kernels for 54%

profile of v6, /device:TPU:1, one launch (start us, length us, event | category | flops | bytes accessed | tf_op | source)
XLA Modules:
  0.0 142.2 jit_solution(11254710572598364110)
XLA Ops:
  1.3 0.7 copy-done.6
  2.0 1.7 %tables.1 = (bf16[512,256]{1,0:T(8,128)(2,1)S(1)}, f32[4,512,128]{2,1,0:T(8,128)S(1)}, f32[4,64,512]{2,1,0:T(8,128)S(1)}, bf16[256,512]{1,0:T(8,128)(2,1)S(1)}, bf16[256,512]{1,0:T(8,128)(2,1)S(1)}) custom-call(s32[2]{0:T(128)S(1)} %pad_add_fusion.ids, s32[2,4,512]{2,1,0:T(4,128)S(1)} %copy-done.6), custom_call_target="tpu_custom_call" | custom-call | flops 1950000000 | tf_op jit(solution)/shard_map/tables/pallas_call | solution.py:45
  4.2 3.8 %project.1 = (bf16[2304,512]{1,0:T(8,128)(2,1)S(1)}, bf16[512,2304]{1,0:T(8,128)(2,1)S(1)}, bf16[768,512]{1,0:T(8,128)(2,1)S(1)}) custom-call(s32[2]{0:T(128)S(1)} %pad_add_fusion.ids, bf16[2,256,768]{2,1,0:T(8,128)(2,1)S(1)} %copy-done.2, bf16[2,256,768]{2,1,0:T(8,128)(2,1)S(1)} %collective-permute-done.other_ref, bf16[768,2304]{1,0:T(8,128)(2,1)S(1)} %copy-done, ...), custom_call_target="tpu_custom_call" | custom-call | flops 3249999872 | tf_op jit(solution)/shard_map/project/pallas_call | solution.py:45
  8.2 13.9 %attend.1 = (bf16[12,512,512]{2,1,0:T(8,128)(2,1)}, bf16[768,512]{1,0:T(8,128)(2,1)S(1)}, f32[6,2,512]{2,1,0:T(2,128)S(1)}, bf16[768,256]{1,0:T(8,128)(2,1)S(1)}, bf16[768,256]{1,0:T(8,128)(2,1)S(1)}) custom-call(s32[2]{0:T(128)S(1)} %pad_add_fusion.ids, s32[2]{0:T(128)S(1)} %copy-done.15, bf16[2304,512]{1,0:T(8,128)(2,1)S(1)} %get-tuple-element.133.qt_ref.vt_ref.kt_ref, ...), custom_call_target="tpu_custom_call" | custom-call | flops 11050000384 | tf_op jit(solution)/shard_map/attend/pallas_call | solution.py:45
  22.2 12.5 %feed.1 = (bf16[768,512]{1,0:T(8,128)(2,1)S(1)}, f32[512,768]{1,0:T(8,128)S(1)}, f32[512,1]{1,0:T(8,128)S(1)}, bf16[512,3072]{1,0:T(8,128)(2,1)S(1)}, bf16[3072,...) custom-call(s32[2]{0:T(128)S(1)} %pad_add_fusion.ids, ...), custom_call_target="tpu_custom_call" | custom-call | flops 9749999616 | tf_op jit(solution)/shard_map/feed/pallas_call | solution.py:45
  35.3 4.4 %hidden_back.1 = (bf16[512,1536]{1,0:T(8,128)(2,1)S(1)}, bf16[512,1536]{1,0:T(8,128)(2,1)S(1)}, f32[1,3072]{1,0:T(1,128)S(1)}) custom-call(s32[2]{0:T(128)S(1)} %pad_add_fusion.ids, bf16[512,768]{1,0:T(8,128)(2,1)S(1)} %get-tuple-element.141.ds_ref.b0_ref, bf16[3072,768]{1,0:T(8,128)(2,1)S(1)} %bitcast.7, bf16[512,3072]{1,0:T(8,128)(2,1)S(1)} %get-tuple-element.142.slope_ref), custom_call_target="tpu_custom_call" | custom-call | flops 3249999872 | tf_op jit(solution)/shard_map/hidden_back/pallas_call | solution.py:45
  41.0 4.7 %down_grad.1 = (bf16[8,192,384]{2,1,0:T(8,128)(2,1)S(1)}, bf16[8,192,384]{2,1,0:T(8,128)(2,1)S(1)}) custom-call(s32[2]{0:T(128)S(1)} %pad_add_fusion.ids, bf16[3072,512]{1,0:T(8,128)(2,1)S(1)} %get-tuple-element.145.a0_ref, bf16[3072,512]{1,0:T(8,128)(2,1)S(1)} %collective-permute-done.3.a1_ref, bf16[512,768]{1,0:T(8,128)(2,1)S(1)} %get-tuple-element.141.ds_ref.b0_ref, ...), custom_call_target="tpu_custom_call" | custom-call | flops 4550000128 | tf_op jit(solution)/shard_map/down_grad/pallas_call | solution.py:45
  45.7 2.4 %collective-permute-start.9 = (bf16[8,192,384]{2,1,0:T(8,128)(2,1)S(1)}, bf16[8,192,384]{2,1,0:T(8,128)(2,1)S(1)}, u32[]{:S(2)}, u32[]{:S(2)}) collective-permute-start(bf16[8,192,384]{2,1,0:T(8,128)(2,1)S(1)} %get-tuple-element.147), channel_id=1, source_target_pairs={{0,2},{1,5},{2,0},{3,7},{4,6},{5,1},{6,4},{7,3},{8,10},{9,13},{10,... | collective-permute-start | bytes 3538952 | tf_op jit(solution)/shard_map/ppermute | solution.py:763
  48.1 6.2 %first_back.1 = (f32[512,768]{1,0:T(8,128)S(1)}, bf16[512,768]{1,0:T(8,128)(2,1)S(1)}, bf16[512,384]{1,0:T(8,128)(2,1)S(1)}, bf16[768,512]{1,0:T(8,128)(2,1)S(1)}, f32[8,768]{1,0:T(8,128)S(1)}) custom-call(s32[2]{0:T(128)S(1)} %pad_add_fusion.ids, bf16[512,1536]{1,0:T(8,128)(2,1)S(1)} %get-tuple-element.149.dsend_ref, ...), custom_call_target="tpu_custom_call" | custom-call | flops 5200000000 | tf_op jit(solution)/shard_map/first_back/pallas_call | solution.py:45
  54.4 0.7 collective-permute-start.8
  55.1 1.3 collective-permute-done.8.c1_ref
  56.4 5.7 %mid_grad.1 = (bf16[8,48,1920]{2,1,0:T(8,128)(2,1)S(1)}, bf16[8,48,1920]{2,1,0:T(8,128)(2,1)S(1)}) custom-call(s32[2]{0:T(128)S(1)} %pad_add_fusion.ids, bf16[768,512]{1,0:T(8,128)(2,1)S(1)} %get-tuple-element.155.f0_ref, bf16[768,512]{1,0:T(8,128)(2,1)S(1)} %collective-permute-done.5.f1_ref, bf16[512,1536]{1,0:T(8,128)(2,1)S(1)} %get-tuple-element.143.down_ref.h0_ref, ...), custom_call_target="tpu_custom_call" | custom-call | flops 3900000000 | tf_op jit(solution)/shard_map/mid_grad/pallas_call | solution.py:45
  62.1 0.9 add_split.12
  63.0 1.4 %collective-permute-start.11 = (bf16[8,48,1920]{2,1,0:T(8,128)(2,1)S(1)}, bf16[8,48,1920]{2,1,0:T(8,128)(2,1)S(1)}, u32[]{:S(2)}, u32[]{:S(2)}) collective-permute-start(bf16[8,48,1920]{2,1,0:T(8,128)(2,1)S(1)} %get-tuple-element.177), channel_id=1, source_target_pairs={{0,2},{1,5},{2,0},{3,7},{4,6},{5,1},{6,4},{7,3},{8,10},{9,13},{10,... | collective-permute-start | bytes 4423688 | tf_op jit(solution)/shard_map/ppermute | solution.py:763
  64.4 1.3 collective-permute-start.10
  65.7 6.8 %attend_back.2 = (bf16[3,384,512]{2,1,0:T(8,128)(2,1)S(1)}, bf16[256,384]{1,0:T(8,128)(2,1)S(1)}, bf16[256,384]{1,0:T(8,128)(2,1)S(1)}, f32[24,384]{1,0:T(8,128)S(1)}) custom-call(s32[2]{0:T(128)S(1)} %pad_add_fusion.ids, bf16[12,512,512]{2,1,0:T(8,128)(2,1)S(1)} %bitcast.11, f32[6,2,512]{2,1,0:T(2,128)S(1)} %get-tuple-element.164.r_ref, ...), custom_call_target="tpu_custom_call" | custom-call | flops 5849999872 | tf_op jit(solution)/shard_map/attend_back/pallas_call | solution.py:45
  72.6 1.8 %collective-permute-start.14 = (bf16[3,384,512]{2,1,0:T(8,128)(2,1)S(1)}, bf16[3,384,512]{2,1,0:T(8,128)(2,1)S(1)}, u32[]{:S(2)}, u32[]{:S(2)}) collective-permute-start(bf16[3,384,512]{2,1,0:T(8,128)(2,1)S(1)} %get-tuple-element.169.ds_ref), channel_id=1, source_target_pairs={{0,1},{1,0},{2,3},{3,2},{4,5},{5,4},{6,7},{7,6},{8,9},{9,8},{10,11... | collective-permute-start | bytes 3538952 | tf_op jit(solution)/shard_map/ppermute | solution.py:758
  74.5 3.2 %collective-permute-done.10.got_ref = bf16[4,192,384]{2,1,0:T(8,128)(2,1)S(1)} collective-permute-done((bf16[4,192,384]{2,1,0:T(8,128)(2,1)S(1)}, bf16[4,192,384]{2,1,0:T(8,128)(2,1)S(1)}, u32[]{:S(2)}, u32[]{:S(2)}) %collective-permute-start.10) | collective-permute-done | bytes 589856 | tf_op jit(solution)/shard_map/ppermute | solution.py:763
  77.7 0.7 add_split.13
  78.4 2.8 %collective-permute-start.12 = (bf16[2,192,384]{2,1,0:T(8,128)(2,1)S(1)}, bf16[2,192,384]{2,1,0:T(8,128)(2,1)S(1)}, u32[]{:S(2)}, u32[]{:S(2)}) collective-permute-start(bf16[2,192,384]{2,1,0:T(8,128)(2,1)S(1)} %get-tuple-element.172), channel_id=1, source_target_pairs={{0,4},{1,3},{2,6},{3,1},{4,0},{5,7},{6,2},{7,5},{8,12},{9,11},{10,... | collective-permute-start | bytes 884744 | tf_op jit(solution)/shard_map/ppermute | solution.py:763
  81.3 6.8 %attend_back.3 = (bf16[3,384,512]{2,1,0:T(8,128)(2,1)S(1)}, bf16[256,384]{1,0:T(8,128)(2,1)S(1)}, bf16[256,384]{1,0:T(8,128)(2,1)S(1)}, f32[24,384]{1,0:T(8,128)S(1)}) custom-call(s32[2]{0:T(128)S(1)} %pad_add_fusion.ids, bf16[12,512,512]{2,1,0:T(8,128)(2,1)S(1)} %bitcast.11, f32[6,2,512]{2,1,0:T(2,128)S(1)} %get-tuple-element.164.r_ref, ...), custom_call_target="tpu_custom_call" | custom-call | flops 5849999872 | tf_op jit(solution)/shard_map/attend_back/pallas_call | solution.py:45
  88.1 1.1 add_split.14
  89.3 1.7 %collective-permute-start.15 = (bf16[256,384]{1,0:T(8,128)(2,1)S(1)}, bf16[256,384]{1,0:T(8,128)(2,1)S(1)}, u32[]{:S(2)}, u32[]{:S(2)}) collective-permute-start(bf16[256,384]{1,0:T(8,128)(2,1)S(1)} %get-tuple-element.192), channel_id=1, source_target_pairs={{0,1},{1,0},{2,3},{3,2},{4,5},{5,4},{6,7},{7,6},{8,9},{9,8},{10,11... | collective-permute-start | bytes 589832 | tf_op jit(solution)/shard_map/ppermute | solution.py:758
  91.7 2.6 %qk_grad.1 = (bf16[8,48,896]{2,1,0:T(8,128)(2,1)S(1)}, bf16[8,48,896]{2,1,0:T(8,128)(2,1)S(1)}) custom-call(s32[2]{0:T(128)S(1)} %pad_add_fusion.ids, bf16[768,512]{1,0:T(8,128)(2,1)S(1)} %get-tuple-element.183.x0_ref, bf16[768,512]{1,0:T(8,128)(2,1)S(1)} %collective-permute-done.13.x1_ref, bf16[3,384,512]{2,1,0:T(8,128)(2,1)S(1)} %get-tuple-element.174.d0_ref.do_ref, ...), custom_call_target="tpu_custom_call" | custom-call | flops 2600000000 | tf_op jit(solution)/shard_map/qk_grad/pallas_call | solution.py:45
  94.4 2.5 %collective-permute-start.17 = (bf16[1,192,384]{2,1,0:T(8,128)(2,1)S(1)}, bf16[1,192,384]{2,1,0:T(8,128)(2,1)S(1)}, u32[]{:S(2)}, u32[]{:S(2)}) collective-permute-start(bf16[1,192,384]{2,1,0:T(8,128)(2,1)S(1)} %get-tuple-element.181), channel_id=1, source_target_pairs={{0,16},{1,17},{2,18},{3,19},{4,20},{5,21},{6,22},{7,23},{8,24},{9,... | collective-permute-start | bytes 442376 | tf_op jit(solution)/shard_map/ppermute | solution.py:763
  96.9 2.5 %vp_grad.1 = (bf16[8,48,640]{2,1,0:T(8,128)(2,1)S(1)}, bf16[8,48,640]{2,1,0:T(8,128)(2,1)S(1)}) custom-call(s32[2]{0:T(128)S(1)} %pad_add_fusion.ids, bf16[768,512]{1,0:T(8,128)(2,1)S(1)} %get-tuple-element.183.x0_ref, bf16[768,512]{1,0:T(8,128)(2,1)S(1)} %collective-permute-done.13.x1_ref, bf16[3,384,512]{2,1,0:T(8,128)(2,1)S(1)} %get-tuple-element.174.d0_ref.do_ref, ...), custom_call_target="tpu_custom_call" | custom-call | flops 1950000000 | tf_op jit(solution)/shard_map/vp_grad/pallas_call | solution.py:45
  99.4 1.3 collective-permute-start.21
  100.7 2.5 %collective-permute-done.17.got_ref = bf16[1,192,384]{2,1,0:T(8,128)(2,1)S(1)} collective-permute-done((bf16[1,192,384]{2,1,0:T(8,128)(2,1)S(1)}, bf16[1,192,384]{2,1,0:T(8,128)(2,1)S(1)}, u32[]{:S(2)}, u32[]{:S(2)}) %collective-permute-start.17) | collective-permute-done | bytes 147488 | tf_op jit(solution)/shard_map/ppermute | solution.py:763
  103.8 0.7 add_split.16
  104.6 4.1 %tokens_back.1 = (bf16[2,256,768]{2,1,0:T(8,128)(2,1)}, bf16[256,768]{1,0:T(8,128)(2,1)S(1)}) custom-call(s32[2]{0:T(128)S(1)} %pad_add_fusion.ids, bf16[768,2304]{1,0:T(8,128)(2,1)S(1)} %copy-done, bf16[3,384,512]{2,1,0:T(8,128)(2,1)S(1)} %get-tuple-element.169.ds_ref, bf16[3,384,512]{2,1,0:T(8,128)(2,1)S(1)} %get-tuple-element.174.d0_ref.do_ref, ...), custom_call_target="tpu_custom_call" | custom-call | flops 3900000000 | tf_op jit(solution)/shard_map/tokens_back/pallas_call | solution.py:45
  108.7 0.7 add_split.17
  109.5 0.7 copy-done.18
  110.2 1.4 collective-permute-start.24
  111.6 3.3 %collective-permute-start.23 = (bf16[192,384]{1,0:T(8,128)(2,1)S(1)}, bf16[192,384]{1,0:T(8,128)(2,1)S(1)}, u32[]{:S(2)}, u32[]{:S(2)}) collective-permute-start(bf16[192,384]{1,0:T(8,128)(2,1)S(1)} %add_last.4.mine_ref), channel_id=1, source_target_pairs={{0,1},{1,0},{2,3},{3,2},{4,5},{5,4},{6,7},{7,6},{8,9},{9,8},{10,11... | collective-permute-start | bytes 442376 | tf_op jit(solution)/shard_map/ppermute | solution.py:758
  115.6 0.7 copy-done.20
  116.3 1.2 collective-permute-start.25
  118.2 2.2 %collective-permute-start.26 = (bf16[1,48,1920]{2,1,0:T(8,128)(2,1)S(1)}, bf16[1,48,1920]{2,1,0:T(8,128)(2,1)S(1)}, u32[]{:S(2)}, u32[]{:S(2)}) collective-permute-start(bf16[1,48,1920]{2,1,0:T(8,128)(2,1)S(1)} %get-tuple-element.212), channel_id=1, source_target_pairs={{0,16},{1,9},{2,18},{3,11},{4,20},{5,13},{6,22},{7,15},{8,24},{9,1... | collective-permute-start | bytes 552968 | tf_op jit(solution)/shard_map/ppermute | solution.py:763
  120.3 1.4 join.2
  122.4 1.3 collective-permute-start.27
  124.4 1.2 collective-permute-start.28
  126.1 0.7 collective-permute-start.29
  126.9 1.0 bitcast_dynamic-update-slice_fusion.1
  127.9 3.4 %collective-permute-done.27.got_ref = bf16[2,48,896]{2,1,0:T(8,128)(2,1)S(1)} collective-permute-done((bf16[2,48,896]{2,1,0:T(8,128)(2,1)S(1)}, bf16[2,48,896]{2,1,0:T(8,128)(2,1)S(1)}, u32[]{:S(2)}, u32[]{:S(2)}) %collective-permute-start.27) | collective-permute-done | bytes 172064 | tf_op jit(solution)/shard_map/ppermute | solution.py:763
  132.0 0.9 collective-permute-done.28.got_ref
  134.1 1.4 %join.3 = (f32[48,3072]{1,0:T(8,128)}, f32[48,768]{1,0:T(8,128)}) custom-call(s32[2]{0:T(128)S(1)} %pad_add_fusion.ids, bf16[48,1920]{1,0:T(8,128)(2,1)S(1)} %add_last.5.mine_ref, bf16[48,1920]{1,0:T(8,128)(2,1)S(1)} %collective-permute-done.29.other_ref), custom_call_target="tpu_custom_call" | custom-call | flops 1300000000 | tf_op jit(solution)/shard_map/join/pallas_call | solution.py:45
  137.6 2.2 %collective-permute-start.33 = (bf16[48,640]{1,0:T(8,128)(2,1)S(1)}, bf16[48,640]{1,0:T(8,128)(2,1)S(1)}, u32[]{:S(2)}, u32[]{:S(2)}) collective-permute-start(bf16[48,640]{1,0:T(8,128)(2,1)S(1)} %add_last.7.vo_mine), channel_id=1, source_target_pairs={{0,1},{1,0},{2,3},{3,2},{4,5},{5,4},{6,7},{7,6},{8,9},{9,8},{10,11... | collective-permute-start | bytes 184328 | tf_op jit(solution)/shard_map/ppermute | solution.py:758
  139.8 0.8 collective-permute-done.33.vo_other
  140.6 1.4 join_last.1
  (130 shorter events, 11.6 us)
Async XLA Ops:
  0.6 3.2 %collective-permute-start = (bf16[2,256,768]{2,1,0:T(8,128)(2,1)}, bf16[2,256,768]{2,1,0:T(8,128)(2,1)S(1)}, u32[]{:S(2)}, u32[]{:S(2)}) collective-permute-start(bf16[2,256,768]{2,1,0:T(8,128)(2,1)} %own_ref.3), channel_id=1, source_target_pairs={{0,1},{1,0},{2,3},{3,2},{4,5},{5,4},{6,7},{7,6},{8,9},{9,8},{10,11... | collective-permute-start | bytes 2359304 | tf_op jit(solution)/shard_map/ppermute | solution.py:758
  0.8 21.3 %collective-permute-start.1 = (bf16[2,256,768]{2,1,0:T(8,128)(2,1)}, bf16[2,256,768]{2,1,0:T(8,128)(2,1)S(1)}, u32[]{:S(2)}, u32[]{:S(2)}) collective-permute-start(bf16[2,256,768]{2,1,0:T(8,128)(2,1)} %cown_ref.1), channel_id=1, source_target_pairs={{0,1},{1,0},{2,3},{3,2},{4,5},{5,4},{6,7},{7,6},{8,9},{9,8},{10,11... | collective-permute-start | bytes 2359304 | tf_op jit(solution)/shard_map/ppermute | solution.py:758
  4.2 17.9 %slice-start = ((s8[4718592]{0:T(1024)(128)(4,1)}), s8[4194304]{0:T(1024)(128)(4,1)S(1)}, s32[]{:S(2)}) async-start(s8[4718592]{0:T(1024)(128)(4,1)} %bitcast.6), calls=%async_computation | async-start | bytes 8388608
  4.2 17.9 %slice-start.2 = ((s8[4718592]{0:T(1024)(128)(4,1)}), s8[4194304]{0:T(1024)(128)(4,1)S(1)}, s32[]{:S(2)}) async-start(s8[4718592]{0:T(1024)(128)(4,1)} %bitcast.8), calls=%async_computation.2 | async-start | bytes 8388608
  8.0 14.0 %copy-start.22 = (bf16[512,2304]{1,0:T(8,128)(2,1)}, bf16[512,2304]{1,0:T(8,128)(2,1)S(1)}, u32[]{:S(2)}) copy-start(bf16[512,2304]{1,0:T(8,128)(2,1)S(1)} %get-tuple-element.134.k_ref.v_ref) | copy-start | bytes 7077892
  8.1 14.0 %slice-start.1 = ((s8[4718592]{0:T(1024)(128)(4,1)}), s8[524288]{0:T(1024)(128)(4,1)S(1)}, s32[]{:S(2)}) async-start(s8[4718592]{0:T(1024)(128)(4,1)} %bitcast.6), calls=%async_computation.1 | async-start | bytes 1048576
  8.1 14.0 %slice-start.3 = ((s8[4718592]{0:T(1024)(128)(4,1)}), s8[524288]{0:T(1024)(128)(4,1)S(1)}, s32[]{:S(2)}) async-start(s8[4718592]{0:T(1024)(128)(4,1)} %bitcast.8), calls=%async_computation.3 | async-start | bytes 1048576
  8.1 14.0 %copy-start.1 = (bf16[768,768]{1,0:T(8,128)(2,1)S(1)}, bf16[768,768]{1,0:T(8,128)(2,1)}, u32[]{:S(2)}) copy-start(bf16[768,768]{1,0:T(8,128)(2,1)} %wo_ref.3) | copy-start | bytes 3538948
  8.1 14.0 %copy-start.3 = (bf16[2,256,768]{2,1,0:T(8,128)(2,1)S(1)}, bf16[2,256,768]{2,1,0:T(8,128)(2,1)}, u32[]{:S(2)}) copy-start(bf16[2,256,768]{2,1,0:T(8,128)(2,1)} %cown_ref.1) | copy-start | bytes 2359300
  8.1 14.0 %copy-start.8 = (bf16[3072]{0:T(1024)(128)(2,1)S(1)}, bf16[3072]{0:T(1024)(128)(2,1)}, u32[]{:S(2)}) copy-start(bf16[3072]{0:T(1024)(128)(2,1)} %bi_ref.1) | copy-start | bytes 18436
  8.1 14.0 %copy-start.9 = (bf16[768]{0:T(1024)(128)(2,1)S(1)}, bf16[768]{0:T(1024)(128)(2,1)}, u32[]{:S(2)}) copy-start(bf16[768]{0:T(1024)(128)(2,1)} %bo_ref.1) | copy-start | bytes 4612
  8.2 14.0 %copy-start.10 = (bf16[768]{0:T(1024)(128)(2,1)S(1)}, bf16[768]{0:T(1024)(128)(2,1)}, u32[]{:S(2)}) copy-start(bf16[768]{0:T(1024)(128)(2,1)} %s1_ref.1) | copy-start | bytes 4612
  8.2 14.0 %copy-start.11 = (bf16[768]{0:T(1024)(128)(2,1)S(1)}, bf16[768]{0:T(1024)(128)(2,1)}, u32[]{:S(2)}) copy-start(bf16[768]{0:T(1024)(128)(2,1)} %bd_ref.1) | copy-start | bytes 4612
  8.2 14.0 %copy-start.12 = (bf16[768]{0:T(1024)(128)(2,1)S(1)}, bf16[768]{0:T(1024)(128)(2,1)}, u32[]{:S(2)}) copy-start(bf16[768]{0:T(1024)(128)(2,1)} %g2_ref.1) | copy-start | bytes 4612
  8.2 14.0 %copy-start.13 = (bf16[768]{0:T(1024)(128)(2,1)S(1)}, bf16[768]{0:T(1024)(128)(2,1)}, u32[]{:S(2)}) copy-start(bf16[768]{0:T(1024)(128)(2,1)} %s2_ref.1) | copy-start | bytes 4612
  8.2 14.0 %copy-start.14 = (bf16[768]{0:T(1024)(128)(2,1)S(1)}, bf16[768]{0:T(1024)(128)(2,1)}, u32[]{:S(2)}) copy-start(bf16[768]{0:T(1024)(128)(2,1)} %g1_ref.3) | copy-start | bytes 4612
  34.8 6.2 %collective-permute-start.3 = (bf16[3072,512]{1,0:T(8,128)(2,1)S(1)}, bf16[3072,512]{1,0:T(8,128)(2,1)S(1)}, u32[]{:S(2)}, u32[]{:S(2)}) collective-permute-start(bf16[3072,512]{1,0:T(8,128)(2,1)S(1)} %get-tuple-element.145.a0_ref), channel_id=1, source_target_pairs={{0,1},{1,0},{2,3},{3,2},{4,5},{5,4},{6,7},{7,6},{8,9},{9,8},{10,11... | collective-permute-start | bytes 9437192 | tf_op jit(solution)/shard_map/ppermute | solution.py:758
  34.9 6.1 %collective-permute-start.4 = (bf16[512,384]{1,0:T(8,128)(2,1)S(1)}, bf16[512,384]{1,0:T(8,128)(2,1)S(1)}, u32[]{:S(2)}, u32[]{:S(2)}) collective-permute-start(bf16[512,384]{1,0:T(8,128)(2,1)S(1)} %get-tuple-element.146), channel_id=1, source_target_pairs={{0,1},{1,0},{2,3},{3,2},{4,5},{5,4},{6,7},{7,6},{8,9},{9,8},{10,11... | collective-permute-start | bytes 1179656 | tf_op jit(solution)/shard_map/ppermute | solution.py:758
  39.7 15.3 %collective-permute-start.6 = (bf16[512,1536]{1,0:T(8,128)(2,1)S(1)}, bf16[512,1536]{1,0:T(8,128)(2,1)S(1)}, u32[]{:S(2)}, u32[]{:S(2)}) collective-permute-start(bf16[512,1536]{1,0:T(8,128)(2,1)S(1)} %get-tuple-element.149.dsend_ref), channel_id=1, source_target_pairs={{0,1},{1,0},{2,3},{3,2},{4,5},{5,4},{6,7},{7,6},{8,9},{9,8},{10,11... | collective-permute-start | bytes 4718600 | tf_op jit(solution)/shard_map/ppermute | solution.py:758
  39.9 15.2 %collective-permute-start.7 = (bf16[768,512]{1,0:T(8,128)(2,1)S(1)}, bf16[768,512]{1,0:T(8,128)(2,1)S(1)}, u32[]{:S(2)}, u32[]{:S(2)}) collective-permute-start(bf16[768,512]{1,0:T(8,128)(2,1)S(1)} %get-tuple-element.138.at_ref.a0_ref), channel_id=1, source_target_pairs={{0,1},{1,0},{2,3},{3,2},{4,5},{5,4},{6,7},{7,6},{8,9},{9,8},{10,11... | collective-permute-start | bytes 2359304 | tf_op jit(solution)/shard_map/ppermute | solution.py:758
  40.3 14.7 %collective-permute-start.5 = (bf16[768,512]{1,0:T(8,128)(2,1)S(1)}, bf16[768,512]{1,0:T(8,128)(2,1)S(1)}, u32[]{:S(2)}, u32[]{:S(2)}) collective-permute-start(bf16[768,512]{1,0:T(8,128)(2,1)S(1)} %get-tuple-element.155.f0_ref), channel_id=1, source_target_pairs={{0,1},{1,0},{2,3},{3,2},{4,5},{5,4},{6,7},{7,6},{8,9},{9,8},{10,11... | collective-permute-start | bytes 2359304 | tf_op jit(solution)/shard_map/ppermute | solution.py:758
  45.7 16.4 %collective-permute-start.9 = (bf16[8,192,384]{2,1,0:T(8,128)(2,1)S(1)}, bf16[8,192,384]{2,1,0:T(8,128)(2,1)S(1)}, u32[]{:S(2)}, u32[]{:S(2)}) collective-permute-start(bf16[8,192,384]{2,1,0:T(8,128)(2,1)S(1)} %get-tuple-element.147), channel_id=1, source_target_pairs={{0,2},{1,5},{2,0},{3,7},{4,6},{5,1},{6,4},{7,3},{8,10},{9,13},{10,... | collective-permute-start | bytes 3538952 | tf_op jit(solution)/shard_map/ppermute | solution.py:763
  54.4 2.0 %collective-permute-start.8 = (bf16[512,384]{1,0:T(8,128)(2,1)S(1)}, bf16[512,384]{1,0:T(8,128)(2,1)S(1)}, u32[]{:S(2)}, u32[]{:S(2)}) collective-permute-start(bf16[512,384]{1,0:T(8,128)(2,1)S(1)} %get-tuple-element.157), channel_id=1, source_target_pairs={{0,1},{1,0},{2,3},{3,2},{4,5},{5,4},{6,7},{7,6},{8,9},{9,8},{10,11... | collective-permute-start | bytes 1179656 | tf_op jit(solution)/shard_map/ppermute | solution.py:758
  63.0 25.1 %collective-permute-start.11 = (bf16[8,48,1920]{2,1,0:T(8,128)(2,1)S(1)}, bf16[8,48,1920]{2,1,0:T(8,128)(2,1)S(1)}, u32[]{:S(2)}, u32[]{:S(2)}) collective-permute-start(bf16[8,48,1920]{2,1,0:T(8,128)(2,1)S(1)} %get-tuple-element.177), channel_id=1, source_target_pairs={{0,2},{1,5},{2,0},{3,7},{4,6},{5,1},{6,4},{7,3},{8,10},{9,13},{10,... | collective-permute-start | bytes 4423688 | tf_op jit(solution)/shard_map/ppermute | solution.py:763
  64.4 13.3 %collective-permute-start.10 = (bf16[4,192,384]{2,1,0:T(8,128)(2,1)S(1)}, bf16[4,192,384]{2,1,0:T(8,128)(2,1)S(1)}, u32[]{:S(2)}, u32[]{:S(2)}) collective-permute-start(bf16[4,192,384]{2,1,0:T(8,128)(2,1)S(1)} %get-tuple-element.161), channel_id=1, source_target_pairs={{0,8},{1,9},{2,10},{3,11},{4,12},{5,13},{6,14},{7,15},{8,0},{9,1},... | collective-permute-start | bytes 1769480 | tf_op jit(solution)/shard_map/ppermute | solution.py:763
  72.6 19.1 %collective-permute-start.14 = (bf16[3,384,512]{2,1,0:T(8,128)(2,1)S(1)}, bf16[3,384,512]{2,1,0:T(8,128)(2,1)S(1)}, u32[]{:S(2)}, u32[]{:S(2)}) collective-permute-start(bf16[3,384,512]{2,1,0:T(8,128)(2,1)S(1)} %get-tuple-element.169.ds_ref), channel_id=1, source_target_pairs={{0,1},{1,0},{2,3},{3,2},{4,5},{5,4},{6,7},{7,6},{8,9},{9,8},{10,11... | collective-permute-start | bytes 3538952 | tf_op jit(solution)/shard_map/ppermute | solution.py:758
  74.4 17.2 %collective-permute-start.13 = (bf16[768,512]{1,0:T(8,128)(2,1)S(1)}, bf16[768,512]{1,0:T(8,128)(2,1)S(1)}, u32[]{:S(2)}, u32[]{:S(2)}) collective-permute-start(bf16[768,512]{1,0:T(8,128)(2,1)S(1)} %get-tuple-element.183.x0_ref), channel_id=1, source_target_pairs={{0,1},{1,0},{2,3},{3,2},{4,5},{5,4},{6,7},{7,6},{8,9},{9,8},{10,11... | collective-permute-start | bytes 2359304 | tf_op jit(solution)/shard_map/ppermute | solution.py:758
  78.4 12.6 %collective-permute-start.12 = (bf16[2,192,384]{2,1,0:T(8,128)(2,1)S(1)}, bf16[2,192,384]{2,1,0:T(8,128)(2,1)S(1)}, u32[]{:S(2)}, u32[]{:S(2)}) collective-permute-start(bf16[2,192,384]{2,1,0:T(8,128)(2,1)S(1)} %get-tuple-element.172), channel_id=1, source_target_pairs={{0,4},{1,3},{2,6},{3,1},{4,0},{5,7},{6,2},{7,5},{8,12},{9,11},{10,... | collective-permute-start | bytes 884744 | tf_op jit(solution)/shard_map/ppermute | solution.py:763
  89.2 14.6 %collective-permute-start.18 = (bf16[4,48,1920]{2,1,0:T(8,128)(2,1)S(1)}, bf16[4,48,1920]{2,1,0:T(8,128)(2,1)S(1)}, u32[]{:S(2)}, u32[]{:S(2)}) collective-permute-start(bf16[4,48,1920]{2,1,0:T(8,128)(2,1)S(1)} %get-tuple-element.178), channel_id=1, source_target_pairs={{0,4},{1,3},{2,6},{3,1},{4,0},{5,7},{6,2},{7,5},{8,12},{9,11},{10,... | collective-permute-start | bytes 2211848 | tf_op jit(solution)/shard_map/ppermute | solution.py:763
  89.3 7.6 %collective-permute-start.15 = (bf16[256,384]{1,0:T(8,128)(2,1)S(1)}, bf16[256,384]{1,0:T(8,128)(2,1)S(1)}, u32[]{:S(2)}, u32[]{:S(2)}) collective-permute-start(bf16[256,384]{1,0:T(8,128)(2,1)S(1)} %get-tuple-element.192), channel_id=1, source_target_pairs={{0,1},{1,0},{2,3},{3,2},{4,5},{5,4},{6,7},{7,6},{8,9},{9,8},{10,11... | collective-permute-start | bytes 589832 | tf_op jit(solution)/shard_map/ppermute | solution.py:758
  91.0 5.9 %collective-permute-start.16 = (bf16[256,384]{1,0:T(8,128)(2,1)S(1)}, bf16[256,384]{1,0:T(8,128)(2,1)S(1)}, u32[]{:S(2)}, u32[]{:S(2)}) collective-permute-start(bf16[256,384]{1,0:T(8,128)(2,1)S(1)} %get-tuple-element.194), channel_id=1, source_target_pairs={{0,1},{1,0},{2,3},{3,2},{4,5},{5,4},{6,7},{7,6},{8,9},{9,8},{10,11... | collective-permute-start | bytes 589832 | tf_op jit(solution)/shard_map/ppermute | solution.py:758
  94.3 14.4 %collective-permute-start.20 = (bf16[8,48,896]{2,1,0:T(8,128)(2,1)S(1)}, bf16[8,48,896]{2,1,0:T(8,128)(2,1)S(1)}, u32[]{:S(2)}, u32[]{:S(2)}) collective-permute-start(bf16[8,48,896]{2,1,0:T(8,128)(2,1)S(1)} %get-tuple-element.189), channel_id=1, source_target_pairs={{0,2},{1,5},{2,0},{3,7},{4,6},{5,1},{6,4},{7,3},{8,10},{9,13},{10,... | collective-permute-start | bytes 2064392 | tf_op jit(solution)/shard_map/ppermute | solution.py:763
  94.4 8.8 %collective-permute-start.17 = (bf16[1,192,384]{2,1,0:T(8,128)(2,1)S(1)}, bf16[1,192,384]{2,1,0:T(8,128)(2,1)S(1)}, u32[]{:S(2)}, u32[]{:S(2)}) collective-permute-start(bf16[1,192,384]{2,1,0:T(8,128)(2,1)S(1)} %get-tuple-element.181), channel_id=1, source_target_pairs={{0,16},{1,17},{2,18},{3,19},{4,20},{5,21},{6,22},{7,23},{8,24},{9,... | collective-permute-start | bytes 442376 | tf_op jit(solution)/shard_map/ppermute | solution.py:763
  99.4 15.5 %collective-permute-start.21 = (bf16[8,48,640]{2,1,0:T(8,128)(2,1)S(1)}, bf16[8,48,640]{2,1,0:T(8,128)(2,1)S(1)}, u32[]{:S(2)}, u32[]{:S(2)}) collective-permute-start(bf16[8,48,640]{2,1,0:T(8,128)(2,1)S(1)} %get-tuple-element.195), channel_id=1, source_target_pairs={{0,2},{1,5},{2,0},{3,7},{4,6},{5,1},{6,4},{7,3},{8,10},{9,13},{10,... | collective-permute-start | bytes 1474568 | tf_op jit(solution)/shard_map/ppermute | solution.py:763
  104.5 13.0 %collective-permute-start.22 = (bf16[2,48,1920]{2,1,0:T(8,128)(2,1)S(1)}, bf16[2,48,1920]{2,1,0:T(8,128)(2,1)S(1)}, u32[]{:S(2)}, u32[]{:S(2)}) collective-permute-start(bf16[2,48,1920]{2,1,0:T(8,128)(2,1)S(1)} %get-tuple-element.200), channel_id=1, source_target_pairs={{0,8},{1,17},{2,10},{3,19},{4,12},{5,21},{6,14},{7,23},{8,0},{9,25... | collective-permute-start | bytes 1105928 | tf_op jit(solution)/shard_map/ppermute | solution.py:763
  110.2 11.5 %collective-permute-start.24 = (bf16[4,48,896]{2,1,0:T(8,128)(2,1)S(1)}, bf16[4,48,896]{2,1,0:T(8,128)(2,1)S(1)}, u32[]{:S(2)}, u32[]{:S(2)}) collective-permute-start(bf16[4,48,896]{2,1,0:T(8,128)(2,1)S(1)} %get-tuple-element.206), channel_id=1, source_target_pairs={{0,4},{1,3},{2,6},{3,1},{4,0},{5,7},{6,2},{7,5},{8,12},{9,11},{10,... | collective-permute-start | bytes 1032200 | tf_op jit(solution)/shard_map/ppermute | solution.py:763
  111.6 6.6 %collective-permute-start.23 = (bf16[192,384]{1,0:T(8,128)(2,1)S(1)}, bf16[192,384]{1,0:T(8,128)(2,1)S(1)}, u32[]{:S(2)}, u32[]{:S(2)}) collective-permute-start(bf16[192,384]{1,0:T(8,128)(2,1)S(1)} %add_last.4.mine_ref), channel_id=1, source_target_pairs={{0,1},{1,0},{2,3},{3,2},{4,5},{5,4},{6,7},{7,6},{8,9},{9,8},{10,11... | collective-permute-start | bytes 442376 | tf_op jit(solution)/shard_map/ppermute | solution.py:758
  114.9 12.0 %collective-permute-start.2 = (bf16[256,768]{1,0:T(8,128)(2,1)S(1)}, bf16[256,768]{1,0:T(8,128)(2,1)}, u32[]{:S(2)}, u32[]{:S(2)}) collective-permute-start(bf16[256,768]{1,0:T(8,128)(2,1)S(1)} %get-tuple-element.140), channel_id=1, source_target_pairs={{0,1},{1,0},{2,3},{3,2},{4,5},{5,4},{6,7},{7,6},{8,9},{9,8},{10,11... | collective-permute-start | bytes 1179656 | tf_op jit(solution)/shard_map/ppermute | solution.py:758
  116.3 7.4 %collective-permute-start.25 = (bf16[4,48,640]{2,1,0:T(8,128)(2,1)S(1)}, bf16[4,48,640]{2,1,0:T(8,128)(2,1)S(1)}, u32[]{:S(2)}, u32[]{:S(2)}) collective-permute-start(bf16[4,48,640]{2,1,0:T(8,128)(2,1)S(1)} %get-tuple-element.209), channel_id=1, source_target_pairs={{0,4},{1,3},{2,6},{3,1},{4,0},{5,7},{6,2},{7,5},{8,12},{9,11},{10,... | collective-permute-start | bytes 737288 | tf_op jit(solution)/shard_map/ppermute | solution.py:763
  117.5 22.2 %collective-permute-start.19 = (bf16[256,768]{1,0:T(8,128)(2,1)S(1)}, bf16[256,768]{1,0:T(8,128)(2,1)S(1)}, u32[]{:S(2)}, u32[]{:S(2)}) collective-permute-start(bf16[256,768]{1,0:T(8,128)(2,1)S(1)} %get-tuple-element.203), channel_id=1, source_target_pairs={{0,1},{1,0},{2,3},{3,2},{4,5},{5,4},{6,7},{7,6},{8,9},{9,8},{10,11... | collective-permute-start | bytes 1179656 | tf_op jit(solution)/shard_map/ppermute | solution.py:758
  118.2 7.4 %collective-permute-start.26 = (bf16[1,48,1920]{2,1,0:T(8,128)(2,1)S(1)}, bf16[1,48,1920]{2,1,0:T(8,128)(2,1)S(1)}, u32[]{:S(2)}, u32[]{:S(2)}) collective-permute-start(bf16[1,48,1920]{2,1,0:T(8,128)(2,1)S(1)} %get-tuple-element.212), channel_id=1, source_target_pairs={{0,16},{1,9},{2,18},{3,11},{4,20},{5,13},{6,22},{7,15},{8,24},{9,1... | collective-permute-start | bytes 552968 | tf_op jit(solution)/shard_map/ppermute | solution.py:763
  122.4 8.9 %collective-permute-start.27 = (bf16[2,48,896]{2,1,0:T(8,128)(2,1)S(1)}, bf16[2,48,896]{2,1,0:T(8,128)(2,1)S(1)}, u32[]{:S(2)}, u32[]{:S(2)}) collective-permute-start(bf16[2,48,896]{2,1,0:T(8,128)(2,1)S(1)} %get-tuple-element.216), channel_id=1, source_target_pairs={{0,8},{1,17},{2,10},{3,19},{4,12},{5,21},{6,14},{7,23},{8,0},{9,25... | collective-permute-start | bytes 516104 | tf_op jit(solution)/shard_map/ppermute | solution.py:763
  124.4 8.6 %collective-permute-start.28 = (bf16[2,48,640]{2,1,0:T(8,128)(2,1)S(1)}, bf16[2,48,640]{2,1,0:T(8,128)(2,1)S(1)}, u32[]{:S(2)}, u32[]{:S(2)}) collective-permute-start(bf16[2,48,640]{2,1,0:T(8,128)(2,1)S(1)} %get-tuple-element.219), channel_id=1, source_target_pairs={{0,8},{1,17},{2,10},{3,19},{4,12},{5,21},{6,14},{7,23},{8,0},{9,25... | collective-permute-start | bytes 368648 | tf_op jit(solution)/shard_map/ppermute | solution.py:763
  126.1 8.0 %collective-permute-start.29 = (bf16[48,1920]{1,0:T(8,128)(2,1)S(1)}, bf16[48,1920]{1,0:T(8,128)(2,1)S(1)}, u32[]{:S(2)}, u32[]{:S(2)}) collective-permute-start(bf16[48,1920]{1,0:T(8,128)(2,1)S(1)} %add_last.5.mine_ref), channel_id=1, source_target_pairs={{0,1},{1,0},{2,3},{3,2},{4,5},{5,4},{6,7},{7,6},{8,9},{9,8},{10,11... | collective-permute-start | bytes 552968 | tf_op jit(solution)/shard_map/ppermute | solution.py:758
  131.9 4.1 %collective-permute-start.30 = (bf16[1,48,896]{2,1,0:T(8,128)(2,1)S(1)}, bf16[1,48,896]{2,1,0:T(8,128)(2,1)S(1)}, u32[]{:S(2)}, u32[]{:S(2)}) collective-permute-start(bf16[1,48,896]{2,1,0:T(8,128)(2,1)S(1)} %get-tuple-element.224), channel_id=1, source_target_pairs={{0,16},{1,9},{2,18},{3,11},{4,20},{5,13},{6,22},{7,15},{8,24},{9,1... | collective-permute-start | bytes 258056 | tf_op jit(solution)/shard_map/ppermute | solution.py:763
  133.5 3.5 %collective-permute-start.32 = (bf16[1,48,640]{2,1,0:T(8,128)(2,1)S(1)}, bf16[1,48,640]{2,1,0:T(8,128)(2,1)S(1)}, u32[]{:S(2)}, u32[]{:S(2)}) collective-permute-start(bf16[1,48,640]{2,1,0:T(8,128)(2,1)S(1)} %get-tuple-element.227), channel_id=1, source_target_pairs={{0,16},{1,9},{2,18},{3,11},{4,20},{5,13},{6,22},{7,15},{8,24},{9,1... | collective-permute-start | bytes 184328 | tf_op jit(solution)/shard_map/ppermute | solution.py:763
  136.6 4.0 %collective-permute-start.31 = (bf16[48,896]{1,0:T(8,128)(2,1)S(1)}, bf16[48,896]{1,0:T(8,128)(2,1)S(1)}, u32[]{:S(2)}, u32[]{:S(2)}) collective-permute-start(bf16[48,896]{1,0:T(8,128)(2,1)S(1)} %add_last.6.qk_mine), channel_id=1, source_target_pairs={{0,1},{1,0},{2,3},{3,2},{4,5},{5,4},{6,7},{7,6},{8,9},{9,8},{10,11... | collective-permute-start | bytes 258056 | tf_op jit(solution)/shard_map/ppermute | solution.py:758
  137.6 3.1 %collective-permute-start.33 = (bf16[48,640]{1,0:T(8,128)(2,1)S(1)}, bf16[48,640]{1,0:T(8,128)(2,1)S(1)}, u32[]{:S(2)}, u32[]{:S(2)}) collective-permute-start(bf16[48,640]{1,0:T(8,128)(2,1)S(1)} %add_last.7.vo_mine), channel_id=1, source_target_pairs={{0,1},{1,0},{2,3},{3,2},{4,5},{5,4},{6,7},{7,6},{8,9},{9,8},{10,11... | collective-permute-start | bytes 184328 | tf_op jit(solution)/shard_map/ppermute | solution.py:758
  (22 other events, 89.2 us)
